TPU v7x, 32 devices: a whole 2x2x4 slice. The times are simulated.
32 devices in a mesh: groups: 2 (over y), outer: 4 (over z), local: 4 (over x, core).
Axes of the slice: x: 2, y: 2, z: 4, core: 2. Of those that a mesh axis runs over, the one named last changes fastest.
Arguments:
- tokens: bfloat16 [2048, 3584], P(('groups', 'outer', 'local')), parts along dimension 0, may hold values from -6 to 6
- routes: int32 [2048, 8], P(('groups', 'outer', 'local')), parts along dimension 0, may hold values from 0 to 31, as said below
- combine_fixed: int32 [2048, 8], P(('groups', 'outer', 'local')), parts along dimension 0, may hold values from 1 to 65535
- gate_weight: bfloat16 [4, 3584, 1024], P('outer', None, 'local'), may hold values from -0.09375 to 0.09375
- up_weight: bfloat16 [4, 3584, 1024], P('outer', None, 'local'), may hold values from -0.09375 to 0.09375
- down_weight: bfloat16 [4, 1024, 3584], P('outer', None, 'local'), may hold values from -0.1875 to 0.1875
Outputs:
- combined: float32 [2048, 3584], P(('groups', 'outer', 'local')), parts along dimension 0
There are 2 independent parts, one for each index of `groups`. A program takes and returns all parts, laid end to end along the dimension named above; an argument that names none is the same for every part. Nothing has to cross between parts.
Inputs may be any that keep to these rules, and one draw needn't show every extreme that they name: `routes`: each row names 8 different experts, lying in at most 4 pods (expert e lies in pod e // 8). The tokens of one device name the round's expert of one pod (an e with e % 8 == 0) at most 24 times, and on every device some pod reaches 24. `combine_fixed`: A route's combine weight is this value times 2**-16.
All inputs are finite; a program needn't handle non-finite values.
Results may differ from a plain program's by a relative error of at most 0.004.
Values may be sent and summed in bfloat16 or wider, within the bound.
No kernel may reach another device: no remote copies, remote signals or barrier semaphores. Data moves between devices by JAX's collectives and lax.ppermute only.
A program may use at most 64 MiB of HBM per device.

v0:
```python
import jax
import jax.numpy as jnp
from jax import lax
from jax.sharding import PartitionSpec as P

EXP_POD = 8


def per_device(tokens, routes, combine_fixed, gate_weight, up_weight, down_weight):
    tok_rows = tokens.shape[0]
    pod_count = lax.axis_size("outer")
    capacity = 3 * tok_rows // (2 * pod_count)
    route_share = combine_fixed.astype(jnp.float32) * (1.0 / 65536.0)
    targets = jnp.arange(pod_count, dtype=jnp.int32) * EXP_POD
    hit_mask = routes[:, :, None] == targets[None, None, :]
    pod_weight = jnp.sum(jnp.where(hit_mask, route_share[:, :, None], 0.0), axis=1)
    is_live = jnp.any(hit_mask, axis=1).astype(jnp.int32)
    slot_index = jnp.where(is_live == 1, jnp.cumsum(is_live, axis=0) - 1, -1)
    placing = slot_index[:, :, None] == jnp.arange(capacity, dtype=jnp.int32)[None, None, :]
    panels = jnp.einsum(
        "tqc,td->qcd", placing.astype(jnp.bfloat16), tokens, preferred_element_type=jnp.float32
    ).astype(jnp.bfloat16)
    gate_local = gate_weight[0]
    up_local = up_weight[0]
    down_local = down_weight[0]
    pod_panels = lax.all_gather(panels[None], "local", axis=0, tiled=True)
    arrived = lax.all_to_all(pod_panels, "outer", split_axis=1, concat_axis=1, tiled=True)
    flat_rows = arrived.reshape(-1, arrived.shape[3])
    gate_proj = jnp.dot(flat_rows, gate_local, preferred_element_type=jnp.float32)
    up_proj = jnp.dot(flat_rows, up_local, preferred_element_type=jnp.float32)
    hidden_part = (jax.nn.silu(gate_proj) * up_proj).astype(jnp.bfloat16)
    summed = jnp.dot(
        lax.all_gather(hidden_part, "local", axis=1, tiled=True),
        down_local,
        preferred_element_type=jnp.float32,
    )
    expert_out = summed.astype(jnp.bfloat16).reshape(-1, pod_count, capacity, down_local.shape[1])
    back = lax.all_to_all(
        lax.all_to_all(expert_out, "outer", split_axis=1, concat_axis=1, tiled=True),
        "local",
        split_axis=0,
        concat_axis=3,
        tiled=True,
    )
    returned = back[0]
    weighted = jnp.where(placing, pod_weight[:, :, None], 0.0)
    combined = jnp.einsum(
        "tqc,qcd->td", weighted, returned.astype(jnp.float32), precision=lax.Precision.HIGHEST
    )
    return combined


def solution(mesh):
    in_specs = (
        P(("groups", "outer", "local"), None),
        P(("groups", "outer", "local"), None),
        P(("groups", "outer", "local"), None),
        P("outer", None, "local"),
        P("outer", None, "local"),
        P("outer", None, "local"),
    )
    out_specs = P(("groups", "outer", "local"), None)
    return jax.shard_map(
        per_device, mesh=mesh, in_specs=in_specs, out_specs=out_specs, check_vma=False
    )
```

profile of v0, /device:TPU:0, one launch (start us, length us, event | category | flops | bytes accessed | tf_op | source)
XLA Modules:
  0.0 165.9 jit_solution(12718292717512129914)
XLA Ops:
  6.5 0.0 copy-start
  6.5 0.0 all-gather.3.cloned.1.call-start
  6.5 0.9 compare_reduce_fusion
  7.5 0.1 copy.41
  7.6 0.1 reduce_window_sum.11
  7.7 0.1 copy.42
  7.7 2.2 %convolution_convert_fusion = bf16[4,24,3584]{2,1,0:T(8,128)(2,1)} fusion(bf16[64,3584]{1,0:T(8,128)(2,1)} %param.6, s32[64,4]{0,1:T(4,128)S(1)} %add_select_fusion), kind=kOutput, calls=%fused_computation | convolution fusion | flops 44390400 | bytes 1147904 | tf_op jit(solution)/shard_map/tqc,td->qcd/dot_general | solution.py:20
  9.9 0.0 all-gather.3.cloned.1.call-update
  9.9 29.2 %all-gather.3.cloned.1.call-done = bf16[16,24,3584]{2,1,0:T(8,128)(2,1)} async-done(((bf16[4,24,3584]{2,1,0:T(8,128)(2,1)}), bf16[16,24,3584]{2,1,0:T(8,128)(2,1)}) %all-gather.3.cloned.1.call-update) | async-done | bytes 2752528 | tf_op jit(solution)/shard_map/all_gather | solution.py:26
  39.1 2.0 %copy.43 = bf16[4,4,24,3584]{3,2,0,1:T(8,128)(2,1)S(1)} copy(bf16[4,4,24,3584]{3,2,1,0:T(8,128)(2,1)} %bitcast.30) | data formatting | bytes 5505024 | tf_op jit(solution)/shard_map/all_gather | solution.py:26
  41.1 67.0 %all_to_all.25 = bf16[4,4,24,3584]{3,2,0,1:T(8,128)(2,1)S(1)} all-to-all(bf16[4,4,24,3584]{3,2,0,1:T(8,128)(2,1)S(1)} %copy.43), channel_id=1, replica_groups=mesh['groups'=2,'outer'=4,'local'=4] {'outer'}, dimensions={1} | all-to-all | bytes 5505024 | tf_op jit(solution)/shard_map/all_to_all | solution.py:27
  108.2 0.2 copy.44
  108.4 1.3 copy-done.3
  109.7 0.9 fusion.4
  110.5 0.6 copy-done.4
  111.2 0.9 fusion.12
  112.0 7.7 %all_gather.7 = bf16[384,1024]{1,0:T(8,128)(2,1)S(1)} all-gather(bf16[384,256]{1,0:T(8,128)(2,1)S(1)} %fusion.12), channel_id=1, replica_groups=mesh['groups'=2,'outer'=4,'local'=4] {'local'}, dimensions={1}, use_global_device_ids=true | all-gather | bytes 983040 | tf_op jit(solution)/shard_map/all_gather | solution.py:33
  119.7 0.0 copy-done
  119.7 1.0 fusion.6
  120.7 0.1 copy.45
  120.8 0.0 copy-start.2
  120.8 0.0 copy-start.1
  120.8 21.2 %all_to_all.26 = bf16[4,4,24,896]{3,2,0,1:T(8,128)(2,1)S(1)} all-to-all(bf16[4,4,24,896]{3,2,0,1:T(8,128)(2,1)S(1)} %copy.45), channel_id=1, replica_groups=mesh['groups'=2,'outer'=4,'local'=4] {'outer'}, dimensions={1} | all-to-all | bytes 1376256 | tf_op jit(solution)/shard_map/all_to_all | solution.py:39
  142.0 0.9 copy.46
  142.9 3.5 %all-to-all-start.2 = ((bf16[4,4,24,896]{3,2,1,0:T(8,128)(2,1)}), bf16[4,4,24,896]{3,2,1,0:T(8,128)(2,1)S(1)}, u32[]{:S(2)}, u32[]{:S(2)}) async-start(bf16[4,4,24,896]{3,2,1,0:T(8,128)(2,1)} %copy.46), calls=%async_computation.2 | async-start | bytes 1376256 | tf_op jit(solution)/shard_map/all_to_all | solution.py:38
  146.4 0.0 copy-done.2
  146.4 0.0 copy-done.1
  146.4 0.1 fusion.21
  146.5 10.4 %all-to-all-done.2 = bf16[4,4,24,896]{3,2,1,0:T(8,128)(2,1)S(1)} async-done(((bf16[4,4,24,896]{3,2,1,0:T(8,128)(2,1)}), bf16[4,4,24,896]{3,2,1,0:T(8,128)(2,1)S(1)}, u32[]{:S(2)}, u32[]{:S(2)}) %all-to-all-start.2) | async-done | bytes 688160 | tf_op jit(solution)/shard_map/all_to_all | solution.py:38
  156.9 0.4 copy.47
  157.3 0.3 squeeze.15
  157.6 1.5 convolution_bitcast_fusion
  (6 shorter events, 0.0 us)
Async XLA Ops:
  6.5 113.2 %copy-start = (bf16[1,1024,896]{2,1,0:T(8,128)(2,1)S(1)}, bf16[1,1024,896]{2,1,0:T(8,128)(2,1)}, u32[]{:S(2)}) copy-start(bf16[1,1024,896]{2,1,0:T(8,128)(2,1)} %param.11) | copy-start | bytes 5505028
  6.5 32.6 %all-gather.3.cloned.1.call-start = ((), (), s32[]{:S(2)}) async-start(), calls=%async_computation.3 | async-start | bytes 3440640 | tf_op jit(solution)/shard_map/all_gather | solution.py:26
  108.2 1.5 copy-start.3
  109.7 1.5 copy-start.4
  120.8 25.6 %copy-start.2 = (s32[64,8]{0,1:T(8,128)S(1)}, s32[64,8]{0,1:T(8,128)}, u32[]{:S(2)}) copy-start(s32[64,8]{0,1:T(8,128)} %param.8) | copy-start | bytes 6148
  120.8 25.6 %copy-start.1 = (s32[64,8]{0,1:T(8,128)S(1)}, s32[64,8]{0,1:T(8,128)}, u32[]{:S(2)}) copy-start(s32[64,8]{0,1:T(8,128)} %param.7) | copy-start | bytes 6148
  142.9 14.1 %all-to-all-start.2 = ((bf16[4,4,24,896]{3,2,1,0:T(8,128)(2,1)}), bf16[4,4,24,896]{3,2,1,0:T(8,128)(2,1)S(1)}, u32[]{:S(2)}, u32[]{:S(2)}) async-start(bf16[4,4,24,896]{3,2,1,0:T(8,128)(2,1)} %copy.46), calls=%async_computation.2 | async-start | bytes 1376256 | tf_op jit(solution)/shard_map/all_to_all | solution.py:38
Sparse Core Ops, SparseCore 0:
  10.1 28.9 all-gather.2
where the time goes:
time: 166 us
  blocking collectives  95.9 us (58%)
  waiting for transfers between devices  39.6 us (24%)
  between operations  13.5 us (8%)
  matrix products  6.41 us (4%)
  local copies, waits for them, and re-layouts  5.88 us (4%)
  starting transfers between devices  3.49 us (2%)
    all_to_all x1, blocking collectives, per_device(): lax.all_to_all(pod_panels, 'outer', split_axis=1, concat_axis=1, tiled=True)  67 us
    all_gather x1, waiting for transfers between devices, per_device(): pod_panels = lax.all_gather(panels[None], 'local', axis=0, tiled=True)  29.2 us
    all_to_all x1, blocking collectives, per_device(): lax.all_to_all(expert_out, 'outer', split_axis=1, concat_axis=1, tiled=True)  21.2 us
    all_to_all x1, waiting for transfers between devices, per_device(): lax.all_to_all(lax.all_to_all(expert_out, 'outer', split_axis=1, concat_a...  10.4 us
    all_gather x1, blocking collectives, per_device(): lax.all_gather(hidden_part, 'local', axis=1, tiled=True)  7.66 us
    all_to_all x1, starting transfers between devices, per_device(): lax.all_to_all(lax.all_to_all(expert_out, 'outer', split_axis=1, concat_a...  3.49 us
  transfers between devices with their start and end apart: 2, of which 2 were waited for; matrix products, arithmetic and copies ran while one was open for 0% of the time, Pallas kernels for 0%

commit v1 on v0

v1 whole, which is shorter than its diff:
```python
import jax
import jax.numpy as jnp
from jax import lax
from jax.sharding import PartitionSpec as P

EXP_POD = 8


def per_device(tokens, routes, combine_fixed, gate_weight, up_weight, down_weight):
    tok_rows, width = tokens.shape
    n_out = lax.axis_size("outer")
    n_loc = lax.axis_size("local")
    capacity = 3 * tok_rows // (2 * n_out)
    part_out = down_weight.shape[2]
    part_hid = gate_weight.shape[2]
    z = lax.axis_index("outer")
    l = lax.axis_index("local")
    gate_local = gate_weight[0]
    up_local = up_weight[0]
    down_local = jnp.concatenate(
        [lax.dynamic_slice_in_dim(down_weight[0], (l ^ m) * part_hid, part_hid, 0) for m in range(n_loc)], axis=0
    )

    targets = (z ^ jnp.arange(n_out, dtype=jnp.int32)) * EXP_POD
    hit_mask = routes[:, :, None] == targets[None, None, :]
    fixed = jnp.sum(jnp.where(hit_mask, combine_fixed[:, :, None], 0), axis=1)
    is_live = jnp.any(hit_mask, axis=1).astype(jnp.int32)
    slot_index = jnp.where(is_live == 1, jnp.cumsum(is_live, axis=0) - 1, -1)
    placing = slot_index[:, :, None] == jnp.arange(capacity, dtype=jnp.int32)[None, None, :]
    panels = jnp.einsum(
        "tqc,td->qcd", placing.astype(jnp.bfloat16), tokens, preferred_element_type=jnp.float32
    ).astype(jnp.bfloat16)

    def outer_xor(v, s):
        return lax.ppermute(v, "outer", [(i, i ^ s) for i in range(n_out)])

    def local_xor(v, m):
        return lax.ppermute(v, "local", [(i, i ^ m) for i in range(n_loc)])

    def both_xor(v, s, m):
        if s == 0 and m == 0:
            return v
        pairs = [(a * n_loc + b, (a ^ s) * n_loc + (b ^ m)) for a in range(n_out) for b in range(n_loc)]
        return lax.ppermute(v, ("outer", "local"), pairs)

    group = max(1, n_out // 4)
    chunks = [list(range(g, g + group)) for g in range(0, n_out, group)]
    pieces = {}
    for steps in chunks:
        mine = jnp.stack([panels[s] if s == 0 else outer_xor(panels[s], s) for s in steps])
        blocks = [None] * n_loc
        for m in range(0, n_loc, 2):
            blocks[m] = mine if m == 0 else local_xor(mine, m)
        for m in range(0, n_loc, 2):
            blocks[m + 1] = local_xor(blocks[m], 1)
        rows = jnp.stack(blocks).reshape(-1, width)
        gate_proj = jnp.dot(rows, gate_local, preferred_element_type=jnp.float32)
        up_proj = jnp.dot(rows, up_local, preferred_element_type=jnp.float32)
        hidden = (jax.nn.silu(gate_proj) * up_proj).astype(jnp.bfloat16)
        parts = [hidden if m == 0 else local_xor(hidden, m) for m in range(n_loc)]
        parts = [v.reshape(n_loc, -1, part_hid) for v in parts]
        full = jnp.concatenate(
            [jnp.concatenate([parts[m][j ^ m] for m in range(n_loc)], axis=1) for j in range(n_loc)], axis=0
        )
        expert_out = jnp.dot(full, down_local, preferred_element_type=jnp.float32).astype(jnp.bfloat16)
        expert_out = expert_out.reshape(n_loc, len(steps), capacity, part_out)
        for at, s in enumerate(steps):
            for m in range(n_loc):
                pieces[s, m] = both_xor(expert_out[m, at], s, m)

    spread = jnp.where(placing, fixed[:, :, None], 0).reshape(tok_rows, -1)
    high = (spread >> 8).astype(jnp.bfloat16)
    low = (spread & 255).astype(jnp.bfloat16)
    combined = jnp.zeros((tok_rows, width), jnp.float32)
    for m in range(n_loc):
        returned = jnp.concatenate([pieces[s, m] for s in range(n_out)], axis=0)
        block = jnp.dot(high, returned, preferred_element_type=jnp.float32) * (1.0 / 256.0)
        block += jnp.dot(low, returned, preferred_element_type=jnp.float32) * (1.0 / 65536.0)
        combined = lax.dynamic_update_slice(combined, block, (0, (l ^ m) * part_out))
    return combined


def solution(mesh):
    in_specs = (
        P(("groups", "outer", "local"), None),
        P(("groups", "outer", "local"), None),
        P(("groups", "outer", "local"), None),
        P("outer", None, "local"),
        P("outer", None, "local"),
        P("outer", None, "local"),
    )
    out_specs = P(("groups", "outer", "local"), None)
    return jax.shard_map(
        per_device, mesh=mesh, in_specs=in_specs, out_specs=out_specs, check_vma=False
    )
```

time: 166 us -> 99.8 us (0.60)
  blocking collectives: 95.9 us -> 0 us
  starting transfers between devices: 3.49 us -> 46.1 us
  between operations: 13.5 us -> 0.47 us
  waiting for transfers between devices: 39.6 us -> 33 us
  other arithmetic: 1.11 us -> 5.73 us
  matrix products: 6.41 us -> 9.02 us
    all_to_all x2 -> x0, blocking collectives: 88.2 us -> none  [the longest x1 67 us: per_device(): lax.all_to_all(pod_panels, 'outer', split_axis=1, concat_axis=1, tiled=True)]
    ppermute x0 -> x42, starting transfers between devices: none -> 46.1 us  [the longest x15 21.6 us: both_xor(): return lax.ppermute(v, ('outer', 'local'), pairs)]
    ppermute x0 -> x42, waiting for transfers between devices: none -> 33 us  [the longest x15 25.9 us: both_xor(): return lax.ppermute(v, ('outer', 'local'), pairs)]
    all_gather x1 -> x0, waiting for transfers between devices: 29.2 us -> none  [per_device(): pod_panels = lax.all_gather(panels[None], 'local', axis=0, tiled=True)]
    all_to_all x1 -> x0, waiting for transfers between devices: 10.4 us -> none  [per_device(): lax.all_to_all(lax.all_to_all(expert_out, 'outer', split_axis=1, concat_a...]
    all_gather x1 -> x0, blocking collectives: 7.66 us -> none  [per_device(): lax.all_gather(hidden_part, 'local', axis=1, tiled=True)]
    another operation x0 -> x4, other arithmetic: none -> 4.54 us  [per_device(): rows = jnp.stack(blocks).reshape(-1, width)]
    all_to_all x1 -> x0, starting transfers between devices: 3.49 us -> none  [per_device(): lax.all_to_all(lax.all_to_all(expert_out, 'outer', split_axis=1, concat_a...]
  transfers between devices with their start and end apart: 2 -> 42, of which waited for: 2 -> 13; matrix products, arithmetic and copies ran while one was open for 0% -> 13% of each run, Pallas kernels for 0% -> 0%
where the time goes in v1:
time: 99.8 us; the launch traced here: 99.5 us
  starting transfers between devices  46.1 us (46%)
  waiting for transfers between devices  33 us (33%)
  matrix products  9.02 us (9%)
  other arithmetic  5.73 us (6%)
  local copies, waits for them, and re-layouts  5.17 us (5%)
    ppermute x15, waiting for transfers between devices, both_xor(): return lax.ppermute(v, ('outer', 'local'), pairs)  25.9 us
    ppermute x15, starting transfers between devices, both_xor(): return lax.ppermute(v, ('outer', 'local'), pairs)  21.6 us
    ppermute x24, starting transfers between devices, local_xor(): return lax.ppermute(v, 'local', [(i, i ^ m) for i in range(n_loc)])  16.4 us
    ppermute x3, starting transfers between devices, outer_xor(): return lax.ppermute(v, 'outer', [(i, i ^ s) for i in range(n_out)])  8.03 us
    ppermute x24, waiting for transfers between devices, local_xor(): return lax.ppermute(v, 'local', [(i, i ^ m) for i in range(n_loc)])  7.13 us
    another operation x4, other arithmetic, per_device(): rows = jnp.stack(blocks).reshape(-1, width)  4.54 us
  transfers between devices with their start and end apart: 42, of which 13 were waited for; matrix products, arithmetic and copies ran while one was open for 13% of the time, Pallas kernels for 0%

profile of v1, /device:TPU:0, one launch (start us, length us, event | category | flops | bytes accessed | tf_op | source)
XLA Modules:
  0.0 99.5 jit_solution(9416888899715873974)
XLA Ops:
  1.8 1.3 %convolution_convert_fusion = bf16[4,24,3584]{2,1,0:T(8,128)(2,1)S(1)} fusion(bf16[64,3584]{1,0:T(8,128)(2,1)} %param.6, s32[64,4]{0,1:T(4,128)S(1)} %add_select_fusion), kind=kOutput, calls=%fused_computation | convolution fusion | flops 44390400 | bytes 1147904 | tf_op jit(solution)/shard_map/tqc,td->qcd/dot_general | solution.py:30
  4.0 2.9 %collective-permute-start.1 = (bf16[1,24,3584]{2,1,0:T(8,128)(2,1)}, bf16[1,24,3584]{2,1,0:T(8,128)(2,1)}, u32[]{:S(2)}, u32[]{:S(2)}) collective-permute-start(bf16[1,24,3584]{2,1,0:T(8,128)(2,1)} %get-tuple-element.13), channel_id=1, source_target_pairs={{0,2},{1,3},{2,0},{3,1},{4,6},{5,7},{6,4},{7,5},{8,10},{9,11},{10,... | collective-permute-start | bytes 516104 | tf_op jit(solution)/shard_map/ppermute | solution.py:38
  6.9 3.6 %collective-permute-start.22 = (bf16[24,3584]{1,0:T(8,128)(2,1)}, bf16[24,3584]{1,0:T(8,128)(2,1)}, u32[]{:S(2)}, u32[]{:S(2)}) collective-permute-start(bf16[24,3584]{1,0:T(8,128)(2,1)} %get-tuple-element.10), channel_id=1, source_target_pairs={{0,12},{4,8},{8,4},{12,0},{1,13},{5,9},{9,5},{13,1},{2,14},{6,10},... | collective-permute-start | bytes 516104 | tf_op jit(solution)/shard_map/ppermute | solution.py:35
  10.5 1.1 %collective-permute-done.1 = bf16[1,24,3584]{2,1,0:T(8,128)(2,1)} collective-permute-done((bf16[1,24,3584]{2,1,0:T(8,128)(2,1)}, bf16[1,24,3584]{2,1,0:T(8,128)(2,1)}, u32[]{:S(2)}, u32[]{:S(2)}) %collective-permute-start.1) | collective-permute-done | bytes 172064 | tf_op jit(solution)/shard_map/ppermute | solution.py:38
  11.6 2.8 %collective-permute-start.14 = (bf16[24,3584]{1,0:T(8,128)(2,1)}, bf16[24,3584]{1,0:T(8,128)(2,1)}, u32[]{:S(2)}, u32[]{:S(2)}) collective-permute-start(bf16[24,3584]{1,0:T(8,128)(2,1)} %get-tuple-element.11), channel_id=1, source_target_pairs={{0,8},{4,12},{8,0},{12,4},{1,9},{5,13},{9,1},{13,5},{2,10},{6,14},... | collective-permute-start | bytes 516104 | tf_op jit(solution)/shard_map/ppermute | solution.py:35
  14.4 1.6 %collective-permute-start.6 = (bf16[24,3584]{1,0:T(8,128)(2,1)S(1)}, bf16[24,3584]{1,0:T(8,128)(2,1)}, u32[]{:S(2)}, u32[]{:S(2)}) collective-permute-start(bf16[24,3584]{1,0:T(8,128)(2,1)S(1)} %get-tuple-element.12), channel_id=1, source_target_pairs={{0,4},{4,0},{8,12},{12,8},{1,5},{5,1},{9,13},{13,9},{2,6},{6,2},{1... | collective-permute-start | bytes 516104 | tf_op jit(solution)/shard_map/ppermute | solution.py:35
  16.0 1.6 %dynamic-slice_bitcast_fusion.3 = (bf16[256,896]{1,0:T(8,128)(2,1)S(1)}, bf16[256,896]{1,0:T(8,128)(2,1)S(1)}, bf16[256,896]{1,0:T(8,128)(2,1)S(1)}, bf16[256,896]{1,0:T(8,128)(2,1)S(1)}) fusion(bf16[1,1024,896]{2,1,0:T(8,128)(2,1)} %param.11, s32[]{:T(128)S(6)} %select_n.44, s32[]{:T(128)S(6)} %select_n.45, s32[]{:T(128)S(6)} %select_n.47, s32[]{:T(128)S(6)} %select_n.46), kind=kLoop, calls=%fused_computation.54 | loop fusion | bytes 3670032 | tf_op jit(solution)/shard_map/dynamic_slice | solution.py:21
  17.6 1.6 %collective-permute-start.24 = (bf16[1,24,3584]{2,1,0:T(8,128)(2,1)}, bf16[1,24,3584]{2,1,0:T(8,128)(2,1)}, u32[]{:S(2)}, u32[]{:S(2)}) collective-permute-start(bf16[1,24,3584]{2,1,0:T(8,128)(2,1)} %bitcast.30), channel_id=1, source_target_pairs={{0,2},{1,3},{2,0},{3,1},{4,6},{5,7},{6,4},{7,5},{8,10},{9,11},{10,... | collective-permute-start | bytes 516104 | tf_op jit(solution)/shard_map/ppermute | solution.py:38
  19.2 1.3 %pad_maximum_fusion.1 = bf16[4,1,24,3584]{3,2,1,0:T(8,128)(2,1)S(1)} fusion(bf16[1,1,24,3584]{3,2,1,0:T(8,128)(2,1)} %bitcast.6, bf16[1,1,24,3584]{3,2,1,0:T(8,128)(2,1)} %bitcast.5, bf16[1,1,24,3584]{3,2,1,0:T(8,128)(2,1)} %bitcast.4, bf16[1,1,24,3584]{3,2,1,0:T(8,128)(2,1)S(1)} %get-tuple-element.9), kind=kLoop, calls=%fused_computation.46 | loop fusion | flops 1032192 | bytes 1376256 | tf_op jit(solution)/shard_map/stack | solution.py:56
  21.5 1.3 %collective-permute-start.4 = (bf16[96,256]{1,0:T(8,128)(2,1)S(1)}, bf16[96,256]{1,0:T(8,128)(2,1)S(1)}, u32[]{:S(2)}, u32[]{:S(2)}) collective-permute-start(bf16[96,256]{1,0:T(8,128)(2,1)S(1)} %fusion.45), channel_id=1, source_target_pairs={{0,2},{1,3},{2,0},{3,1},{4,6},{5,7},{6,4},{7,5},{8,10},{9,11},{10,... | collective-permute-start | bytes 147464 | tf_op jit(solution)/shard_map/ppermute | solution.py:38
  22.7 2.7 %collective-permute-done.5 = bf16[96,256]{1,0:T(8,128)(2,1)S(1)} collective-permute-done((bf16[96,256]{1,0:T(8,128)(2,1)S(1)}, bf16[96,256]{1,0:T(8,128)(2,1)S(1)}, u32[]{:S(2)}, u32[]{:S(2)}) %collective-permute-start.5) | collective-permute-done | bytes 49184 | tf_op jit(solution)/shard_map/ppermute | solution.py:38
  28.7 1.1 %collective-permute-start.16 = (bf16[1,24,3584]{2,1,0:T(8,128)(2,1)}, bf16[1,24,3584]{2,1,0:T(8,128)(2,1)S(1)}, u32[]{:S(2)}, u32[]{:S(2)}) collective-permute-start(bf16[1,24,3584]{2,1,0:T(8,128)(2,1)} %bitcast.23), channel_id=1, source_target_pairs={{0,2},{1,3},{2,0},{3,1},{4,6},{5,7},{6,4},{7,5},{8,10},{9,11},{10,... | collective-permute-start | bytes 516104 | tf_op jit(solution)/shard_map/ppermute | solution.py:38
  30.8 1.1 %collective-permute-start.34 = (bf16[24,896]{1,0:T(8,128)(2,1)S(1)}, bf16[24,896]{1,0:T(8,128)(2,1)S(1)}, u32[]{:S(2)}, u32[]{:S(2)}) collective-permute-start(bf16[24,896]{1,0:T(8,128)(2,1)S(1)} %get-tuple-element.27), channel_id=1, source_target_pairs={{0,2},{1,3},{2,0},{3,1},{4,6},{5,7},{6,4},{7,5},{8,10},{9,11},{10,... | collective-permute-start | bytes 129032 | tf_op jit(solution)/shard_map/ppermute | solution.py:44
  31.9 8.1 %collective-permute-done.34 = bf16[24,896]{1,0:T(8,128)(2,1)S(1)} collective-permute-done((bf16[24,896]{1,0:T(8,128)(2,1)S(1)}, bf16[24,896]{1,0:T(8,128)(2,1)S(1)}, u32[]{:S(2)}, u32[]{:S(2)}) %collective-permute-start.34) | collective-permute-done | bytes 43040 | tf_op jit(solution)/shard_map/ppermute | solution.py:44
  40.4 3.5 %collective-permute-done.38 = bf16[24,896]{1,0:T(8,128)(2,1)S(1)} collective-permute-done((bf16[24,896]{1,0:T(8,128)(2,1)}, bf16[24,896]{1,0:T(8,128)(2,1)S(1)}, u32[]{:S(2)}, u32[]{:S(2)}) %collective-permute-start.38) | collective-permute-done | bytes 43040 | tf_op jit(solution)/shard_map/ppermute | solution.py:44
  45.0 1.2 %pad_maximum_fusion.4 = bf16[4,1,24,3584]{3,2,1,0:T(8,128)(2,1)S(1)} fusion(bf16[1,1,24,3584]{3,2,1,0:T(8,128)(2,1)S(1)} %bitcast.127, bf16[1,1,24,3584]{3,2,1,0:T(8,128)(2,1)} %bitcast.32, bf16[1,1,24,3584]{3,2,1,0:T(8,128)(2,1)S(1)} %bitcast.123, bf16[1,1,24,3584]{3,2,1,0:T(8,128)(2,1)} %bitcast.29), kind=kLoop, calls=%fused_computation.49 | loop fusion | flops 1032192 | bytes 1376256 | tf_op jit(solution)/shard_map/stack | solution.py:56
  51.1 1.2 %collective-permute-start.20 = (bf16[96,256]{1,0:T(8,128)(2,1)S(1)}, bf16[96,256]{1,0:T(8,128)(2,1)S(1)}, u32[]{:S(2)}, u32[]{:S(2)}) collective-permute-start(bf16[96,256]{1,0:T(8,128)(2,1)S(1)} %fusion.39), channel_id=1, source_target_pairs={{0,3},{1,2},{2,1},{3,0},{4,7},{5,6},{6,5},{7,4},{8,11},{9,10},{10,... | collective-permute-start | bytes 147464 | tf_op jit(solution)/shard_map/ppermute | solution.py:38
  55.1 1.3 %collective-permute-start.12 = (bf16[96,256]{1,0:T(8,128)(2,1)S(1)}, bf16[96,256]{1,0:T(8,128)(2,1)S(1)}, u32[]{:S(2)}, u32[]{:S(2)}) collective-permute-start(bf16[96,256]{1,0:T(8,128)(2,1)S(1)} %fusion.42), channel_id=1, source_target_pairs={{0,3},{1,2},{2,1},{3,0},{4,7},{5,6},{6,5},{7,4},{8,11},{9,10},{10,... | collective-permute-start | bytes 147464 | tf_op jit(solution)/shard_map/ppermute | solution.py:38
  59.4 1.2 %collective-permute-done.11 = bf16[96,256]{1,0:T(8,128)(2,1)S(1)} collective-permute-done((bf16[96,256]{1,0:T(8,128)(2,1)S(1)}, bf16[96,256]{1,0:T(8,128)(2,1)S(1)}, u32[]{:S(2)}, u32[]{:S(2)}) %collective-permute-start.11) | collective-permute-done | bytes 49184 | tf_op jit(solution)/shard_map/ppermute | solution.py:38
  61.1 4.3 %collective-permute-start.39 = (bf16[24,896]{1,0:T(8,128)(2,1)S(1)}, bf16[24,896]{1,0:T(8,128)(2,1)S(1)}, u32[]{:S(2)}, u32[]{:S(2)}) collective-permute-start(bf16[24,896]{1,0:T(8,128)(2,1)S(1)} %get-tuple-element.22), channel_id=1, source_target_pairs={{0,7},{1,6},{2,5},{3,4},{4,3},{5,2},{6,1},{7,0},{8,15},{9,14},{10,... | collective-permute-start | bytes 129032 | tf_op jit(solution)/shard_map/ppermute | solution.py:44
  66.2 1.9 %collective-permute-start.31 = (bf16[24,896]{1,0:T(8,128)(2,1)S(1)}, bf16[24,896]{1,0:T(8,128)(2,1)S(1)}, u32[]{:S(2)}, u32[]{:S(2)}) collective-permute-start(bf16[24,896]{1,0:T(8,128)(2,1)S(1)} %get-tuple-element.24), channel_id=1, source_target_pairs={{0,5},{1,4},{2,7},{3,6},{4,1},{5,0},{6,3},{7,2},{8,13},{9,12},{10,... | collective-permute-start | bytes 129032 | tf_op jit(solution)/shard_map/ppermute | solution.py:44
  68.6 2.2 %collective-permute-start.40 = (bf16[24,896]{1,0:T(8,128)(2,1)S(1)}, bf16[24,896]{1,0:T(8,128)(2,1)S(1)}, u32[]{:S(2)}, u32[]{:S(2)}) collective-permute-start(bf16[24,896]{1,0:T(8,128)(2,1)S(1)} %get-tuple-element.18), channel_id=1, source_target_pairs={{0,11},{1,10},{2,9},{3,8},{4,15},{5,14},{6,13},{7,12},{8,3},{9,2},... | collective-permute-start | bytes 129032 | tf_op jit(solution)/shard_map/ppermute | solution.py:44
  70.9 1.3 %collective-permute-start.36 = (bf16[24,896]{1,0:T(8,128)(2,1)S(1)}, bf16[24,896]{1,0:T(8,128)(2,1)S(1)}, u32[]{:S(2)}, u32[]{:S(2)}) collective-permute-start(bf16[24,896]{1,0:T(8,128)(2,1)S(1)} %get-tuple-element.19), channel_id=1, source_target_pairs={{0,10},{1,11},{2,8},{3,9},{4,14},{5,15},{6,12},{7,13},{8,2},{9,3},... | collective-permute-start | bytes 129032 | tf_op jit(solution)/shard_map/ppermute | solution.py:44
  72.2 1.9 %collective-permute-done.40 = bf16[24,896]{1,0:T(8,128)(2,1)S(1)} collective-permute-done((bf16[24,896]{1,0:T(8,128)(2,1)S(1)}, bf16[24,896]{1,0:T(8,128)(2,1)S(1)}, u32[]{:S(2)}, u32[]{:S(2)}) %collective-permute-start.40) | collective-permute-done | bytes 43040 | tf_op jit(solution)/shard_map/ppermute | solution.py:44
  74.1 2.0 %collective-permute-start.41 = (bf16[24,896]{1,0:T(8,128)(2,1)S(1)}, bf16[24,896]{1,0:T(8,128)(2,1)S(1)}, u32[]{:S(2)}, u32[]{:S(2)}) collective-permute-start(bf16[24,896]{1,0:T(8,128)(2,1)S(1)} %get-tuple-element.14), channel_id=1, source_target_pairs={{0,15},{1,14},{2,13},{3,12},{4,11},{5,10},{6,9},{7,8},{8,7},{9,6},... | collective-permute-start | bytes 129032 | tf_op jit(solution)/shard_map/ppermute | solution.py:44
  76.0 4.3 %collective-permute-done.41 = bf16[24,896]{1,0:T(8,128)(2,1)S(1)} collective-permute-done((bf16[24,896]{1,0:T(8,128)(2,1)S(1)}, bf16[24,896]{1,0:T(8,128)(2,1)S(1)}, u32[]{:S(2)}, u32[]{:S(2)}) %collective-permute-start.41) | collective-permute-done | bytes 43040 | tf_op jit(solution)/shard_map/ppermute | solution.py:44
  80.6 2.7 %collective-permute-start.21 = (bf16[24,896]{1,0:T(8,128)(2,1)S(1)}, bf16[24,896]{1,0:T(8,128)(2,1)S(1)}, u32[]{:S(2)}, u32[]{:S(2)}) collective-permute-start(bf16[24,896]{1,0:T(8,128)(2,1)S(1)} %get-tuple-element.21), channel_id=1, source_target_pairs={{0,8},{1,9},{2,10},{3,11},{4,12},{5,13},{6,14},{7,15},{8,0},{9,1},... | collective-permute-start | bytes 129032 | tf_op jit(solution)/shard_map/ppermute | solution.py:44
  83.4 2.4 %collective-permute-start.37 = (bf16[24,896]{1,0:T(8,128)(2,1)S(1)}, bf16[24,896]{1,0:T(8,128)(2,1)S(1)}, u32[]{:S(2)}, u32[]{:S(2)}) collective-permute-start(bf16[24,896]{1,0:T(8,128)(2,1)S(1)} %get-tuple-element.15), channel_id=1, source_target_pairs={{0,14},{1,15},{2,12},{3,13},{4,10},{5,11},{6,8},{7,9},{8,6},{9,7},... | collective-permute-start | bytes 129032 | tf_op jit(solution)/shard_map/ppermute | solution.py:44
  85.7 4.4 %collective-permute-done.37 = bf16[24,896]{1,0:T(8,128)(2,1)S(1)} collective-permute-done((bf16[24,896]{1,0:T(8,128)(2,1)S(1)}, bf16[24,896]{1,0:T(8,128)(2,1)S(1)}, u32[]{:S(2)}, u32[]{:S(2)}) %collective-permute-start.37) | collective-permute-done | bytes 43040 | tf_op jit(solution)/shard_map/ppermute | solution.py:44
  90.8 2.0 %collective-permute-start.29 = (bf16[24,896]{1,0:T(8,128)(2,1)S(1)}, bf16[24,896]{1,0:T(8,128)(2,1)S(1)}, u32[]{:S(2)}, u32[]{:S(2)}) collective-permute-start(bf16[24,896]{1,0:T(8,128)(2,1)S(1)} %get-tuple-element.17), channel_id=1, source_target_pairs={{0,12},{1,13},{2,14},{3,15},{4,8},{5,9},{6,10},{7,11},{8,4},{9,5},... | collective-permute-start | bytes 129032 | tf_op jit(solution)/shard_map/ppermute | solution.py:44
  92.9 2.6 %collective-permute-done.33 = bf16[24,896]{1,0:T(8,128)(2,1)S(1)} collective-permute-done((bf16[24,896]{1,0:T(8,128)(2,1)S(1)}, bf16[24,896]{1,0:T(8,128)(2,1)S(1)}, u32[]{:S(2)}, u32[]{:S(2)}) %collective-permute-start.33) | collective-permute-done | bytes 43040 | tf_op jit(solution)/shard_map/ppermute | solution.py:44
  95.7 1.1 %collective-permute-done.29 = bf16[24,896]{1,0:T(8,128)(2,1)S(1)} collective-permute-done((bf16[24,896]{1,0:T(8,128)(2,1)S(1)}, bf16[24,896]{1,0:T(8,128)(2,1)S(1)}, u32[]{:S(2)}, u32[]{:S(2)}) %collective-permute-start.29) | collective-permute-done | bytes 43040 | tf_op jit(solution)/shard_map/ppermute | solution.py:44
  (149 shorter events, 25.4 us)
Async XLA Ops:
  4.0 7.6 %collective-permute-start.1 = (bf16[1,24,3584]{2,1,0:T(8,128)(2,1)}, bf16[1,24,3584]{2,1,0:T(8,128)(2,1)}, u32[]{:S(2)}, u32[]{:S(2)}) collective-permute-start(bf16[1,24,3584]{2,1,0:T(8,128)(2,1)} %get-tuple-element.13), channel_id=1, source_target_pairs={{0,2},{1,3},{2,0},{3,1},{4,6},{5,7},{6,4},{7,5},{8,10},{9,11},{10,... | collective-permute-start | bytes 516104 | tf_op jit(solution)/shard_map/ppermute | solution.py:38
  6.9 10.7 %collective-permute-start.22 = (bf16[24,3584]{1,0:T(8,128)(2,1)}, bf16[24,3584]{1,0:T(8,128)(2,1)}, u32[]{:S(2)}, u32[]{:S(2)}) collective-permute-start(bf16[24,3584]{1,0:T(8,128)(2,1)} %get-tuple-element.10), channel_id=1, source_target_pairs={{0,12},{4,8},{8,4},{12,0},{1,13},{5,9},{9,5},{13,1},{2,14},{6,10},... | collective-permute-start | bytes 516104 | tf_op jit(solution)/shard_map/ppermute | solution.py:35
  10.5 8.7 %collective-permute-start = (bf16[1,24,3584]{2,1,0:T(8,128)(2,1)}, bf16[1,24,3584]{2,1,0:T(8,128)(2,1)}, u32[]{:S(2)}, u32[]{:S(2)}) collective-permute-start(bf16[1,24,3584]{2,1,0:T(8,128)(2,1)} %get-tuple-element.13), channel_id=1, source_target_pairs={{0,1},{1,0},{2,3},{3,2},{4,5},{5,4},{6,7},{7,6},{8,9},{9,8},{10,11... | collective-permute-start | bytes 516104 | tf_op jit(solution)/shard_map/ppermute | solution.py:38
  11.6 7.6 %collective-permute-start.2 = (bf16[1,24,3584]{2,1,0:T(8,128)(2,1)}, bf16[1,24,3584]{2,1,0:T(8,128)(2,1)}, u32[]{:S(2)}, u32[]{:S(2)}) collective-permute-start(bf16[1,24,3584]{2,1,0:T(8,128)(2,1)} %collective-permute-done.1), channel_id=1, source_target_pairs={{0,1},{1,0},{2,3},{3,2},{4,5},{5,4},{6,7},{7,6},{8,9},{9,8},{10,11... | collective-permute-start | bytes 516104 | tf_op jit(solution)/shard_map/ppermute | solution.py:38
  11.6 17.2 %collective-permute-start.14 = (bf16[24,3584]{1,0:T(8,128)(2,1)}, bf16[24,3584]{1,0:T(8,128)(2,1)}, u32[]{:S(2)}, u32[]{:S(2)}) collective-permute-start(bf16[24,3584]{1,0:T(8,128)(2,1)} %get-tuple-element.11), channel_id=1, source_target_pairs={{0,8},{4,12},{8,0},{12,4},{1,9},{5,13},{9,1},{13,5},{2,10},{6,14},... | collective-permute-start | bytes 516104 | tf_op jit(solution)/shard_map/ppermute | solution.py:35
  14.4 15.4 %collective-permute-start.6 = (bf16[24,3584]{1,0:T(8,128)(2,1)S(1)}, bf16[24,3584]{1,0:T(8,128)(2,1)}, u32[]{:S(2)}, u32[]{:S(2)}) collective-permute-start(bf16[24,3584]{1,0:T(8,128)(2,1)S(1)} %get-tuple-element.12), channel_id=1, source_target_pairs={{0,4},{4,0},{8,12},{12,8},{1,5},{5,1},{9,13},{13,9},{2,6},{6,2},{1... | collective-permute-start | bytes 516104 | tf_op jit(solution)/shard_map/ppermute | solution.py:35
  17.6 13.2 %collective-permute-start.24 = (bf16[1,24,3584]{2,1,0:T(8,128)(2,1)}, bf16[1,24,3584]{2,1,0:T(8,128)(2,1)}, u32[]{:S(2)}, u32[]{:S(2)}) collective-permute-start(bf16[1,24,3584]{2,1,0:T(8,128)(2,1)} %bitcast.30), channel_id=1, source_target_pairs={{0,2},{1,3},{2,0},{3,1},{4,6},{5,7},{6,4},{7,5},{8,10},{9,11},{10,... | collective-permute-start | bytes 516104 | tf_op jit(solution)/shard_map/ppermute | solution.py:38
  28.3 15.6 %collective-permute-start.23 = (bf16[1,24,3584]{2,1,0:T(8,128)(2,1)}, bf16[1,24,3584]{2,1,0:T(8,128)(2,1)S(1)}, u32[]{:S(2)}, u32[]{:S(2)}) collective-permute-start(bf16[1,24,3584]{2,1,0:T(8,128)(2,1)} %bitcast.30), channel_id=1, source_target_pairs={{0,1},{1,0},{2,3},{3,2},{4,5},{5,4},{6,7},{7,6},{8,9},{9,8},{10,11... | collective-permute-start | bytes 516104 | tf_op jit(solution)/shard_map/ppermute | solution.py:38
  28.7 15.8 %collective-permute-start.16 = (bf16[1,24,3584]{2,1,0:T(8,128)(2,1)}, bf16[1,24,3584]{2,1,0:T(8,128)(2,1)S(1)}, u32[]{:S(2)}, u32[]{:S(2)}) collective-permute-start(bf16[1,24,3584]{2,1,0:T(8,128)(2,1)} %bitcast.23), channel_id=1, source_target_pairs={{0,2},{1,3},{2,0},{3,1},{4,6},{5,7},{6,4},{7,5},{8,10},{9,11},{10,... | collective-permute-start | bytes 516104 | tf_op jit(solution)/shard_map/ppermute | solution.py:38
  29.8 14.8 %collective-permute-start.8 = (bf16[1,24,3584]{2,1,0:T(8,128)(2,1)}, bf16[1,24,3584]{2,1,0:T(8,128)(2,1)S(1)}, u32[]{:S(2)}, u32[]{:S(2)}) collective-permute-start(bf16[1,24,3584]{2,1,0:T(8,128)(2,1)} %bitcast.16), channel_id=1, source_target_pairs={{0,2},{1,3},{2,0},{3,1},{4,6},{5,7},{6,4},{7,5},{8,10},{9,11},{10,... | collective-permute-start | bytes 516104 | tf_op jit(solution)/shard_map/ppermute | solution.py:38
  30.8 14.2 %collective-permute-start.25 = (bf16[1,24,3584]{2,1,0:T(8,128)(2,1)}, bf16[1,24,3584]{2,1,0:T(8,128)(2,1)S(1)}, u32[]{:S(2)}, u32[]{:S(2)}) collective-permute-start(bf16[1,24,3584]{2,1,0:T(8,128)(2,1)} %collective-permute-done.24), channel_id=1, source_target_pairs={{0,1},{1,0},{2,3},{3,2},{4,5},{5,4},{6,7},{7,6},{8,9},{9,8},{10,11... | collective-permute-start | bytes 516104 | tf_op jit(solution)/shard_map/ppermute | solution.py:38
  30.8 9.2 %collective-permute-start.34 = (bf16[24,896]{1,0:T(8,128)(2,1)S(1)}, bf16[24,896]{1,0:T(8,128)(2,1)S(1)}, u32[]{:S(2)}, u32[]{:S(2)}) collective-permute-start(bf16[24,896]{1,0:T(8,128)(2,1)S(1)} %get-tuple-element.27), channel_id=1, source_target_pairs={{0,2},{1,3},{2,0},{3,1},{4,6},{5,7},{6,4},{7,5},{8,10},{9,11},{10,... | collective-permute-start | bytes 129032 | tf_op jit(solution)/shard_map/ppermute | solution.py:44
  44.0 7.1 %collective-permute-start.7 = (bf16[1,24,3584]{2,1,0:T(8,128)(2,1)}, bf16[1,24,3584]{2,1,0:T(8,128)(2,1)S(1)}, u32[]{:S(2)}, u32[]{:S(2)}) collective-permute-start(bf16[1,24,3584]{2,1,0:T(8,128)(2,1)} %bitcast.16), channel_id=1, source_target_pairs={{0,1},{1,0},{2,3},{3,2},{4,5},{5,4},{6,7},{7,6},{8,9},{9,8},{10,11... | collective-permute-start | bytes 516104 | tf_op jit(solution)/shard_map/ppermute | solution.py:38
  44.6 7.6 %collective-permute-start.9 = (bf16[1,24,3584]{2,1,0:T(8,128)(2,1)S(1)}, bf16[1,24,3584]{2,1,0:T(8,128)(2,1)S(1)}, u32[]{:S(2)}, u32[]{:S(2)}) collective-permute-start(bf16[1,24,3584]{2,1,0:T(8,128)(2,1)S(1)} %collective-permute-done.8), channel_id=1, source_target_pairs={{0,1},{1,0},{2,3},{3,2},{4,5},{5,4},{6,7},{7,6},{8,9},{9,8},{10,11... | collective-permute-start | bytes 516104 | tf_op jit(solution)/shard_map/ppermute | solution.py:38
  47.1 7.9 %collective-permute-start.28 = (bf16[96,256]{1,0:T(8,128)(2,1)S(1)}, bf16[96,256]{1,0:T(8,128)(2,1)S(1)}, u32[]{:S(2)}, u32[]{:S(2)}) collective-permute-start(bf16[96,256]{1,0:T(8,128)(2,1)S(1)} %fusion.36), channel_id=1, source_target_pairs={{0,3},{1,2},{2,1},{3,0},{4,7},{5,6},{6,5},{7,4},{8,11},{9,10},{10,... | collective-permute-start | bytes 147464 | tf_op jit(solution)/shard_map/ppermute | solution.py:38
  48.1 7.0 %collective-permute-start.27 = (bf16[96,256]{1,0:T(8,128)(2,1)S(1)}, bf16[96,256]{1,0:T(8,128)(2,1)S(1)}, u32[]{:S(2)}, u32[]{:S(2)}) collective-permute-start(bf16[96,256]{1,0:T(8,128)(2,1)S(1)} %fusion.36), channel_id=1, source_target_pairs={{0,2},{1,3},{2,0},{3,1},{4,6},{5,7},{6,4},{7,5},{8,10},{9,11},{10,... | collective-permute-start | bytes 147464 | tf_op jit(solution)/shard_map/ppermute | solution.py:38
  49.0 7.5 %collective-permute-start.26 = (bf16[96,256]{1,0:T(8,128)(2,1)S(1)}, bf16[96,256]{1,0:T(8,128)(2,1)S(1)}, u32[]{:S(2)}, u32[]{:S(2)}) collective-permute-start(bf16[96,256]{1,0:T(8,128)(2,1)S(1)} %fusion.36), channel_id=1, source_target_pairs={{0,1},{1,0},{2,3},{3,2},{4,5},{5,4},{6,7},{7,6},{8,9},{9,8},{10,11... | collective-permute-start | bytes 147464 | tf_op jit(solution)/shard_map/ppermute | solution.py:38
  51.1 14.4 %collective-permute-start.20 = (bf16[96,256]{1,0:T(8,128)(2,1)S(1)}, bf16[96,256]{1,0:T(8,128)(2,1)S(1)}, u32[]{:S(2)}, u32[]{:S(2)}) collective-permute-start(bf16[96,256]{1,0:T(8,128)(2,1)S(1)} %fusion.39), channel_id=1, source_target_pairs={{0,3},{1,2},{2,1},{3,0},{4,7},{5,6},{6,5},{7,4},{8,11},{9,10},{10,... | collective-permute-start | bytes 147464 | tf_op jit(solution)/shard_map/ppermute | solution.py:38
  52.2 13.2 %collective-permute-start.19 = (bf16[96,256]{1,0:T(8,128)(2,1)S(1)}, bf16[96,256]{1,0:T(8,128)(2,1)S(1)}, u32[]{:S(2)}, u32[]{:S(2)}) collective-permute-start(bf16[96,256]{1,0:T(8,128)(2,1)S(1)} %fusion.39), channel_id=1, source_target_pairs={{0,2},{1,3},{2,0},{3,1},{4,6},{5,7},{6,4},{7,5},{8,10},{9,11},{10,... | collective-permute-start | bytes 147464 | tf_op jit(solution)/shard_map/ppermute | solution.py:38
  55.0 10.4 %collective-permute-start.18 = (bf16[96,256]{1,0:T(8,128)(2,1)S(1)}, bf16[96,256]{1,0:T(8,128)(2,1)S(1)}, u32[]{:S(2)}, u32[]{:S(2)}) collective-permute-start(bf16[96,256]{1,0:T(8,128)(2,1)S(1)} %fusion.39), channel_id=1, source_target_pairs={{0,1},{1,0},{2,3},{3,2},{4,5},{5,4},{6,7},{7,6},{8,9},{9,8},{10,11... | collective-permute-start | bytes 147464 | tf_op jit(solution)/shard_map/ppermute | solution.py:38
  61.1 9.7 %collective-permute-start.39 = (bf16[24,896]{1,0:T(8,128)(2,1)S(1)}, bf16[24,896]{1,0:T(8,128)(2,1)S(1)}, u32[]{:S(2)}, u32[]{:S(2)}) collective-permute-start(bf16[24,896]{1,0:T(8,128)(2,1)S(1)} %get-tuple-element.22), channel_id=1, source_target_pairs={{0,7},{1,6},{2,5},{3,4},{4,3},{5,2},{6,1},{7,0},{8,15},{9,14},{10,... | collective-permute-start | bytes 129032 | tf_op jit(solution)/shard_map/ppermute | solution.py:44
  66.0 14.6 %collective-permute-start.35 = (bf16[24,896]{1,0:T(8,128)(2,1)S(1)}, bf16[24,896]{1,0:T(8,128)(2,1)S(1)}, u32[]{:S(2)}, u32[]{:S(2)}) collective-permute-start(bf16[24,896]{1,0:T(8,128)(2,1)S(1)} %get-tuple-element.23), channel_id=1, source_target_pairs={{0,6},{1,7},{2,4},{3,5},{4,2},{5,3},{6,0},{7,1},{8,14},{9,15},{10,... | collective-permute-start | bytes 129032 | tf_op jit(solution)/shard_map/ppermute | solution.py:44
  66.2 24.6 %collective-permute-start.31 = (bf16[24,896]{1,0:T(8,128)(2,1)S(1)}, bf16[24,896]{1,0:T(8,128)(2,1)S(1)}, u32[]{:S(2)}, u32[]{:S(2)}) collective-permute-start(bf16[24,896]{1,0:T(8,128)(2,1)S(1)} %get-tuple-element.24), channel_id=1, source_target_pairs={{0,5},{1,4},{2,7},{3,6},{4,1},{5,0},{6,3},{7,2},{8,13},{9,12},{10,... | collective-permute-start | bytes 129032 | tf_op jit(solution)/shard_map/ppermute | solution.py:44
  68.1 27.6 %collective-permute-start.13 = (bf16[24,896]{1,0:T(8,128)(2,1)S(1)}, bf16[24,896]{1,0:T(8,128)(2,1)S(1)}, u32[]{:S(2)}, u32[]{:S(2)}) collective-permute-start(bf16[24,896]{1,0:T(8,128)(2,1)S(1)} %get-tuple-element.25), channel_id=1, source_target_pairs={{0,4},{1,5},{2,6},{3,7},{4,0},{5,1},{6,2},{7,3},{8,12},{9,13},{10,... | collective-permute-start | bytes 129032 | tf_op jit(solution)/shard_map/ppermute | solution.py:44
  68.6 5.4 %collective-permute-start.40 = (bf16[24,896]{1,0:T(8,128)(2,1)S(1)}, bf16[24,896]{1,0:T(8,128)(2,1)S(1)}, u32[]{:S(2)}, u32[]{:S(2)}) collective-permute-start(bf16[24,896]{1,0:T(8,128)(2,1)S(1)} %get-tuple-element.18), channel_id=1, source_target_pairs={{0,11},{1,10},{2,9},{3,8},{4,15},{5,14},{6,13},{7,12},{8,3},{9,2},... | collective-permute-start | bytes 129032 | tf_op jit(solution)/shard_map/ppermute | solution.py:44
  70.9 12.5 %collective-permute-start.36 = (bf16[24,896]{1,0:T(8,128)(2,1)S(1)}, bf16[24,896]{1,0:T(8,128)(2,1)S(1)}, u32[]{:S(2)}, u32[]{:S(2)}) collective-permute-start(bf16[24,896]{1,0:T(8,128)(2,1)S(1)} %get-tuple-element.19), channel_id=1, source_target_pairs={{0,10},{1,11},{2,8},{3,9},{4,14},{5,15},{6,12},{7,13},{8,2},{9,3},... | collective-permute-start | bytes 129032 | tf_op jit(solution)/shard_map/ppermute | solution.py:44
  74.1 6.3 %collective-permute-start.41 = (bf16[24,896]{1,0:T(8,128)(2,1)S(1)}, bf16[24,896]{1,0:T(8,128)(2,1)S(1)}, u32[]{:S(2)}, u32[]{:S(2)}) collective-permute-start(bf16[24,896]{1,0:T(8,128)(2,1)S(1)} %get-tuple-element.14), channel_id=1, source_target_pairs={{0,15},{1,14},{2,13},{3,12},{4,11},{5,10},{6,9},{7,8},{8,7},{9,6},... | collective-permute-start | bytes 129032 | tf_op jit(solution)/shard_map/ppermute | solution.py:44
  80.4 12.5 %collective-permute-start.32 = (bf16[24,896]{1,0:T(8,128)(2,1)S(1)}, bf16[24,896]{1,0:T(8,128)(2,1)S(1)}, u32[]{:S(2)}, u32[]{:S(2)}) collective-permute-start(bf16[24,896]{1,0:T(8,128)(2,1)S(1)} %get-tuple-element.20), channel_id=1, source_target_pairs={{0,9},{1,8},{2,11},{3,10},{4,13},{5,12},{6,15},{7,14},{8,1},{9,0},... | collective-permute-start | bytes 129032 | tf_op jit(solution)/shard_map/ppermute | solution.py:44
  80.6 15.0 %collective-permute-start.21 = (bf16[24,896]{1,0:T(8,128)(2,1)S(1)}, bf16[24,896]{1,0:T(8,128)(2,1)S(1)}, u32[]{:S(2)}, u32[]{:S(2)}) collective-permute-start(bf16[24,896]{1,0:T(8,128)(2,1)S(1)} %get-tuple-element.21), channel_id=1, source_target_pairs={{0,8},{1,9},{2,10},{3,11},{4,12},{5,13},{6,14},{7,15},{8,0},{9,1},... | collective-permute-start | bytes 129032 | tf_op jit(solution)/shard_map/ppermute | solution.py:44
  83.4 6.8 %collective-permute-start.37 = (bf16[24,896]{1,0:T(8,128)(2,1)S(1)}, bf16[24,896]{1,0:T(8,128)(2,1)S(1)}, u32[]{:S(2)}, u32[]{:S(2)}) collective-permute-start(bf16[24,896]{1,0:T(8,128)(2,1)S(1)} %get-tuple-element.15), channel_id=1, source_target_pairs={{0,14},{1,15},{2,12},{3,13},{4,10},{5,11},{6,8},{7,9},{8,6},{9,7},... | collective-permute-start | bytes 129032 | tf_op jit(solution)/shard_map/ppermute | solution.py:44
  90.2 5.2 %collective-permute-start.33 = (bf16[24,896]{1,0:T(8,128)(2,1)S(1)}, bf16[24,896]{1,0:T(8,128)(2,1)S(1)}, u32[]{:S(2)}, u32[]{:S(2)}) collective-permute-start(bf16[24,896]{1,0:T(8,128)(2,1)S(1)} %get-tuple-element.16), channel_id=1, source_target_pairs={{0,13},{1,12},{2,15},{3,14},{4,9},{5,8},{6,11},{7,10},{8,5},{9,4},... | collective-permute-start | bytes 129032 | tf_op jit(solution)/shard_map/ppermute | solution.py:44
  90.8 5.9 %collective-permute-start.29 = (bf16[24,896]{1,0:T(8,128)(2,1)S(1)}, bf16[24,896]{1,0:T(8,128)(2,1)S(1)}, u32[]{:S(2)}, u32[]{:S(2)}) collective-permute-start(bf16[24,896]{1,0:T(8,128)(2,1)S(1)} %get-tuple-element.17), channel_id=1, source_target_pairs={{0,12},{1,13},{2,14},{3,15},{4,8},{5,9},{6,10},{7,11},{8,4},{9,5},... | collective-permute-start | bytes 129032 | tf_op jit(solution)/shard_map/ppermute | solution.py:44
  (23 other events, 109.7 us)

commit v2 on v1

--- a/solution.py
+++ b/solution.py
@@ -10,6 +10,7 @@
     tok_rows, width = tokens.shape
     n_out = lax.axis_size("outer")
     n_loc = lax.axis_size("local")
+    n_chip = n_loc // 2
     capacity = 3 * tok_rows // (2 * n_out)
     part_out = down_weight.shape[2]
     part_hid = gate_weight.shape[2]
@@ -17,9 +18,17 @@
     l = lax.axis_index("local")
     gate_local = gate_weight[0]
     up_local = up_weight[0]
-    down_local = jnp.concatenate(
-        [lax.dynamic_slice_in_dim(down_weight[0], (l ^ m) * part_hid, part_hid, 0) for m in range(n_loc)], axis=0
-    )
+
+    def down_rows(core):
+        return jnp.concatenate(
+            [
+                lax.dynamic_slice_in_dim(down_weight[0], (l ^ (2 * x + core)) * part_hid, part_hid, 0)
+                for x in range(n_chip)
+            ],
+            axis=0,
+        )
+
+    down_same, down_other = down_rows(0), down_rows(1)
 
     targets = (z ^ jnp.arange(n_out, dtype=jnp.int32)) * EXP_POD
     hit_mask = routes[:, :, None] == targets[None, None, :]
@@ -43,30 +52,45 @@
         pairs = [(a * n_loc + b, (a ^ s) * n_loc + (b ^ m)) for a in range(n_out) for b in range(n_loc)]
         return lax.ppermute(v, ("outer", "local"), pairs)
 
-    group = max(1, n_out // 4)
-    chunks = [list(range(g, g + group)) for g in range(0, n_out, group)]
+    half = n_out // 2
     pieces = {}
-    for steps in chunks:
-        mine = jnp.stack([panels[s] if s == 0 else outer_xor(panels[s], s) for s in steps])
-        blocks = [None] * n_loc
-        for m in range(0, n_loc, 2):
-            blocks[m] = mine if m == 0 else local_xor(mine, m)
-        for m in range(0, n_loc, 2):
-            blocks[m + 1] = local_xor(blocks[m], 1)
-        rows = jnp.stack(blocks).reshape(-1, width)
-        gate_proj = jnp.dot(rows, gate_local, preferred_element_type=jnp.float32)
-        up_proj = jnp.dot(rows, up_local, preferred_element_type=jnp.float32)
-        hidden = (jax.nn.silu(gate_proj) * up_proj).astype(jnp.bfloat16)
-        parts = [hidden if m == 0 else local_xor(hidden, m) for m in range(n_loc)]
-        parts = [v.reshape(n_loc, -1, part_hid) for v in parts]
-        full = jnp.concatenate(
-            [jnp.concatenate([parts[m][j ^ m] for m in range(n_loc)], axis=1) for j in range(n_loc)], axis=0
+    for steps in (list(range(half)), list(range(half, n_out))):
+        count = len(steps)
+        mine = {s: panels[s] if s == 0 else outer_xor(panels[s], s) for s in steps}
+        rows_same = jnp.concatenate(
+            [mine[s] if x == 0 else local_xor(mine[s], 2 * x) for x in range(n_chip) for s in steps], axis=0
         )
-        expert_out = jnp.dot(full, down_local, preferred_element_type=jnp.float32).astype(jnp.bfloat16)
-        expert_out = expert_out.reshape(n_loc, len(steps), capacity, part_out)
+        rows_other = local_xor(rows_same, 1)
+
+        def first_half(rows):
+            gate_proj = jnp.dot(rows, gate_local, preferred_element_type=jnp.float32)
+            up_proj = jnp.dot(rows, up_local, preferred_element_type=jnp.float32)
+            return (jax.nn.silu(gate_proj) * up_proj).astype(jnp.bfloat16)
+
+        hidden = jnp.concatenate([first_half(rows_same), first_half(rows_other)], axis=0)
+        sides = []
+        for x in range(n_chip):
+            side = hidden if x == 0 else local_xor(hidden, 2 * x)
+            side = side.reshape(2, n_chip, -1, part_hid)
+            sides.append(jnp.concatenate([side[:, y ^ x : (y ^ x) + 1] for y in range(n_chip)], axis=1))
+        hidden_same = jnp.concatenate(sides, axis=3).reshape(2 * n_chip * count * capacity, n_chip * part_hid)
+        hidden_other = local_xor(hidden_same, 1)
+        out_same = jnp.dot(hidden_same, down_same, preferred_element_type=jnp.float32)
+        out_other = jnp.dot(hidden_other, down_other, preferred_element_type=jnp.float32)
+        out_other = out_other.reshape(2, -1, part_out)
+        out_other = jnp.concatenate([out_other[1:], out_other[:1]], axis=0).reshape(out_same.shape)
+        expert_out = (out_same + out_other).astype(jnp.bfloat16)
+        expert_out = expert_out.reshape(2, n_chip, count, capacity, part_out)
+        landed = {
+            (at, x): both_xor(expert_out[:, x, at], s, 2 * x) for at, s in enumerate(steps) for x in range(n_chip)
+        }
+        swapped = local_xor(
+            jnp.stack([landed[at, x][1] for at in range(count) for x in range(n_chip)]), 1
+        )
         for at, s in enumerate(steps):
-            for m in range(n_loc):
-                pieces[s, m] = both_xor(expert_out[m, at], s, m)
+            for x in range(n_chip):
+                pieces[s, 2 * x] = landed[at, x][0]
+                pieces[s, 2 * x + 1] = swapped[at * n_chip + x]
 
     spread = jnp.where(placing, fixed[:, :, None], 0).reshape(tok_rows, -1)
     high = (spread >> 8).astype(jnp.bfloat16)

time: 99.8 us -> 69.7 us (0.70)
  starting transfers between devices: 46.1 us -> 23.9 us
  other arithmetic: 5.73 us -> 1.48 us
  waiting for transfers between devices: 33 us -> 30.1 us
  local copies, waits for them, and re-layouts: 5.17 us -> 3.95 us
    ppermute x15 -> x7, waiting for transfers between devices: 25.9 us -> 8.8 us  [both_xor(): return lax.ppermute(v, ('outer', 'local'), pairs)]
    ppermute x3, waiting for transfers between devices: 0.01 us -> 10.6 us  [outer_xor(): return lax.ppermute(v, 'outer', [(i, i ^ s) for i in range(n_out)])]
    ppermute x15 -> x7, starting transfers between devices: 21.6 us -> 11.1 us  [both_xor(): return lax.ppermute(v, ('outer', 'local'), pairs)]
    ppermute x24 -> x12, starting transfers between devices: 16.4 us -> 6.97 us  [local_xor(): return lax.ppermute(v, 'local', [(i, i ^ m) for i in range(n_loc)])]
    another operation x4 -> x2, other arithmetic: 4.54 us -> 0.07 us  [per_device(): jnp.stack([landed[at, x][1] for at in range(count) for x in range(n_chip)])]
    ppermute x24 -> x12, waiting for transfers between devices: 7.13 us -> 10.6 us  [local_xor(): return lax.ppermute(v, 'local', [(i, i ^ m) for i in range(n_loc)])]
    ppermute x3, starting transfers between devices: 8.03 us -> 5.91 us  [outer_xor(): return lax.ppermute(v, 'outer', [(i, i ^ s) for i in range(n_out)])]
  transfers between devices with their start and end apart: 42 -> 22, of which waited for: 13 -> 9; matrix products, arithmetic and copies ran while one was open for 13% -> 12% of each run, Pallas kernels for 0% -> 0%
where the time goes in v2:
time: 69.7 us; the launch traced here: 68.7 us
  waiting for transfers between devices  30.1 us (43%)
  starting transfers between devices  23.9 us (34%)
  matrix products  8.73 us (13%)
  local copies, waits for them, and re-layouts  3.95 us (6%)
  other arithmetic  1.48 us (2%)
    ppermute x7, starting transfers between devices, both_xor(): return lax.ppermute(v, ('outer', 'local'), pairs)  11.1 us
    ppermute x12, waiting for transfers between devices, local_xor(): return lax.ppermute(v, 'local', [(i, i ^ m) for i in range(n_loc)])  10.6 us
    ppermute x3, waiting for transfers between devices, outer_xor(): return lax.ppermute(v, 'outer', [(i, i ^ s) for i in range(n_out)])  10.6 us
    ppermute x7, waiting for transfers between devices, both_xor(): return lax.ppermute(v, ('outer', 'local'), pairs)  8.8 us
    ppermute x12, starting transfers between devices, local_xor(): return lax.ppermute(v, 'local', [(i, i ^ m) for i in range(n_loc)])  6.97 us
    ppermute x3, starting transfers between devices, outer_xor(): return lax.ppermute(v, 'outer', [(i, i ^ s) for i in range(n_out)])  5.91 us
    dot_general x4, matrix products, first_half(): up_proj = jnp.dot(rows, up_local, preferred_element_type=jnp.float32)  1.74 us
    dot_general x4, matrix products, first_half(): gate_proj = jnp.dot(rows, gate_local, preferred_element_type=jnp.float32)  1.73 us
  transfers between devices with their start and end apart: 22, of which 9 were waited for; matrix products, arithmetic and copies ran while one was open for 12% of the time, Pallas kernels for 0%

profile of v2, /device:TPU:0, one launch (start us, length us, event | category | flops | bytes accessed | tf_op | source)
XLA Modules:
  0.0 68.7 jit_solution(7890482934931031816)
XLA Ops:
  0.0 0.9 %compare_reduce_fusion = pred[64,4]{0,1:T(4,128)(4,1)S(1)} fusion(s32[64,8]{0,1:T(8,128)} %param.7, s32[4]{0:T(128)S(1)} %xor_multiply_fusion), kind=kLoop, calls=%fused_computation.106 | loop fusion | flops 3840 | bytes 2320 | tf_op jit(solution)/shard_map/reduce_or | solution.py:36
  1.2 1.3 %convolution_convert_fusion = bf16[4,24,3584]{2,1,0:T(8,128)(2,1)S(1)} fusion(bf16[64,3584]{1,0:T(8,128)(2,1)} %param.6, s32[64,4]{0,1:T(4,128)S(1)} %add_select_fusion), kind=kOutput, calls=%fused_computation | convolution fusion | flops 44390400 | bytes 1147904 | tf_op jit(solution)/shard_map/tqc,td->qcd/dot_general | solution.py:39
  2.6 3.1 %collective-permute-start = (bf16[24,3584]{1,0:T(8,128)(2,1)S(1)}, bf16[24,3584]{1,0:T(8,128)(2,1)S(1)}, u32[]{:S(2)}, u32[]{:S(2)}) collective-permute-start(bf16[24,3584]{1,0:T(8,128)(2,1)S(1)} %get-tuple-element.14), channel_id=1, source_target_pairs={{0,4},{4,0},{8,12},{12,8},{1,5},{5,1},{9,13},{13,9},{2,6},{6,2},{1... | collective-permute-start | bytes 516104 | tf_op jit(solution)/shard_map/ppermute | solution.py:44
  5.7 1.5 %collective-permute-start.1 = (bf16[24,3584]{1,0:T(8,128)(2,1)S(1)}, bf16[24,3584]{1,0:T(8,128)(2,1)S(1)}, u32[]{:S(2)}, u32[]{:S(2)}) collective-permute-start(bf16[24,3584]{1,0:T(8,128)(2,1)S(1)} %get-tuple-element.11), channel_id=1, source_target_pairs={{0,2},{1,3},{2,0},{3,1},{4,6},{5,7},{6,4},{7,5},{8,10},{9,11},{10,... | collective-permute-start | bytes 516104 | tf_op jit(solution)/shard_map/ppermute | solution.py:47
  7.2 2.6 %collective-permute-start.7 = (bf16[24,3584]{1,0:T(8,128)(2,1)S(1)}, bf16[24,3584]{1,0:T(8,128)(2,1)S(1)}, u32[]{:S(2)}, u32[]{:S(2)}) collective-permute-start(bf16[24,3584]{1,0:T(8,128)(2,1)S(1)} %get-tuple-element.13), channel_id=1, source_target_pairs={{0,8},{4,12},{8,0},{12,4},{1,9},{5,13},{9,1},{13,5},{2,10},{6,14},... | collective-permute-start | bytes 516104 | tf_op jit(solution)/shard_map/ppermute | solution.py:44
  10.3 1.6 %dynamic-slice_bitcast_fusion.3 = (bf16[256,896]{1,0:T(8,128)(2,1)S(1)}, bf16[256,896]{1,0:T(8,128)(2,1)S(1)}, bf16[256,896]{1,0:T(8,128)(2,1)S(1)}, bf16[256,896]{1,0:T(8,128)(2,1)S(1)}) fusion(bf16[1,1024,896]{2,1,0:T(8,128)(2,1)} %param.11, s32[]{:T(128)S(6)} %select_n.44, s32[]{:T(128)S(6)} %select_n.45, s32[]{:T(128)S(6)} %select_n.47, s32[]{:T(128)S(6)} %select_n.46), kind=kLoop, calls=%fused_computation.48 | loop fusion | bytes 3670032 | tf_op jit(solution)/shard_map/dynamic_slice | solution.py:25
  11.9 10.6 %collective-permute-done.7 = bf16[24,3584]{1,0:T(8,128)(2,1)S(1)} collective-permute-done((bf16[24,3584]{1,0:T(8,128)(2,1)S(1)}, bf16[24,3584]{1,0:T(8,128)(2,1)S(1)}, u32[]{:S(2)}, u32[]{:S(2)}) %collective-permute-start.7) | collective-permute-done | bytes 172064 | tf_op jit(solution)/shard_map/ppermute | solution.py:44
  22.5 0.9 %collective-permute-start.9 = (bf16[24,3584]{1,0:T(8,128)(2,1)S(1)}, bf16[24,3584]{1,0:T(8,128)(2,1)S(1)}, u32[]{:S(2)}, u32[]{:S(2)}) collective-permute-start(bf16[24,3584]{1,0:T(8,128)(2,1)S(1)} %collective-permute-done.7), channel_id=1, source_target_pairs={{0,2},{1,3},{2,0},{3,1},{4,6},{5,7},{6,4},{7,5},{8,10},{9,11},{10,... | collective-permute-start | bytes 516104 | tf_op jit(solution)/shard_map/ppermute | solution.py:47
  23.4 1.2 %collective-permute-start.2 = (bf16[24,3584]{1,0:T(8,128)(2,1)S(1)}, bf16[24,3584]{1,0:T(8,128)(2,1)S(1)}, u32[]{:S(2)}, u32[]{:S(2)}) collective-permute-start(bf16[24,3584]{1,0:T(8,128)(2,1)S(1)} %collective-permute-done), channel_id=1, source_target_pairs={{0,2},{1,3},{2,0},{3,1},{4,6},{5,7},{6,4},{7,5},{8,10},{9,11},{10,... | collective-permute-start | bytes 516104 | tf_op jit(solution)/shard_map/ppermute | solution.py:47
  24.6 0.8 %collective-permute-start.10 = (bf16[24,3584]{1,0:T(8,128)(2,1)S(1)}, bf16[24,3584]{1,0:T(8,128)(2,1)S(1)}, u32[]{:S(2)}, u32[]{:S(2)}) collective-permute-start(bf16[24,3584]{1,0:T(8,128)(2,1)S(1)} %collective-permute-done.8), channel_id=1, source_target_pairs={{0,2},{1,3},{2,0},{3,1},{4,6},{5,7},{6,4},{7,5},{8,10},{9,11},{10,... | collective-permute-start | bytes 516104 | tf_op jit(solution)/shard_map/ppermute | solution.py:47
  25.5 4.4 %collective-permute-done.2 = bf16[24,3584]{1,0:T(8,128)(2,1)S(1)} collective-permute-done((bf16[24,3584]{1,0:T(8,128)(2,1)S(1)}, bf16[24,3584]{1,0:T(8,128)(2,1)S(1)}, u32[]{:S(2)}, u32[]{:S(2)}) %collective-permute-start.2) | collective-permute-done | bytes 172064 | tf_op jit(solution)/shard_map/ppermute | solution.py:47
  30.0 1.7 %collective-permute-done.10 = bf16[24,3584]{1,0:T(8,128)(2,1)S(1)} collective-permute-done((bf16[24,3584]{1,0:T(8,128)(2,1)S(1)}, bf16[24,3584]{1,0:T(8,128)(2,1)S(1)}, u32[]{:S(2)}, u32[]{:S(2)}) %collective-permute-start.10) | collective-permute-done | bytes 172064 | tf_op jit(solution)/shard_map/ppermute | solution.py:47
  31.8 0.4 fusion.14
  32.2 1.0 %copy-done.1 = bf16[1,3584,256]{2,1,0:T(8,128)(2,1)S(1)} copy-done((bf16[1,3584,256]{2,1,0:T(8,128)(2,1)S(1)}, bf16[1,3584,256]{2,1,0:T(8,128)(2,1)}, u32[]{:S(2)}) %copy-start.1) | copy-done | bytes 1835032
  34.1 0.4 multiply_convert_fusion.1
  35.0 0.4 multiply_convert_fusion.2
  35.4 0.9 %collective-permute-start.4 = (bf16[192,256]{1,0:T(8,128)(2,1)S(1)}, bf16[192,256]{1,0:T(8,128)(2,1)S(1)}, u32[]{:S(2)}, u32[]{:S(2)}) collective-permute-start(bf16[192,256]{1,0:T(8,128)(2,1)S(1)} %pad_maximum_fusion.17), channel_id=1, source_target_pairs={{0,2},{1,3},{2,0},{3,1},{4,6},{5,7},{6,4},{7,5},{8,10},{9,11},{10,... | collective-permute-start | bytes 294920 | tf_op jit(solution)/shard_map/ppermute | solution.py:47
  36.7 0.4 multiply_convert_fusion
  37.2 1.3 %collective-permute-start.12 = (bf16[192,256]{1,0:T(8,128)(2,1)S(1)}, bf16[192,256]{1,0:T(8,128)(2,1)S(1)}, u32[]{:S(2)}, u32[]{:S(2)}) collective-permute-start(bf16[192,256]{1,0:T(8,128)(2,1)S(1)} %pad_maximum_fusion.19), channel_id=1, source_target_pairs={{0,2},{1,3},{2,0},{3,1},{4,6},{5,7},{6,4},{7,5},{8,10},{9,11},{10,... | collective-permute-start | bytes 294920 | tf_op jit(solution)/shard_map/ppermute | solution.py:47
  38.4 2.6 %collective-permute-done.4 = bf16[192,256]{1,0:T(8,128)(2,1)S(1)} collective-permute-done((bf16[192,256]{1,0:T(8,128)(2,1)S(1)}, bf16[192,256]{1,0:T(8,128)(2,1)S(1)}, u32[]{:S(2)}, u32[]{:S(2)}) %collective-permute-start.4) | collective-permute-done | bytes 98336 | tf_op jit(solution)/shard_map/ppermute | solution.py:47
  41.2 1.0 %collective-permute-done.12 = bf16[192,256]{1,0:T(8,128)(2,1)S(1)} collective-permute-done((bf16[192,256]{1,0:T(8,128)(2,1)S(1)}, bf16[192,256]{1,0:T(8,128)(2,1)S(1)}, u32[]{:S(2)}, u32[]{:S(2)}) %collective-permute-start.12) | collective-permute-done | bytes 98336 | tf_op jit(solution)/shard_map/ppermute | solution.py:47
  43.6 0.6 collective-permute-start.16
  44.2 2.2 %collective-permute-start.17 = (bf16[2,24,896]{2,1,0:T(8,128)(2,1)S(1)}, bf16[2,24,896]{2,1,0:T(8,128)(2,1)S(1)}, u32[]{:S(2)}, u32[]{:S(2)}) collective-permute-start(bf16[2,24,896]{2,1,0:T(8,128)(2,1)S(1)} %get-tuple-element.21), channel_id=1, source_target_pairs={{0,6},{1,7},{2,4},{3,5},{4,2},{5,3},{6,0},{7,1},{8,14},{9,15},{10,... | collective-permute-start | bytes 258056 | tf_op jit(solution)/shard_map/ppermute | solution.py:53
  46.4 0.7 %collective-permute-start.6 = (bf16[2,24,896]{2,1,0:T(8,128)(2,1)S(1)}, bf16[2,24,896]{2,1,0:T(8,128)(2,1)S(1)}, u32[]{:S(2)}, u32[]{:S(2)}) collective-permute-start(bf16[2,24,896]{2,1,0:T(8,128)(2,1)S(1)} %get-tuple-element.20), channel_id=1, source_target_pairs={{0,4},{1,5},{2,6},{3,7},{4,0},{5,1},{6,2},{7,3},{8,12},{9,13},{10,... | collective-permute-start | bytes 258056 | tf_op jit(solution)/shard_map/ppermute | solution.py:53
  48.1 3.0 %collective-permute-start.19 = (bf16[2,24,896]{2,1,0:T(8,128)(2,1)S(1)}, bf16[2,24,896]{2,1,0:T(8,128)(2,1)S(1)}, u32[]{:S(2)}, u32[]{:S(2)}) collective-permute-start(bf16[2,24,896]{2,1,0:T(8,128)(2,1)S(1)} %get-tuple-element.22), channel_id=1, source_target_pairs={{0,10},{1,11},{2,8},{3,9},{4,14},{5,15},{6,12},{7,13},{8,2},{9,3},... | collective-permute-start | bytes 258056 | tf_op jit(solution)/shard_map/ppermute | solution.py:53
  51.1 1.6 %collective-permute-start.20 = (bf16[2,24,896]{2,1,0:T(8,128)(2,1)S(1)}, bf16[2,24,896]{2,1,0:T(8,128)(2,1)S(1)}, u32[]{:S(2)}, u32[]{:S(2)}) collective-permute-start(bf16[2,24,896]{2,1,0:T(8,128)(2,1)S(1)} %get-tuple-element.25), channel_id=1, source_target_pairs={{0,14},{1,15},{2,12},{3,13},{4,10},{5,11},{6,8},{7,9},{8,6},{9,7},... | collective-permute-start | bytes 258056 | tf_op jit(solution)/shard_map/ppermute | solution.py:53
  52.7 2.5 %collective-permute-start.14 = (bf16[2,24,896]{2,1,0:T(8,128)(2,1)S(1)}, bf16[2,24,896]{2,1,0:T(8,128)(2,1)S(1)}, u32[]{:S(2)}, u32[]{:S(2)}) collective-permute-start(bf16[2,24,896]{2,1,0:T(8,128)(2,1)S(1)} %get-tuple-element.24), channel_id=1, source_target_pairs={{0,8},{1,9},{2,10},{3,11},{4,12},{5,13},{6,14},{7,15},{8,0},{9,1},... | collective-permute-start | bytes 258056 | tf_op jit(solution)/shard_map/ppermute | solution.py:53
  55.8 4.9 %collective-permute-done.19 = bf16[2,24,896]{2,1,0:T(8,128)(2,1)S(1)} collective-permute-done((bf16[2,24,896]{2,1,0:T(8,128)(2,1)S(1)}, bf16[2,24,896]{2,1,0:T(8,128)(2,1)S(1)}, u32[]{:S(2)}, u32[]{:S(2)}) %collective-permute-start.19) | collective-permute-done | bytes 86048 | tf_op jit(solution)/shard_map/ppermute | solution.py:53
  60.7 3.9 %collective-permute-done.14 = bf16[2,24,896]{2,1,0:T(8,128)(2,1)S(1)} collective-permute-done((bf16[2,24,896]{2,1,0:T(8,128)(2,1)S(1)}, bf16[2,24,896]{2,1,0:T(8,128)(2,1)S(1)}, u32[]{:S(2)}, u32[]{:S(2)}) %collective-permute-start.14) | collective-permute-done | bytes 86048 | tf_op jit(solution)/shard_map/ppermute | solution.py:53
  65.5 0.6 collective-permute-done.21
  67.1 0.7 %copy-done.2 = f32[64,3584]{1,0:T(8,128)} copy-done((f32[64,3584]{1,0:T(8,128)}, f32[64,3584]{1,0:T(8,128)S(1)}, u32[]{:S(2)}) %copy-start.2) | copy-done | bytes 917528
  67.8 0.9 %fusion.19 = f32[64,3584]{1,0:T(8,128)} fusion(f32[64,3584]{1,0:T(8,128)} %copy-done.2, s32[]{:T(128)S(6)} %select_n.51, f32[64,896]{1,0:T(8,128)S(1)} %convolution_multiply_fusion.1, bf16[64,96]{0,1:T(8,128)(2,1)S(1)} %get-tuple-element.52, bf16[24,896]{1,0:T(8,128)(2,1)S(1)} %get-tuple-element.31, bf16[24,896]{1,0:T(8,128)(2,1)S(1)} %get-tuple-element.30, ...), kind=kOutput, calls=%fused_computation.23 | convolution fusion | flops 11812864 | bytes 643076 | tf_op jit(solution)/shard_map/dot_general | solution.py:102
  (88 shorter events, 7.4 us)
Async XLA Ops:
  0.0 31.8 %copy-start = (bf16[1,3584,256]{2,1,0:T(8,128)(2,1)S(1)}, bf16[1,3584,256]{2,1,0:T(8,128)(2,1)}, u32[]{:S(2)}) copy-start(bf16[1,3584,256]{2,1,0:T(8,128)(2,1)} %param.9) | copy-start | bytes 5505028
  0.0 10.0 %copy-start.3 = (s32[64,8]{0,1:T(8,128)S(1)}, s32[64,8]{0,1:T(8,128)}, u32[]{:S(2)}) copy-start(s32[64,8]{0,1:T(8,128)} %param.7) | copy-start | bytes 6148
  0.0 10.0 %copy-start.4 = (s32[64,8]{0,1:T(8,128)S(1)}, s32[64,8]{0,1:T(8,128)}, u32[]{:S(2)}) copy-start(s32[64,8]{0,1:T(8,128)} %param.8) | copy-start | bytes 6148
  2.6 20.8 %collective-permute-start = (bf16[24,3584]{1,0:T(8,128)(2,1)S(1)}, bf16[24,3584]{1,0:T(8,128)(2,1)S(1)}, u32[]{:S(2)}, u32[]{:S(2)}) collective-permute-start(bf16[24,3584]{1,0:T(8,128)(2,1)S(1)} %get-tuple-element.14), channel_id=1, source_target_pairs={{0,4},{4,0},{8,12},{12,8},{1,5},{5,1},{9,13},{13,9},{2,6},{6,2},{1... | collective-permute-start | bytes 516104 | tf_op jit(solution)/shard_map/ppermute | solution.py:44
  5.7 19.7 %collective-permute-start.1 = (bf16[24,3584]{1,0:T(8,128)(2,1)S(1)}, bf16[24,3584]{1,0:T(8,128)(2,1)S(1)}, u32[]{:S(2)}, u32[]{:S(2)}) collective-permute-start(bf16[24,3584]{1,0:T(8,128)(2,1)S(1)} %get-tuple-element.11), channel_id=1, source_target_pairs={{0,2},{1,3},{2,0},{3,1},{4,6},{5,7},{6,4},{7,5},{8,10},{9,11},{10,... | collective-permute-start | bytes 516104 | tf_op jit(solution)/shard_map/ppermute | solution.py:47
  7.2 15.3 %collective-permute-start.7 = (bf16[24,3584]{1,0:T(8,128)(2,1)S(1)}, bf16[24,3584]{1,0:T(8,128)(2,1)S(1)}, u32[]{:S(2)}, u32[]{:S(2)}) collective-permute-start(bf16[24,3584]{1,0:T(8,128)(2,1)S(1)} %get-tuple-element.13), channel_id=1, source_target_pairs={{0,8},{4,12},{8,0},{12,4},{1,9},{5,13},{9,1},{13,5},{2,10},{6,14},... | collective-permute-start | bytes 516104 | tf_op jit(solution)/shard_map/ppermute | solution.py:44
  9.8 14.8 %collective-permute-start.8 = (bf16[24,3584]{1,0:T(8,128)(2,1)S(1)}, bf16[24,3584]{1,0:T(8,128)(2,1)S(1)}, u32[]{:S(2)}, u32[]{:S(2)}) collective-permute-start(bf16[24,3584]{1,0:T(8,128)(2,1)S(1)} %get-tuple-element.12), channel_id=1, source_target_pairs={{0,12},{4,8},{8,4},{12,0},{1,13},{5,9},{9,5},{13,1},{2,14},{6,10},... | collective-permute-start | bytes 516104 | tf_op jit(solution)/shard_map/ppermute | solution.py:44
  22.5 7.5 %collective-permute-start.9 = (bf16[24,3584]{1,0:T(8,128)(2,1)S(1)}, bf16[24,3584]{1,0:T(8,128)(2,1)S(1)}, u32[]{:S(2)}, u32[]{:S(2)}) collective-permute-start(bf16[24,3584]{1,0:T(8,128)(2,1)S(1)} %collective-permute-done.7), channel_id=1, source_target_pairs={{0,2},{1,3},{2,0},{3,1},{4,6},{5,7},{6,4},{7,5},{8,10},{9,11},{10,... | collective-permute-start | bytes 516104 | tf_op jit(solution)/shard_map/ppermute | solution.py:47
  23.4 6.4 %collective-permute-start.2 = (bf16[24,3584]{1,0:T(8,128)(2,1)S(1)}, bf16[24,3584]{1,0:T(8,128)(2,1)S(1)}, u32[]{:S(2)}, u32[]{:S(2)}) collective-permute-start(bf16[24,3584]{1,0:T(8,128)(2,1)S(1)} %collective-permute-done), channel_id=1, source_target_pairs={{0,2},{1,3},{2,0},{3,1},{4,6},{5,7},{6,4},{7,5},{8,10},{9,11},{10,... | collective-permute-start | bytes 516104 | tf_op jit(solution)/shard_map/ppermute | solution.py:47
  24.6 7.1 %collective-permute-start.10 = (bf16[24,3584]{1,0:T(8,128)(2,1)S(1)}, bf16[24,3584]{1,0:T(8,128)(2,1)S(1)}, u32[]{:S(2)}, u32[]{:S(2)}) collective-permute-start(bf16[24,3584]{1,0:T(8,128)(2,1)S(1)} %collective-permute-done.8), channel_id=1, source_target_pairs={{0,2},{1,3},{2,0},{3,1},{4,6},{5,7},{6,4},{7,5},{8,10},{9,11},{10,... | collective-permute-start | bytes 516104 | tf_op jit(solution)/shard_map/ppermute | solution.py:47
  29.9 4.6 %collective-permute-start.3 = (bf16[96,3584]{1,0:T(8,128)(2,1)S(1)}, bf16[96,3584]{1,0:T(8,128)(2,1)S(1)}, u32[]{:S(2)}, u32[]{:S(2)}) collective-permute-start(bf16[96,3584]{1,0:T(8,128)(2,1)S(1)} %pad_maximum_fusion.2), channel_id=1, source_target_pairs={{0,1},{1,0},{2,3},{3,2},{4,5},{5,4},{6,7},{7,6},{8,9},{9,8},{10,11... | collective-permute-start | bytes 2064392 | tf_op jit(solution)/shard_map/ppermute | solution.py:47
  31.7 1.5 %copy-start.1 = (bf16[1,3584,256]{2,1,0:T(8,128)(2,1)S(1)}, bf16[1,3584,256]{2,1,0:T(8,128)(2,1)}, u32[]{:S(2)}) copy-start(bf16[1,3584,256]{2,1,0:T(8,128)(2,1)} %param.10) | copy-start | bytes 5505028
  31.7 4.6 %collective-permute-start.11 = (bf16[96,3584]{1,0:T(8,128)(2,1)S(1)}, bf16[96,3584]{1,0:T(8,128)(2,1)S(1)}, u32[]{:S(2)}, u32[]{:S(2)}) collective-permute-start(bf16[96,3584]{1,0:T(8,128)(2,1)S(1)} %constant_dynamic-update-slice_fusion), channel_id=1, source_target_pairs={{0,1},{1,0},{2,3},{3,2},{4,5},{5,4},{6,7},{7,6},{8,9},{9,8},{10,11... | collective-permute-start | bytes 2064392 | tf_op jit(solution)/shard_map/ppermute | solution.py:47
  35.4 5.7 %collective-permute-start.4 = (bf16[192,256]{1,0:T(8,128)(2,1)S(1)}, bf16[192,256]{1,0:T(8,128)(2,1)S(1)}, u32[]{:S(2)}, u32[]{:S(2)}) collective-permute-start(bf16[192,256]{1,0:T(8,128)(2,1)S(1)} %pad_maximum_fusion.17), channel_id=1, source_target_pairs={{0,2},{1,3},{2,0},{3,1},{4,6},{5,7},{6,4},{7,5},{8,10},{9,11},{10,... | collective-permute-start | bytes 294920 | tf_op jit(solution)/shard_map/ppermute | solution.py:47
  37.2 5.0 %collective-permute-start.12 = (bf16[192,256]{1,0:T(8,128)(2,1)S(1)}, bf16[192,256]{1,0:T(8,128)(2,1)S(1)}, u32[]{:S(2)}, u32[]{:S(2)}) collective-permute-start(bf16[192,256]{1,0:T(8,128)(2,1)S(1)} %pad_maximum_fusion.19), channel_id=1, source_target_pairs={{0,2},{1,3},{2,0},{3,1},{4,6},{5,7},{6,4},{7,5},{8,10},{9,11},{10,... | collective-permute-start | bytes 294920 | tf_op jit(solution)/shard_map/ppermute | solution.py:47
  41.2 1.5 %collective-permute-start.5 = (bf16[192,512]{1,0:T(8,128)(2,1)S(1)}, bf16[192,512]{1,0:T(8,128)(2,1)S(1)}, u32[]{:S(2)}, u32[]{:S(2)}) collective-permute-start(bf16[192,512]{1,0:T(8,128)(2,1)S(1)} %pad_maximum_fusion.9), channel_id=1, source_target_pairs={{0,1},{1,0},{2,3},{3,2},{4,5},{5,4},{6,7},{7,6},{8,9},{9,8},{10,11... | collective-permute-start | bytes 589832 | tf_op jit(solution)/shard_map/ppermute | solution.py:47
  42.2 4.9 %collective-permute-start.13 = (bf16[192,512]{1,0:T(8,128)(2,1)S(1)}, bf16[192,512]{1,0:T(8,128)(2,1)S(1)}, u32[]{:S(2)}, u32[]{:S(2)}) collective-permute-start(bf16[192,512]{1,0:T(8,128)(2,1)S(1)} %pad_maximum_fusion.10), channel_id=1, source_target_pairs={{0,1},{1,0},{2,3},{3,2},{4,5},{5,4},{6,7},{7,6},{8,9},{9,8},{10,11... | collective-permute-start | bytes 589832 | tf_op jit(solution)/shard_map/ppermute | solution.py:47
  43.6 9.1 %collective-permute-start.16 = (bf16[2,24,896]{2,1,0:T(8,128)(2,1)S(1)}, bf16[2,24,896]{2,1,0:T(8,128)(2,1)S(1)}, u32[]{:S(2)}, u32[]{:S(2)}) collective-permute-start(bf16[2,24,896]{2,1,0:T(8,128)(2,1)S(1)} %get-tuple-element.19), channel_id=1, source_target_pairs={{0,2},{1,3},{2,0},{3,1},{4,6},{5,7},{6,4},{7,5},{8,10},{9,11},{10,... | collective-permute-start | bytes 258056 | tf_op jit(solution)/shard_map/ppermute | solution.py:53
  44.2 11.0 %collective-permute-start.17 = (bf16[2,24,896]{2,1,0:T(8,128)(2,1)S(1)}, bf16[2,24,896]{2,1,0:T(8,128)(2,1)S(1)}, u32[]{:S(2)}, u32[]{:S(2)}) collective-permute-start(bf16[2,24,896]{2,1,0:T(8,128)(2,1)S(1)} %get-tuple-element.21), channel_id=1, source_target_pairs={{0,6},{1,7},{2,4},{3,5},{4,2},{5,3},{6,0},{7,1},{8,14},{9,15},{10,... | collective-permute-start | bytes 258056 | tf_op jit(solution)/shard_map/ppermute | solution.py:53
  46.4 9.2 %collective-permute-start.6 = (bf16[2,24,896]{2,1,0:T(8,128)(2,1)S(1)}, bf16[2,24,896]{2,1,0:T(8,128)(2,1)S(1)}, u32[]{:S(2)}, u32[]{:S(2)}) collective-permute-start(bf16[2,24,896]{2,1,0:T(8,128)(2,1)S(1)} %get-tuple-element.20), channel_id=1, source_target_pairs={{0,4},{1,5},{2,6},{3,7},{4,0},{5,1},{6,2},{7,3},{8,12},{9,13},{10,... | collective-permute-start | bytes 258056 | tf_op jit(solution)/shard_map/ppermute | solution.py:53
  48.1 12.6 %collective-permute-start.19 = (bf16[2,24,896]{2,1,0:T(8,128)(2,1)S(1)}, bf16[2,24,896]{2,1,0:T(8,128)(2,1)S(1)}, u32[]{:S(2)}, u32[]{:S(2)}) collective-permute-start(bf16[2,24,896]{2,1,0:T(8,128)(2,1)S(1)} %get-tuple-element.22), channel_id=1, source_target_pairs={{0,10},{1,11},{2,8},{3,9},{4,14},{5,15},{6,12},{7,13},{8,2},{9,3},... | collective-permute-start | bytes 258056 | tf_op jit(solution)/shard_map/ppermute | solution.py:53
  51.1 9.6 %collective-permute-start.20 = (bf16[2,24,896]{2,1,0:T(8,128)(2,1)S(1)}, bf16[2,24,896]{2,1,0:T(8,128)(2,1)S(1)}, u32[]{:S(2)}, u32[]{:S(2)}) collective-permute-start(bf16[2,24,896]{2,1,0:T(8,128)(2,1)S(1)} %get-tuple-element.25), channel_id=1, source_target_pairs={{0,14},{1,15},{2,12},{3,13},{4,10},{5,11},{6,8},{7,9},{8,6},{9,7},... | collective-permute-start | bytes 258056 | tf_op jit(solution)/shard_map/ppermute | solution.py:53
  52.7 11.9 %collective-permute-start.14 = (bf16[2,24,896]{2,1,0:T(8,128)(2,1)S(1)}, bf16[2,24,896]{2,1,0:T(8,128)(2,1)S(1)}, u32[]{:S(2)}, u32[]{:S(2)}) collective-permute-start(bf16[2,24,896]{2,1,0:T(8,128)(2,1)S(1)} %get-tuple-element.24), channel_id=1, source_target_pairs={{0,8},{1,9},{2,10},{3,11},{4,12},{5,13},{6,14},{7,15},{8,0},{9,1},... | collective-permute-start | bytes 258056 | tf_op jit(solution)/shard_map/ppermute | solution.py:53
  55.2 9.4 %collective-permute-start.15 = (bf16[2,24,896]{2,1,0:T(8,128)(2,1)S(1)}, bf16[2,24,896]{2,1,0:T(8,128)(2,1)S(1)}, u32[]{:S(2)}, u32[]{:S(2)}) collective-permute-start(bf16[2,24,896]{2,1,0:T(8,128)(2,1)S(1)} %get-tuple-element.23), channel_id=1, source_target_pairs={{0,12},{1,13},{2,14},{3,15},{4,8},{5,9},{6,10},{7,11},{8,4},{9,5},... | collective-permute-start | bytes 258056 | tf_op jit(solution)/shard_map/ppermute | solution.py:53
  55.7 9.8 %collective-permute-start.18 = (bf16[4,24,896]{2,1,0:T(8,128)(2,1)S(1)}, bf16[4,24,896]{2,1,0:T(8,128)(2,1)S(1)}, u32[]{:S(2)}, u32[]{:S(2)}) collective-permute-start(bf16[4,24,896]{2,1,0:T(8,128)(2,1)S(1)} %pad_maximum_fusion.12), channel_id=1, source_target_pairs={{0,1},{1,0},{2,3},{3,2},{4,5},{5,4},{6,7},{7,6},{8,9},{9,8},{10,11... | collective-permute-start | bytes 516104 | tf_op jit(solution)/shard_map/ppermute | solution.py:47
  64.7 1.5 %collective-permute-start.21 = (bf16[4,24,896]{2,1,0:T(8,128)(2,1)S(1)}, bf16[4,24,896]{2,1,0:T(8,128)(2,1)S(1)}, u32[]{:S(2)}, u32[]{:S(2)}) collective-permute-start(bf16[4,24,896]{2,1,0:T(8,128)(2,1)S(1)} %pad_maximum_fusion.13), channel_id=1, source_target_pairs={{0,1},{1,0},{2,3},{3,2},{4,5},{5,4},{6,7},{7,6},{8,9},{9,8},{10,11... | collective-permute-start | bytes 516104 | tf_op jit(solution)/shard_map/ppermute | solution.py:47
  66.8 0.9 %copy-start.2 = (f32[64,3584]{1,0:T(8,128)}, f32[64,3584]{1,0:T(8,128)S(1)}, u32[]{:S(2)}) copy-start(f32[64,3584]{1,0:T(8,128)S(1)} %fusion.21) | copy-start | bytes 2752516

commit v3 on v2

--- a/solution.py
+++ b/solution.py
@@ -4,6 +4,10 @@
 from jax.sharding import PartitionSpec as P
 
 EXP_POD = 8
+
+
+def after(value, *earlier):
+    return lax.optimization_barrier((value,) + earlier)[0]
 
 
 def per_device(tokens, routes, combine_fixed, gate_weight, up_weight, down_weight):
@@ -52,44 +56,84 @@
         pairs = [(a * n_loc + b, (a ^ s) * n_loc + (b ^ m)) for a in range(n_out) for b in range(n_loc)]
         return lax.ppermute(v, ("outer", "local"), pairs)
 
-    half = n_out // 2
+    def first_half(rows):
+        gate_proj = jnp.dot(rows, gate_local, preferred_element_type=jnp.float32)
+        up_proj = jnp.dot(rows, up_local, preferred_element_type=jnp.float32)
+        return (jax.nn.silu(gate_proj) * up_proj).astype(jnp.bfloat16)
+
+    quarter = max(1, n_out // 4)
+    near = list(range(n_out - 2 * quarter))
+    far = list(range(n_out - quarter, n_out))
+    mid = list(range(n_out - 2 * quarter, n_out - quarter))
+
+    mine = {0: panels[0]}
+    chip_of = {}
+
+    def to_chips(steps):
+        for s in steps:
+            chip_of[s, 0] = mine[s]
+            for x in range(1, n_chip):
+                chip_of[s, x] = local_xor(mine[s], 2 * x)
+
+    for s in near[1:] + far:
+        mine[s] = outer_xor(panels[s], s)
+    to_chips(near)
+    for s in mid:
+        mine[s] = outer_xor(after(panels[s], mine[near[-1]]), s)
+    for s in far:
+        mine[s] = after(mine[s], chip_of[near[-1], n_chip - 1])
+    to_chips(far)
+    for s in mid:
+        mine[s] = after(mine[s], chip_of[far[-1], n_chip - 1])
+    to_chips(mid)
+
     pieces = {}
-    for steps in (list(range(half)), list(range(half, n_out))):
+    landed = {}
+    for steps in (near, far, mid):
         count = len(steps)
-        mine = {s: panels[s] if s == 0 else outer_xor(panels[s], s) for s in steps}
-        rows_same = jnp.concatenate(
-            [mine[s] if x == 0 else local_xor(mine[s], 2 * x) for x in range(n_chip) for s in steps], axis=0
-        )
-        rows_other = local_xor(rows_same, 1)
-
-        def first_half(rows):
-            gate_proj = jnp.dot(rows, gate_local, preferred_element_type=jnp.float32)
-            up_proj = jnp.dot(rows, up_local, preferred_element_type=jnp.float32)
-            return (jax.nn.silu(gate_proj) * up_proj).astype(jnp.bfloat16)
-
-        hidden = jnp.concatenate([first_half(rows_same), first_half(rows_other)], axis=0)
+        pairs = []
+        for x in range(n_chip):
+            if steps is mid and x > 0:
+                for s in steps:
+                    chip_of[s, x] = after(chip_of[s, x], hidden_other)
+            same = jnp.concatenate([chip_of[s, x] for s in steps], axis=0)
+            pairs.append(first_half(jnp.concatenate([same, local_xor(same, 1)], axis=0)))
+        hidden = jnp.concatenate(pairs, axis=0)
         sides = []
         for x in range(n_chip):
             side = hidden if x == 0 else local_xor(hidden, 2 * x)
-            side = side.reshape(2, n_chip, -1, part_hid)
-            sides.append(jnp.concatenate([side[:, y ^ x : (y ^ x) + 1] for y in range(n_chip)], axis=1))
-        hidden_same = jnp.concatenate(sides, axis=3).reshape(2 * n_chip * count * capacity, n_chip * part_hid)
+            side = side.reshape(n_chip, -1, part_hid)
+            sides.append(jnp.concatenate([side[y ^ x : (y ^ x) + 1] for y in range(n_chip)], axis=0))
+        hidden_same = jnp.concatenate(sides, axis=2).reshape(2 * n_chip * count * capacity, n_chip * part_hid)
         hidden_other = local_xor(hidden_same, 1)
         out_same = jnp.dot(hidden_same, down_same, preferred_element_type=jnp.float32)
         out_other = jnp.dot(hidden_other, down_other, preferred_element_type=jnp.float32)
-        out_other = out_other.reshape(2, -1, part_out)
-        out_other = jnp.concatenate([out_other[1:], out_other[:1]], axis=0).reshape(out_same.shape)
+        out_other = out_other.reshape(n_chip, 2, -1, part_out)
+        out_other = jnp.concatenate([out_other[:, 1:], out_other[:, :1]], axis=1).reshape(out_same.shape)
         expert_out = (out_same + out_other).astype(jnp.bfloat16)
-        expert_out = expert_out.reshape(2, n_chip, count, capacity, part_out)
-        landed = {
-            (at, x): both_xor(expert_out[:, x, at], s, 2 * x) for at, s in enumerate(steps) for x in range(n_chip)
-        }
-        swapped = local_xor(
-            jnp.stack([landed[at, x][1] for at in range(count) for x in range(n_chip)]), 1
-        )
+        expert_out = expert_out.reshape(n_chip, 2, count, capacity, part_out)
+        if steps is near:
+            for x in range(n_chip):
+                block = expert_out[x] if x == 0 else local_xor(expert_out[x], 2 * x)
+                for at, s in enumerate(steps):
+                    landed[s, x] = block[:, at]
+            for s in steps[1:]:
+                moved = outer_xor(jnp.stack([landed[s, x] for x in range(n_chip)]), s)
+                for x in range(n_chip):
+                    landed[s, x] = moved[x]
+        else:
+            for at, s in enumerate(steps):
+                for x in range(n_chip):
+                    landed[s, x] = both_xor(expert_out[x, :, at], s, 2 * x)
+
+    for steps in (far + near, mid):
+        for s in steps:
+            for x in range(n_chip):
+                landed[s, x] = after(landed[s, x], swapped if steps is mid else expert_out)
+        swapped = local_xor(jnp.stack([landed[s, x][1] for s in steps for x in range(n_chip)]), 1)
         for at, s in enumerate(steps):
             for x in range(n_chip):
-                pieces[s, 2 * x] = landed[at, x][0]
+                pieces[s, 2 * x] = landed[s, x][0]
                 pieces[s, 2 * x + 1] = swapped[at * n_chip + x]
 
     spread = jnp.where(placing, fixed[:, :, None], 0).reshape(tok_rows, -1)

time: 69.7 us -> 76.7 us (1.10); the launches traced: 68.7 us -> 76.5 us
  starting transfers between devices: 23.9 us -> 31.6 us
  matrix products: 8.73 us -> 10.9 us
  waiting for transfers between devices: 30.1 us -> 28.7 us
  local copies, waits for them, and re-layouts: 3.95 us -> 3.18 us
    ppermute x12 -> x19, starting transfers between devices: 6.97 us -> 12.6 us  [local_xor(): return lax.ppermute(v, 'local', [(i, i ^ m) for i in range(n_loc)])]
    ppermute x3 -> x4, waiting for transfers between devices: 10.6 us -> 5.25 us  [outer_xor(): return lax.ppermute(v, 'outer', [(i, i ^ s) for i in range(n_out)])]
    ppermute x3 -> x4, starting transfers between devices: 5.91 us -> 10.7 us  [outer_xor(): return lax.ppermute(v, 'outer', [(i, i ^ s) for i in range(n_out)])]
    ppermute x12 -> x19, waiting for transfers between devices: 10.6 us -> 15.3 us  [local_xor(): return lax.ppermute(v, 'local', [(i, i ^ m) for i in range(n_loc)])]
    ppermute x7 -> x4, starting transfers between devices: 11.1 us -> 8.38 us  [both_xor(): return lax.ppermute(v, ('outer', 'local'), pairs)]
    unnamed x13 -> x17, local copies, waits for them, and re-layouts: 1.71 us -> 0.8 us
    dot_general x4 -> x6, matrix products: 1.73 us -> 2.57 us  [first_half(): gate_proj = jnp.dot(rows, gate_local, preferred_element_type=jnp.float32)]
    dot_general x4 -> x6, matrix products: 1.74 us -> 2.59 us  [first_half(): up_proj = jnp.dot(rows, up_local, preferred_element_type=jnp.float32)]
  transfers between devices with their start and end apart: 22 -> 27, of which waited for: 9 -> 12; matrix products, arithmetic and copies ran while one was open for 12% -> 14% of each run, Pallas kernels for 0% -> 0%
where the time goes in v3:
time: 76.7 us; the launch traced here: 76.5 us
  starting transfers between devices  31.6 us (41%)
  waiting for transfers between devices  28.7 us (37%)
  matrix products  10.9 us (14%)
  local copies, waits for them, and re-layouts  3.18 us (4%)
  other arithmetic  1.45 us (2%)
    ppermute x19, waiting for transfers between devices, local_xor(): return lax.ppermute(v, 'local', [(i, i ^ m) for i in range(n_loc)])  15.3 us
    ppermute x19, starting transfers between devices, local_xor(): return lax.ppermute(v, 'local', [(i, i ^ m) for i in range(n_loc)])  12.6 us
    ppermute x4, starting transfers between devices, outer_xor(): return lax.ppermute(v, 'outer', [(i, i ^ s) for i in range(n_out)])  10.7 us
    ppermute x4, starting transfers between devices, both_xor(): return lax.ppermute(v, ('outer', 'local'), pairs)  8.38 us
    ppermute x4, waiting for transfers between devices, both_xor(): return lax.ppermute(v, ('outer', 'local'), pairs)  8.23 us
    ppermute x4, waiting for transfers between devices, outer_xor(): return lax.ppermute(v, 'outer', [(i, i ^ s) for i in range(n_out)])  5.25 us
    dot_general x6, matrix products, first_half(): up_proj = jnp.dot(rows, up_local, preferred_element_type=jnp.float32)  2.59 us
    dot_general x6, matrix products, first_half(): gate_proj = jnp.dot(rows, gate_local, preferred_element_type=jnp.float32)  2.57 us
  transfers between devices with their start and end apart: 27, of which 12 were waited for; matrix products, arithmetic and copies ran while one was open for 14% of the time, Pallas kernels for 0%

profile of v3, /device:TPU:0, one launch (start us, length us, event | category | flops | bytes accessed | tf_op | source)
XLA Modules:
  0.0 76.5 jit_solution(6510901231574983178)
XLA Ops:
  0.0 0.9 %compare_reduce_fusion = pred[64,4]{0,1:T(4,128)(4,1)S(1)} fusion(s32[64,8]{0,1:T(8,128)} %param.7, s32[4]{0:T(128)S(1)} %xor_multiply_fusion), kind=kLoop, calls=%fused_computation.139 | loop fusion | flops 3840 | bytes 2320 | tf_op jit(solution)/shard_map/reduce_or | solution.py:40
  1.2 1.3 %convolution_convert_fusion = bf16[4,24,3584]{2,1,0:T(8,128)(2,1)S(1)} fusion(bf16[64,3584]{1,0:T(8,128)(2,1)} %param.6, s32[64,4]{0,1:T(4,128)S(1)} %add_select_fusion), kind=kOutput, calls=%fused_computation | convolution fusion | flops 44390400 | bytes 1147904 | tf_op jit(solution)/shard_map/tqc,td->qcd/dot_general | solution.py:43
  2.6 3.1 %collective-permute-start = (bf16[24,3584]{1,0:T(8,128)(2,1)S(1)}, bf16[24,3584]{1,0:T(8,128)(2,1)S(1)}, u32[]{:S(2)}, u32[]{:S(2)}) collective-permute-start(bf16[24,3584]{1,0:T(8,128)(2,1)S(1)} %get-tuple-element.38), channel_id=1, source_target_pairs={{0,4},{4,0},{8,12},{12,8},{1,5},{5,1},{9,13},{13,9},{2,6},{6,2},{1... | collective-permute-start | bytes 516104 | tf_op jit(solution)/shard_map/ppermute | solution.py:48
  5.7 2.5 %collective-permute-start.8 = (bf16[24,3584]{1,0:T(8,128)(2,1)S(1)}, bf16[24,3584]{1,0:T(8,128)(2,1)S(1)}, u32[]{:S(2)}, u32[]{:S(2)}) collective-permute-start(bf16[24,3584]{1,0:T(8,128)(2,1)S(1)} %get-tuple-element.36), channel_id=1, source_target_pairs={{0,12},{4,8},{8,4},{12,0},{1,13},{5,9},{9,5},{13,1},{2,14},{6,10},... | collective-permute-start | bytes 516104 | tf_op jit(solution)/shard_map/ppermute | solution.py:48
  8.2 1.5 %collective-permute-start.2 = (bf16[24,3584]{1,0:T(8,128)(2,1)S(1)}, bf16[24,3584]{1,0:T(8,128)(2,1)S(1)}, u32[]{:S(2)}, u32[]{:S(2)}) collective-permute-start(bf16[24,3584]{1,0:T(8,128)(2,1)S(1)} %get-tuple-element.35), channel_id=1, source_target_pairs={{0,2},{1,3},{2,0},{3,1},{4,6},{5,7},{6,4},{7,5},{8,10},{9,11},{10,... | collective-permute-start | bytes 516104 | tf_op jit(solution)/shard_map/ppermute | solution.py:51
  9.7 1.6 %dynamic-slice_bitcast_fusion.3 = (bf16[256,896]{1,0:T(8,128)(2,1)S(1)}, bf16[256,896]{1,0:T(8,128)(2,1)S(1)}, bf16[256,896]{1,0:T(8,128)(2,1)S(1)}, bf16[256,896]{1,0:T(8,128)(2,1)S(1)}) fusion(bf16[1,1024,896]{2,1,0:T(8,128)(2,1)} %param.11, s32[]{:T(128)S(6)} %select_n.44, s32[]{:T(128)S(6)} %select_n.45, s32[]{:T(128)S(6)} %select_n.47, s32[]{:T(128)S(6)} %select_n.46), kind=kLoop, calls=%fused_computation.55 | loop fusion | bytes 3670032 | tf_op jit(solution)/shard_map/dynamic_slice | solution.py:29
  11.3 2.6 %collective-permute-start.7 = (bf16[24,3584]{1,0:T(8,128)(2,1)S(1)}, bf16[24,3584]{1,0:T(8,128)(2,1)S(1)}, u32[]{:S(2)}, u32[]{:S(2)}) collective-permute-start(bf16[24,3584]{1,0:T(8,128)(2,1)S(1)} %get-tuple-element.17), channel_id=1, source_target_pairs={{0,8},{4,12},{8,0},{12,4},{1,9},{5,13},{9,1},{13,5},{2,10},{6,14},... | collective-permute-start | bytes 516104 | tf_op jit(solution)/shard_map/ppermute | solution.py:48
  14.1 1.6 %collective-permute-start.3 = (bf16[24,3584]{1,0:T(8,128)(2,1)S(1)}, bf16[24,3584]{1,0:T(8,128)(2,1)S(1)}, u32[]{:S(2)}, u32[]{:S(2)}) collective-permute-start(bf16[24,3584]{1,0:T(8,128)(2,1)S(1)} %collective-permute-done), channel_id=1, source_target_pairs={{0,2},{1,3},{2,0},{3,1},{4,6},{5,7},{6,4},{7,5},{8,10},{9,11},{10,... | collective-permute-start | bytes 516104 | tf_op jit(solution)/shard_map/ppermute | solution.py:51
  15.6 1.5 %collective-permute-done.8 = bf16[24,3584]{1,0:T(8,128)(2,1)S(1)} collective-permute-done((bf16[24,3584]{1,0:T(8,128)(2,1)S(1)}, bf16[24,3584]{1,0:T(8,128)(2,1)S(1)}, u32[]{:S(2)}, u32[]{:S(2)}) %collective-permute-start.8) | collective-permute-done | bytes 172064 | tf_op jit(solution)/shard_map/ppermute | solution.py:48
  17.2 3.7 %collective-permute-done.3 = bf16[24,3584]{1,0:T(8,128)(2,1)S(1)} collective-permute-done((bf16[24,3584]{1,0:T(8,128)(2,1)S(1)}, bf16[24,3584]{1,0:T(8,128)(2,1)S(1)}, u32[]{:S(2)}, u32[]{:S(2)}) %collective-permute-start.3) | collective-permute-done | bytes 172064 | tf_op jit(solution)/shard_map/ppermute | solution.py:51
  20.9 1.5 %collective-permute-start.9 = (bf16[24,3584]{1,0:T(8,128)(2,1)S(1)}, bf16[24,3584]{1,0:T(8,128)(2,1)S(1)}, u32[]{:S(2)}, u32[]{:S(2)}) collective-permute-start(bf16[24,3584]{1,0:T(8,128)(2,1)S(1)} %collective-permute-done.8), channel_id=1, source_target_pairs={{0,2},{1,3},{2,0},{3,1},{4,6},{5,7},{6,4},{7,5},{8,10},{9,11},{10,... | collective-permute-start | bytes 516104 | tf_op jit(solution)/shard_map/ppermute | solution.py:51
  22.5 0.6 collective-permute-start.4
  23.4 3.4 %collective-permute-done.9 = bf16[24,3584]{1,0:T(8,128)(2,1)S(1)} collective-permute-done((bf16[24,3584]{1,0:T(8,128)(2,1)S(1)}, bf16[24,3584]{1,0:T(8,128)(2,1)S(1)}, u32[]{:S(2)}, u32[]{:S(2)}) %collective-permute-start.9) | collective-permute-done | bytes 172064 | tf_op jit(solution)/shard_map/ppermute | solution.py:51
  26.8 1.5 %collective-permute-start.11 = (bf16[24,3584]{1,0:T(8,128)(2,1)S(1)}, bf16[24,3584]{1,0:T(8,128)(2,1)S(1)}, u32[]{:S(2)}, u32[]{:S(2)}) collective-permute-start(bf16[24,3584]{1,0:T(8,128)(2,1)S(1)} %collective-permute-done.7), channel_id=1, source_target_pairs={{0,2},{1,3},{2,0},{3,1},{4,6},{5,7},{6,4},{7,5},{8,10},{9,11},{10,... | collective-permute-start | bytes 516104 | tf_op jit(solution)/shard_map/ppermute | solution.py:51
  28.9 0.6 collective-permute-start.13
  31.7 0.6 collective-permute-start.14
  34.1 1.6 %collective-permute-start.5 = (bf16[192,256]{1,0:T(8,128)(2,1)S(1)}, bf16[192,256]{1,0:T(8,128)(2,1)S(1)}, u32[]{:S(2)}, u32[]{:S(2)}) collective-permute-start(bf16[192,256]{1,0:T(8,128)(2,1)S(1)} %pad_maximum_fusion.21), channel_id=1, source_target_pairs={{0,2},{1,3},{2,0},{3,1},{4,6},{5,7},{6,4},{7,5},{8,10},{9,11},{10,... | collective-permute-start | bytes 294920 | tf_op jit(solution)/shard_map/ppermute | solution.py:51
  35.9 2.9 %collective-permute-done.5 = bf16[192,256]{1,0:T(8,128)(2,1)S(1)} collective-permute-done((bf16[192,256]{1,0:T(8,128)(2,1)S(1)}, bf16[192,256]{1,0:T(8,128)(2,1)S(1)}, u32[]{:S(2)}, u32[]{:S(2)}) %collective-permute-start.5) | collective-permute-done | bytes 98336 | tf_op jit(solution)/shard_map/ppermute | solution.py:51
  40.2 3.5 %collective-permute-start.23 = (bf16[2,24,896]{2,1,0:T(8,128)(2,1)S(1)}, bf16[2,24,896]{2,1,0:T(8,128)(2,1)S(1)}, u32[]{:S(2)}, u32[]{:S(2)}) collective-permute-start(bf16[2,24,896]{2,1,0:T(8,128)(2,1)S(1)} %bitcast.202), channel_id=1, source_target_pairs={{0,14},{1,15},{2,12},{3,13},{4,10},{5,11},{6,8},{7,9},{8,6},{9,7},... | collective-permute-start | bytes 258056 | tf_op jit(solution)/shard_map/ppermute | solution.py:57
  43.7 1.3 %collective-permute-start.22 = (bf16[2,24,896]{2,1,0:T(8,128)(2,1)S(1)}, bf16[2,24,896]{2,1,0:T(8,128)(2,1)S(1)}, u32[]{:S(2)}, u32[]{:S(2)}) collective-permute-start(bf16[2,24,896]{2,1,0:T(8,128)(2,1)S(1)} %bitcast.201), channel_id=1, source_target_pairs={{0,12},{1,13},{2,14},{3,15},{4,8},{5,9},{6,10},{7,11},{8,4},{9,5},... | collective-permute-start | bytes 258056 | tf_op jit(solution)/shard_map/ppermute | solution.py:57
  46.8 0.6 collective-permute-start.17
  47.5 1.6 %collective-permute-start.19 = (bf16[2,2,24,896]{3,2,1,0:T(8,128)(2,1)S(1)}, bf16[2,2,24,896]{3,2,1,0:T(8,128)(2,1)S(1)}, u32[]{:S(2)}, u32[]{:S(2)}) collective-permute-start(bf16[2,2,24,896]{3,2,1,0:T(8,128)(2,1)S(1)} %bitcast.196), channel_id=1, source_target_pairs={{0,2},{1,3},{2,0},{3,1},{4,6},{5,7},{6,4},{7,5},{8,10},{9,11},{10,... | collective-permute-start | bytes 516104 | tf_op jit(solution)/shard_map/ppermute | solution.py:51
  49.0 2.6 %collective-permute-done.17 = bf16[96,256]{1,0:T(8,128)(2,1)S(1)} collective-permute-done((bf16[96,256]{1,0:T(8,128)(2,1)S(1)}, bf16[96,256]{1,0:T(8,128)(2,1)S(1)}, u32[]{:S(2)}, u32[]{:S(2)}) %collective-permute-start.17) | collective-permute-done | bytes 49184 | tf_op jit(solution)/shard_map/ppermute | solution.py:51
  51.7 2.0 %collective-permute-done.19 = bf16[2,2,24,896]{3,2,1,0:T(8,128)(2,1)S(1)} collective-permute-done((bf16[2,2,24,896]{3,2,1,0:T(8,128)(2,1)S(1)}, bf16[2,2,24,896]{3,2,1,0:T(8,128)(2,1)S(1)}, u32[]{:S(2)}, u32[]{:S(2)}) %collective-permute-start.19) | collective-permute-done | bytes 172064 | tf_op jit(solution)/shard_map/ppermute | solution.py:51
  53.8 2.5 %collective-permute-start.20 = (bf16[2,2,24,896]{3,2,1,0:T(8,128)(2,1)S(1)}, bf16[2,2,24,896]{3,2,1,0:T(8,128)(2,1)S(1)}, u32[]{:S(2)}, u32[]{:S(2)}) collective-permute-start(bf16[2,2,24,896]{3,2,1,0:T(8,128)(2,1)S(1)} %pad_maximum_fusion.16), channel_id=1, source_target_pairs={{0,4},{4,0},{8,12},{12,8},{1,5},{5,1},{9,13},{13,9},{2,6},{6,2},{1... | collective-permute-start | bytes 516104 | tf_op jit(solution)/shard_map/ppermute | solution.py:48
  57.1 3.4 %collective-permute-done.20 = bf16[2,2,24,896]{3,2,1,0:T(8,128)(2,1)S(1)} collective-permute-done((bf16[2,2,24,896]{3,2,1,0:T(8,128)(2,1)S(1)}, bf16[2,2,24,896]{3,2,1,0:T(8,128)(2,1)S(1)}, u32[]{:S(2)}, u32[]{:S(2)}) %collective-permute-start.20) | collective-permute-done | bytes 172064 | tf_op jit(solution)/shard_map/ppermute | solution.py:48
  60.6 1.0 %collective-permute-start.21 = (bf16[2,24,896]{2,1,0:T(8,128)(2,1)S(1)}, bf16[2,24,896]{2,1,0:T(8,128)(2,1)S(1)}, u32[]{:S(2)}, u32[]{:S(2)}) collective-permute-start(bf16[2,24,896]{2,1,0:T(8,128)(2,1)S(1)} %bitcast.204), channel_id=1, source_target_pairs={{0,8},{1,9},{2,10},{3,11},{4,12},{5,13},{6,14},{7,15},{8,0},{9,1},... | collective-permute-start | bytes 258056 | tf_op jit(solution)/shard_map/ppermute | solution.py:57
  61.6 2.6 %collective-permute-start.25 = (bf16[2,24,896]{2,1,0:T(8,128)(2,1)S(1)}, bf16[2,24,896]{2,1,0:T(8,128)(2,1)S(1)}, u32[]{:S(2)}, u32[]{:S(2)}) collective-permute-start(bf16[2,24,896]{2,1,0:T(8,128)(2,1)S(1)} %bitcast.203), channel_id=1, source_target_pairs={{0,10},{1,11},{2,8},{3,9},{4,14},{5,15},{6,12},{7,13},{8,2},{9,3},... | collective-permute-start | bytes 258056 | tf_op jit(solution)/shard_map/ppermute | solution.py:57
  64.4 6.2 %collective-permute-done.21 = bf16[2,24,896]{2,1,0:T(8,128)(2,1)S(1)} collective-permute-done((bf16[2,24,896]{2,1,0:T(8,128)(2,1)S(1)}, bf16[2,24,896]{2,1,0:T(8,128)(2,1)S(1)}, u32[]{:S(2)}, u32[]{:S(2)}) %collective-permute-start.21) | collective-permute-done | bytes 86048 | tf_op jit(solution)/shard_map/ppermute | solution.py:57
  70.6 2.0 %collective-permute-done.25 = bf16[2,24,896]{2,1,0:T(8,128)(2,1)S(1)} collective-permute-done((bf16[2,24,896]{2,1,0:T(8,128)(2,1)S(1)}, bf16[2,24,896]{2,1,0:T(8,128)(2,1)S(1)}, u32[]{:S(2)}, u32[]{:S(2)}) %collective-permute-start.25) | collective-permute-done | bytes 86048 | tf_op jit(solution)/shard_map/ppermute | solution.py:57
  74.9 0.7 copy-done.2
  75.6 0.9 %fusion.28 = f32[64,3584]{1,0:T(8,128)} fusion(f32[64,3584]{1,0:T(8,128)} %copy-done.2, s32[]{:T(128)S(6)} %select_n.51, f32[64,896]{1,0:T(8,128)S(1)} %convolution_multiply_fusion.1, bf16[64,96]{0,1:T(8,128)(2,1)S(1)} %get-tuple-element.85, bf16[24,896]{1,0:T(8,128)(2,1)S(1)} %get-tuple-element.46, bf16[24,896]{1,0:T(8,128)(2,1)S(1)} %get-tuple-element.63, ...), kind=kOutput, calls=%fused_computation.33 | convolution fusion | flops 11812864 | bytes 643076 | tf_op jit(solution)/shard_map/dot_general | solution.py:146
  (118 shorter events, 12.2 us)
Async XLA Ops:
  0.0 28.4 %copy-start = (bf16[1,3584,256]{2,1,0:T(8,128)(2,1)S(1)}, bf16[1,3584,256]{2,1,0:T(8,128)(2,1)}, u32[]{:S(2)}) copy-start(bf16[1,3584,256]{2,1,0:T(8,128)(2,1)} %param.9) | copy-start | bytes 5505028
  2.6 8.7 %collective-permute-start = (bf16[24,3584]{1,0:T(8,128)(2,1)S(1)}, bf16[24,3584]{1,0:T(8,128)(2,1)S(1)}, u32[]{:S(2)}, u32[]{:S(2)}) collective-permute-start(bf16[24,3584]{1,0:T(8,128)(2,1)S(1)} %get-tuple-element.38), channel_id=1, source_target_pairs={{0,4},{4,0},{8,12},{12,8},{1,5},{5,1},{9,13},{13,9},{2,6},{6,2},{1... | collective-permute-start | bytes 516104 | tf_op jit(solution)/shard_map/ppermute | solution.py:48
  5.7 11.5 %collective-permute-start.8 = (bf16[24,3584]{1,0:T(8,128)(2,1)S(1)}, bf16[24,3584]{1,0:T(8,128)(2,1)S(1)}, u32[]{:S(2)}, u32[]{:S(2)}) collective-permute-start(bf16[24,3584]{1,0:T(8,128)(2,1)S(1)} %get-tuple-element.36), channel_id=1, source_target_pairs={{0,12},{4,8},{8,4},{12,0},{1,13},{5,9},{9,5},{13,1},{2,14},{6,10},... | collective-permute-start | bytes 516104 | tf_op jit(solution)/shard_map/ppermute | solution.py:48
  8.2 7.5 %collective-permute-start.2 = (bf16[24,3584]{1,0:T(8,128)(2,1)S(1)}, bf16[24,3584]{1,0:T(8,128)(2,1)S(1)}, u32[]{:S(2)}, u32[]{:S(2)}) collective-permute-start(bf16[24,3584]{1,0:T(8,128)(2,1)S(1)} %get-tuple-element.35), channel_id=1, source_target_pairs={{0,2},{1,3},{2,0},{3,1},{4,6},{5,7},{6,4},{7,5},{8,10},{9,11},{10,... | collective-permute-start | bytes 516104 | tf_op jit(solution)/shard_map/ppermute | solution.py:51
  11.3 12.0 %collective-permute-start.7 = (bf16[24,3584]{1,0:T(8,128)(2,1)S(1)}, bf16[24,3584]{1,0:T(8,128)(2,1)S(1)}, u32[]{:S(2)}, u32[]{:S(2)}) collective-permute-start(bf16[24,3584]{1,0:T(8,128)(2,1)S(1)} %get-tuple-element.17), channel_id=1, source_target_pairs={{0,8},{4,12},{8,0},{12,4},{1,9},{5,13},{9,1},{13,5},{2,10},{6,14},... | collective-permute-start | bytes 516104 | tf_op jit(solution)/shard_map/ppermute | solution.py:48
  14.0 15.9 %collective-permute-start.1 = (bf16[48,3584]{1,0:T(8,128)(2,1)S(1)}, bf16[48,3584]{1,0:T(8,128)(2,1)S(1)}, u32[]{:S(2)}, u32[]{:S(2)}) collective-permute-start(bf16[48,3584]{1,0:T(8,128)(2,1)S(1)} %pad_maximum_fusion.4), channel_id=1, source_target_pairs={{0,1},{1,0},{2,3},{3,2},{4,5},{5,4},{6,7},{7,6},{8,9},{9,8},{10,11... | collective-permute-start | bytes 1032200 | tf_op jit(solution)/shard_map/ppermute | solution.py:51
  14.1 6.8 %collective-permute-start.3 = (bf16[24,3584]{1,0:T(8,128)(2,1)S(1)}, bf16[24,3584]{1,0:T(8,128)(2,1)S(1)}, u32[]{:S(2)}, u32[]{:S(2)}) collective-permute-start(bf16[24,3584]{1,0:T(8,128)(2,1)S(1)} %collective-permute-done), channel_id=1, source_target_pairs={{0,2},{1,3},{2,0},{3,1},{4,6},{5,7},{6,4},{7,5},{8,10},{9,11},{10,... | collective-permute-start | bytes 516104 | tf_op jit(solution)/shard_map/ppermute | solution.py:51
  20.9 5.9 %collective-permute-start.9 = (bf16[24,3584]{1,0:T(8,128)(2,1)S(1)}, bf16[24,3584]{1,0:T(8,128)(2,1)S(1)}, u32[]{:S(2)}, u32[]{:S(2)}) collective-permute-start(bf16[24,3584]{1,0:T(8,128)(2,1)S(1)} %collective-permute-done.8), channel_id=1, source_target_pairs={{0,2},{1,3},{2,0},{3,1},{4,6},{5,7},{6,4},{7,5},{8,10},{9,11},{10,... | collective-permute-start | bytes 516104 | tf_op jit(solution)/shard_map/ppermute | solution.py:51
  22.4 6.0 %collective-permute-start.12 = (bf16[24,3584]{1,0:T(8,128)(2,1)S(1)}, bf16[24,3584]{1,0:T(8,128)(2,1)S(1)}, u32[]{:S(2)}, u32[]{:S(2)}) collective-permute-start(bf16[24,3584]{1,0:T(8,128)(2,1)S(1)} %collective-permute-done.8), channel_id=1, source_target_pairs={{0,1},{1,0},{2,3},{3,2},{4,5},{5,4},{6,7},{7,6},{8,9},{9,8},{10,11... | collective-permute-start | bytes 516104 | tf_op jit(solution)/shard_map/ppermute | solution.py:51
  22.5 7.0 %copy-start.1 = (bf16[1,3584,256]{2,1,0:T(8,128)(2,1)S(1)}, bf16[1,3584,256]{2,1,0:T(8,128)(2,1)}, u32[]{:S(2)}) copy-start(bf16[1,3584,256]{2,1,0:T(8,128)(2,1)} %param.10) | copy-start | bytes 5505028
  22.5 10.7 %collective-permute-start.4 = (bf16[48,3584]{1,0:T(8,128)(2,1)S(1)}, bf16[48,3584]{1,0:T(8,128)(2,1)S(1)}, u32[]{:S(2)}, u32[]{:S(2)}) collective-permute-start(bf16[48,3584]{1,0:T(8,128)(2,1)S(1)} %pad_maximum_fusion.5), channel_id=1, source_target_pairs={{0,1},{1,0},{2,3},{3,2},{4,5},{5,4},{6,7},{7,6},{8,9},{9,8},{10,11... | collective-permute-start | bytes 1032200 | tf_op jit(solution)/shard_map/ppermute | solution.py:51
  26.8 12.1 %collective-permute-start.11 = (bf16[24,3584]{1,0:T(8,128)(2,1)S(1)}, bf16[24,3584]{1,0:T(8,128)(2,1)S(1)}, u32[]{:S(2)}, u32[]{:S(2)}) collective-permute-start(bf16[24,3584]{1,0:T(8,128)(2,1)S(1)} %collective-permute-done.7), channel_id=1, source_target_pairs={{0,2},{1,3},{2,0},{3,1},{4,6},{5,7},{6,4},{7,5},{8,10},{9,11},{10,... | collective-permute-start | bytes 516104 | tf_op jit(solution)/shard_map/ppermute | solution.py:51
  28.3 4.0 %collective-permute-start.10 = (bf16[24,3584]{1,0:T(8,128)(2,1)S(1)}, bf16[24,3584]{1,0:T(8,128)(2,1)S(1)}, u32[]{:S(2)}, u32[]{:S(2)}) collective-permute-start(bf16[24,3584]{1,0:T(8,128)(2,1)S(1)} %collective-permute-done.7), channel_id=1, source_target_pairs={{0,1},{1,0},{2,3},{3,2},{4,5},{5,4},{6,7},{7,6},{8,9},{9,8},{10,11... | collective-permute-start | bytes 516104 | tf_op jit(solution)/shard_map/ppermute | solution.py:51
  28.9 1.9 %collective-permute-start.13 = (bf16[24,3584]{1,0:T(8,128)(2,1)S(1)}, bf16[24,3584]{1,0:T(8,128)(2,1)S(1)}, u32[]{:S(2)}, u32[]{:S(2)}) collective-permute-start(bf16[24,3584]{1,0:T(8,128)(2,1)S(1)} %collective-permute-done.9), channel_id=1, source_target_pairs={{0,1},{1,0},{2,3},{3,2},{4,5},{5,4},{6,7},{7,6},{8,9},{9,8},{10,11... | collective-permute-start | bytes 516104 | tf_op jit(solution)/shard_map/ppermute | solution.py:51
  31.7 4.2 %collective-permute-start.14 = (bf16[96,256]{1,0:T(8,128)(2,1)S(1)}, bf16[96,256]{1,0:T(8,128)(2,1)S(1)}, u32[]{:S(2)}, u32[]{:S(2)}) collective-permute-start(bf16[96,256]{1,0:T(8,128)(2,1)S(1)} %pad_maximum_fusion.23), channel_id=1, source_target_pairs={{0,2},{1,3},{2,0},{3,1},{4,6},{5,7},{6,4},{7,5},{8,10},{9,11},{10,... | collective-permute-start | bytes 147464 | tf_op jit(solution)/shard_map/ppermute | solution.py:51
  34.1 4.7 %collective-permute-start.5 = (bf16[192,256]{1,0:T(8,128)(2,1)S(1)}, bf16[192,256]{1,0:T(8,128)(2,1)S(1)}, u32[]{:S(2)}, u32[]{:S(2)}) collective-permute-start(bf16[192,256]{1,0:T(8,128)(2,1)S(1)} %pad_maximum_fusion.21), channel_id=1, source_target_pairs={{0,2},{1,3},{2,0},{3,1},{4,6},{5,7},{6,4},{7,5},{8,10},{9,11},{10,... | collective-permute-start | bytes 294920 | tf_op jit(solution)/shard_map/ppermute | solution.py:51
  35.9 3.1 %collective-permute-start.15 = (bf16[96,512]{1,0:T(8,128)(2,1)S(1)}, bf16[96,512]{1,0:T(8,128)(2,1)S(1)}, u32[]{:S(2)}, u32[]{:S(2)}) collective-permute-start(bf16[96,512]{1,0:T(8,128)(2,1)S(1)} %bitcast.197), channel_id=1, source_target_pairs={{0,1},{1,0},{2,3},{3,2},{4,5},{5,4},{6,7},{7,6},{8,9},{9,8},{10,11... | collective-permute-start | bytes 294920 | tf_op jit(solution)/shard_map/ppermute | solution.py:51
  38.8 6.2 %collective-permute-start.6 = (bf16[192,512]{1,0:T(8,128)(2,1)S(1)}, bf16[192,512]{1,0:T(8,128)(2,1)S(1)}, u32[]{:S(2)}, u32[]{:S(2)}) collective-permute-start(bf16[192,512]{1,0:T(8,128)(2,1)S(1)} %bitcast.193), channel_id=1, source_target_pairs={{0,1},{1,0},{2,3},{3,2},{4,5},{5,4},{6,7},{7,6},{8,9},{9,8},{10,11... | collective-permute-start | bytes 589832 | tf_op jit(solution)/shard_map/ppermute | solution.py:51
  38.9 7.0 %collective-permute-start.16 = (bf16[24,3584]{1,0:T(8,128)(2,1)S(1)}, bf16[24,3584]{1,0:T(8,128)(2,1)S(1)}, u32[]{:S(2)}, u32[]{:S(2)}) collective-permute-start(bf16[24,3584]{1,0:T(8,128)(2,1)S(1)} %collective-permute-done.11), channel_id=1, source_target_pairs={{0,1},{1,0},{2,3},{3,2},{4,5},{5,4},{6,7},{7,6},{8,9},{9,8},{10,11... | collective-permute-start | bytes 516104 | tf_op jit(solution)/shard_map/ppermute | solution.py:51
  40.2 16.8 %collective-permute-start.23 = (bf16[2,24,896]{2,1,0:T(8,128)(2,1)S(1)}, bf16[2,24,896]{2,1,0:T(8,128)(2,1)S(1)}, u32[]{:S(2)}, u32[]{:S(2)}) collective-permute-start(bf16[2,24,896]{2,1,0:T(8,128)(2,1)S(1)} %bitcast.202), channel_id=1, source_target_pairs={{0,14},{1,15},{2,12},{3,13},{4,10},{5,11},{6,8},{7,9},{8,6},{9,7},... | collective-permute-start | bytes 258056 | tf_op jit(solution)/shard_map/ppermute | solution.py:57
  43.7 13.3 %collective-permute-start.22 = (bf16[2,24,896]{2,1,0:T(8,128)(2,1)S(1)}, bf16[2,24,896]{2,1,0:T(8,128)(2,1)S(1)}, u32[]{:S(2)}, u32[]{:S(2)}) collective-permute-start(bf16[2,24,896]{2,1,0:T(8,128)(2,1)S(1)} %bitcast.201), channel_id=1, source_target_pairs={{0,12},{1,13},{2,14},{3,15},{4,8},{5,9},{6,10},{7,11},{8,4},{9,5},... | collective-permute-start | bytes 258056 | tf_op jit(solution)/shard_map/ppermute | solution.py:57
  46.8 4.7 %collective-permute-start.17 = (bf16[96,256]{1,0:T(8,128)(2,1)S(1)}, bf16[96,256]{1,0:T(8,128)(2,1)S(1)}, u32[]{:S(2)}, u32[]{:S(2)}) collective-permute-start(bf16[96,256]{1,0:T(8,128)(2,1)S(1)} %pad_maximum_fusion.24), channel_id=1, source_target_pairs={{0,2},{1,3},{2,0},{3,1},{4,6},{5,7},{6,4},{7,5},{8,10},{9,11},{10,... | collective-permute-start | bytes 147464 | tf_op jit(solution)/shard_map/ppermute | solution.py:51
  47.5 6.2 %collective-permute-start.19 = (bf16[2,2,24,896]{3,2,1,0:T(8,128)(2,1)S(1)}, bf16[2,2,24,896]{3,2,1,0:T(8,128)(2,1)S(1)}, u32[]{:S(2)}, u32[]{:S(2)}) collective-permute-start(bf16[2,2,24,896]{3,2,1,0:T(8,128)(2,1)S(1)} %bitcast.196), channel_id=1, source_target_pairs={{0,2},{1,3},{2,0},{3,1},{4,6},{5,7},{6,4},{7,5},{8,10},{9,11},{10,... | collective-permute-start | bytes 516104 | tf_op jit(solution)/shard_map/ppermute | solution.py:51
  51.6 4.6 %collective-permute-start.18 = (bf16[96,512]{1,0:T(8,128)(2,1)S(1)}, bf16[96,512]{1,0:T(8,128)(2,1)S(1)}, u32[]{:S(2)}, u32[]{:S(2)}) collective-permute-start(bf16[96,512]{1,0:T(8,128)(2,1)S(1)} %bitcast.199), channel_id=1, source_target_pairs={{0,1},{1,0},{2,3},{3,2},{4,5},{5,4},{6,7},{7,6},{8,9},{9,8},{10,11... | collective-permute-start | bytes 294920 | tf_op jit(solution)/shard_map/ppermute | solution.py:51
  53.8 6.7 %collective-permute-start.20 = (bf16[2,2,24,896]{3,2,1,0:T(8,128)(2,1)S(1)}, bf16[2,2,24,896]{3,2,1,0:T(8,128)(2,1)S(1)}, u32[]{:S(2)}, u32[]{:S(2)}) collective-permute-start(bf16[2,2,24,896]{3,2,1,0:T(8,128)(2,1)S(1)} %pad_maximum_fusion.16), channel_id=1, source_target_pairs={{0,4},{4,0},{8,12},{12,8},{1,5},{5,1},{9,13},{13,9},{2,6},{6,2},{1... | collective-permute-start | bytes 516104 | tf_op jit(solution)/shard_map/ppermute | solution.py:48
  56.6 7.6 %copy-start.3 = (s32[64,8]{0,1:T(8,128)S(1)}, s32[64,8]{0,1:T(8,128)}, u32[]{:S(2)}) copy-start(s32[64,8]{0,1:T(8,128)} %param.7) | copy-start | bytes 6148
  56.6 7.5 %copy-start.4 = (s32[64,8]{0,1:T(8,128)S(1)}, s32[64,8]{0,1:T(8,128)}, u32[]{:S(2)}) copy-start(s32[64,8]{0,1:T(8,128)} %param.8) | copy-start | bytes 6148
  60.5 10.1 %collective-permute-start.24 = (bf16[6,24,896]{2,1,0:T(8,128)(2,1)S(1)}, bf16[6,24,896]{2,1,0:T(8,128)(2,1)S(1)}, u32[]{:S(2)}, u32[]{:S(2)}) collective-permute-start(bf16[6,24,896]{2,1,0:T(8,128)(2,1)S(1)} %get-tuple-element.68), channel_id=1, source_target_pairs={{0,1},{1,0},{2,3},{3,2},{4,5},{5,4},{6,7},{7,6},{8,9},{9,8},{10,11... | collective-permute-start | bytes 774152 | tf_op jit(solution)/shard_map/ppermute | solution.py:51
  60.6 10.0 %collective-permute-start.21 = (bf16[2,24,896]{2,1,0:T(8,128)(2,1)S(1)}, bf16[2,24,896]{2,1,0:T(8,128)(2,1)S(1)}, u32[]{:S(2)}, u32[]{:S(2)}) collective-permute-start(bf16[2,24,896]{2,1,0:T(8,128)(2,1)S(1)} %bitcast.204), channel_id=1, source_target_pairs={{0,8},{1,9},{2,10},{3,11},{4,12},{5,13},{6,14},{7,15},{8,0},{9,1},... | collective-permute-start | bytes 258056 | tf_op jit(solution)/shard_map/ppermute | solution.py:57
  61.6 11.0 %collective-permute-start.25 = (bf16[2,24,896]{2,1,0:T(8,128)(2,1)S(1)}, bf16[2,24,896]{2,1,0:T(8,128)(2,1)S(1)}, u32[]{:S(2)}, u32[]{:S(2)}) collective-permute-start(bf16[2,24,896]{2,1,0:T(8,128)(2,1)S(1)} %bitcast.203), channel_id=1, source_target_pairs={{0,10},{1,11},{2,8},{3,9},{4,14},{5,15},{6,12},{7,13},{8,2},{9,3},... | collective-permute-start | bytes 258056 | tf_op jit(solution)/shard_map/ppermute | solution.py:57
  72.7 1.3 %collective-permute-start.26 = (bf16[2,24,896]{2,1,0:T(8,128)(2,1)S(1)}, bf16[2,24,896]{2,1,0:T(8,128)(2,1)S(1)}, u32[]{:S(2)}, u32[]{:S(2)}) collective-permute-start(bf16[2,24,896]{2,1,0:T(8,128)(2,1)S(1)} %pad_maximum_fusion.22), channel_id=1, source_target_pairs={{0,1},{1,0},{2,3},{3,2},{4,5},{5,4},{6,7},{7,6},{8,9},{9,8},{10,11... | collective-permute-start | bytes 258056 | tf_op jit(solution)/shard_map/ppermute | solution.py:51
  74.7 0.9 %copy-start.2 = (f32[64,3584]{1,0:T(8,128)}, f32[64,3584]{1,0:T(8,128)S(1)}, u32[]{:S(2)}) copy-start(f32[64,3584]{1,0:T(8,128)S(1)} %fusion.30) | copy-start | bytes 2752516

commit v4 on v3

--- a/solution.py
+++ b/solution.py
@@ -68,6 +68,9 @@
 
     mine = {0: panels[0]}
     chip_of = {}
+    hidden_of = {}
+    landed = {}
+    pieces = {}
 
     def to_chips(steps):
         for s in steps:
@@ -75,30 +78,13 @@
             for x in range(1, n_chip):
                 chip_of[s, x] = local_xor(mine[s], 2 * x)
 
-    for s in near[1:] + far:
-        mine[s] = outer_xor(panels[s], s)
-    to_chips(near)
-    for s in mid:
-        mine[s] = outer_xor(after(panels[s], mine[near[-1]]), s)
-    for s in far:
-        mine[s] = after(mine[s], chip_of[near[-1], n_chip - 1])
-    to_chips(far)
-    for s in mid:
-        mine[s] = after(mine[s], chip_of[far[-1], n_chip - 1])
-    to_chips(mid)
+    def make_hidden(steps):
+        same = jnp.concatenate([chip_of[s, x] for x in range(n_chip) for s in steps], axis=0)
+        other = local_xor(same, 1)
+        halves = [first_half(rows).reshape(n_chip, -1, part_hid) for rows in (same, other)]
+        return jnp.stack(halves, axis=1).reshape(-1, part_hid)
 
-    pieces = {}
-    landed = {}
-    for steps in (near, far, mid):
-        count = len(steps)
-        pairs = []
-        for x in range(n_chip):
-            if steps is mid and x > 0:
-                for s in steps:
-                    chip_of[s, x] = after(chip_of[s, x], hidden_other)
-            same = jnp.concatenate([chip_of[s, x] for s in steps], axis=0)
-            pairs.append(first_half(jnp.concatenate([same, local_xor(same, 1)], axis=0)))
-        hidden = jnp.concatenate(pairs, axis=0)
+    def make_out(hidden, count):
         sides = []
         for x in range(n_chip):
             side = hidden if x == 0 else local_xor(hidden, 2 * x)
@@ -111,30 +97,44 @@
         out_other = out_other.reshape(n_chip, 2, -1, part_out)
         out_other = jnp.concatenate([out_other[:, 1:], out_other[:, :1]], axis=1).reshape(out_same.shape)
         expert_out = (out_same + out_other).astype(jnp.bfloat16)
-        expert_out = expert_out.reshape(n_chip, 2, count, capacity, part_out)
-        if steps is near:
-            for x in range(n_chip):
-                block = expert_out[x] if x == 0 else local_xor(expert_out[x], 2 * x)
-                for at, s in enumerate(steps):
-                    landed[s, x] = block[:, at]
-            for s in steps[1:]:
-                moved = outer_xor(jnp.stack([landed[s, x] for x in range(n_chip)]), s)
-                for x in range(n_chip):
-                    landed[s, x] = moved[x]
-        else:
-            for at, s in enumerate(steps):
-                for x in range(n_chip):
-                    landed[s, x] = both_xor(expert_out[x, :, at], s, 2 * x)
+        return expert_out.reshape(n_chip, 2, count, capacity, part_out), hidden_other
 
-    for steps in (far + near, mid):
-        for s in steps:
-            for x in range(n_chip):
-                landed[s, x] = after(landed[s, x], swapped if steps is mid else expert_out)
-        swapped = local_xor(jnp.stack([landed[s, x][1] for s in steps for x in range(n_chip)]), 1)
-        for at, s in enumerate(steps):
-            for x in range(n_chip):
-                pieces[s, 2 * x] = landed[s, x][0]
-                pieces[s, 2 * x + 1] = swapped[at * n_chip + x]
+    for s in far + near[1:] + mid:
+        mine[s] = outer_xor(panels[s], s)
+    chip_of[0, 0] = after(mine[0], mine[far[-1]])
+    for x in range(1, n_chip):
+        chip_of[0, x] = after(local_xor(mine[0], 2 * x), mine[far[-1]])
+    for s in near[1:]:
+        mine[s] = after(mine[s], mine[far[-1]])
+    to_chips(near[1:])
+    to_chips(far)
+    for s in mid:
+        mine[s] = after(mine[s], chip_of[near[-1], n_chip - 1])
+    to_chips(mid)
+    hidden_near = make_hidden(near)
+    out_near, seen = make_out(hidden_near, len(near))
+    for x in range(1, n_chip):
+        for s in mid:
+            chip_of[s, x] = after(chip_of[s, x], seen)
+    hidden_far = make_hidden(far + mid)
+    out_far, seen = make_out(hidden_far, len(far + mid))
+    for at, s in enumerate(far + mid):
+        for x in range(n_chip):
+            landed[s, x] = both_xor(out_far[x, :, at], s, 2 * x)
+    for x in range(n_chip):
+        block = out_near[x] if x == 0 else local_xor(after(out_near[x], hidden_far), 2 * x)
+        for at, s in enumerate(near):
+            landed[s, x] = block[:, at]
+    for s in near[1:]:
+        sent = jnp.stack([landed[s, x] for x in range(n_chip)])
+        moved = outer_xor(after(sent, out_far), s)
+        for x in range(n_chip):
+            landed[s, x] = moved[x]
+    swapped = local_xor(jnp.stack([landed[s, x][1] for s in range(n_out) for x in range(n_chip)]), 1)
+    for s in range(n_out):
+        for x in range(n_chip):
+            pieces[s, 2 * x] = landed[s, x][0]
+            pieces[s, 2 * x + 1] = swapped[s * n_chip + x]
 
     spread = jnp.where(placing, fixed[:, :, None], 0).reshape(tok_rows, -1)
     high = (spread >> 8).astype(jnp.bfloat16)

time: 76.7 us -> 70 us (0.913)
  starting transfers between devices: 31.6 us -> 23.1 us
  waiting for transfers between devices: 28.7 us -> 33 us
  matrix products: 10.9 us -> 8.73 us
    ppermute x19 -> x12, waiting for transfers between devices: 15.3 us -> 19.8 us  [local_xor(): return lax.ppermute(v, 'local', [(i, i ^ m) for i in range(n_loc)])]
    ppermute x4, starting transfers between devices: 10.7 us -> 6.56 us  [outer_xor(): return lax.ppermute(v, 'outer', [(i, i ^ s) for i in range(n_out)])]
    ppermute x19 -> x12, starting transfers between devices: 12.6 us -> 8.84 us  [local_xor(): return lax.ppermute(v, 'local', [(i, i ^ m) for i in range(n_loc)])]
    dot_general x6 -> x4, matrix products: 2.57 us -> 1.71 us  [first_half(): gate_proj = jnp.dot(rows, gate_local, preferred_element_type=jnp.float32)]
    dot_general x6 -> x4, matrix products: 2.59 us -> 1.73 us  [first_half(): up_proj = jnp.dot(rows, up_local, preferred_element_type=jnp.float32)]
    dot_general x6 -> x4, matrix products: 1.98 us -> 1.53 us  [the longest x2 0.78 us: make_out(): jnp.dot(hidden_same, down_same, preferred_element_type=jnp.float32)]
  transfers between devices with their start and end apart: 27 -> 20, of which waited for: 12 -> 11; matrix products, arithmetic and copies ran while one was open for 14% -> 9% of each run, Pallas kernels for 0% -> 0%
where the time goes in v4:
time: 70 us; the launch traced here: 69.8 us
  waiting for transfers between devices  33 us (47%)
  starting transfers between devices  23.1 us (33%)
  matrix products  8.73 us (12%)
  local copies, waits for them, and re-layouts  3.11 us (4%)
  other arithmetic  1.38 us (2%)
    ppermute x12, waiting for transfers between devices, local_xor(): return lax.ppermute(v, 'local', [(i, i ^ m) for i in range(n_loc)])  19.8 us
    ppermute x12, starting transfers between devices, local_xor(): return lax.ppermute(v, 'local', [(i, i ^ m) for i in range(n_loc)])  8.84 us
    ppermute x4, waiting for transfers between devices, both_xor(): return lax.ppermute(v, ('outer', 'local'), pairs)  8.27 us
    ppermute x4, starting transfers between devices, both_xor(): return lax.ppermute(v, ('outer', 'local'), pairs)  7.71 us
    ppermute x4, starting transfers between devices, outer_xor(): return lax.ppermute(v, 'outer', [(i, i ^ s) for i in range(n_out)])  6.56 us
    ppermute x4, waiting for transfers between devices, outer_xor(): return lax.ppermute(v, 'outer', [(i, i ^ s) for i in range(n_out)])  4.98 us
    dot_general x4, matrix products, first_half(): up_proj = jnp.dot(rows, up_local, preferred_element_type=jnp.float32)  1.73 us
    dot_general x4, matrix products, first_half(): gate_proj = jnp.dot(rows, gate_local, preferred_element_type=jnp.float32)  1.71 us
  transfers between devices with their start and end apart: 20, of which 11 were waited for; matrix products, arithmetic and copies ran while one was open for 9% of the time, Pallas kernels for 0%

profile of v4, /device:TPU:0, one launch (start us, length us, event | category | flops | bytes accessed | tf_op | source)
XLA Modules:
  0.0 69.8 jit_solution(3929026210727576026)
XLA Ops:
  0.0 0.9 %compare_reduce_fusion = pred[64,4]{0,1:T(4,128)(4,1)S(1)} fusion(s32[64,8]{0,1:T(8,128)} %param.7, s32[4]{0:T(128)S(1)} %xor_multiply_fusion), kind=kLoop, calls=%fused_computation.132 | loop fusion | flops 3840 | bytes 2320 | tf_op jit(solution)/shard_map/reduce_or | solution.py:40
  1.2 1.3 %convolution_convert_fusion = bf16[4,24,3584]{2,1,0:T(8,128)(2,1)S(1)} fusion(bf16[64,3584]{1,0:T(8,128)(2,1)} %param.6, s32[64,4]{0,1:T(4,128)S(1)} %add_select_fusion), kind=kOutput, calls=%fused_computation | convolution fusion | flops 44390400 | bytes 1147904 | tf_op jit(solution)/shard_map/tqc,td->qcd/dot_general | solution.py:43
  2.6 5.1 %collective-permute-start = (bf16[24,3584]{1,0:T(8,128)(2,1)S(1)}, bf16[24,3584]{1,0:T(8,128)(2,1)S(1)}, u32[]{:S(2)}, u32[]{:S(2)}) collective-permute-start(bf16[24,3584]{1,0:T(8,128)(2,1)S(1)} %get-tuple-element.30), channel_id=1, source_target_pairs={{0,12},{4,8},{8,4},{12,0},{1,13},{5,9},{9,5},{13,1},{2,14},{6,10},... | collective-permute-start | bytes 516104 | tf_op jit(solution)/shard_map/ppermute | solution.py:48
  7.7 1.5 %collective-permute-start.2 = (bf16[24,3584]{1,0:T(8,128)(2,1)S(1)}, bf16[24,3584]{1,0:T(8,128)(2,1)S(1)}, u32[]{:S(2)}, u32[]{:S(2)}) collective-permute-start(bf16[24,3584]{1,0:T(8,128)(2,1)S(1)} %get-tuple-element.12), channel_id=1, source_target_pairs={{0,2},{1,3},{2,0},{3,1},{4,6},{5,7},{6,4},{7,5},{8,10},{9,11},{10,... | collective-permute-start | bytes 516104 | tf_op jit(solution)/shard_map/ppermute | solution.py:51
  9.2 0.8 %collective-permute-start.7 = (bf16[24,3584]{1,0:T(8,128)(2,1)S(1)}, bf16[24,3584]{1,0:T(8,128)(2,1)S(1)}, u32[]{:S(2)}, u32[]{:S(2)}) collective-permute-start(bf16[24,3584]{1,0:T(8,128)(2,1)S(1)} %get-tuple-element.28), channel_id=1, source_target_pairs={{0,8},{4,12},{8,0},{12,4},{1,9},{5,13},{9,1},{13,5},{2,10},{6,14},... | collective-permute-start | bytes 516104 | tf_op jit(solution)/shard_map/ppermute | solution.py:48
  10.3 1.6 %dynamic-slice_bitcast_fusion.3 = (bf16[256,896]{1,0:T(8,128)(2,1)S(1)}, bf16[256,896]{1,0:T(8,128)(2,1)S(1)}, bf16[256,896]{1,0:T(8,128)(2,1)S(1)}, bf16[256,896]{1,0:T(8,128)(2,1)S(1)}) fusion(bf16[1,1024,896]{2,1,0:T(8,128)(2,1)} %param.11, s32[]{:T(128)S(6)} %select_n.44, s32[]{:T(128)S(6)} %select_n.45, s32[]{:T(128)S(6)} %select_n.47, s32[]{:T(128)S(6)} %select_n.46), kind=kLoop, calls=%fused_computation.47 | loop fusion | bytes 3670032 | tf_op jit(solution)/shard_map/dynamic_slice | solution.py:29
  11.9 1.1 %collective-permute-done = bf16[24,3584]{1,0:T(8,128)(2,1)S(1)} collective-permute-done((bf16[24,3584]{1,0:T(8,128)(2,1)S(1)}, bf16[24,3584]{1,0:T(8,128)(2,1)S(1)}, u32[]{:S(2)}, u32[]{:S(2)}) %collective-permute-start) | collective-permute-done | bytes 172064 | tf_op jit(solution)/shard_map/ppermute | solution.py:48
  13.0 3.9 %collective-permute-done.1 = bf16[24,3584]{1,0:T(8,128)(2,1)S(1)} collective-permute-done((bf16[24,3584]{1,0:T(8,128)(2,1)S(1)}, bf16[24,3584]{1,0:T(8,128)(2,1)S(1)}, u32[]{:S(2)}, u32[]{:S(2)}) %collective-permute-start.1) | collective-permute-done | bytes 172064 | tf_op jit(solution)/shard_map/ppermute | solution.py:48
  16.9 1.4 %collective-permute-start.3 = (bf16[24,3584]{1,0:T(8,128)(2,1)S(1)}, bf16[24,3584]{1,0:T(8,128)(2,1)S(1)}, u32[]{:S(2)}, u32[]{:S(2)}) collective-permute-start(bf16[24,3584]{1,0:T(8,128)(2,1)S(1)} %collective-permute-done.1), channel_id=1, source_target_pairs={{0,2},{1,3},{2,0},{3,1},{4,6},{5,7},{6,4},{7,5},{8,10},{9,11},{10,... | collective-permute-start | bytes 516104 | tf_op jit(solution)/shard_map/ppermute | solution.py:51
  18.4 0.7 collective-permute-start.8
  19.1 5.1 %collective-permute-done.3 = bf16[24,3584]{1,0:T(8,128)(2,1)S(1)} collective-permute-done((bf16[24,3584]{1,0:T(8,128)(2,1)S(1)}, bf16[24,3584]{1,0:T(8,128)(2,1)S(1)}, u32[]{:S(2)}, u32[]{:S(2)}) %collective-permute-start.3) | collective-permute-done | bytes 172064 | tf_op jit(solution)/shard_map/ppermute | solution.py:51
  24.7 1.5 %collective-permute-start.9 = (bf16[24,3584]{1,0:T(8,128)(2,1)S(1)}, bf16[24,3584]{1,0:T(8,128)(2,1)S(1)}, u32[]{:S(2)}, u32[]{:S(2)}) collective-permute-start(bf16[24,3584]{1,0:T(8,128)(2,1)S(1)} %collective-permute-done.7), channel_id=1, source_target_pairs={{0,2},{1,3},{2,0},{3,1},{4,6},{5,7},{6,4},{7,5},{8,10},{9,11},{10,... | collective-permute-start | bytes 516104 | tf_op jit(solution)/shard_map/ppermute | solution.py:51
  27.0 0.4 multiply_convert_fusion.2
  27.5 1.2 %collective-permute-start.5 = (bf16[192,256]{1,0:T(8,128)(2,1)S(1)}, bf16[192,256]{1,0:T(8,128)(2,1)S(1)}, u32[]{:S(2)}, u32[]{:S(2)}) collective-permute-start(bf16[192,256]{1,0:T(8,128)(2,1)S(1)} %bitcast.214), channel_id=1, source_target_pairs={{0,2},{1,3},{2,0},{3,1},{4,6},{5,7},{6,4},{7,5},{8,10},{9,11},{10,... | collective-permute-start | bytes 294920 | tf_op jit(solution)/shard_map/ppermute | solution.py:51
  28.7 4.9 %collective-permute-done.5 = bf16[192,256]{1,0:T(8,128)(2,1)S(1)} collective-permute-done((bf16[192,256]{1,0:T(8,128)(2,1)S(1)}, bf16[192,256]{1,0:T(8,128)(2,1)S(1)}, u32[]{:S(2)}, u32[]{:S(2)}) %collective-permute-start.5) | collective-permute-done | bytes 98336 | tf_op jit(solution)/shard_map/ppermute | solution.py:51
  33.8 1.4 %collective-permute-done.6 = bf16[192,512]{1,0:T(8,128)(2,1)S(1)} collective-permute-done((bf16[192,512]{1,0:T(8,128)(2,1)S(1)}, bf16[192,512]{1,0:T(8,128)(2,1)S(1)}, u32[]{:S(2)}, u32[]{:S(2)}) %collective-permute-start.6) | collective-permute-done | bytes 196640 | tf_op jit(solution)/shard_map/ppermute | solution.py:51
  36.8 0.4 multiply_convert_fusion.1
  37.2 1.1 %collective-permute-done.10 = bf16[96,3584]{1,0:T(8,128)(2,1)S(1)} collective-permute-done((bf16[96,3584]{1,0:T(8,128)(2,1)S(1)}, bf16[96,3584]{1,0:T(8,128)(2,1)S(1)}, u32[]{:S(2)}, u32[]{:S(2)}) %collective-permute-start.10) | collective-permute-done | bytes 688160 | tf_op jit(solution)/shard_map/ppermute | solution.py:51
  39.3 1.5 %collective-permute-start.12 = (bf16[192,256]{1,0:T(8,128)(2,1)S(1)}, bf16[192,256]{1,0:T(8,128)(2,1)S(1)}, u32[]{:S(2)}, u32[]{:S(2)}) collective-permute-start(bf16[192,256]{1,0:T(8,128)(2,1)S(1)} %bitcast.213), channel_id=1, source_target_pairs={{0,2},{1,3},{2,0},{3,1},{4,6},{5,7},{6,4},{7,5},{8,10},{9,11},{10,... | collective-permute-start | bytes 294920 | tf_op jit(solution)/shard_map/ppermute | solution.py:51
  40.7 0.6 collective-permute-start.11
  41.4 3.6 %collective-permute-done.12 = bf16[192,256]{1,0:T(8,128)(2,1)S(1)} collective-permute-done((bf16[192,256]{1,0:T(8,128)(2,1)S(1)}, bf16[192,256]{1,0:T(8,128)(2,1)S(1)}, u32[]{:S(2)}, u32[]{:S(2)}) %collective-permute-start.12) | collective-permute-done | bytes 98336 | tf_op jit(solution)/shard_map/ppermute | solution.py:51
  45.1 2.8 %collective-permute-done.11 = bf16[2,2,24,896]{3,2,1,0:T(8,128)(2,1)S(1)} collective-permute-done((bf16[2,2,24,896]{3,2,1,0:T(8,128)(2,1)S(1)}, bf16[2,2,24,896]{3,2,1,0:T(8,128)(2,1)S(1)}, u32[]{:S(2)}, u32[]{:S(2)}) %collective-permute-start.11) | collective-permute-done | bytes 172064 | tf_op jit(solution)/shard_map/ppermute | solution.py:51
  48.8 0.6 collective-permute-start.14
  49.5 0.6 collective-permute-start.15
  50.1 3.3 %collective-permute-start.17 = (bf16[2,24,896]{2,1,0:T(8,128)(2,1)S(1)}, bf16[2,24,896]{2,1,0:T(8,128)(2,1)S(1)}, u32[]{:S(2)}, u32[]{:S(2)}) collective-permute-start(bf16[2,24,896]{2,1,0:T(8,128)(2,1)S(1)} %get-tuple-element.40), channel_id=1, source_target_pairs={{0,10},{1,11},{2,8},{3,9},{4,14},{5,15},{6,12},{7,13},{8,2},{9,3},... | collective-permute-start | bytes 258056 | tf_op jit(solution)/shard_map/ppermute | solution.py:57
  53.4 0.9 %collective-permute-start.16 = (bf16[2,24,896]{2,1,0:T(8,128)(2,1)S(1)}, bf16[2,24,896]{2,1,0:T(8,128)(2,1)S(1)}, u32[]{:S(2)}, u32[]{:S(2)}) collective-permute-start(bf16[2,24,896]{2,1,0:T(8,128)(2,1)S(1)} %get-tuple-element.41), channel_id=1, source_target_pairs={{0,12},{1,13},{2,14},{3,15},{4,8},{5,9},{6,10},{7,11},{8,4},{9,5},... | collective-permute-start | bytes 258056 | tf_op jit(solution)/shard_map/ppermute | solution.py:57
  54.3 2.9 %collective-permute-start.18 = (bf16[2,24,896]{2,1,0:T(8,128)(2,1)S(1)}, bf16[2,24,896]{2,1,0:T(8,128)(2,1)S(1)}, u32[]{:S(2)}, u32[]{:S(2)}) collective-permute-start(bf16[2,24,896]{2,1,0:T(8,128)(2,1)S(1)} %get-tuple-element.39), channel_id=1, source_target_pairs={{0,14},{1,15},{2,12},{3,13},{4,10},{5,11},{6,8},{7,9},{8,6},{9,7},... | collective-permute-start | bytes 258056 | tf_op jit(solution)/shard_map/ppermute | solution.py:57
  57.2 5.5 %collective-permute-done.15 = bf16[2,24,896]{2,1,0:T(8,128)(2,1)S(1)} collective-permute-done((bf16[2,24,896]{2,1,0:T(8,128)(2,1)S(1)}, bf16[2,24,896]{2,1,0:T(8,128)(2,1)S(1)}, u32[]{:S(2)}, u32[]{:S(2)}) %collective-permute-start.15) | collective-permute-done | bytes 86048 | tf_op jit(solution)/shard_map/ppermute | solution.py:57
  62.7 2.8 %collective-permute-done.17 = bf16[2,24,896]{2,1,0:T(8,128)(2,1)S(1)} collective-permute-done((bf16[2,24,896]{2,1,0:T(8,128)(2,1)S(1)}, bf16[2,24,896]{2,1,0:T(8,128)(2,1)S(1)}, u32[]{:S(2)}, u32[]{:S(2)}) %collective-permute-start.17) | collective-permute-done | bytes 86048 | tf_op jit(solution)/shard_map/ppermute | solution.py:57
  66.4 0.9 %collective-permute-done.19 = bf16[8,24,896]{2,1,0:T(8,128)(2,1)S(1)} collective-permute-done((bf16[8,24,896]{2,1,0:T(8,128)(2,1)S(1)}, bf16[8,24,896]{2,1,0:T(8,128)(2,1)S(1)}, u32[]{:S(2)}, u32[]{:S(2)}) %collective-permute-start.19) | collective-permute-done | bytes 344096 | tf_op jit(solution)/shard_map/ppermute | solution.py:51
  68.2 0.7 copy-done.2
  68.9 0.9 %fusion.19 = f32[64,3584]{1,0:T(8,128)} fusion(f32[64,3584]{1,0:T(8,128)} %copy-done.2, s32[]{:T(128)S(6)} %select_n.51, f32[64,896]{1,0:T(8,128)S(1)} %convolution_multiply_fusion.1, bf16[64,96]{0,1:T(8,128)(2,1)S(1)} %get-tuple-element.63, bf16[24,896]{1,0:T(8,128)(2,1)S(1)} %get-tuple-element.32, bf16[24,896]{1,0:T(8,128)(2,1)S(1)} %get-tuple-element.33, ...), kind=kOutput, calls=%fused_computation.23 | convolution fusion | flops 11812864 | bytes 643076 | tf_op jit(solution)/shard_map/dot_general | solution.py:146
  (90 shorter events, 7.4 us)
Async XLA Ops:
  0.0 24.2 %copy-start = (bf16[1,3584,256]{2,1,0:T(8,128)(2,1)S(1)}, bf16[1,3584,256]{2,1,0:T(8,128)(2,1)}, u32[]{:S(2)}) copy-start(bf16[1,3584,256]{2,1,0:T(8,128)(2,1)} %param.9) | copy-start | bytes 5505028
  0.0 10.0 %copy-start.3 = (s32[64,8]{0,1:T(8,128)S(1)}, s32[64,8]{0,1:T(8,128)}, u32[]{:S(2)}) copy-start(s32[64,8]{0,1:T(8,128)} %param.7) | copy-start | bytes 6148
  0.0 10.0 %copy-start.4 = (s32[64,8]{0,1:T(8,128)S(1)}, s32[64,8]{0,1:T(8,128)}, u32[]{:S(2)}) copy-start(s32[64,8]{0,1:T(8,128)} %param.8) | copy-start | bytes 6148
  2.6 10.4 %collective-permute-start = (bf16[24,3584]{1,0:T(8,128)(2,1)S(1)}, bf16[24,3584]{1,0:T(8,128)(2,1)S(1)}, u32[]{:S(2)}, u32[]{:S(2)}) collective-permute-start(bf16[24,3584]{1,0:T(8,128)(2,1)S(1)} %get-tuple-element.30), channel_id=1, source_target_pairs={{0,12},{4,8},{8,4},{12,0},{1,13},{5,9},{9,5},{13,1},{2,14},{6,10},... | collective-permute-start | bytes 516104 | tf_op jit(solution)/shard_map/ppermute | solution.py:48
  7.7 9.2 %collective-permute-start.1 = (bf16[24,3584]{1,0:T(8,128)(2,1)S(1)}, bf16[24,3584]{1,0:T(8,128)(2,1)S(1)}, u32[]{:S(2)}, u32[]{:S(2)}) collective-permute-start(bf16[24,3584]{1,0:T(8,128)(2,1)S(1)} %get-tuple-element.29), channel_id=1, source_target_pairs={{0,4},{4,0},{8,12},{12,8},{1,5},{5,1},{9,13},{13,9},{2,6},{6,2},{1... | collective-permute-start | bytes 516104 | tf_op jit(solution)/shard_map/ppermute | solution.py:48
  7.7 10.6 %collective-permute-start.2 = (bf16[24,3584]{1,0:T(8,128)(2,1)S(1)}, bf16[24,3584]{1,0:T(8,128)(2,1)S(1)}, u32[]{:S(2)}, u32[]{:S(2)}) collective-permute-start(bf16[24,3584]{1,0:T(8,128)(2,1)S(1)} %get-tuple-element.12), channel_id=1, source_target_pairs={{0,2},{1,3},{2,0},{3,1},{4,6},{5,7},{6,4},{7,5},{8,10},{9,11},{10,... | collective-permute-start | bytes 516104 | tf_op jit(solution)/shard_map/ppermute | solution.py:51
  9.2 15.5 %collective-permute-start.7 = (bf16[24,3584]{1,0:T(8,128)(2,1)S(1)}, bf16[24,3584]{1,0:T(8,128)(2,1)S(1)}, u32[]{:S(2)}, u32[]{:S(2)}) collective-permute-start(bf16[24,3584]{1,0:T(8,128)(2,1)S(1)} %get-tuple-element.28), channel_id=1, source_target_pairs={{0,8},{4,12},{8,0},{12,4},{1,9},{5,13},{9,1},{13,5},{2,10},{6,14},... | collective-permute-start | bytes 516104 | tf_op jit(solution)/shard_map/ppermute | solution.py:48
  16.9 7.2 %collective-permute-start.3 = (bf16[24,3584]{1,0:T(8,128)(2,1)S(1)}, bf16[24,3584]{1,0:T(8,128)(2,1)S(1)}, u32[]{:S(2)}, u32[]{:S(2)}) collective-permute-start(bf16[24,3584]{1,0:T(8,128)(2,1)S(1)} %collective-permute-done.1), channel_id=1, source_target_pairs={{0,2},{1,3},{2,0},{3,1},{4,6},{5,7},{6,4},{7,5},{8,10},{9,11},{10,... | collective-permute-start | bytes 516104 | tf_op jit(solution)/shard_map/ppermute | solution.py:51
  18.3 7.8 %copy-start.1 = (bf16[1,3584,256]{2,1,0:T(8,128)(2,1)S(1)}, bf16[1,3584,256]{2,1,0:T(8,128)(2,1)}, u32[]{:S(2)}) copy-start(bf16[1,3584,256]{2,1,0:T(8,128)(2,1)} %param.10) | copy-start | bytes 5505028
  18.4 15.4 %collective-permute-start.8 = (bf16[24,3584]{1,0:T(8,128)(2,1)S(1)}, bf16[24,3584]{1,0:T(8,128)(2,1)S(1)}, u32[]{:S(2)}, u32[]{:S(2)}) collective-permute-start(bf16[24,3584]{1,0:T(8,128)(2,1)S(1)} %collective-permute-done), channel_id=1, source_target_pairs={{0,2},{1,3},{2,0},{3,1},{4,6},{5,7},{6,4},{7,5},{8,10},{9,11},{10,... | collective-permute-start | bytes 516104 | tf_op jit(solution)/shard_map/ppermute | solution.py:51
  24.2 2.5 %collective-permute-start.4 = (bf16[96,3584]{1,0:T(8,128)(2,1)S(1)}, bf16[96,3584]{1,0:T(8,128)(2,1)S(1)}, u32[]{:S(2)}, u32[]{:S(2)}) collective-permute-start(bf16[96,3584]{1,0:T(8,128)(2,1)S(1)} %constant_dynamic-update-slice_fusion), channel_id=1, source_target_pairs={{0,1},{1,0},{2,3},{3,2},{4,5},{5,4},{6,7},{7,6},{8,9},{9,8},{10,11... | collective-permute-start | bytes 2064392 | tf_op jit(solution)/shard_map/ppermute | solution.py:51
  24.7 11.4 %collective-permute-start.9 = (bf16[24,3584]{1,0:T(8,128)(2,1)S(1)}, bf16[24,3584]{1,0:T(8,128)(2,1)S(1)}, u32[]{:S(2)}, u32[]{:S(2)}) collective-permute-start(bf16[24,3584]{1,0:T(8,128)(2,1)S(1)} %collective-permute-done.7), channel_id=1, source_target_pairs={{0,2},{1,3},{2,0},{3,1},{4,6},{5,7},{6,4},{7,5},{8,10},{9,11},{10,... | collective-permute-start | bytes 516104 | tf_op jit(solution)/shard_map/ppermute | solution.py:51
  27.5 6.1 %collective-permute-start.5 = (bf16[192,256]{1,0:T(8,128)(2,1)S(1)}, bf16[192,256]{1,0:T(8,128)(2,1)S(1)}, u32[]{:S(2)}, u32[]{:S(2)}) collective-permute-start(bf16[192,256]{1,0:T(8,128)(2,1)S(1)} %bitcast.214), channel_id=1, source_target_pairs={{0,2},{1,3},{2,0},{3,1},{4,6},{5,7},{6,4},{7,5},{8,10},{9,11},{10,... | collective-permute-start | bytes 294920 | tf_op jit(solution)/shard_map/ppermute | solution.py:51
  33.7 1.5 %collective-permute-start.6 = (bf16[192,512]{1,0:T(8,128)(2,1)S(1)}, bf16[192,512]{1,0:T(8,128)(2,1)S(1)}, u32[]{:S(2)}, u32[]{:S(2)}) collective-permute-start(bf16[192,512]{1,0:T(8,128)(2,1)S(1)} %bitcast.206), channel_id=1, source_target_pairs={{0,1},{1,0},{2,3},{3,2},{4,5},{5,4},{6,7},{7,6},{8,9},{9,8},{10,11... | collective-permute-start | bytes 589832 | tf_op jit(solution)/shard_map/ppermute | solution.py:51
  36.2 2.2 %collective-permute-start.10 = (bf16[96,3584]{1,0:T(8,128)(2,1)S(1)}, bf16[96,3584]{1,0:T(8,128)(2,1)S(1)}, u32[]{:S(2)}, u32[]{:S(2)}) collective-permute-start(bf16[96,3584]{1,0:T(8,128)(2,1)S(1)} %constant_dynamic-update-slice_fusion.4), channel_id=1, source_target_pairs={{0,1},{1,0},{2,3},{3,2},{4,5},{5,4},{6,7},{7,6},{8,9},{9,8},{10,11... | collective-permute-start | bytes 2064392 | tf_op jit(solution)/shard_map/ppermute | solution.py:51
  39.3 5.7 %collective-permute-start.12 = (bf16[192,256]{1,0:T(8,128)(2,1)S(1)}, bf16[192,256]{1,0:T(8,128)(2,1)S(1)}, u32[]{:S(2)}, u32[]{:S(2)}) collective-permute-start(bf16[192,256]{1,0:T(8,128)(2,1)S(1)} %bitcast.213), channel_id=1, source_target_pairs={{0,2},{1,3},{2,0},{3,1},{4,6},{5,7},{6,4},{7,5},{8,10},{9,11},{10,... | collective-permute-start | bytes 294920 | tf_op jit(solution)/shard_map/ppermute | solution.py:51
  40.7 7.1 %collective-permute-start.11 = (bf16[2,2,24,896]{3,2,1,0:T(8,128)(2,1)S(1)}, bf16[2,2,24,896]{3,2,1,0:T(8,128)(2,1)S(1)}, u32[]{:S(2)}, u32[]{:S(2)}) collective-permute-start(bf16[2,2,24,896]{3,2,1,0:T(8,128)(2,1)S(1)} %bitcast.212), channel_id=1, source_target_pairs={{0,2},{1,3},{2,0},{3,1},{4,6},{5,7},{6,4},{7,5},{8,10},{9,11},{10,... | collective-permute-start | bytes 516104 | tf_op jit(solution)/shard_map/ppermute | solution.py:51
  45.0 2.9 %collective-permute-start.13 = (bf16[192,512]{1,0:T(8,128)(2,1)S(1)}, bf16[192,512]{1,0:T(8,128)(2,1)S(1)}, u32[]{:S(2)}, u32[]{:S(2)}) collective-permute-start(bf16[192,512]{1,0:T(8,128)(2,1)S(1)} %bitcast.204), channel_id=1, source_target_pairs={{0,1},{1,0},{2,3},{3,2},{4,5},{5,4},{6,7},{7,6},{8,9},{9,8},{10,11... | collective-permute-start | bytes 589832 | tf_op jit(solution)/shard_map/ppermute | solution.py:51
  48.8 8.4 %collective-permute-start.14 = (bf16[2,2,24,896]{3,2,1,0:T(8,128)(2,1)S(1)}, bf16[2,2,24,896]{3,2,1,0:T(8,128)(2,1)S(1)}, u32[]{:S(2)}, u32[]{:S(2)}) collective-permute-start(bf16[2,2,24,896]{3,2,1,0:T(8,128)(2,1)S(1)} %pad_maximum_fusion.8), channel_id=1, source_target_pairs={{0,4},{4,0},{8,12},{12,8},{1,5},{5,1},{9,13},{13,9},{2,6},{6,2},{1... | collective-permute-start | bytes 516104 | tf_op jit(solution)/shard_map/ppermute | solution.py:48
  49.5 13.2 %collective-permute-start.15 = (bf16[2,24,896]{2,1,0:T(8,128)(2,1)S(1)}, bf16[2,24,896]{2,1,0:T(8,128)(2,1)S(1)}, u32[]{:S(2)}, u32[]{:S(2)}) collective-permute-start(bf16[2,24,896]{2,1,0:T(8,128)(2,1)S(1)} %get-tuple-element.42), channel_id=1, source_target_pairs={{0,8},{1,9},{2,10},{3,11},{4,12},{5,13},{6,14},{7,15},{8,0},{9,1},... | collective-permute-start | bytes 258056 | tf_op jit(solution)/shard_map/ppermute | solution.py:57
  50.1 15.4 %collective-permute-start.17 = (bf16[2,24,896]{2,1,0:T(8,128)(2,1)S(1)}, bf16[2,24,896]{2,1,0:T(8,128)(2,1)S(1)}, u32[]{:S(2)}, u32[]{:S(2)}) collective-permute-start(bf16[2,24,896]{2,1,0:T(8,128)(2,1)S(1)} %get-tuple-element.40), channel_id=1, source_target_pairs={{0,10},{1,11},{2,8},{3,9},{4,14},{5,15},{6,12},{7,13},{8,2},{9,3},... | collective-permute-start | bytes 258056 | tf_op jit(solution)/shard_map/ppermute | solution.py:57
  53.4 12.1 %collective-permute-start.16 = (bf16[2,24,896]{2,1,0:T(8,128)(2,1)S(1)}, bf16[2,24,896]{2,1,0:T(8,128)(2,1)S(1)}, u32[]{:S(2)}, u32[]{:S(2)}) collective-permute-start(bf16[2,24,896]{2,1,0:T(8,128)(2,1)S(1)} %get-tuple-element.41), channel_id=1, source_target_pairs={{0,12},{1,13},{2,14},{3,15},{4,8},{5,9},{6,10},{7,11},{8,4},{9,5},... | collective-permute-start | bytes 258056 | tf_op jit(solution)/shard_map/ppermute | solution.py:57
  54.3 11.3 %collective-permute-start.18 = (bf16[2,24,896]{2,1,0:T(8,128)(2,1)S(1)}, bf16[2,24,896]{2,1,0:T(8,128)(2,1)S(1)}, u32[]{:S(2)}, u32[]{:S(2)}) collective-permute-start(bf16[2,24,896]{2,1,0:T(8,128)(2,1)S(1)} %get-tuple-element.39), channel_id=1, source_target_pairs={{0,14},{1,15},{2,12},{3,13},{4,10},{5,11},{6,8},{7,9},{8,6},{9,7},... | collective-permute-start | bytes 258056 | tf_op jit(solution)/shard_map/ppermute | solution.py:57
  65.6 1.7 %collective-permute-start.19 = (bf16[8,24,896]{2,1,0:T(8,128)(2,1)S(1)}, bf16[8,24,896]{2,1,0:T(8,128)(2,1)S(1)}, u32[]{:S(2)}, u32[]{:S(2)}) collective-permute-start(bf16[8,24,896]{2,1,0:T(8,128)(2,1)S(1)} %get-tuple-element.58), channel_id=1, source_target_pairs={{0,1},{1,0},{2,3},{3,2},{4,5},{5,4},{6,7},{7,6},{8,9},{9,8},{10,11... | collective-permute-start | bytes 1032200 | tf_op jit(solution)/shard_map/ppermute | solution.py:51
  68.0 0.9 %copy-start.2 = (f32[64,3584]{1,0:T(8,128)}, f32[64,3584]{1,0:T(8,128)S(1)}, u32[]{:S(2)}) copy-start(f32[64,3584]{1,0:T(8,128)S(1)} %fusion.21) | copy-start | bytes 2752516

commit v5 on v1

v5 whole, which is shorter than its diff:
```python
import jax
import jax.numpy as jnp
from jax import lax
from jax.experimental import pallas as pl
from jax.experimental.pallas import tpu as pltpu
from jax.sharding import PartitionSpec as P
import functools

EXP_POD = 8
CFG = {'C': [[0, 3], [1, 2]], 'H': [[0], [1]], 'order': [['z', 0], ['x', [0]], ['z', 2], ['x', [2]], ['z', 3], ['x', [3]], ['z', 1], ['x', [1]], ['c', 1], ['h', 1], ['r', 2], ['c', 0], ['h', 0], ['r', 3], ['t', [0, 1]], ['w', [0, 1, 2, 3]]], 'gates': {'rs31': ['xd01'], 'rs20': ['zd2'], 'xs21': ['zd2'], 'cs1': ['zd3', 'xd01'], 'td01': ['xd01']}}


def sort_kernel(n_out, capacity, pods, tokens, routes, fixed, *outs):
    tok_rows = tokens.shape[0]
    rows = lax.broadcasted_iota(jnp.int32, (tok_rows, tok_rows), 0)
    cols = lax.broadcasted_iota(jnp.int32, (tok_rows, tok_rows), 1)
    upto = jnp.where(rows <= cols, 1.0, 0.0).astype(jnp.bfloat16)
    slot_of = lax.broadcasted_iota(jnp.int32, (capacity, tok_rows), 0)
    live, share = [], []
    for s in range(n_out):
        hit = routes[...] == pods[s]
        live.append(jnp.sum(jnp.where(hit, 1.0, 0.0), axis=0, keepdims=True))
        share.append(jnp.sum(jnp.where(hit, fixed[...], 0), axis=0, keepdims=True))
    flags = jnp.concatenate(live + [jnp.zeros((8 - n_out % 8, tok_rows), jnp.float32)] if n_out % 8 else live, axis=0)
    count = jnp.dot(flags.astype(jnp.bfloat16), upto, preferred_element_type=jnp.float32)
    place = []
    for s in range(n_out):
        slot = jnp.where(live[s] > 0.0, count[s : s + 1].astype(jnp.int32) - 1, -1)
        here = slot_of == slot
        place.append(jnp.where(here, 1.0, 0.0))
        spread = jnp.where(here, share[s], 0)
        outs[n_out][s] = (spread >> 8).astype(jnp.float32).astype(jnp.bfloat16)
        outs[n_out + 1][s] = (spread & 255).astype(jnp.float32).astype(jnp.bfloat16)
    chosen = jnp.concatenate(place, axis=0).astype(jnp.bfloat16)
    panels = jnp.dot(chosen, tokens[...], preferred_element_type=jnp.float32)
    for s in range(n_out):
        outs[s][...] = panels[s * capacity : (s + 1) * capacity].astype(jnp.bfloat16)

def sort_call(tokens, routes, fixed, pods, n_out, capacity):
    tok_rows, width = tokens.shape
    vmem = pl.BlockSpec(memory_space=pltpu.VMEM)
    outs = [jax.ShapeDtypeStruct((capacity, width), jnp.bfloat16)] * n_out
    outs += [jax.ShapeDtypeStruct((n_out, capacity, tok_rows), jnp.bfloat16)] * 2
    return pl.pallas_call(
        functools.partial(sort_kernel, n_out, capacity),
        in_specs=[pl.BlockSpec(memory_space=pltpu.SMEM), vmem, vmem, vmem],
        out_specs=[vmem] * len(outs), out_shape=outs,
        compiler_params=pltpu.CompilerParams(vmem_limit_bytes=16 * 1024 * 1024),
        name="pick_rows",
    )(pods, tokens, routes.T, fixed.T)

def combine_kernel(n_out, n_chip, groups, cols, weights, *refs):
    landed, swaps, out = refs[: n_out * n_chip], refs[n_out * n_chip : -1], refs[-1]
    tok_rows = out.shape[0]

    def rows_of(s, x, core):
        if not core:
            return landed[s * n_chip + x][0]
        for at, steps in enumerate(groups):
            if s in steps:
                return swaps[at][steps.index(s) * n_chip + x]

    for m in range(2 * n_chip):

        @pl.when(pl.program_id(0) == m)
        def _(m=m):
            parts = [rows_of(s, m // 2, m % 2).astype(jnp.float32) for s in range(n_out)]
            rows = jnp.concatenate(parts, axis=0).astype(jnp.bfloat16)
            both = jnp.dot(weights[...], rows, preferred_element_type=jnp.float32)
            out[...] = both[:tok_rows] * (1.0 / 256.0) + both[tok_rows:] * (1.0 / 65536.0)


def combine_call(weights, landed, swaps, cols, n_out, n_chip, capacity, tok_rows):
    arrived = [landed[s, x] for s in range(n_out) for x in range(n_chip)]
    groups = [tuple(steps) for steps, _ in swaps]
    traded = [v for _, v in swaps]
    part_out = traded[0].shape[-1]
    n_loc = 2 * n_chip
    spec_l = pl.BlockSpec((1, capacity, part_out), lambda m, cols: (0, 0, 0))
    return pl.pallas_call(
        functools.partial(combine_kernel, n_out, n_chip, groups),
        grid_spec=pltpu.PrefetchScalarGridSpec(
            num_scalar_prefetch=1,
            grid=(n_loc,),
            in_specs=[pl.BlockSpec(weights.shape, lambda m, cols: (0, 0))]
            + [spec_l] * len(arrived)
            + [pl.BlockSpec(v.shape, lambda m, cols: (0, 0, 0)) for v in traded],
            out_specs=pl.BlockSpec((tok_rows, part_out), lambda m, cols: (0, cols[m])),
        ),
        out_shape=jax.ShapeDtypeStruct((tok_rows, n_loc * part_out), jnp.float32),
        compiler_params=pltpu.CompilerParams(vmem_limit_bytes=16 * 1024 * 1024),
        name="weigh_rows",
    )(cols, weights, *arrived, *traded)


def per_device(tokens, routes, combine_fixed, gate_weight, up_weight, down_weight):
    tok_rows, width = tokens.shape
    n_out = lax.axis_size("outer")
    n_loc = lax.axis_size("local")
    n_chip = n_loc // 2
    capacity = 3 * tok_rows // (2 * n_out)
    part_out = down_weight.shape[2]
    part_hid = gate_weight.shape[2]
    z = lax.axis_index("outer")
    l = lax.axis_index("local")
    gate_local = gate_weight[0]
    up_local = up_weight[0]
    seen = {}
    gates = CFG["gates"]

    def gated(name, value):
        names = [g for g in gates.get(name, ()) if g in seen]
        if names:
            value = lax.optimization_barrier((value,) + tuple(seen[g] for g in names))[0]
        seen[name] = value
        return value

    def down_rows(core):
        return jnp.concatenate(
            [
                lax.dynamic_slice_in_dim(down_weight[0], (l ^ (2 * x + core)) * part_hid, part_hid, 0)
                for x in range(n_chip)
            ],
            axis=0,
        )

    down_same, down_other = down_rows(0), down_rows(1)
    pods = (z ^ jnp.arange(n_out, dtype=jnp.int32)) * EXP_POD
    in_kernels = n_out == 4 and capacity % 8 == 0 and part_out % 128 == 0
    if in_kernels:
        *panels, high, low = sort_call(tokens, routes, combine_fixed, pods, n_out, capacity)
        high = high.reshape(-1, tok_rows).T
        low = low.reshape(-1, tok_rows).T
    else:
        hit_mask = routes[:, :, None] == pods[None, None, :]
        fixed = jnp.sum(jnp.where(hit_mask, combine_fixed[:, :, None], 0), axis=1)
        is_live = jnp.any(hit_mask, axis=1).astype(jnp.int32)
        slot_index = jnp.where(is_live == 1, jnp.cumsum(is_live, axis=0) - 1, -1)
        placing = slot_index[:, :, None] == jnp.arange(capacity, dtype=jnp.int32)[None, None, :]
        panels = jnp.einsum(
            "tqc,td->qcd", placing.astype(jnp.bfloat16), tokens, preferred_element_type=jnp.float32
        ).astype(jnp.bfloat16)
        panels = panels.reshape(4, -1, width)
        spread = jnp.where(placing, fixed[:, :, None], 0).reshape(tok_rows, -1)
        high = (spread >> 8).astype(jnp.bfloat16)
        low = (spread & 255).astype(jnp.bfloat16)

    span = n_out // 4

    def by_pod(v, s, axis, move):
        if span == 1:
            return move(v, s) if s else v
        parts = jnp.split(v, span, axis=axis)
        parts = [move(p, s * span + i) if s * span + i else p for i, p in enumerate(parts)]
        return jnp.concatenate(parts, axis=axis)

    def outer_xor(v, s, axis):
        return by_pod(v, s, axis, lambda p, t: lax.ppermute(p, "outer", [(i, i ^ t) for i in range(n_out)]))

    def local_xor(v, m):
        return lax.ppermute(v, "local", [(i, i ^ m) for i in range(n_loc)])

    def both_xor(v, s, m):
        if m == 0:
            return outer_xor(v, s, 1)

        def move(p, t):
            pairs = [(a * n_loc + b, (a ^ t) * n_loc + (b ^ m)) for a in range(n_out) for b in range(n_loc)]
            return lax.ppermute(p, ("outer", "local"), pairs)

        if span == 1:
            return move(v, s)
        parts = jnp.split(v, span, axis=1)
        return jnp.concatenate([move(p, s * span + i) for i, p in enumerate(parts)], axis=1)

    def first_half(rows):
        gate_proj = jnp.dot(rows, gate_local, preferred_element_type=jnp.float32)
        up_proj = jnp.dot(rows, up_local, preferred_element_type=jnp.float32)
        return (jax.nn.silu(gate_proj) * up_proj).astype(jnp.bfloat16)

    chip_of = {}
    hid = []
    outs = {}
    landed = {}
    pieces = {}
    swaps = []
    mine = {}
    todo = list(CFG["order"])
    for item in todo:
        kind, arg = item
        if kind == "z":
            s = arg
            mine[s] = gated(f"zd{s}", outer_xor(gated(f"zs{s}", panels[s]), s, 0))
        elif kind == "x":
            for s in arg:
                chip_of[s, 0] = mine[s]
            for x in range(1, n_chip):
                held = [mine[s] for s in arg]
                held = held[0] if len(arg) == 1 else jnp.stack(held)
                got = gated(f"xd{arg[0]}{x}", local_xor(gated(f"xs{arg[0]}{x}", held), 2 * x))
                for at, s in enumerate(arg):
                    chip_of[s, x] = got if len(arg) == 1 else got[at]
        elif kind == "c":
            steps = CFG["C"][arg]
            same = jnp.concatenate([chip_of[s, x] for x in range(n_chip) for s in steps], axis=0)
            other = gated(f"cd{arg}", local_xor(gated(f"cs{arg}", same), 1))
            halves = [first_half(rows).reshape(n_chip, -1, part_hid) for rows in (same, other)]
            hid.append((arg, jnp.stack(halves, axis=1)))
        elif kind == "h":
            cs = CFG["H"][arg]
            steps = [s for c in cs for s in CFG["C"][c]]
            count = len(steps)
            hd = dict(hid)
            hidden = jnp.concatenate([hd[c] for c in cs], axis=2)
            hidden = gated(f"hs{arg}", hidden)
            sides = []
            for x in range(n_chip):
                side = hidden if x == 0 else gated(f"hd{arg}{x}", local_xor(hidden, 2 * x))
                sides.append(jnp.concatenate([side[y ^ x : (y ^ x) + 1] for y in range(n_chip)], axis=0))
            hidden_same = jnp.concatenate(sides, axis=3).reshape(2 * n_chip * count * span * capacity, n_chip * part_hid)
            hidden_other = gated(f"kd{arg}", local_xor(gated(f"ks{arg}", hidden_same), 1))
            out_same = jnp.dot(hidden_same, down_same, preferred_element_type=jnp.float32)
            out_other = jnp.dot(hidden_other, down_other, preferred_element_type=jnp.float32)
            out_other = out_other.reshape(n_chip, 2, -1, part_out)
            out_other = jnp.concatenate([out_other[:, 1:], out_other[:, :1]], axis=1).reshape(out_same.shape)
            expert_out = (out_same + out_other).astype(jnp.bfloat16)
            expert_out = expert_out.reshape(n_chip, 2, count, span * capacity, part_out)
            for at, s in enumerate(steps):
                outs[s] = expert_out[:, :, at]
        elif kind == "r":
            s = arg
            for x in range(n_chip):
                landed[s, x] = gated(f"rd{s}{x}", both_xor(gated(f"rs{s}{x}", outs[s][x]), s, 2 * x))
        elif kind == "t":
            for x in range(n_chip):
                block = jnp.stack([outs[s][x] for s in arg], axis=1)
                if x:
                    block = gated(f"td{arg[0]}{x}", local_xor(gated(f"ts{arg[0]}{x}", block), 2 * x))
                for at, s in enumerate(arg):
                    landed[s, x] = block[:, at]
            for s in arg:
                if s or span > 1:
                    moved = outer_xor(gated(f"rs{s}0", jnp.stack([landed[s, x] for x in range(n_chip)])), s, 2)
                    moved = gated(f"rd{s}0", moved)
                    for x in range(n_chip):
                        landed[s, x] = moved[x]
        elif kind == "w":
            steps = arg
            stack = gated(f"ws{steps[0]}", jnp.stack([landed[s, x][1] for s in steps for x in range(n_chip)]))
            swapped = gated(f"wd{steps[0]}", local_xor(stack, 1))
            for at, s in enumerate(steps):
                for x in range(n_chip):
                    pieces[s, 2 * x] = landed[s, x][0]
                    pieces[s, 2 * x + 1] = swapped[at * n_chip + x]
            swaps.append((steps, swapped))

    if in_kernels:
        cols = l ^ jnp.arange(n_loc, dtype=jnp.int32)
        weights = jnp.concatenate([high, low], axis=0)
        return combine_call(weights, landed, swaps, cols, n_out, n_chip, capacity, tok_rows)
    combined = jnp.zeros((tok_rows, width), jnp.float32)
    for m in range(n_loc):
        returned = jnp.concatenate([pieces[s, m] for s in range(4)], axis=0)
        block = jnp.dot(high, returned, preferred_element_type=jnp.float32) * (1.0 / 256.0)
        block += jnp.dot(low, returned, preferred_element_type=jnp.float32) * (1.0 / 65536.0)
        combined = lax.dynamic_update_slice(combined, block, (0, (l ^ m) * part_out))
    return combined


def solution(mesh):
    in_specs = (
        P(("groups", "outer", "local"), None),
        P(("groups", "outer", "local"), None),
        P(("groups", "outer", "local"), None),
        P("outer", None, "local"),
        P("outer", None, "local"),
        P("outer", None, "local"),
    )
    out_specs = P(("groups", "outer", "local"), None)
    return jax.shard_map(
        per_device, mesh=mesh, in_specs=in_specs, out_specs=out_specs, check_vma=False
    )
```

time: 99.8 us -> 65.9 us (0.66)
  starting transfers between devices: 46.1 us -> 24.4 us
  waiting for transfers between devices: 33 us -> 24.4 us
  other arithmetic: 5.73 us -> 0.22 us
  matrix products: 9.02 us -> 5 us
  Pallas kernels: 0 us -> 3.63 us
  local copies, waits for them, and re-layouts: 5.17 us -> 7.48 us
    ppermute x18 -> x8, starting transfers between devices: 29.7 us -> 14.8 us  [the longest x6 13.9 us: outer_xor(): lax.ppermute(p, 'outer', [(i, i ^ t) for i in range(n_out)])]
    ppermute x18 -> x8, waiting for transfers between devices: 25.9 us -> 14.5 us  [the longest x6 14.5 us: outer_xor(): lax.ppermute(p, 'outer', [(i, i ^ t) for i in range(n_out)])]
    ppermute x24 -> x12, starting transfers between devices: 16.4 us -> 9.59 us  [local_xor(): return lax.ppermute(v, 'local', [(i, i ^ m) for i in range(n_loc)])]
    another operation x5 -> x4, other arithmetic: 4.63 us -> 0.07 us  [the longest x2 0.02 us: per_device(): hid.append((arg, jnp.stack(halves, axis=1)))]
    dot_general x21 -> x12, matrix products: 9.02 us -> 5 us  [the longest x4 1.73 us: first_half(): up_proj = jnp.dot(rows, up_local, preferred_element_type=jnp.float32)]
    unnamed x35 -> x23, local copies, waits for them, and re-layouts: 1.64 us -> 5.47 us
    pallas_call x0 -> x2, Pallas kernels: none -> 3.63 us  [the longest x1 2.63 us: combine_call(): pl.pallas_call(functools.partial(combine_kernel, n_out, n_chip, groups),...]
    ppermute x24 -> x12, waiting for transfers between devices: 7.13 us -> 9.97 us  [local_xor(): return lax.ppermute(v, 'local', [(i, i ^ m) for i in range(n_loc)])]
  transfers between devices with their start and end apart: 42 -> 20, of which waited for: 13 -> 9; matrix products, arithmetic and copies ran while one was open for 13% -> 14% of each run, Pallas kernels for 0% -> 0%
where the time goes in v5:
time: 65.9 us; the launch traced here: 65.6 us
  starting transfers between devices  24.4 us (37%)
  waiting for transfers between devices  24.4 us (37%)
  local copies, waits for them, and re-layouts  7.48 us (11%)
  matrix products  5 us (8%)
  Pallas kernels  3.63 us (6%)
    ppermute x6, waiting for transfers between devices, outer_xor(): lax.ppermute(p, 'outer', [(i, i ^ t) for i in range(n_out)])  14.5 us
    ppermute x6, starting transfers between devices, outer_xor(): lax.ppermute(p, 'outer', [(i, i ^ t) for i in range(n_out)])  13.9 us
    ppermute x12, waiting for transfers between devices, local_xor(): return lax.ppermute(v, 'local', [(i, i ^ m) for i in range(n_loc)])  9.97 us
    ppermute x12, starting transfers between devices, local_xor(): return lax.ppermute(v, 'local', [(i, i ^ m) for i in range(n_loc)])  9.59 us
    unnamed x23, local copies, waits for them, and re-layouts  5.47 us
    pallas_call x1, Pallas kernels, combine_call(): pl.pallas_call(functools.partial(combine_kernel, n_out, n_chip, groups),...  2.63 us
    dot_general x4, matrix products, first_half(): up_proj = jnp.dot(rows, up_local, preferred_element_type=jnp.float32)  1.73 us
    dot_general x4, matrix products, first_half(): gate_proj = jnp.dot(rows, gate_local, preferred_element_type=jnp.float32)  1.72 us
  transfers between devices with their start and end apart: 20, of which 9 were waited for; matrix products, arithmetic and copies ran while one was open for 14% of the time, Pallas kernels for 0%

profile of v5, /device:TPU:0, one launch (start us, length us, event | category | flops | bytes accessed | tf_op | source)
XLA Modules:
  0.0 65.6 jit_solution(13789934797844636455)
XLA Ops:
  0.0 1.1 %copy-done.1 = bf16[64,3584]{1,0:T(8,128)(2,1)S(1)} copy-done((bf16[64,3584]{1,0:T(8,128)(2,1)S(1)}, bf16[64,3584]{1,0:T(8,128)(2,1)}, u32[]{:S(2)}) %copy-start.1) | copy-done | bytes 458776
  1.2 0.7 %copy-done.2 = s32[64,8]{0,1:T(8,128)S(1)} copy-done((s32[64,8]{0,1:T(8,128)S(1)}, s32[64,8]{0,1:T(8,128)}, u32[]{:S(2)}) %copy-start.2) | copy-done | bytes 2072
  1.9 0.7 %copy-done.3 = s32[64,8]{0,1:T(8,128)S(1)} copy-done((s32[64,8]{0,1:T(8,128)S(1)}, s32[64,8]{0,1:T(8,128)}, u32[]{:S(2)}) %copy-start.3) | copy-done | bytes 2072
  2.5 1.0 %pick_rows.1 = (bf16[24,3584]{1,0:T(8,128)(2,1)S(1)}, bf16[24,3584]{1,0:T(8,128)(2,1)S(1)}, bf16[24,3584]{1,0:T(8,128)(2,1)S(1)}, bf16[24,3584]{1,0:T(8,128)(2,1...) custom-call(s32[4]{0:T(128)S(1)} %xor_multiply_fusion.pods, bf16[64,3584]{1,0:T(8,128)(2,1)S(1)} %copy-done.1, ...), custom_call_target="tpu_custom_call" | custom-call | tf_op jit(solution)/shard_map/pick_rows/pallas_call | solution.py:44
  3.5 4.1 %collective-permute-start.7 = (bf16[24,3584]{1,0:T(8,128)(2,1)S(1)}, bf16[24,3584]{1,0:T(8,128)(2,1)S(1)}, u32[]{:S(2)}, u32[]{:S(2)}) collective-permute-start(bf16[24,3584]{1,0:T(8,128)(2,1)S(1)} %get-tuple-element.21), channel_id=1, source_target_pairs={{0,8},{4,12},{8,0},{12,4},{1,9},{5,13},{9,1},{13,5},{2,10},{6,14},... | collective-permute-start | bytes 516104 | tf_op jit(solution)/shard_map/ppermute | solution.py:158
  7.6 1.6 %collective-permute-start.6 = (bf16[24,3584]{1,0:T(8,128)(2,1)S(1)}, bf16[24,3584]{1,0:T(8,128)(2,1)}, u32[]{:S(2)}, u32[]{:S(2)}) collective-permute-start(bf16[24,3584]{1,0:T(8,128)(2,1)S(1)} %get-tuple-element.20), channel_id=1, source_target_pairs={{0,4},{4,0},{8,12},{12,8},{1,5},{5,1},{9,13},{13,9},{2,6},{6,2},{1... | collective-permute-start | bytes 516104 | tf_op jit(solution)/shard_map/ppermute | solution.py:158
  9.2 1.5 %collective-permute-start.1 = (bf16[24,3584]{1,0:T(8,128)(2,1)S(1)}, bf16[24,3584]{1,0:T(8,128)(2,1)}, u32[]{:S(2)}, u32[]{:S(2)}) collective-permute-start(bf16[24,3584]{1,0:T(8,128)(2,1)S(1)} %get-tuple-element.18), channel_id=1, source_target_pairs={{0,2},{1,3},{2,0},{3,1},{4,6},{5,7},{6,4},{7,5},{8,10},{9,11},{10,... | collective-permute-start | bytes 516104 | tf_op jit(solution)/shard_map/ppermute | solution.py:161
  11.0 1.6 %dynamic-slice_bitcast_fusion.3 = (bf16[256,896]{1,0:T(8,128)(2,1)S(1)}, bf16[256,896]{1,0:T(8,128)(2,1)S(1)}, bf16[256,896]{1,0:T(8,128)(2,1)S(1)}, bf16[256,896]{1,0:T(8,128)(2,1)S(1)}) fusion(bf16[1,1024,896]{2,1,0:T(8,128)(2,1)} %param.11, s32[]{:T(128)S(6)} %select_n.12, s32[]{:T(128)S(6)} %select_n.13, s32[]{:T(128)S(6)} %select_n.15, s32[]{:T(128)S(6)} %select_n.14), kind=kLoop, calls=%fused_computation.29 | loop fusion | bytes 3670032 | tf_op jit(solution)/shard_map/dynamic_slice | solution.py:121
  12.6 4.8 %collective-permute-done.7 = bf16[24,3584]{1,0:T(8,128)(2,1)S(1)} collective-permute-done((bf16[24,3584]{1,0:T(8,128)(2,1)S(1)}, bf16[24,3584]{1,0:T(8,128)(2,1)S(1)}, u32[]{:S(2)}, u32[]{:S(2)}) %collective-permute-start.7) | collective-permute-done | bytes 172064 | tf_op jit(solution)/shard_map/ppermute | solution.py:158
  17.4 2.1 %collective-permute-start.9 = (bf16[24,3584]{1,0:T(8,128)(2,1)S(1)}, bf16[24,3584]{1,0:T(8,128)(2,1)S(1)}, u32[]{:S(2)}, u32[]{:S(2)}) collective-permute-start(bf16[24,3584]{1,0:T(8,128)(2,1)S(1)} %collective-permute-done.7), channel_id=1, source_target_pairs={{0,2},{1,3},{2,0},{3,1},{4,6},{5,7},{6,4},{7,5},{8,10},{9,11},{10,... | collective-permute-start | bytes 516104 | tf_op jit(solution)/shard_map/ppermute | solution.py:161
  19.5 0.9 %constant_dynamic-update-slice_fusion.7 = bf16[96,3584]{1,0:T(8,128)(2,1)S(1)} fusion(bf16[24,3584]{1,0:T(8,128)(2,1)} %collective-permute-done.6), kind=kLoop, calls=%fused_computation.70 | loop fusion | bytes 344064
  20.7 1.9 %collective-permute-start.2 = (bf16[24,3584]{1,0:T(8,128)(2,1)}, bf16[24,3584]{1,0:T(8,128)(2,1)S(1)}, u32[]{:S(2)}, u32[]{:S(2)}) collective-permute-start(bf16[24,3584]{1,0:T(8,128)(2,1)} %collective-permute-done), channel_id=1, source_target_pairs={{0,2},{1,3},{2,0},{3,1},{4,6},{5,7},{6,4},{7,5},{8,10},{9,11},{10,... | collective-permute-start | bytes 516104 | tf_op jit(solution)/shard_map/ppermute | solution.py:161
  22.6 1.0 %constant_dynamic-update-slice_fusion.2 = bf16[96,3584]{1,0:T(8,128)(2,1)S(1)} fusion(bf16[96,3584]{1,0:T(8,128)(2,1)S(1)} %constant_dynamic-update-slice_fusion.3, bf16[24,3584]{1,0:T(8,128)(2,1)} %collective-permute-done), kind=kLoop, calls=%fused_computation.65 | loop fusion | bytes 344064
  23.6 0.9 %constant_dynamic-update-slice_fusion.1 = bf16[96,3584]{1,0:T(8,128)(2,1)S(1)} fusion(bf16[96,3584]{1,0:T(8,128)(2,1)S(1)} %constant_dynamic-update-slice_fusion.2, bf16[24,3584]{1,0:T(8,128)(2,1)} %collective-permute-done.1), kind=kLoop, calls=%fused_computation.64 | loop fusion | bytes 344064
  24.5 2.6 %collective-permute-done.8 = bf16[24,3584]{1,0:T(8,128)(2,1)S(1)} collective-permute-done((bf16[24,3584]{1,0:T(8,128)(2,1)}, bf16[24,3584]{1,0:T(8,128)(2,1)S(1)}, u32[]{:S(2)}, u32[]{:S(2)}) %collective-permute-start.8) | collective-permute-done | bytes 172064 | tf_op jit(solution)/shard_map/ppermute | solution.py:161
  27.7 1.3 %collective-permute-done.2 = bf16[24,3584]{1,0:T(8,128)(2,1)S(1)} collective-permute-done((bf16[24,3584]{1,0:T(8,128)(2,1)}, bf16[24,3584]{1,0:T(8,128)(2,1)S(1)}, u32[]{:S(2)}, u32[]{:S(2)}) %collective-permute-start.2) | collective-permute-done | bytes 172064 | tf_op jit(solution)/shard_map/ppermute | solution.py:161
  29.9 0.4 multiply_convert_fusion.3
  30.4 0.4 fusion.8
  30.8 0.4 multiply_convert_fusion
  31.3 1.5 %collective-permute-start.11 = (bf16[2,2,48,256]{3,2,1,0:T(8,128)(2,1)S(1)}, bf16[2,2,48,256]{3,2,1,0:T(8,128)(2,1)S(1)}, u32[]{:S(2)}, u32[]{:S(2)}) collective-permute-start(bf16[2,2,48,256]{3,2,1,0:T(8,128)(2,1)S(1)} %pad_maximum_fusion.11), channel_id=1, source_target_pairs={{0,2},{1,3},{2,0},{3,1},{4,6},{5,7},{6,4},{7,5},{8,10},{9,11},{10,... | collective-permute-start | bytes 294920 | tf_op jit(solution)/shard_map/ppermute | solution.py:161
  33.2 0.4 multiply_convert_fusion.2
  33.7 0.6 collective-permute-start.4
  34.3 2.2 %collective-permute-done.11 = bf16[2,2,48,256]{3,2,1,0:T(8,128)(2,1)S(1)} collective-permute-done((bf16[2,2,48,256]{3,2,1,0:T(8,128)(2,1)S(1)}, bf16[2,2,48,256]{3,2,1,0:T(8,128)(2,1)S(1)}, u32[]{:S(2)}, u32[]{:S(2)}) %collective-permute-start.11) | collective-permute-done | bytes 98336 | tf_op jit(solution)/shard_map/ppermute | solution.py:161
  36.7 2.0 %collective-permute-done.4 = bf16[2,2,48,256]{3,2,1,0:T(8,128)(2,1)S(1)} collective-permute-done((bf16[2,2,48,256]{3,2,1,0:T(8,128)(2,1)S(1)}, bf16[2,2,48,256]{3,2,1,0:T(8,128)(2,1)S(1)}, u32[]{:S(2)}, u32[]{:S(2)}) %collective-permute-start.4) | collective-permute-done | bytes 98336 | tf_op jit(solution)/shard_map/ppermute | solution.py:161
  39.7 0.5 collective-permute-done.5
  41.2 1.5 %collective-permute-start.13 = (bf16[2,2,24,896]{3,2,0,1:T(8,128)(2,1)S(1)}, bf16[2,2,24,896]{3,2,0,1:T(8,128)(2,1)S(1)}, u32[]{:S(2)}, u32[]{:S(2)}) collective-permute-start(bf16[2,2,24,896]{3,2,0,1:T(8,128)(2,1)S(1)} %pad_maximum_fusion.8), channel_id=1, source_target_pairs={{0,2},{1,3},{2,0},{3,1},{4,6},{5,7},{6,4},{7,5},{8,10},{9,11},{10,... | collective-permute-start | bytes 516104 | tf_op jit(solution)/shard_map/ppermute | solution.py:161
  42.7 3.4 %collective-permute-start.15 = (bf16[2,24,896]{2,1,0:T(8,128)(2,1)S(1)}, bf16[2,24,896]{2,1,0:T(8,128)(2,1)S(1)}, u32[]{:S(2)}, u32[]{:S(2)}) collective-permute-start(bf16[2,24,896]{2,1,0:T(8,128)(2,1)S(1)} %get-tuple-element.25), channel_id=1, source_target_pairs={{0,8},{4,12},{8,0},{12,4},{1,9},{5,13},{9,1},{13,5},{2,10},{6,14},... | collective-permute-start | bytes 258056 | tf_op jit(solution)/shard_map/ppermute | solution.py:158
  46.1 4.5 %collective-permute-start.17 = (bf16[2,24,896]{2,1,0:T(8,128)(2,1)S(1)}, bf16[2,24,896]{2,1,0:T(8,128)(2,1)S(1)}, u32[]{:S(2)}, u32[]{:S(2)}) collective-permute-start(bf16[2,24,896]{2,1,0:T(8,128)(2,1)S(1)} %get-tuple-element.36), channel_id=1, source_target_pairs={{0,12},{4,8},{8,4},{12,0},{1,13},{5,9},{9,5},{13,1},{2,14},{6,10},... | collective-permute-start | bytes 258056 | tf_op jit(solution)/shard_map/ppermute | solution.py:158
  50.6 0.9 %collective-permute-start.18 = (bf16[2,24,896]{2,1,0:T(8,128)(2,1)S(1)}, bf16[2,24,896]{2,1,0:T(8,128)(2,1)S(1)}, u32[]{:S(2)}, u32[]{:S(2)}) collective-permute-start(bf16[2,24,896]{2,1,0:T(8,128)(2,1)S(1)} %get-tuple-element.26), channel_id=1, source_target_pairs={{0,14},{1,15},{2,12},{3,13},{4,10},{5,11},{6,8},{7,9},{8,6},{9,7},... | collective-permute-start | bytes 258056 | tf_op jit(solution)/shard_map/ppermute | solution.py:169
  51.6 9.5 %collective-permute-done.14 = bf16[2,2,24,896]{3,2,1,0:T(8,128)(2,1)S(1)} collective-permute-done((bf16[2,2,24,896]{3,2,1,0:T(8,128)(2,1)S(1)}, bf16[2,2,24,896]{3,2,1,0:T(8,128)(2,1)S(1)}, u32[]{:S(2)}, u32[]{:S(2)}) %collective-permute-start.14) | collective-permute-done | bytes 172064 | tf_op jit(solution)/shard_map/ppermute | solution.py:158
  61.6 1.4 %collective-permute-done.19.refs_8_ = bf16[8,24,896]{2,1,0:T(8,128)(2,1)S(1)} collective-permute-done((bf16[8,24,896]{2,1,0:T(8,128)(2,1)S(1)}, bf16[8,24,896]{2,1,0:T(8,128)(2,1)S(1)}, u32[]{:S(2)}, u32[]{:S(2)}) %collective-permute-start.19) | collective-permute-done | bytes 344096 | tf_op jit(solution)/shard_map/ppermute | solution.py:161
  63.0 2.6 %weigh_rows.1 = f32[64,3584]{1,0:T(8,128)} custom-call(s32[4]{0:T(128)S(1)} %iota_xor_fusion.cols, bf16[128,96]{1,0:T(8,128)(2,1)S(1)} %pad_maximum_fusion.12.weights, bf16[2,24,896]{2,1,0:T(8,128)(2,1)S(1)} %get-tuple-element.38.refs_0_, bf16[2,24,896]{2,1,0:T(8,128)(2,1)S(1)} %get-tuple-element.46.refs_1_, ...), custom_call_target="tpu_custom_call" | custom-call | tf_op jit(solution)/shard_map/weigh_rows/pallas_call | solution.py:80
  (70 shorter events, 5.0 us)
Async XLA Ops:
  0.0 27.3 %copy-start = (bf16[1,3584,256]{2,1,0:T(8,128)(2,1)S(1)}, bf16[1,3584,256]{2,1,0:T(8,128)(2,1)}, u32[]{:S(2)}) copy-start(bf16[1,3584,256]{2,1,0:T(8,128)(2,1)} %param.9) | copy-start | bytes 5505028
  0.0 1.2 %copy-start.1 = (bf16[64,3584]{1,0:T(8,128)(2,1)S(1)}, bf16[64,3584]{1,0:T(8,128)(2,1)}, u32[]{:S(2)}) copy-start(bf16[64,3584]{1,0:T(8,128)(2,1)} %tokens.1) | copy-start | bytes 1376260
  1.2 0.7 %copy-start.2 = (s32[64,8]{0,1:T(8,128)S(1)}, s32[64,8]{0,1:T(8,128)}, u32[]{:S(2)}) copy-start(s32[64,8]{0,1:T(8,128)} %param.7) | copy-start | bytes 6148
  1.8 0.7 %copy-start.3 = (s32[64,8]{0,1:T(8,128)S(1)}, s32[64,8]{0,1:T(8,128)}, u32[]{:S(2)}) copy-start(s32[64,8]{0,1:T(8,128)} %param.8) | copy-start | bytes 6148
  3.5 13.8 %collective-permute-start.7 = (bf16[24,3584]{1,0:T(8,128)(2,1)S(1)}, bf16[24,3584]{1,0:T(8,128)(2,1)S(1)}, u32[]{:S(2)}, u32[]{:S(2)}) collective-permute-start(bf16[24,3584]{1,0:T(8,128)(2,1)S(1)} %get-tuple-element.21), channel_id=1, source_target_pairs={{0,8},{4,12},{8,0},{12,4},{1,9},{5,13},{9,1},{13,5},{2,10},{6,14},... | collective-permute-start | bytes 516104 | tf_op jit(solution)/shard_map/ppermute | solution.py:158
  7.6 11.8 %collective-permute-start.6 = (bf16[24,3584]{1,0:T(8,128)(2,1)S(1)}, bf16[24,3584]{1,0:T(8,128)(2,1)}, u32[]{:S(2)}, u32[]{:S(2)}) collective-permute-start(bf16[24,3584]{1,0:T(8,128)(2,1)S(1)} %get-tuple-element.20), channel_id=1, source_target_pairs={{0,4},{4,0},{8,12},{12,8},{1,5},{5,1},{9,13},{13,9},{2,6},{6,2},{1... | collective-permute-start | bytes 516104 | tf_op jit(solution)/shard_map/ppermute | solution.py:158
  9.2 14.4 %collective-permute-start.1 = (bf16[24,3584]{1,0:T(8,128)(2,1)S(1)}, bf16[24,3584]{1,0:T(8,128)(2,1)}, u32[]{:S(2)}, u32[]{:S(2)}) collective-permute-start(bf16[24,3584]{1,0:T(8,128)(2,1)S(1)} %get-tuple-element.18), channel_id=1, source_target_pairs={{0,2},{1,3},{2,0},{3,1},{4,6},{5,7},{6,4},{7,5},{8,10},{9,11},{10,... | collective-permute-start | bytes 516104 | tf_op jit(solution)/shard_map/ppermute | solution.py:161
  10.7 10.0 %collective-permute-start = (bf16[24,3584]{1,0:T(8,128)(2,1)S(1)}, bf16[24,3584]{1,0:T(8,128)(2,1)}, u32[]{:S(2)}, u32[]{:S(2)}) collective-permute-start(bf16[24,3584]{1,0:T(8,128)(2,1)S(1)} %get-tuple-element.19), channel_id=1, source_target_pairs={{0,12},{4,8},{8,4},{12,0},{1,13},{5,9},{9,5},{13,1},{2,14},{6,10},... | collective-permute-start | bytes 516104 | tf_op jit(solution)/shard_map/ppermute | solution.py:158
  17.4 9.8 %collective-permute-start.9 = (bf16[24,3584]{1,0:T(8,128)(2,1)S(1)}, bf16[24,3584]{1,0:T(8,128)(2,1)S(1)}, u32[]{:S(2)}, u32[]{:S(2)}) collective-permute-start(bf16[24,3584]{1,0:T(8,128)(2,1)S(1)} %collective-permute-done.7), channel_id=1, source_target_pairs={{0,2},{1,3},{2,0},{3,1},{4,6},{5,7},{6,4},{7,5},{8,10},{9,11},{10,... | collective-permute-start | bytes 516104 | tf_op jit(solution)/shard_map/ppermute | solution.py:161
  20.4 6.7 %collective-permute-start.8 = (bf16[24,3584]{1,0:T(8,128)(2,1)}, bf16[24,3584]{1,0:T(8,128)(2,1)S(1)}, u32[]{:S(2)}, u32[]{:S(2)}) collective-permute-start(bf16[24,3584]{1,0:T(8,128)(2,1)} %collective-permute-done.6), channel_id=1, source_target_pairs={{0,2},{1,3},{2,0},{3,1},{4,6},{5,7},{6,4},{7,5},{8,10},{9,11},{10,... | collective-permute-start | bytes 516104 | tf_op jit(solution)/shard_map/ppermute | solution.py:161
  20.7 8.3 %collective-permute-start.2 = (bf16[24,3584]{1,0:T(8,128)(2,1)}, bf16[24,3584]{1,0:T(8,128)(2,1)S(1)}, u32[]{:S(2)}, u32[]{:S(2)}) collective-permute-start(bf16[24,3584]{1,0:T(8,128)(2,1)} %collective-permute-done), channel_id=1, source_target_pairs={{0,2},{1,3},{2,0},{3,1},{4,6},{5,7},{6,4},{7,5},{8,10},{9,11},{10,... | collective-permute-start | bytes 516104 | tf_op jit(solution)/shard_map/ppermute | solution.py:161
  27.2 3.2 %collective-permute-start.10 = (bf16[96,3584]{1,0:T(8,128)(2,1)S(1)}, bf16[96,3584]{1,0:T(8,128)(2,1)S(1)}, u32[]{:S(2)}, u32[]{:S(2)}) collective-permute-start(bf16[96,3584]{1,0:T(8,128)(2,1)S(1)} %constant_dynamic-update-slice_fusion.4), channel_id=1, source_target_pairs={{0,1},{1,0},{2,3},{3,2},{4,5},{5,4},{6,7},{7,6},{8,9},{9,8},{10,11... | collective-permute-start | bytes 2064392 | tf_op jit(solution)/shard_map/ppermute | solution.py:161
  27.7 1.8 %copy-start.4 = (bf16[1,3584,256]{2,1,0:T(8,128)(2,1)S(1)}, bf16[1,3584,256]{2,1,0:T(8,128)(2,1)}, u32[]{:S(2)}) copy-start(bf16[1,3584,256]{2,1,0:T(8,128)(2,1)} %param.10) | copy-start | bytes 5505028
  29.0 3.8 %collective-permute-start.3 = (bf16[96,3584]{1,0:T(8,128)(2,1)S(1)}, bf16[96,3584]{1,0:T(8,128)(2,1)S(1)}, u32[]{:S(2)}, u32[]{:S(2)}) collective-permute-start(bf16[96,3584]{1,0:T(8,128)(2,1)S(1)} %constant_dynamic-update-slice_fusion), channel_id=1, source_target_pairs={{0,1},{1,0},{2,3},{3,2},{4,5},{5,4},{6,7},{7,6},{8,9},{9,8},{10,11... | collective-permute-start | bytes 2064392 | tf_op jit(solution)/shard_map/ppermute | solution.py:161
  31.3 5.3 %collective-permute-start.11 = (bf16[2,2,48,256]{3,2,1,0:T(8,128)(2,1)S(1)}, bf16[2,2,48,256]{3,2,1,0:T(8,128)(2,1)S(1)}, u32[]{:S(2)}, u32[]{:S(2)}) collective-permute-start(bf16[2,2,48,256]{3,2,1,0:T(8,128)(2,1)S(1)} %pad_maximum_fusion.11), channel_id=1, source_target_pairs={{0,2},{1,3},{2,0},{3,1},{4,6},{5,7},{6,4},{7,5},{8,10},{9,11},{10,... | collective-permute-start | bytes 294920 | tf_op jit(solution)/shard_map/ppermute | solution.py:161
  33.7 5.0 %collective-permute-start.4 = (bf16[2,2,48,256]{3,2,1,0:T(8,128)(2,1)S(1)}, bf16[2,2,48,256]{3,2,1,0:T(8,128)(2,1)S(1)}, u32[]{:S(2)}, u32[]{:S(2)}) collective-permute-start(bf16[2,2,48,256]{3,2,1,0:T(8,128)(2,1)S(1)} %pad_maximum_fusion.10), channel_id=1, source_target_pairs={{0,2},{1,3},{2,0},{3,1},{4,6},{5,7},{6,4},{7,5},{8,10},{9,11},{10,... | collective-permute-start | bytes 294920 | tf_op jit(solution)/shard_map/ppermute | solution.py:161
  36.6 2.2 %collective-permute-start.12 = (bf16[192,512]{1,0:T(8,128)(2,1)S(1)}, bf16[192,512]{1,0:T(8,128)(2,1)S(1)}, u32[]{:S(2)}, u32[]{:S(2)}) collective-permute-start(bf16[192,512]{1,0:T(8,128)(2,1)S(1)} %bitcast.147), channel_id=1, source_target_pairs={{0,1},{1,0},{2,3},{3,2},{4,5},{5,4},{6,7},{7,6},{8,9},{9,8},{10,11... | collective-permute-start | bytes 589832 | tf_op jit(solution)/shard_map/ppermute | solution.py:161
  38.7 1.5 %collective-permute-start.5 = (bf16[192,512]{1,0:T(8,128)(2,1)S(1)}, bf16[192,512]{1,0:T(8,128)(2,1)S(1)}, u32[]{:S(2)}, u32[]{:S(2)}) collective-permute-start(bf16[192,512]{1,0:T(8,128)(2,1)S(1)} %bitcast.145), channel_id=1, source_target_pairs={{0,1},{1,0},{2,3},{3,2},{4,5},{5,4},{6,7},{7,6},{8,9},{9,8},{10,11... | collective-permute-start | bytes 589832 | tf_op jit(solution)/shard_map/ppermute | solution.py:161
  41.2 10.3 %collective-permute-start.13 = (bf16[2,2,24,896]{3,2,0,1:T(8,128)(2,1)S(1)}, bf16[2,2,24,896]{3,2,0,1:T(8,128)(2,1)S(1)}, u32[]{:S(2)}, u32[]{:S(2)}) collective-permute-start(bf16[2,2,24,896]{3,2,0,1:T(8,128)(2,1)S(1)} %pad_maximum_fusion.8), channel_id=1, source_target_pairs={{0,2},{1,3},{2,0},{3,1},{4,6},{5,7},{6,4},{7,5},{8,10},{9,11},{10,... | collective-permute-start | bytes 516104 | tf_op jit(solution)/shard_map/ppermute | solution.py:161
  42.7 18.5 %collective-permute-start.15 = (bf16[2,24,896]{2,1,0:T(8,128)(2,1)S(1)}, bf16[2,24,896]{2,1,0:T(8,128)(2,1)S(1)}, u32[]{:S(2)}, u32[]{:S(2)}) collective-permute-start(bf16[2,24,896]{2,1,0:T(8,128)(2,1)S(1)} %get-tuple-element.25), channel_id=1, source_target_pairs={{0,8},{4,12},{8,0},{12,4},{1,9},{5,13},{9,1},{13,5},{2,10},{6,14},... | collective-permute-start | bytes 258056 | tf_op jit(solution)/shard_map/ppermute | solution.py:158
  46.1 15.1 %collective-permute-start.16 = (bf16[2,24,896]{2,1,0:T(8,128)(2,1)S(1)}, bf16[2,24,896]{2,1,0:T(8,128)(2,1)S(1)}, u32[]{:S(2)}, u32[]{:S(2)}) collective-permute-start(bf16[2,24,896]{2,1,0:T(8,128)(2,1)S(1)} %get-tuple-element.39), channel_id=1, source_target_pairs={{0,10},{1,11},{2,8},{3,9},{4,14},{5,15},{6,12},{7,13},{8,2},{9,3},... | collective-permute-start | bytes 258056 | tf_op jit(solution)/shard_map/ppermute | solution.py:169
  46.1 15.1 %collective-permute-start.17 = (bf16[2,24,896]{2,1,0:T(8,128)(2,1)S(1)}, bf16[2,24,896]{2,1,0:T(8,128)(2,1)S(1)}, u32[]{:S(2)}, u32[]{:S(2)}) collective-permute-start(bf16[2,24,896]{2,1,0:T(8,128)(2,1)S(1)} %get-tuple-element.36), channel_id=1, source_target_pairs={{0,12},{4,8},{8,4},{12,0},{1,13},{5,9},{9,5},{13,1},{2,14},{6,10},... | collective-permute-start | bytes 258056 | tf_op jit(solution)/shard_map/ppermute | solution.py:158
  50.6 10.6 %collective-permute-start.18 = (bf16[2,24,896]{2,1,0:T(8,128)(2,1)S(1)}, bf16[2,24,896]{2,1,0:T(8,128)(2,1)S(1)}, u32[]{:S(2)}, u32[]{:S(2)}) collective-permute-start(bf16[2,24,896]{2,1,0:T(8,128)(2,1)S(1)} %get-tuple-element.26), channel_id=1, source_target_pairs={{0,14},{1,15},{2,12},{3,13},{4,10},{5,11},{6,8},{7,9},{8,6},{9,7},... | collective-permute-start | bytes 258056 | tf_op jit(solution)/shard_map/ppermute | solution.py:169
  51.5 9.6 %collective-permute-start.14 = (bf16[2,2,24,896]{3,2,1,0:T(8,128)(2,1)S(1)}, bf16[2,2,24,896]{3,2,1,0:T(8,128)(2,1)S(1)}, u32[]{:S(2)}, u32[]{:S(2)}) collective-permute-start(bf16[2,2,24,896]{3,2,1,0:T(8,128)(2,1)S(1)} %pad_maximum_fusion.9), channel_id=1, source_target_pairs={{0,4},{4,0},{8,12},{12,8},{1,5},{5,1},{9,13},{13,9},{2,6},{6,2},{1... | collective-permute-start | bytes 516104 | tf_op jit(solution)/shard_map/ppermute | solution.py:158
  61.2 1.7 %collective-permute-start.19 = (bf16[8,24,896]{2,1,0:T(8,128)(2,1)S(1)}, bf16[8,24,896]{2,1,0:T(8,128)(2,1)S(1)}, u32[]{:S(2)}, u32[]{:S(2)}) collective-permute-start(bf16[8,24,896]{2,1,0:T(8,128)(2,1)S(1)} %slice_dynamic-update-slice_fusion), channel_id=1, source_target_pairs={{0,1},{1,0},{2,3},{3,2},{4,5},{5,4},{6,7},{7,6},{8,9},{9,8},{10,11... | collective-permute-start | bytes 1032200 | tf_op jit(solution)/shard_map/ppermute | solution.py:161

commit v6 on v5

--- a/solution.py
+++ b/solution.py
@@ -7,67 +7,99 @@
 import functools
 
 EXP_POD = 8
-CFG = {'C': [[0, 3], [1, 2]], 'H': [[0], [1]], 'order': [['z', 0], ['x', [0]], ['z', 2], ['x', [2]], ['z', 3], ['x', [3]], ['z', 1], ['x', [1]], ['c', 1], ['h', 1], ['r', 2], ['c', 0], ['h', 0], ['r', 3], ['t', [0, 1]], ['w', [0, 1, 2, 3]]], 'gates': {'rs31': ['xd01'], 'rs20': ['zd2'], 'xs21': ['zd2'], 'cs1': ['zd3', 'xd01'], 'td01': ['xd01']}}
-
-
-def sort_kernel(n_out, capacity, pods, tokens, routes, fixed, *outs):
+CFG = {'C': [[0, 3], [1, 2]], 'H': [[0], [1]], 'order': [['z', 3], ['x', [3]], ['z', 2], ['x', [2]], ['z', 0], ['z', 1], ['x', [1]], ['x', [0]], ['c', 1], ['h', 1], ['r', 2], ['c', 0], ['h', 0], ['r', 3], ['t', [0, 1]], ['w', [0, 1, 2, 3]]], 'gates': {'rs31': ['xd01'], 'rs20': ['zd2'], 'cs1': ['zd3', 'xd01'], 'td01': ['xd01'], 'rd30': ['hd11']}, 'apart': False}
+
+
+def pick_kernel(n_out, capacity, pods, tokens_hbm, routes_hbm, fixed_hbm, *refs):
+    panels, (high, low) = refs[:n_out], refs[n_out : n_out + 2]
+    tokens, routes, fixed, sems = refs[n_out + 2 :]
+    copies = [
+        pltpu.make_async_copy(src, dst, sems.at[i])
+        for i, (src, dst) in enumerate(((routes_hbm, routes), (fixed_hbm, fixed), (tokens_hbm, tokens)))
+    ]
+    for copy in copies:
+        copy.start()
     tok_rows = tokens.shape[0]
     rows = lax.broadcasted_iota(jnp.int32, (tok_rows, tok_rows), 0)
     cols = lax.broadcasted_iota(jnp.int32, (tok_rows, tok_rows), 1)
     upto = jnp.where(rows <= cols, 1.0, 0.0).astype(jnp.bfloat16)
     slot_of = lax.broadcasted_iota(jnp.int32, (capacity, tok_rows), 0)
-    live, share = [], []
-    for s in range(n_out):
-        hit = routes[...] == pods[s]
-        live.append(jnp.sum(jnp.where(hit, 1.0, 0.0), axis=0, keepdims=True))
-        share.append(jnp.sum(jnp.where(hit, fixed[...], 0), axis=0, keepdims=True))
-    flags = jnp.concatenate(live + [jnp.zeros((8 - n_out % 8, tok_rows), jnp.float32)] if n_out % 8 else live, axis=0)
-    count = jnp.dot(flags.astype(jnp.bfloat16), upto, preferred_element_type=jnp.float32)
-    place = []
+    copies[0].wait()
+    hits = [routes[...] == pods[s] for s in range(n_out)]
+    live = [jnp.sum(jnp.where(hit, 1.0, 0.0), axis=0, keepdims=True) for hit in hits]
+    spare = [jnp.zeros((8 - n_out, tok_rows), jnp.float32)]
+    count = jnp.dot(jnp.concatenate(live + spare, axis=0).astype(jnp.bfloat16), upto, preferred_element_type=jnp.float32)
+    here = []
     for s in range(n_out):
         slot = jnp.where(live[s] > 0.0, count[s : s + 1].astype(jnp.int32) - 1, -1)
-        here = slot_of == slot
-        place.append(jnp.where(here, 1.0, 0.0))
-        spread = jnp.where(here, share[s], 0)
-        outs[n_out][s] = (spread >> 8).astype(jnp.float32).astype(jnp.bfloat16)
-        outs[n_out + 1][s] = (spread & 255).astype(jnp.float32).astype(jnp.bfloat16)
-    chosen = jnp.concatenate(place, axis=0).astype(jnp.bfloat16)
-    panels = jnp.dot(chosen, tokens[...], preferred_element_type=jnp.float32)
+        here.append(slot_of == slot)
+    chosen = jnp.concatenate([jnp.where(h, 1.0, 0.0) for h in here], axis=0).astype(jnp.bfloat16)
+    copies[2].wait()
+    picked = jnp.dot(chosen, tokens[...], preferred_element_type=jnp.float32)
     for s in range(n_out):
-        outs[s][...] = panels[s * capacity : (s + 1) * capacity].astype(jnp.bfloat16)
-
-def sort_call(tokens, routes, fixed, pods, n_out, capacity):
+        panels[s][...] = picked[s * capacity : (s + 1) * capacity].astype(jnp.bfloat16)
+    copies[1].wait()
+    for s in range(n_out):
+        share = jnp.sum(jnp.where(hits[s], fixed[...], 0), axis=0, keepdims=True)
+        spread = jnp.where(here[s], share, 0)
+        high[s] = (spread >> 8).astype(jnp.float32)
+        low[s] = (spread & 255).astype(jnp.float32)
+
+
+def pick_call(tokens, routes, fixed, pods, n_out, capacity):
     tok_rows, width = tokens.shape
     vmem = pl.BlockSpec(memory_space=pltpu.VMEM)
+    away = pl.BlockSpec(memory_space=pl.ANY)
     outs = [jax.ShapeDtypeStruct((capacity, width), jnp.bfloat16)] * n_out
-    outs += [jax.ShapeDtypeStruct((n_out, capacity, tok_rows), jnp.bfloat16)] * 2
+    outs += [jax.ShapeDtypeStruct((n_out, capacity, tok_rows), jnp.float32)] * 2
     return pl.pallas_call(
-        functools.partial(sort_kernel, n_out, capacity),
-        in_specs=[pl.BlockSpec(memory_space=pltpu.SMEM), vmem, vmem, vmem],
-        out_specs=[vmem] * len(outs), out_shape=outs,
-        compiler_params=pltpu.CompilerParams(vmem_limit_bytes=16 * 1024 * 1024),
+        functools.partial(pick_kernel, n_out, capacity),
+        in_specs=[pl.BlockSpec(memory_space=pltpu.SMEM), away, away, away],
+        out_specs=[vmem] * len(outs),
+        out_shape=outs,
+        scratch_shapes=[
+            pltpu.VMEM(tokens.shape, tokens.dtype),
+            pltpu.VMEM(routes.shape[::-1], routes.dtype),
+            pltpu.VMEM(fixed.shape[::-1], fixed.dtype),
+            pltpu.SemaphoreType.DMA((3,)),
+        ],
+        compiler_params=pltpu.CompilerParams(vmem_limit_bytes=56 * 1024 * 1024),
         name="pick_rows",
     )(pods, tokens, routes.T, fixed.T)
 
+
 def combine_kernel(n_out, n_chip, groups, cols, weights, *refs):
-    landed, swaps, out = refs[: n_out * n_chip], refs[n_out * n_chip : -1], refs[-1]
-    tok_rows = out.shape[0]
-
-    def rows_of(s, x, core):
-        if not core:
-            return landed[s * n_chip + x][0]
-        for at, steps in enumerate(groups):
-            if s in steps:
-                return swaps[at][steps.index(s) * n_chip + x]
-
-    for m in range(2 * n_chip):
-
-        @pl.when(pl.program_id(0) == m)
-        def _(m=m):
-            parts = [rows_of(s, m // 2, m % 2).astype(jnp.float32) for s in range(n_out)]
-            rows = jnp.concatenate(parts, axis=0).astype(jnp.bfloat16)
+    n_in = n_out * n_chip
+    landed, traded, out = refs[:n_in], refs[n_in : n_in + len(groups)], refs[n_in + len(groups)]
+    own, other, sums, sems, out_sems = refs[n_in + len(groups) + 1 :]
+    tok_rows, part_out = sums.shape[1:]
+    own_copies = [pltpu.make_async_copy(landed[i].at[0], own.at[i], sems.at[i]) for i in range(n_in)]
+    other_copies, first = [], 0
+    for i, ref in enumerate(traded):
+        count = ref.shape[0]
+        other_copies.append(pltpu.make_async_copy(ref, other.at[pl.ds(first, count)], sems.at[n_in + i]))
+        first += count
+    for copy in own_copies + other_copies:
+        copy.start()
+    order = [s for steps in groups for s in steps]
+    finals = []
+    for core in range(2):
+        for copy in (own_copies, other_copies)[core]:
+            copy.wait()
+        for x in range(n_chip):
+            if core:
+                parts = [other[order.index(s) * n_chip + x] for s in range(n_out)]
+            else:
+                parts = [own[s * n_chip + x] for s in range(n_out)]
+            rows = jnp.concatenate([p.astype(jnp.float32) for p in parts], axis=0).astype(jnp.bfloat16)
             both = jnp.dot(weights[...], rows, preferred_element_type=jnp.float32)
-            out[...] = both[:tok_rows] * (1.0 / 256.0) + both[tok_rows:] * (1.0 / 65536.0)
+            m = 2 * x + core
+            sums[m] = both[:tok_rows] * (1.0 / 256.0) + both[tok_rows:] * (1.0 / 65536.0)
+            columns = pl.ds(pl.multiple_of(cols[m] * part_out, 128), part_out)
+            finals.append(pltpu.make_async_copy(sums.at[m], out.at[:, columns], out_sems.at[m]))
+            finals[-1].start()
+    for copy in finals:
+        copy.wait()
 
 
 def combine_call(weights, landed, swaps, cols, n_out, n_chip, capacity, tok_rows):
@@ -76,18 +108,20 @@
     traded = [v for _, v in swaps]
     part_out = traded[0].shape[-1]
     n_loc = 2 * n_chip
-    spec_l = pl.BlockSpec((1, capacity, part_out), lambda m, cols: (0, 0, 0))
+    away = pl.BlockSpec(memory_space=pl.ANY)
     return pl.pallas_call(
         functools.partial(combine_kernel, n_out, n_chip, groups),
-        grid_spec=pltpu.PrefetchScalarGridSpec(
-            num_scalar_prefetch=1,
-            grid=(n_loc,),
-            in_specs=[pl.BlockSpec(weights.shape, lambda m, cols: (0, 0))]
-            + [spec_l] * len(arrived)
-            + [pl.BlockSpec(v.shape, lambda m, cols: (0, 0, 0)) for v in traded],
-            out_specs=pl.BlockSpec((tok_rows, part_out), lambda m, cols: (0, cols[m])),
-        ),
+        in_specs=[pl.BlockSpec(memory_space=pltpu.SMEM), pl.BlockSpec(memory_space=pltpu.VMEM)]
+        + [away] * (len(arrived) + len(traded)),
+        out_specs=away,
         out_shape=jax.ShapeDtypeStruct((tok_rows, n_loc * part_out), jnp.float32),
+        scratch_shapes=[
+            pltpu.VMEM((n_out * n_chip, capacity, part_out), jnp.bfloat16),
+            pltpu.VMEM((n_out * n_chip, capacity, part_out), jnp.bfloat16),
+            pltpu.VMEM((n_loc, tok_rows, part_out), jnp.float32),
+            pltpu.SemaphoreType.DMA((len(arrived) + len(traded),)),
+            pltpu.SemaphoreType.DMA((n_loc,)),
+        ],
         compiler_params=pltpu.CompilerParams(vmem_limit_bytes=16 * 1024 * 1024),
         name="weigh_rows",
     )(cols, weights, *arrived, *traded)
@@ -128,9 +162,9 @@
     pods = (z ^ jnp.arange(n_out, dtype=jnp.int32)) * EXP_POD
     in_kernels = n_out == 4 and capacity % 8 == 0 and part_out % 128 == 0
     if in_kernels:
-        *panels, high, low = sort_call(tokens, routes, combine_fixed, pods, n_out, capacity)
-        high = high.reshape(-1, tok_rows).T
-        low = low.reshape(-1, tok_rows).T
+        *panels, high, low = pick_call(tokens, routes, combine_fixed, pods, n_out, capacity)
+        high = high.reshape(-1, tok_rows).T.astype(jnp.bfloat16)
+        low = low.reshape(-1, tok_rows).T.astype(jnp.bfloat16)
     else:
         hit_mask = routes[:, :, None] == pods[None, None, :]
         fixed = jnp.sum(jnp.where(hit_mask, combine_fixed[:, :, None], 0), axis=1)
@@ -202,10 +236,18 @@
                     chip_of[s, x] = got if len(arg) == 1 else got[at]
         elif kind == "c":
             steps = CFG["C"][arg]
-            same = jnp.concatenate([chip_of[s, x] for x in range(n_chip) for s in steps], axis=0)
-            other = gated(f"cd{arg}", local_xor(gated(f"cs{arg}", same), 1))
-            halves = [first_half(rows).reshape(n_chip, -1, part_hid) for rows in (same, other)]
-            hid.append((arg, jnp.stack(halves, axis=1)))
+            if CFG["apart"]:
+                sides = []
+                for x in range(n_chip):
+                    same = jnp.concatenate([chip_of[s, x] for s in steps], axis=0)
+                    other = gated(f"cd{arg}{x}", local_xor(gated(f"cs{arg}{x}", same), 1))
+                    sides.append(first_half(jnp.concatenate([same, other], axis=0)).reshape(2, -1, part_hid))
+                hid.append((arg, jnp.stack(sides)))
+            else:
+                same = jnp.concatenate([chip_of[s, x] for x in range(n_chip) for s in steps], axis=0)
+                other = gated(f"cd{arg}", local_xor(gated(f"cs{arg}", same), 1))
+                halves = [first_half(rows).reshape(n_chip, -1, part_hid) for rows in (same, other)]
+                hid.append((arg, jnp.stack(halves, axis=1)))
         elif kind == "h":
             cs = CFG["H"][arg]
             steps = [s for c in cs for s in CFG["C"][c]]

time: 65.9 us -> 68.6 us (1.041)
  waiting for transfers between devices: 24.4 us -> 29.9 us
  local copies, waits for them, and re-layouts: 7.48 us -> 3.59 us
  Pallas kernels: 3.63 us -> 5.51 us
  starting transfers between devices: 24.4 us -> 23.2 us
    ppermute x6, starting transfers between devices: 13.9 us -> 7.14 us  [outer_xor(): lax.ppermute(p, 'outer', [(i, i ^ t) for i in range(n_out)])]
    ppermute x2, starting transfers between devices: 0.92 us -> 6.38 us  [move(): return lax.ppermute(p, ('outer', 'local'), pairs)]
    unnamed x23 -> x21, local copies, waits for them, and re-layouts: 5.47 us -> 1.59 us
    ppermute x6, waiting for transfers between devices: 14.5 us -> 17.2 us  [outer_xor(): lax.ppermute(p, 'outer', [(i, i ^ t) for i in range(n_out)])]
    ppermute x12, waiting for transfers between devices: 9.97 us -> 12.7 us  [local_xor(): return lax.ppermute(v, 'local', [(i, i ^ m) for i in range(n_loc)])]
    pallas_call x1, Pallas kernels: 1 us -> 3.05 us  [pick_call(): pl.pallas_call(functools.partial(pick_kernel, n_out, capacity), in_specs=...]
  transfers between devices with their start and end apart: 20 -> 20, of which waited for: 9 -> 9; matrix products, arithmetic and copies ran while one was open for 14% -> 11% of each run, Pallas kernels for 0% -> 0%
where the time goes in v6:
time: 68.6 us; the launch traced here: 68.4 us
  waiting for transfers between devices  29.9 us (44%)
  starting transfers between devices  23.2 us (34%)
  Pallas kernels  5.51 us (8%)
  matrix products  4.99 us (7%)
  local copies, waits for them, and re-layouts  3.59 us (5%)
  other arithmetic  0.76 us (1%)
    ppermute x6, waiting for transfers between devices, outer_xor(): lax.ppermute(p, 'outer', [(i, i ^ t) for i in range(n_out)])  17.2 us
    ppermute x12, waiting for transfers between devices, local_xor(): return lax.ppermute(v, 'local', [(i, i ^ m) for i in range(n_loc)])  12.7 us
    ppermute x12, starting transfers between devices, local_xor(): return lax.ppermute(v, 'local', [(i, i ^ m) for i in range(n_loc)])  9.67 us
    ppermute x6, starting transfers between devices, outer_xor(): lax.ppermute(p, 'outer', [(i, i ^ t) for i in range(n_out)])  7.14 us
    ppermute x2, starting transfers between devices, move(): return lax.ppermute(p, ('outer', 'local'), pairs)  6.38 us
    pallas_call x1, Pallas kernels, pick_call(): pl.pallas_call(functools.partial(pick_kernel, n_out, capacity), in_specs=...  3.05 us
    pallas_call x1, Pallas kernels, combine_call(): pl.pallas_call(functools.partial(combine_kernel, n_out, n_chip, groups),...  2.46 us
    dot_general x4, matrix products, first_half(): up_proj = jnp.dot(rows, up_local, preferred_element_type=jnp.float32)  1.73 us
  transfers between devices with their start and end apart: 20, of which 9 were waited for; matrix products, arithmetic and copies ran while one was open for 11% of the time, Pallas kernels for 0%

profile of v6, /device:TPU:0, one launch (start us, length us, event | category | flops | bytes accessed | tf_op | source)
XLA Modules:
  0.0 68.4 jit_solution(2015556223396731637)
XLA Ops:
  0.0 0.5 xor_multiply_fusion.pods
  0.5 3.1 %pick_rows.1 = (bf16[24,3584]{1,0:T(8,128)(2,1)}, bf16[24,3584]{1,0:T(8,128)(2,1)}, bf16[24,3584]{1,0:T(8,128)(2,1)}, bf16[24,3584]{1,0:T(8,128)(2,1)}, f32[4,24,64]{2,1,0:T(8,128)}, /*index=5*/f32[4,24,64]{2,1,0:T(8,128)}) custom-call(s32[4]{0:T(128)} %xor_multiply_fusion.pods, bf16[64,3584]{1,0:T(8,128)(2,1)} %tokens_hbm.1, s32[8,64]{1,0:T(8,128)} %bitcast.149, ...), custom_call_target="tpu_custom_call" | custom-call | tf_op jit(solution)/shard_map/pick_rows/pallas_call | solution.py:55
  3.6 5.1 %collective-permute-start = (bf16[24,3584]{1,0:T(8,128)(2,1)}, bf16[24,3584]{1,0:T(8,128)(2,1)S(1)}, u32[]{:S(2)}, u32[]{:S(2)}) collective-permute-start(bf16[24,3584]{1,0:T(8,128)(2,1)} %get-tuple-element.19), channel_id=1, source_target_pairs={{0,12},{4,8},{8,4},{12,0},{1,13},{5,9},{9,5},{13,1},{2,14},{6,10},... | collective-permute-start | bytes 516104 | tf_op jit(solution)/shard_map/ppermute | solution.py:192
  8.7 0.6 collective-permute-start.7
  9.4 1.6 %collective-permute-start.1 = (bf16[24,3584]{1,0:T(8,128)(2,1)}, bf16[24,3584]{1,0:T(8,128)(2,1)S(1)}, u32[]{:S(2)}, u32[]{:S(2)}) collective-permute-start(bf16[24,3584]{1,0:T(8,128)(2,1)} %get-tuple-element.18), channel_id=1, source_target_pairs={{0,2},{1,3},{2,0},{3,1},{4,6},{5,7},{6,4},{7,5},{8,10},{9,11},{10,... | collective-permute-start | bytes 516104 | tf_op jit(solution)/shard_map/ppermute | solution.py:195
  11.0 1.0 %constant_dynamic-update-slice_fusion.3 = bf16[96,3584]{1,0:T(8,128)(2,1)S(1)} fusion(bf16[24,3584]{1,0:T(8,128)(2,1)} %get-tuple-element.18), kind=kLoop, calls=%fused_computation.66 | loop fusion | bytes 344064
  12.0 1.6 %dynamic-slice_bitcast_fusion.3 = (bf16[256,896]{1,0:T(8,128)(2,1)S(1)}, bf16[256,896]{1,0:T(8,128)(2,1)S(1)}, bf16[256,896]{1,0:T(8,128)(2,1)S(1)}, bf16[256,896]{1,0:T(8,128)(2,1)S(1)}) fusion(bf16[1,1024,896]{2,1,0:T(8,128)(2,1)} %param.11, s32[]{:T(128)S(6)} %select_n.12, s32[]{:T(128)S(6)} %select_n.13, s32[]{:T(128)S(6)} %select_n.15, s32[]{:T(128)S(6)} %select_n.14), kind=kLoop, calls=%fused_computation.29 | loop fusion | bytes 3670032 | tf_op jit(solution)/shard_map/dynamic_slice | solution.py:155
  13.6 4.5 %collective-permute-done.6 = bf16[24,3584]{1,0:T(8,128)(2,1)S(1)} collective-permute-done((bf16[24,3584]{1,0:T(8,128)(2,1)}, bf16[24,3584]{1,0:T(8,128)(2,1)S(1)}, u32[]{:S(2)}, u32[]{:S(2)}) %collective-permute-start.6) | collective-permute-done | bytes 172064 | tf_op jit(solution)/shard_map/ppermute | solution.py:192
  18.1 1.4 %collective-permute-start.8 = (bf16[24,3584]{1,0:T(8,128)(2,1)S(1)}, bf16[24,3584]{1,0:T(8,128)(2,1)S(1)}, u32[]{:S(2)}, u32[]{:S(2)}) collective-permute-start(bf16[24,3584]{1,0:T(8,128)(2,1)S(1)} %collective-permute-done.6), channel_id=1, source_target_pairs={{0,2},{1,3},{2,0},{3,1},{4,6},{5,7},{6,4},{7,5},{8,10},{9,11},{10,... | collective-permute-start | bytes 516104 | tf_op jit(solution)/shard_map/ppermute | solution.py:195
  19.5 0.7 collective-permute-start.2
  20.2 3.3 %collective-permute-done.7 = bf16[24,3584]{1,0:T(8,128)(2,1)S(1)} collective-permute-done((bf16[24,3584]{1,0:T(8,128)(2,1)}, bf16[24,3584]{1,0:T(8,128)(2,1)S(1)}, u32[]{:S(2)}, u32[]{:S(2)}) %collective-permute-start.7) | collective-permute-done | bytes 172064 | tf_op jit(solution)/shard_map/ppermute | solution.py:192
  23.5 1.5 %collective-permute-start.9 = (bf16[24,3584]{1,0:T(8,128)(2,1)S(1)}, bf16[24,3584]{1,0:T(8,128)(2,1)S(1)}, u32[]{:S(2)}, u32[]{:S(2)}) collective-permute-start(bf16[24,3584]{1,0:T(8,128)(2,1)S(1)} %collective-permute-done.7), channel_id=1, source_target_pairs={{0,2},{1,3},{2,0},{3,1},{4,6},{5,7},{6,4},{7,5},{8,10},{9,11},{10,... | collective-permute-start | bytes 516104 | tf_op jit(solution)/shard_map/ppermute | solution.py:195
  25.3 6.4 %collective-permute-done.9 = bf16[24,3584]{1,0:T(8,128)(2,1)S(1)} collective-permute-done((bf16[24,3584]{1,0:T(8,128)(2,1)S(1)}, bf16[24,3584]{1,0:T(8,128)(2,1)S(1)}, u32[]{:S(2)}, u32[]{:S(2)}) %collective-permute-start.9) | collective-permute-done | bytes 172064 | tf_op jit(solution)/shard_map/ppermute | solution.py:195
  32.3 0.4 fusion.14
  32.7 0.6 collective-permute-start.3
  33.3 0.5 copy-done.1
  33.8 0.4 multiply_convert_fusion.1
  34.2 0.4 multiply_convert_fusion.3
  35.1 0.4 multiply_convert_fusion
  35.5 1.5 %collective-permute-start.11 = (bf16[2,2,48,256]{3,2,1,0:T(8,128)(2,1)S(1)}, bf16[2,2,48,256]{3,2,1,0:T(8,128)(2,1)S(1)}, u32[]{:S(2)}, u32[]{:S(2)}) collective-permute-start(bf16[2,2,48,256]{3,2,1,0:T(8,128)(2,1)S(1)} %pad_maximum_fusion.11), channel_id=1, source_target_pairs={{0,2},{1,3},{2,0},{3,1},{4,6},{5,7},{6,4},{7,5},{8,10},{9,11},{10,... | collective-permute-start | bytes 294920 | tf_op jit(solution)/shard_map/ppermute | solution.py:195
  37.4 0.4 multiply_convert_fusion.2
  37.9 0.7 %collective-permute-start.4 = (bf16[2,2,48,256]{3,2,1,0:T(8,128)(2,1)S(1)}, bf16[2,2,48,256]{3,2,1,0:T(8,128)(2,1)S(1)}, u32[]{:S(2)}, u32[]{:S(2)}) collective-permute-start(bf16[2,2,48,256]{3,2,1,0:T(8,128)(2,1)S(1)} %pad_maximum_fusion.10), channel_id=1, source_target_pairs={{0,2},{1,3},{2,0},{3,1},{4,6},{5,7},{6,4},{7,5},{8,10},{9,11},{10,... | collective-permute-start | bytes 294920 | tf_op jit(solution)/shard_map/ppermute | solution.py:195
  38.6 2.2 %collective-permute-done.11 = bf16[2,2,48,256]{3,2,1,0:T(8,128)(2,1)S(1)} collective-permute-done((bf16[2,2,48,256]{3,2,1,0:T(8,128)(2,1)S(1)}, bf16[2,2,48,256]{3,2,1,0:T(8,128)(2,1)S(1)}, u32[]{:S(2)}, u32[]{:S(2)}) %collective-permute-start.11) | collective-permute-done | bytes 98336 | tf_op jit(solution)/shard_map/ppermute | solution.py:195
  40.9 2.0 %collective-permute-done.4 = bf16[2,2,48,256]{3,2,1,0:T(8,128)(2,1)S(1)} collective-permute-done((bf16[2,2,48,256]{3,2,1,0:T(8,128)(2,1)S(1)}, bf16[2,2,48,256]{3,2,1,0:T(8,128)(2,1)S(1)}, u32[]{:S(2)}, u32[]{:S(2)}) %collective-permute-start.4) | collective-permute-done | bytes 98336 | tf_op jit(solution)/shard_map/ppermute | solution.py:195
  43.9 0.5 collective-permute-done.5
  45.5 1.5 %collective-permute-start.13 = (bf16[2,2,24,896]{3,2,0,1:T(8,128)(2,1)S(1)}, bf16[2,2,24,896]{3,2,0,1:T(8,128)(2,1)S(1)}, u32[]{:S(2)}, u32[]{:S(2)}) collective-permute-start(bf16[2,2,24,896]{3,2,0,1:T(8,128)(2,1)S(1)} %pad_maximum_fusion.8), channel_id=1, source_target_pairs={{0,2},{1,3},{2,0},{3,1},{4,6},{5,7},{6,4},{7,5},{8,10},{9,11},{10,... | collective-permute-start | bytes 516104 | tf_op jit(solution)/shard_map/ppermute | solution.py:195
  47.0 1.2 %collective-permute-start.15 = (bf16[2,24,896]{2,1,0:T(8,128)(2,1)S(1)}, bf16[2,24,896]{2,1,0:T(8,128)(2,1)S(1)}, u32[]{:S(2)}, u32[]{:S(2)}) collective-permute-start(bf16[2,24,896]{2,1,0:T(8,128)(2,1)S(1)} %get-tuple-element.24), channel_id=1, source_target_pairs={{0,8},{4,12},{8,0},{12,4},{1,9},{5,13},{9,1},{13,5},{2,10},{6,14},... | collective-permute-start | bytes 258056 | tf_op jit(solution)/shard_map/ppermute | solution.py:192
  48.2 1.7 %collective-permute-start.16 = (bf16[2,24,896]{2,1,0:T(8,128)(2,1)S(1)}, bf16[2,24,896]{2,1,0:T(8,128)(2,1)S(1)}, u32[]{:S(2)}, u32[]{:S(2)}) collective-permute-start(bf16[2,24,896]{2,1,0:T(8,128)(2,1)S(1)} %get-tuple-element.39), channel_id=1, source_target_pairs={{0,10},{1,11},{2,8},{3,9},{4,14},{5,15},{6,12},{7,13},{8,2},{9,3},... | collective-permute-start | bytes 258056 | tf_op jit(solution)/shard_map/ppermute | solution.py:203
  50.0 4.6 %collective-permute-start.18 = (bf16[2,24,896]{2,1,0:T(8,128)(2,1)S(1)}, bf16[2,24,896]{2,1,0:T(8,128)(2,1)S(1)}, u32[]{:S(2)}, u32[]{:S(2)}) collective-permute-start(bf16[2,24,896]{2,1,0:T(8,128)(2,1)S(1)} %get-tuple-element.26), channel_id=1, source_target_pairs={{0,14},{1,15},{2,12},{3,13},{4,10},{5,11},{6,8},{7,9},{8,6},{9,7},... | collective-permute-start | bytes 258056 | tf_op jit(solution)/shard_map/ppermute | solution.py:203
  54.7 9.4 %collective-permute-done.14 = bf16[2,2,24,896]{3,2,1,0:T(8,128)(2,1)S(1)} collective-permute-done((bf16[2,2,24,896]{3,2,1,0:T(8,128)(2,1)S(1)}, bf16[2,2,24,896]{3,2,1,0:T(8,128)(2,1)S(1)}, u32[]{:S(2)}, u32[]{:S(2)}) %collective-permute-start.14) | collective-permute-done | bytes 172064 | tf_op jit(solution)/shard_map/ppermute | solution.py:192
  64.6 1.3 %collective-permute-done.19.refs_8_ = bf16[8,24,896]{2,1,0:T(8,128)(2,1)S(1)} collective-permute-done((bf16[8,24,896]{2,1,0:T(8,128)(2,1)S(1)}, bf16[8,24,896]{2,1,0:T(8,128)(2,1)S(1)}, u32[]{:S(2)}, u32[]{:S(2)}) %collective-permute-start.19) | collective-permute-done | bytes 344096 | tf_op jit(solution)/shard_map/ppermute | solution.py:195
  66.0 2.5 %weigh_rows.1 = f32[64,3584]{1,0:T(8,128)} custom-call(s32[4]{0:T(128)S(1)} %iota_xor_fusion.cols, bf16[128,96]{1,0:T(8,128)(2,1)S(1)} %pad_maximum_fusion.12.weights, bf16[2,24,896]{2,1,0:T(8,128)(2,1)S(1)} %get-tuple-element.38.refs_0_, bf16[2,24,896]{2,1,0:T(8,128)(2,1)S(1)} %get-tuple-element.46.refs_1_, ...), custom_call_target="tpu_custom_call" | custom-call | tf_op jit(solution)/shard_map/weigh_rows/pallas_call | solution.py:112
  (70 shorter events, 4.3 us)
Async XLA Ops:
  0.0 31.8 %copy-start = (bf16[1,3584,256]{2,1,0:T(8,128)(2,1)S(1)}, bf16[1,3584,256]{2,1,0:T(8,128)(2,1)}, u32[]{:S(2)}) copy-start(bf16[1,3584,256]{2,1,0:T(8,128)(2,1)} %param.9) | copy-start | bytes 5505028
  3.6 15.9 %collective-permute-start = (bf16[24,3584]{1,0:T(8,128)(2,1)}, bf16[24,3584]{1,0:T(8,128)(2,1)S(1)}, u32[]{:S(2)}, u32[]{:S(2)}) collective-permute-start(bf16[24,3584]{1,0:T(8,128)(2,1)} %get-tuple-element.19), channel_id=1, source_target_pairs={{0,12},{4,8},{8,4},{12,0},{1,13},{5,9},{9,5},{13,1},{2,14},{6,10},... | collective-permute-start | bytes 516104 | tf_op jit(solution)/shard_map/ppermute | solution.py:192
  8.7 9.4 %collective-permute-start.6 = (bf16[24,3584]{1,0:T(8,128)(2,1)}, bf16[24,3584]{1,0:T(8,128)(2,1)S(1)}, u32[]{:S(2)}, u32[]{:S(2)}) collective-permute-start(bf16[24,3584]{1,0:T(8,128)(2,1)} %get-tuple-element.20), channel_id=1, source_target_pairs={{0,4},{4,0},{8,12},{12,8},{1,5},{5,1},{9,13},{13,9},{2,6},{6,2},{1... | collective-permute-start | bytes 516104 | tf_op jit(solution)/shard_map/ppermute | solution.py:192
  8.7 14.8 %collective-permute-start.7 = (bf16[24,3584]{1,0:T(8,128)(2,1)}, bf16[24,3584]{1,0:T(8,128)(2,1)S(1)}, u32[]{:S(2)}, u32[]{:S(2)}) collective-permute-start(bf16[24,3584]{1,0:T(8,128)(2,1)} %get-tuple-element.21), channel_id=1, source_target_pairs={{0,8},{4,12},{8,0},{12,4},{1,9},{5,13},{9,1},{13,5},{2,10},{6,14},... | collective-permute-start | bytes 516104 | tf_op jit(solution)/shard_map/ppermute | solution.py:192
  9.4 15.7 %collective-permute-start.1 = (bf16[24,3584]{1,0:T(8,128)(2,1)}, bf16[24,3584]{1,0:T(8,128)(2,1)S(1)}, u32[]{:S(2)}, u32[]{:S(2)}) collective-permute-start(bf16[24,3584]{1,0:T(8,128)(2,1)} %get-tuple-element.18), channel_id=1, source_target_pairs={{0,2},{1,3},{2,0},{3,1},{4,6},{5,7},{6,4},{7,5},{8,10},{9,11},{10,... | collective-permute-start | bytes 516104 | tf_op jit(solution)/shard_map/ppermute | solution.py:195
  18.1 7.2 %collective-permute-start.8 = (bf16[24,3584]{1,0:T(8,128)(2,1)S(1)}, bf16[24,3584]{1,0:T(8,128)(2,1)S(1)}, u32[]{:S(2)}, u32[]{:S(2)}) collective-permute-start(bf16[24,3584]{1,0:T(8,128)(2,1)S(1)} %collective-permute-done.6), channel_id=1, source_target_pairs={{0,2},{1,3},{2,0},{3,1},{4,6},{5,7},{6,4},{7,5},{8,10},{9,11},{10,... | collective-permute-start | bytes 516104 | tf_op jit(solution)/shard_map/ppermute | solution.py:195
  19.5 12.8 %collective-permute-start.2 = (bf16[24,3584]{1,0:T(8,128)(2,1)S(1)}, bf16[24,3584]{1,0:T(8,128)(2,1)S(1)}, u32[]{:S(2)}, u32[]{:S(2)}) collective-permute-start(bf16[24,3584]{1,0:T(8,128)(2,1)S(1)} %collective-permute-done), channel_id=1, source_target_pairs={{0,2},{1,3},{2,0},{3,1},{4,6},{5,7},{6,4},{7,5},{8,10},{9,11},{10,... | collective-permute-start | bytes 516104 | tf_op jit(solution)/shard_map/ppermute | solution.py:195
  23.5 8.2 %collective-permute-start.9 = (bf16[24,3584]{1,0:T(8,128)(2,1)S(1)}, bf16[24,3584]{1,0:T(8,128)(2,1)S(1)}, u32[]{:S(2)}, u32[]{:S(2)}) collective-permute-start(bf16[24,3584]{1,0:T(8,128)(2,1)S(1)} %collective-permute-done.7), channel_id=1, source_target_pairs={{0,2},{1,3},{2,0},{3,1},{4,6},{5,7},{6,4},{7,5},{8,10},{9,11},{10,... | collective-permute-start | bytes 516104 | tf_op jit(solution)/shard_map/ppermute | solution.py:195
  31.7 2.9 %collective-permute-start.10 = (bf16[96,3584]{1,0:T(8,128)(2,1)S(1)}, bf16[96,3584]{1,0:T(8,128)(2,1)S(1)}, u32[]{:S(2)}, u32[]{:S(2)}) collective-permute-start(bf16[96,3584]{1,0:T(8,128)(2,1)S(1)} %constant_dynamic-update-slice_fusion.4), channel_id=1, source_target_pairs={{0,1},{1,0},{2,3},{3,2},{4,5},{5,4},{6,7},{7,6},{8,9},{9,8},{10,11... | collective-permute-start | bytes 2064392 | tf_op jit(solution)/shard_map/ppermute | solution.py:195
  32.3 1.5 %copy-start.1 = (bf16[1,3584,256]{2,1,0:T(8,128)(2,1)S(1)}, bf16[1,3584,256]{2,1,0:T(8,128)(2,1)}, u32[]{:S(2)}) copy-start(bf16[1,3584,256]{2,1,0:T(8,128)(2,1)} %param.10) | copy-start | bytes 5505028
  32.7 4.3 %collective-permute-start.3 = (bf16[96,3584]{1,0:T(8,128)(2,1)S(1)}, bf16[96,3584]{1,0:T(8,128)(2,1)S(1)}, u32[]{:S(2)}, u32[]{:S(2)}) collective-permute-start(bf16[96,3584]{1,0:T(8,128)(2,1)S(1)} %constant_dynamic-update-slice_fusion), channel_id=1, source_target_pairs={{0,1},{1,0},{2,3},{3,2},{4,5},{5,4},{6,7},{7,6},{8,9},{9,8},{10,11... | collective-permute-start | bytes 2064392 | tf_op jit(solution)/shard_map/ppermute | solution.py:195
  35.5 5.3 %collective-permute-start.11 = (bf16[2,2,48,256]{3,2,1,0:T(8,128)(2,1)S(1)}, bf16[2,2,48,256]{3,2,1,0:T(8,128)(2,1)S(1)}, u32[]{:S(2)}, u32[]{:S(2)}) collective-permute-start(bf16[2,2,48,256]{3,2,1,0:T(8,128)(2,1)S(1)} %pad_maximum_fusion.11), channel_id=1, source_target_pairs={{0,2},{1,3},{2,0},{3,1},{4,6},{5,7},{6,4},{7,5},{8,10},{9,11},{10,... | collective-permute-start | bytes 294920 | tf_op jit(solution)/shard_map/ppermute | solution.py:195
  37.9 5.0 %collective-permute-start.4 = (bf16[2,2,48,256]{3,2,1,0:T(8,128)(2,1)S(1)}, bf16[2,2,48,256]{3,2,1,0:T(8,128)(2,1)S(1)}, u32[]{:S(2)}, u32[]{:S(2)}) collective-permute-start(bf16[2,2,48,256]{3,2,1,0:T(8,128)(2,1)S(1)} %pad_maximum_fusion.10), channel_id=1, source_target_pairs={{0,2},{1,3},{2,0},{3,1},{4,6},{5,7},{6,4},{7,5},{8,10},{9,11},{10,... | collective-permute-start | bytes 294920 | tf_op jit(solution)/shard_map/ppermute | solution.py:195
  40.8 2.2 %collective-permute-start.12 = (bf16[192,512]{1,0:T(8,128)(2,1)S(1)}, bf16[192,512]{1,0:T(8,128)(2,1)S(1)}, u32[]{:S(2)}, u32[]{:S(2)}) collective-permute-start(bf16[192,512]{1,0:T(8,128)(2,1)S(1)} %bitcast.143), channel_id=1, source_target_pairs={{0,1},{1,0},{2,3},{3,2},{4,5},{5,4},{6,7},{7,6},{8,9},{9,8},{10,11... | collective-permute-start | bytes 589832 | tf_op jit(solution)/shard_map/ppermute | solution.py:195
  42.9 1.5 %collective-permute-start.5 = (bf16[192,512]{1,0:T(8,128)(2,1)S(1)}, bf16[192,512]{1,0:T(8,128)(2,1)S(1)}, u32[]{:S(2)}, u32[]{:S(2)}) collective-permute-start(bf16[192,512]{1,0:T(8,128)(2,1)S(1)} %bitcast.141), channel_id=1, source_target_pairs={{0,1},{1,0},{2,3},{3,2},{4,5},{5,4},{6,7},{7,6},{8,9},{9,8},{10,11... | collective-permute-start | bytes 589832 | tf_op jit(solution)/shard_map/ppermute | solution.py:195
  44.9 19.4 %copy-start.3 = (f32[4,24,64]{2,1,0:T(8,128)S(1)}, f32[4,24,64]{2,1,0:T(8,128)}, u32[]{:S(2)}) copy-start(f32[4,24,64]{2,1,0:T(8,128)} %get-tuple-element.16) | copy-start | bytes 73732
  45.0 19.5 %copy-start.2 = (f32[4,24,64]{2,1,0:T(8,128)S(1)}, f32[4,24,64]{2,1,0:T(8,128)}, u32[]{:S(2)}) copy-start(f32[4,24,64]{2,1,0:T(8,128)} %get-tuple-element.17) | copy-start | bytes 73732
  45.4 9.2 %collective-permute-start.17 = (bf16[2,24,896]{2,1,0:T(8,128)(2,1)S(1)}, bf16[2,24,896]{2,1,0:T(8,128)(2,1)S(1)}, u32[]{:S(2)}, u32[]{:S(2)}) collective-permute-start(bf16[2,24,896]{2,1,0:T(8,128)(2,1)S(1)} %get-tuple-element.36), channel_id=1, source_target_pairs={{0,12},{4,8},{8,4},{12,0},{1,13},{5,9},{9,5},{13,1},{2,14},{6,10},... | collective-permute-start | bytes 258056 | tf_op jit(solution)/shard_map/ppermute | solution.py:192
  45.5 9.1 %collective-permute-start.13 = (bf16[2,2,24,896]{3,2,0,1:T(8,128)(2,1)S(1)}, bf16[2,2,24,896]{3,2,0,1:T(8,128)(2,1)S(1)}, u32[]{:S(2)}, u32[]{:S(2)}) collective-permute-start(bf16[2,2,24,896]{3,2,0,1:T(8,128)(2,1)S(1)} %pad_maximum_fusion.8), channel_id=1, source_target_pairs={{0,2},{1,3},{2,0},{3,1},{4,6},{5,7},{6,4},{7,5},{8,10},{9,11},{10,... | collective-permute-start | bytes 516104 | tf_op jit(solution)/shard_map/ppermute | solution.py:195
  47.0 17.2 %collective-permute-start.15 = (bf16[2,24,896]{2,1,0:T(8,128)(2,1)S(1)}, bf16[2,24,896]{2,1,0:T(8,128)(2,1)S(1)}, u32[]{:S(2)}, u32[]{:S(2)}) collective-permute-start(bf16[2,24,896]{2,1,0:T(8,128)(2,1)S(1)} %get-tuple-element.24), channel_id=1, source_target_pairs={{0,8},{4,12},{8,0},{12,4},{1,9},{5,13},{9,1},{13,5},{2,10},{6,14},... | collective-permute-start | bytes 258056 | tf_op jit(solution)/shard_map/ppermute | solution.py:192
  48.2 16.0 %collective-permute-start.16 = (bf16[2,24,896]{2,1,0:T(8,128)(2,1)S(1)}, bf16[2,24,896]{2,1,0:T(8,128)(2,1)S(1)}, u32[]{:S(2)}, u32[]{:S(2)}) collective-permute-start(bf16[2,24,896]{2,1,0:T(8,128)(2,1)S(1)} %get-tuple-element.39), channel_id=1, source_target_pairs={{0,10},{1,11},{2,8},{3,9},{4,14},{5,15},{6,12},{7,13},{8,2},{9,3},... | collective-permute-start | bytes 258056 | tf_op jit(solution)/shard_map/ppermute | solution.py:203
  50.0 14.3 %collective-permute-start.18 = (bf16[2,24,896]{2,1,0:T(8,128)(2,1)S(1)}, bf16[2,24,896]{2,1,0:T(8,128)(2,1)S(1)}, u32[]{:S(2)}, u32[]{:S(2)}) collective-permute-start(bf16[2,24,896]{2,1,0:T(8,128)(2,1)S(1)} %get-tuple-element.26), channel_id=1, source_target_pairs={{0,14},{1,15},{2,12},{3,13},{4,10},{5,11},{6,8},{7,9},{8,6},{9,7},... | collective-permute-start | bytes 258056 | tf_op jit(solution)/shard_map/ppermute | solution.py:203
  54.6 9.5 %collective-permute-start.14 = (bf16[2,2,24,896]{3,2,1,0:T(8,128)(2,1)S(1)}, bf16[2,2,24,896]{3,2,1,0:T(8,128)(2,1)S(1)}, u32[]{:S(2)}, u32[]{:S(2)}) collective-permute-start(bf16[2,2,24,896]{3,2,1,0:T(8,128)(2,1)S(1)} %pad_maximum_fusion.9), channel_id=1, source_target_pairs={{0,4},{4,0},{8,12},{12,8},{1,5},{5,1},{9,13},{13,9},{2,6},{6,2},{1... | collective-permute-start | bytes 516104 | tf_op jit(solution)/shard_map/ppermute | solution.py:192
  64.2 1.7 %collective-permute-start.19 = (bf16[8,24,896]{2,1,0:T(8,128)(2,1)S(1)}, bf16[8,24,896]{2,1,0:T(8,128)(2,1)S(1)}, u32[]{:S(2)}, u32[]{:S(2)}) collective-permute-start(bf16[8,24,896]{2,1,0:T(8,128)(2,1)S(1)} %slice_dynamic-update-slice_fusion), channel_id=1, source_target_pairs={{0,1},{1,0},{2,3},{3,2},{4,5},{5,4},{6,7},{7,6},{8,9},{9,8},{10,11... | collective-permute-start | bytes 1032200 | tf_op jit(solution)/shard_map/ppermute | solution.py:195

commit v7 on v6

--- a/solution.py
+++ b/solution.py
@@ -7,7 +7,7 @@
 import functools
 
 EXP_POD = 8
-CFG = {'C': [[0, 3], [1, 2]], 'H': [[0], [1]], 'order': [['z', 3], ['x', [3]], ['z', 2], ['x', [2]], ['z', 0], ['z', 1], ['x', [1]], ['x', [0]], ['c', 1], ['h', 1], ['r', 2], ['c', 0], ['h', 0], ['r', 3], ['t', [0, 1]], ['w', [0, 1, 2, 3]]], 'gates': {'rs31': ['xd01'], 'rs20': ['zd2'], 'cs1': ['zd3', 'xd01'], 'td01': ['xd01'], 'rd30': ['hd11']}, 'apart': False}
+CFG = {'C': [[0, 3], [1, 2]], 'H': [[0], [1]], 'order': [('z', 0), ('z', 3), ('z', 1), ('x', (0,)), ('z', 2), ('x', (3,)), ('c', 0), ('h', 0), ('x', (1,)), ('x', (2,)), ('c', 1), ('h', 1), ('q', (3, 0)), ('q', (2, 1)), ('v', ((3, 0), (2, 1)))], 'gates': {'qd3': ['xd11']}, 'apart': False}
 
 
 def pick_kernel(n_out, capacity, pods, tokens_hbm, routes_hbm, fixed_hbm, *refs):
@@ -160,7 +160,7 @@
 
     down_same, down_other = down_rows(0), down_rows(1)
     pods = (z ^ jnp.arange(n_out, dtype=jnp.int32)) * EXP_POD
-    in_kernels = n_out == 4 and capacity % 8 == 0 and part_out % 128 == 0
+    in_kernels = False and capacity % 8 == 0 and part_out % 128 == 0
     if in_kernels:
         *panels, high, low = pick_call(tokens, routes, combine_fixed, pods, n_out, capacity)
         high = high.reshape(-1, tok_rows).T.astype(jnp.bfloat16)
@@ -217,6 +217,8 @@
     outs = {}
     landed = {}
     pieces = {}
+    back = {}
+    shared = []
     swaps = []
     mine = {}
     todo = list(CFG["order"])
@@ -286,6 +288,35 @@
                     moved = gated(f"rd{s}0", moved)
                     for x in range(n_chip):
                         landed[s, x] = moved[x]
+        elif kind == "q":
+            a, b = arg
+            core = l & 1
+            kept = jnp.where(core == 0, outs[a], outs[b])
+            given = gated(f"qs{a}", jnp.where(core == 0, outs[b], outs[a])[:, ::-1])
+            taken = gated(f"qd{a}", local_xor(given, 1))
+            for x in range(n_chip):
+                block = gated(f"us{a}{x}", jnp.stack([kept[x], taken[x]]))
+
+                def move(p, i, x=x):
+                    pairs = []
+                    for zz in range(n_out):
+                        for ll in range(n_loc):
+                            t = (b if ll & 1 else a) * span + i
+                            pairs.append((zz * n_loc + ll, (zz ^ t) * n_loc + (ll ^ (2 * x))))
+                    return lax.ppermute(p, ("outer", "local"), pairs)
+
+                parts = [move(p, i) for i, p in enumerate(jnp.split(block, span, axis=2) if span > 1 else [block])]
+                back[a, x] = gated(f"ud{a}{x}", parts[0] if span == 1 else jnp.concatenate(parts, axis=2))
+        elif kind == "v":
+            stack = jnp.stack([back[a, x][:, 1] for a, b in arg for x in range(n_chip)])
+            swapped = gated(f"wd{arg[0][0]}", local_xor(gated(f"ws{arg[0][0]}", stack), 1))
+            for at, (a, b) in enumerate(arg):
+                for x in range(n_chip):
+                    pieces[a, 2 * x] = back[a, x][0, 0]
+                    pieces[a, 2 * x + 1] = back[a, x][1, 0]
+                    pieces[b, 2 * x] = swapped[at * n_chip + x, 1]
+                    pieces[b, 2 * x + 1] = swapped[at * n_chip + x, 0]
+                shared.append((a, b))
         elif kind == "w":
             steps = arg
             stack = gated(f"ws{steps[0]}", jnp.stack([landed[s, x][1] for s in steps for x in range(n_chip)]))
@@ -300,6 +331,13 @@
         cols = l ^ jnp.arange(n_loc, dtype=jnp.int32)
         weights = jnp.concatenate([high, low], axis=0)
         return combine_call(weights, landed, swaps, cols, n_out, n_chip, capacity, tok_rows)
+    def in_turn(w):
+        cuts = jnp.split(w, 4, axis=1)
+        for a, b in shared:
+            cuts[a], cuts[b] = (jnp.where((l & 1) == 0, cuts[i], cuts[j]) for i, j in ((a, b), (b, a)))
+        return jnp.concatenate(cuts, axis=1)
+
+    high, low = in_turn(high), in_turn(low)
     combined = jnp.zeros((tok_rows, width), jnp.float32)
     for m in range(n_loc):
         returned = jnp.concatenate([pieces[s, m] for s in range(4)], axis=0)

time: 68.6 us -> 67.2 us (0.980)
  Pallas kernels: 5.51 us -> 0 us
  matrix products: 4.99 us -> 8.76 us
  waiting for transfers between devices: 29.9 us -> 27.9 us
  starting transfers between devices: 23.2 us -> 24.2 us
  other arithmetic: 0.76 us -> 1.64 us
    ppermute x6 -> x3, waiting for transfers between devices: 17.2 us -> 7.55 us  [outer_xor(): lax.ppermute(p, 'outer', [(i, i ^ t) for i in range(n_out)])]
    ppermute x2 -> x4, waiting for transfers between devices: 0.01 us -> 8.04 us  [move(): return lax.ppermute(p, ('outer', 'local'), pairs)]
    pallas_call x2 -> x0, Pallas kernels: 5.51 us -> none  [the longest x1 3.05 us: pick_call(): pl.pallas_call(functools.partial(pick_kernel, n_out, capacity), in_specs=...]
    dot_general x0 -> x9, matrix products: none -> 3.78 us  [the longest x4 1.58 us: per_device(): jnp.dot(low, returned, preferred_element_type=jnp.float32) * (1.0 / 65536.0)]
    ppermute x2 -> x4, starting transfers between devices: 6.38 us -> 9.75 us  [move(): return lax.ppermute(p, ('outer', 'local'), pairs)]
    ppermute x6 -> x3, starting transfers between devices: 7.14 us -> 5.69 us  [outer_xor(): lax.ppermute(p, 'outer', [(i, i ^ t) for i in range(n_out)])]
    ppermute x12 -> x13, starting transfers between devices: 9.67 us -> 8.72 us  [local_xor(): return lax.ppermute(v, 'local', [(i, i ^ m) for i in range(n_loc)])]
    reduce_or x0 -> x1, other arithmetic: none -> 0.91 us  [per_device(): is_live = jnp.any(hit_mask, axis=1).astype(jnp.int32)]
  transfers between devices with their start and end apart: 20 -> 20, of which waited for: 9 -> 12; matrix products, arithmetic and copies ran while one was open for 11% -> 9% of each run, Pallas kernels for 0% -> 0%
where the time goes in v7:
time: 67.2 us; the launch traced here: 67 us
  waiting for transfers between devices  27.9 us (42%)
  starting transfers between devices  24.2 us (36%)
  matrix products  8.76 us (13%)
  local copies, waits for them, and re-layouts  3.98 us (6%)
  other arithmetic  1.64 us (2%)
    ppermute x13, waiting for transfers between devices, local_xor(): return lax.ppermute(v, 'local', [(i, i ^ m) for i in range(n_loc)])  12.3 us
    ppermute x4, starting transfers between devices, move(): return lax.ppermute(p, ('outer', 'local'), pairs)  9.75 us
    ppermute x13, starting transfers between devices, local_xor(): return lax.ppermute(v, 'local', [(i, i ^ m) for i in range(n_loc)])  8.72 us
    ppermute x4, waiting for transfers between devices, move(): return lax.ppermute(p, ('outer', 'local'), pairs)  8.04 us
    ppermute x3, waiting for transfers between devices, outer_xor(): lax.ppermute(p, 'outer', [(i, i ^ t) for i in range(n_out)])  7.55 us
    ppermute x3, starting transfers between devices, outer_xor(): lax.ppermute(p, 'outer', [(i, i ^ t) for i in range(n_out)])  5.69 us
    dot_general x4, matrix products, first_half(): up_proj = jnp.dot(rows, up_local, preferred_element_type=jnp.float32)  1.74 us
    dot_general x4, matrix products, first_half(): gate_proj = jnp.dot(rows, gate_local, preferred_element_type=jnp.float32)  1.72 us
  transfers between devices with their start and end apart: 20, of which 12 were waited for; matrix products, arithmetic and copies ran while one was open for 9% of the time, Pallas kernels for 0%

profile of v7, /device:TPU:0, one launch (start us, length us, event | category | flops | bytes accessed | tf_op | source)
XLA Modules:
  0.0 67.0 jit_solution(17932574800075762904)
XLA Ops:
  0.0 0.9 %compare_reduce_fusion = pred[64,4]{0,1:T(4,128)(4,1)S(1)} fusion(s32[64,8]{0,1:T(8,128)} %param.7, s32[4]{0:T(128)S(1)} %xor_multiply_fusion), kind=kLoop, calls=%fused_computation.112 | loop fusion | flops 3840 | bytes 2320 | tf_op jit(solution)/shard_map/reduce_or | solution.py:171
  1.2 1.3 %convolution_convert_fusion = bf16[4,24,3584]{2,1,0:T(8,128)(2,1)S(1)} fusion(bf16[64,3584]{1,0:T(8,128)(2,1)} %param.6, s32[64,4]{0,1:T(4,128)S(1)} %add_select_fusion), kind=kOutput, calls=%fused_computation | convolution fusion | flops 44390400 | bytes 1147904 | tf_op jit(solution)/shard_map/tqc,td->qcd/dot_general | solution.py:174
  2.6 3.1 %collective-permute-start.7 = (bf16[24,3584]{1,0:T(8,128)(2,1)S(1)}, bf16[24,3584]{1,0:T(8,128)(2,1)S(1)}, u32[]{:S(2)}, u32[]{:S(2)}) collective-permute-start(bf16[24,3584]{1,0:T(8,128)(2,1)S(1)} %get-tuple-element.14), channel_id=1, source_target_pairs={{0,4},{4,0},{8,12},{12,8},{1,5},{5,1},{9,13},{13,9},{2,6},{6,2},{1... | collective-permute-start | bytes 516104 | tf_op jit(solution)/shard_map/ppermute | solution.py:192
  5.7 2.6 %collective-permute-start.11 = (bf16[24,3584]{1,0:T(8,128)(2,1)S(1)}, bf16[24,3584]{1,0:T(8,128)(2,1)S(1)}, u32[]{:S(2)}, u32[]{:S(2)}) collective-permute-start(bf16[24,3584]{1,0:T(8,128)(2,1)S(1)} %get-tuple-element.13), channel_id=1, source_target_pairs={{0,8},{4,12},{8,0},{12,4},{1,9},{5,13},{9,1},{13,5},{2,10},{6,14},... | collective-permute-start | bytes 516104 | tf_op jit(solution)/shard_map/ppermute | solution.py:192
  8.3 1.7 %collective-permute-start.1 = (bf16[24,3584]{1,0:T(8,128)(2,1)S(1)}, bf16[24,3584]{1,0:T(8,128)(2,1)S(1)}, u32[]{:S(2)}, u32[]{:S(2)}) collective-permute-start(bf16[24,3584]{1,0:T(8,128)(2,1)S(1)} %get-tuple-element.16), channel_id=1, source_target_pairs={{0,2},{1,3},{2,0},{3,1},{4,6},{5,7},{6,4},{7,5},{8,10},{9,11},{10,... | collective-permute-start | bytes 516104 | tf_op jit(solution)/shard_map/ppermute | solution.py:195
  10.3 1.6 %dynamic-slice_bitcast_fusion.3 = (bf16[256,896]{1,0:T(8,128)(2,1)S(1)}, bf16[256,896]{1,0:T(8,128)(2,1)S(1)}, bf16[256,896]{1,0:T(8,128)(2,1)S(1)}, bf16[256,896]{1,0:T(8,128)(2,1)S(1)}) fusion(bf16[1,1024,896]{2,1,0:T(8,128)(2,1)} %param.11, s32[]{:T(128)S(6)} %select_n.114, s32[]{:T(128)S(6)} %select_n.115, s32[]{:T(128)S(6)} %select_n.117, s32[]{:T(128)S(6)} %select_n.116), kind=kLoop, calls=%fused_computation.48 | loop fusion | bytes 3670032 | tf_op jit(solution)/shard_map/dynamic_slice | solution.py:155
  11.9 0.8 %collective-permute-done.7 = bf16[24,3584]{1,0:T(8,128)(2,1)S(1)} collective-permute-done((bf16[24,3584]{1,0:T(8,128)(2,1)S(1)}, bf16[24,3584]{1,0:T(8,128)(2,1)S(1)}, u32[]{:S(2)}, u32[]{:S(2)}) %collective-permute-start.7) | collective-permute-done | bytes 172064 | tf_op jit(solution)/shard_map/ppermute | solution.py:192
  12.8 1.8 %collective-permute-start.8 = (bf16[24,3584]{1,0:T(8,128)(2,1)S(1)}, bf16[24,3584]{1,0:T(8,128)(2,1)S(1)}, u32[]{:S(2)}, u32[]{:S(2)}) collective-permute-start(bf16[24,3584]{1,0:T(8,128)(2,1)S(1)} %collective-permute-done.7), channel_id=1, source_target_pairs={{0,2},{1,3},{2,0},{3,1},{4,6},{5,7},{6,4},{7,5},{8,10},{9,11},{10,... | collective-permute-start | bytes 516104 | tf_op jit(solution)/shard_map/ppermute | solution.py:195
  14.6 6.7 %collective-permute-done.11 = bf16[24,3584]{1,0:T(8,128)(2,1)S(1)} collective-permute-done((bf16[24,3584]{1,0:T(8,128)(2,1)S(1)}, bf16[24,3584]{1,0:T(8,128)(2,1)S(1)}, u32[]{:S(2)}, u32[]{:S(2)}) %collective-permute-start.11) | collective-permute-done | bytes 172064 | tf_op jit(solution)/shard_map/ppermute | solution.py:192
  21.3 1.5 %collective-permute-start.12 = (bf16[24,3584]{1,0:T(8,128)(2,1)S(1)}, bf16[24,3584]{1,0:T(8,128)(2,1)S(1)}, u32[]{:S(2)}, u32[]{:S(2)}) collective-permute-start(bf16[24,3584]{1,0:T(8,128)(2,1)S(1)} %collective-permute-done.11), channel_id=1, source_target_pairs={{0,2},{1,3},{2,0},{3,1},{4,6},{5,7},{6,4},{7,5},{8,10},{9,11},{10,... | collective-permute-start | bytes 516104 | tf_op jit(solution)/shard_map/ppermute | solution.py:195
  22.8 0.6 collective-permute-start.2
  23.4 3.3 %collective-permute-done.12 = bf16[24,3584]{1,0:T(8,128)(2,1)S(1)} collective-permute-done((bf16[24,3584]{1,0:T(8,128)(2,1)S(1)}, bf16[24,3584]{1,0:T(8,128)(2,1)S(1)}, u32[]{:S(2)}, u32[]{:S(2)}) %collective-permute-start.12) | collective-permute-done | bytes 172064 | tf_op jit(solution)/shard_map/ppermute | solution.py:195
  26.8 1.7 %collective-permute-done.2 = bf16[24,3584]{1,0:T(8,128)(2,1)S(1)} collective-permute-done((bf16[24,3584]{1,0:T(8,128)(2,1)S(1)}, bf16[24,3584]{1,0:T(8,128)(2,1)S(1)}, u32[]{:S(2)}, u32[]{:S(2)}) %collective-permute-start.2) | collective-permute-done | bytes 172064 | tf_op jit(solution)/shard_map/ppermute | solution.py:195
  29.1 1.0 %copy-done.1 = bf16[1,3584,256]{2,1,0:T(8,128)(2,1)S(1)} copy-done((bf16[1,3584,256]{2,1,0:T(8,128)(2,1)S(1)}, bf16[1,3584,256]{2,1,0:T(8,128)(2,1)}, u32[]{:S(2)}) %copy-start.1) | copy-done | bytes 1835032
  31.0 0.4 multiply_convert_fusion.1
  31.8 0.4 multiply_convert_fusion
  32.3 1.6 %collective-permute-start.14 = (bf16[2,2,48,256]{3,2,1,0:T(8,128)(2,1)S(1)}, bf16[2,2,48,256]{3,2,1,0:T(8,128)(2,1)S(1)}, u32[]{:S(2)}, u32[]{:S(2)}) collective-permute-start(bf16[2,2,48,256]{3,2,1,0:T(8,128)(2,1)S(1)} %pad_maximum_fusion.19), channel_id=1, source_target_pairs={{0,2},{1,3},{2,0},{3,1},{4,6},{5,7},{6,4},{7,5},{8,10},{9,11},{10,... | collective-permute-start | bytes 294920 | tf_op jit(solution)/shard_map/ppermute | solution.py:195
  34.7 0.6 collective-permute-start.4
  35.3 2.0 %collective-permute-done.14 = bf16[2,2,48,256]{3,2,1,0:T(8,128)(2,1)S(1)} collective-permute-done((bf16[2,2,48,256]{3,2,1,0:T(8,128)(2,1)S(1)}, bf16[2,2,48,256]{3,2,1,0:T(8,128)(2,1)S(1)}, u32[]{:S(2)}, u32[]{:S(2)}) %collective-permute-start.14) | collective-permute-done | bytes 98336 | tf_op jit(solution)/shard_map/ppermute | solution.py:195
  37.5 2.0 %collective-permute-done.4 = bf16[2,2,48,256]{3,2,1,0:T(8,128)(2,1)S(1)} collective-permute-done((bf16[2,2,48,256]{3,2,1,0:T(8,128)(2,1)S(1)}, bf16[2,2,48,256]{3,2,1,0:T(8,128)(2,1)S(1)}, u32[]{:S(2)}, u32[]{:S(2)}) %collective-permute-start.4) | collective-permute-done | bytes 98336 | tf_op jit(solution)/shard_map/ppermute | solution.py:195
  40.0 1.0 %collective-permute-done.5 = bf16[192,512]{1,0:T(8,128)(2,1)S(1)} collective-permute-done((bf16[192,512]{1,0:T(8,128)(2,1)S(1)}, bf16[192,512]{1,0:T(8,128)(2,1)S(1)}, u32[]{:S(2)}, u32[]{:S(2)}) %collective-permute-start.5) | collective-permute-done | bytes 196640 | tf_op jit(solution)/shard_map/ppermute | solution.py:195
  42.6 0.4 collective-permute-start.16
  43.1 0.8 %collective-permute-done.6 = bf16[2,2,24,896]{3,2,1,0:T(8,128)(2,1)S(1)} collective-permute-done((bf16[2,2,24,896]{3,2,1,0:T(8,128)(2,1)S(1)}, bf16[2,2,24,896]{3,2,1,0:T(8,128)(2,1)S(1)}, u32[]{:S(2)}, u32[]{:S(2)}) %collective-permute-start.6) | collective-permute-done | bytes 172064 | tf_op jit(solution)/shard_map/ppermute | solution.py:195
  43.9 2.8 %collective-permute-start.10 = (bf16[2,2,24,896]{3,2,1,0:T(8,128)(2,1)S(1)}, bf16[2,2,24,896]{3,2,1,0:T(8,128)(2,1)S(1)}, u32[]{:S(2)}, u32[]{:S(2)}) collective-permute-start(bf16[2,2,24,896]{3,2,1,0:T(8,128)(2,1)S(1)} %pad_maximum_fusion.11), channel_id=1, source_target_pairs={{0,14},{1,3},{2,12},{3,1},{4,10},{5,7},{6,8},{7,5},{8,6},{9,11},{1... | collective-permute-start | bytes 516104 | tf_op jit(solution)/shard_map/ppermute | solution.py:306
  46.8 1.1 %collective-permute-start.18 = (bf16[2,2,24,896]{3,2,1,0:T(8,128)(2,1)S(1)}, bf16[2,2,24,896]{3,2,1,0:T(8,128)(2,1)S(1)}, u32[]{:S(2)}, u32[]{:S(2)}) collective-permute-start(bf16[2,2,24,896]{3,2,1,0:T(8,128)(2,1)S(1)} %pad_maximum_fusion.13), channel_id=1, source_target_pairs={{0,10},{1,7},{2,8},{3,5},{4,14},{5,3},{6,12},{7,1},{8,2},{9,15},{1... | collective-permute-start | bytes 516104 | tf_op jit(solution)/shard_map/ppermute | solution.py:306
  47.9 2.5 %collective-permute-start.17 = (bf16[2,2,24,896]{3,2,1,0:T(8,128)(2,1)S(1)}, bf16[2,2,24,896]{3,2,1,0:T(8,128)(2,1)S(1)}, u32[]{:S(2)}, u32[]{:S(2)}) collective-permute-start(bf16[2,2,24,896]{3,2,1,0:T(8,128)(2,1)S(1)} %pad_maximum_fusion.12), channel_id=1, source_target_pairs={{0,8},{1,5},{2,10},{3,7},{4,12},{5,1},{6,14},{7,3},{8,0},{9,13},{1... | collective-permute-start | bytes 516104 | tf_op jit(solution)/shard_map/ppermute | solution.py:306
  50.4 3.4 %collective-permute-start.9 = (bf16[2,2,24,896]{3,2,1,0:T(8,128)(2,1)S(1)}, bf16[2,2,24,896]{3,2,1,0:T(8,128)(2,1)S(1)}, u32[]{:S(2)}, u32[]{:S(2)}) collective-permute-start(bf16[2,2,24,896]{3,2,1,0:T(8,128)(2,1)S(1)} %pad_maximum_fusion.10), channel_id=1, source_target_pairs={{0,12},{1,1},{2,14},{3,3},{4,8},{5,5},{6,10},{7,7},{8,4},{9,9},{10... | collective-permute-start | bytes 516104 | tf_op jit(solution)/shard_map/ppermute | solution.py:306
  53.9 2.0 %collective-permute-done.18 = bf16[2,2,24,896]{3,2,1,0:T(8,128)(2,1)S(1)} collective-permute-done((bf16[2,2,24,896]{3,2,1,0:T(8,128)(2,1)S(1)}, bf16[2,2,24,896]{3,2,1,0:T(8,128)(2,1)S(1)}, u32[]{:S(2)}, u32[]{:S(2)}) %collective-permute-start.18) | collective-permute-done | bytes 172064 | tf_op jit(solution)/shard_map/ppermute | solution.py:306
  55.9 5.9 %collective-permute-done.17 = bf16[2,2,24,896]{3,2,1,0:T(8,128)(2,1)S(1)} collective-permute-done((bf16[2,2,24,896]{3,2,1,0:T(8,128)(2,1)S(1)}, bf16[2,2,24,896]{3,2,1,0:T(8,128)(2,1)S(1)}, u32[]{:S(2)}, u32[]{:S(2)}) %collective-permute-start.17) | collective-permute-done | bytes 172064 | tf_op jit(solution)/shard_map/ppermute | solution.py:306
  62.1 1.6 %collective-permute-done.19 = bf16[4,2,24,896]{3,2,1,0:T(8,128)(2,1)S(1)} collective-permute-done((bf16[4,2,24,896]{3,2,1,0:T(8,128)(2,1)S(1)}, bf16[4,2,24,896]{3,2,1,0:T(8,128)(2,1)S(1)}, u32[]{:S(2)}, u32[]{:S(2)}) %collective-permute-start.19) | collective-permute-done | bytes 344096 | tf_op jit(solution)/shard_map/ppermute | solution.py:195
  65.4 0.7 %copy-done.2 = f32[64,3584]{1,0:T(8,128)} copy-done((f32[64,3584]{1,0:T(8,128)}, f32[64,3584]{1,0:T(8,128)S(1)}, u32[]{:S(2)}) %copy-start.2) | copy-done | bytes 917528
  66.1 0.9 %fusion.19 = f32[64,3584]{1,0:T(8,128)} fusion(f32[64,3584]{1,0:T(8,128)} %copy-done.2, s32[]{:T(128)S(6)} %select_n.131, f32[64,896]{1,0:T(8,128)S(1)} %convolution_multiply_fusion.1, bf16[24,896]{1,0:T(8,128)(2,1)S(1)} %get-tuple-element.31, bf16[24,896]{1,0:T(8,128)(2,1)S(1)} %get-tuple-element.29, bf16[24,896]{1,0:T(8,128)(2,1)S(1)} %get-tuple-element.20, ...), kind=kOutput, calls=%fused_computation.23 | convolution fusion | flops 11862016 | bytes 643076 | tf_op jit(solution)/shard_map/dot_general | solution.py:345
  (91 shorter events, 7.8 us)
Async XLA Ops:
  0.0 28.7 %copy-start = (bf16[1,3584,256]{2,1,0:T(8,128)(2,1)S(1)}, bf16[1,3584,256]{2,1,0:T(8,128)(2,1)}, u32[]{:S(2)}) copy-start(bf16[1,3584,256]{2,1,0:T(8,128)(2,1)} %param.9) | copy-start | bytes 5505028
  0.0 10.0 %copy-start.3 = (s32[64,8]{0,1:T(8,128)S(1)}, s32[64,8]{0,1:T(8,128)}, u32[]{:S(2)}) copy-start(s32[64,8]{0,1:T(8,128)} %param.7) | copy-start | bytes 6148
  0.0 10.0 %copy-start.4 = (s32[64,8]{0,1:T(8,128)S(1)}, s32[64,8]{0,1:T(8,128)}, u32[]{:S(2)}) copy-start(s32[64,8]{0,1:T(8,128)} %param.8) | copy-start | bytes 6148
  2.6 10.2 %collective-permute-start.7 = (bf16[24,3584]{1,0:T(8,128)(2,1)S(1)}, bf16[24,3584]{1,0:T(8,128)(2,1)S(1)}, u32[]{:S(2)}, u32[]{:S(2)}) collective-permute-start(bf16[24,3584]{1,0:T(8,128)(2,1)S(1)} %get-tuple-element.14), channel_id=1, source_target_pairs={{0,4},{4,0},{8,12},{12,8},{1,5},{5,1},{9,13},{13,9},{2,6},{6,2},{1... | collective-permute-start | bytes 516104 | tf_op jit(solution)/shard_map/ppermute | solution.py:192
  5.7 15.6 %collective-permute-start.11 = (bf16[24,3584]{1,0:T(8,128)(2,1)S(1)}, bf16[24,3584]{1,0:T(8,128)(2,1)S(1)}, u32[]{:S(2)}, u32[]{:S(2)}) collective-permute-start(bf16[24,3584]{1,0:T(8,128)(2,1)S(1)} %get-tuple-element.13), channel_id=1, source_target_pairs={{0,8},{4,12},{8,0},{12,4},{1,9},{5,13},{9,1},{13,5},{2,10},{6,14},... | collective-permute-start | bytes 516104 | tf_op jit(solution)/shard_map/ppermute | solution.py:192
  8.3 14.5 %collective-permute-start = (bf16[24,3584]{1,0:T(8,128)(2,1)S(1)}, bf16[24,3584]{1,0:T(8,128)(2,1)S(1)}, u32[]{:S(2)}, u32[]{:S(2)}) collective-permute-start(bf16[24,3584]{1,0:T(8,128)(2,1)S(1)} %get-tuple-element.15), channel_id=1, source_target_pairs={{0,12},{4,8},{8,4},{12,0},{1,13},{5,9},{9,5},{13,1},{2,14},{6,10},... | collective-permute-start | bytes 516104 | tf_op jit(solution)/shard_map/ppermute | solution.py:192
  8.3 18.5 %collective-permute-start.1 = (bf16[24,3584]{1,0:T(8,128)(2,1)S(1)}, bf16[24,3584]{1,0:T(8,128)(2,1)S(1)}, u32[]{:S(2)}, u32[]{:S(2)}) collective-permute-start(bf16[24,3584]{1,0:T(8,128)(2,1)S(1)} %get-tuple-element.16), channel_id=1, source_target_pairs={{0,2},{1,3},{2,0},{3,1},{4,6},{5,7},{6,4},{7,5},{8,10},{9,11},{10,... | collective-permute-start | bytes 516104 | tf_op jit(solution)/shard_map/ppermute | solution.py:195
  12.8 10.6 %collective-permute-start.8 = (bf16[24,3584]{1,0:T(8,128)(2,1)S(1)}, bf16[24,3584]{1,0:T(8,128)(2,1)S(1)}, u32[]{:S(2)}, u32[]{:S(2)}) collective-permute-start(bf16[24,3584]{1,0:T(8,128)(2,1)S(1)} %collective-permute-done.7), channel_id=1, source_target_pairs={{0,2},{1,3},{2,0},{3,1},{4,6},{5,7},{6,4},{7,5},{8,10},{9,11},{10,... | collective-permute-start | bytes 516104 | tf_op jit(solution)/shard_map/ppermute | solution.py:195
  21.3 5.4 %collective-permute-start.12 = (bf16[24,3584]{1,0:T(8,128)(2,1)S(1)}, bf16[24,3584]{1,0:T(8,128)(2,1)S(1)}, u32[]{:S(2)}, u32[]{:S(2)}) collective-permute-start(bf16[24,3584]{1,0:T(8,128)(2,1)S(1)} %collective-permute-done.11), channel_id=1, source_target_pairs={{0,2},{1,3},{2,0},{3,1},{4,6},{5,7},{6,4},{7,5},{8,10},{9,11},{10,... | collective-permute-start | bytes 516104 | tf_op jit(solution)/shard_map/ppermute | solution.py:195
  22.8 5.7 %collective-permute-start.2 = (bf16[24,3584]{1,0:T(8,128)(2,1)S(1)}, bf16[24,3584]{1,0:T(8,128)(2,1)S(1)}, u32[]{:S(2)}, u32[]{:S(2)}) collective-permute-start(bf16[24,3584]{1,0:T(8,128)(2,1)S(1)} %collective-permute-done), channel_id=1, source_target_pairs={{0,2},{1,3},{2,0},{3,1},{4,6},{5,7},{6,4},{7,5},{8,10},{9,11},{10,... | collective-permute-start | bytes 516104 | tf_op jit(solution)/shard_map/ppermute | solution.py:195
  26.7 4.7 %collective-permute-start.13 = (bf16[96,3584]{1,0:T(8,128)(2,1)S(1)}, bf16[96,3584]{1,0:T(8,128)(2,1)S(1)}, u32[]{:S(2)}, u32[]{:S(2)}) collective-permute-start(bf16[96,3584]{1,0:T(8,128)(2,1)S(1)} %constant_dynamic-update-slice_fusion), channel_id=1, source_target_pairs={{0,1},{1,0},{2,3},{3,2},{4,5},{5,4},{6,7},{7,6},{8,9},{9,8},{10,11... | collective-permute-start | bytes 2064392 | tf_op jit(solution)/shard_map/ppermute | solution.py:195
  28.6 1.5 %copy-start.1 = (bf16[1,3584,256]{2,1,0:T(8,128)(2,1)S(1)}, bf16[1,3584,256]{2,1,0:T(8,128)(2,1)}, u32[]{:S(2)}) copy-start(bf16[1,3584,256]{2,1,0:T(8,128)(2,1)} %param.10) | copy-start | bytes 5505028
  28.6 5.2 %collective-permute-start.3 = (bf16[96,3584]{1,0:T(8,128)(2,1)S(1)}, bf16[96,3584]{1,0:T(8,128)(2,1)S(1)}, u32[]{:S(2)}, u32[]{:S(2)}) collective-permute-start(bf16[96,3584]{1,0:T(8,128)(2,1)S(1)} %pad_maximum_fusion.2), channel_id=1, source_target_pairs={{0,1},{1,0},{2,3},{3,2},{4,5},{5,4},{6,7},{7,6},{8,9},{9,8},{10,11... | collective-permute-start | bytes 2064392 | tf_op jit(solution)/shard_map/ppermute | solution.py:195
  32.3 5.0 %collective-permute-start.14 = (bf16[2,2,48,256]{3,2,1,0:T(8,128)(2,1)S(1)}, bf16[2,2,48,256]{3,2,1,0:T(8,128)(2,1)S(1)}, u32[]{:S(2)}, u32[]{:S(2)}) collective-permute-start(bf16[2,2,48,256]{3,2,1,0:T(8,128)(2,1)S(1)} %pad_maximum_fusion.19), channel_id=1, source_target_pairs={{0,2},{1,3},{2,0},{3,1},{4,6},{5,7},{6,4},{7,5},{8,10},{9,11},{10,... | collective-permute-start | bytes 294920 | tf_op jit(solution)/shard_map/ppermute | solution.py:195
  34.7 4.7 %collective-permute-start.4 = (bf16[2,2,48,256]{3,2,1,0:T(8,128)(2,1)S(1)}, bf16[2,2,48,256]{3,2,1,0:T(8,128)(2,1)S(1)}, u32[]{:S(2)}, u32[]{:S(2)}) collective-permute-start(bf16[2,2,48,256]{3,2,1,0:T(8,128)(2,1)S(1)} %pad_maximum_fusion.18), channel_id=1, source_target_pairs={{0,2},{1,3},{2,0},{3,1},{4,6},{5,7},{6,4},{7,5},{8,10},{9,11},{10,... | collective-permute-start | bytes 294920 | tf_op jit(solution)/shard_map/ppermute | solution.py:195
  37.4 2.2 %collective-permute-start.15 = (bf16[192,512]{1,0:T(8,128)(2,1)S(1)}, bf16[192,512]{1,0:T(8,128)(2,1)S(1)}, u32[]{:S(2)}, u32[]{:S(2)}) collective-permute-start(bf16[192,512]{1,0:T(8,128)(2,1)S(1)} %bitcast.184), channel_id=1, source_target_pairs={{0,1},{1,0},{2,3},{3,2},{4,5},{5,4},{6,7},{7,6},{8,9},{9,8},{10,11... | collective-permute-start | bytes 589832 | tf_op jit(solution)/shard_map/ppermute | solution.py:195
  39.5 1.5 %collective-permute-start.5 = (bf16[192,512]{1,0:T(8,128)(2,1)S(1)}, bf16[192,512]{1,0:T(8,128)(2,1)S(1)}, u32[]{:S(2)}, u32[]{:S(2)}) collective-permute-start(bf16[192,512]{1,0:T(8,128)(2,1)S(1)} %bitcast.186), channel_id=1, source_target_pairs={{0,1},{1,0},{2,3},{3,2},{4,5},{5,4},{6,7},{7,6},{8,9},{9,8},{10,11... | collective-permute-start | bytes 589832 | tf_op jit(solution)/shard_map/ppermute | solution.py:195
  42.4 1.5 %collective-permute-start.6 = (bf16[2,2,24,896]{3,2,1,0:T(8,128)(2,1)S(1)}, bf16[2,2,24,896]{3,2,1,0:T(8,128)(2,1)S(1)}, u32[]{:S(2)}, u32[]{:S(2)}) collective-permute-start(bf16[2,2,24,896]{3,2,1,0:T(8,128)(2,1)S(1)} %rev.6), channel_id=1, source_target_pairs={{0,1},{1,0},{2,3},{3,2},{4,5},{5,4},{6,7},{7,6},{8,9},{9,8},{10,11... | collective-permute-start | bytes 516104 | tf_op jit(solution)/shard_map/ppermute | solution.py:195
  42.6 4.1 %collective-permute-start.16 = (bf16[2,2,24,896]{3,2,1,0:T(8,128)(2,1)S(1)}, bf16[2,2,24,896]{3,2,1,0:T(8,128)(2,1)S(1)}, u32[]{:S(2)}, u32[]{:S(2)}) collective-permute-start(bf16[2,2,24,896]{3,2,1,0:T(8,128)(2,1)S(1)} %rev.7), channel_id=1, source_target_pairs={{0,1},{1,0},{2,3},{3,2},{4,5},{5,4},{6,7},{7,6},{8,9},{9,8},{10,11... | collective-permute-start | bytes 516104 | tf_op jit(solution)/shard_map/ppermute | solution.py:195
  43.9 10.0 %collective-permute-start.10 = (bf16[2,2,24,896]{3,2,1,0:T(8,128)(2,1)S(1)}, bf16[2,2,24,896]{3,2,1,0:T(8,128)(2,1)S(1)}, u32[]{:S(2)}, u32[]{:S(2)}) collective-permute-start(bf16[2,2,24,896]{3,2,1,0:T(8,128)(2,1)S(1)} %pad_maximum_fusion.11), channel_id=1, source_target_pairs={{0,14},{1,3},{2,12},{3,1},{4,10},{5,7},{6,8},{7,5},{8,6},{9,11},{1... | collective-permute-start | bytes 516104 | tf_op jit(solution)/shard_map/ppermute | solution.py:306
  46.8 9.1 %collective-permute-start.18 = (bf16[2,2,24,896]{3,2,1,0:T(8,128)(2,1)S(1)}, bf16[2,2,24,896]{3,2,1,0:T(8,128)(2,1)S(1)}, u32[]{:S(2)}, u32[]{:S(2)}) collective-permute-start(bf16[2,2,24,896]{3,2,1,0:T(8,128)(2,1)S(1)} %pad_maximum_fusion.13), channel_id=1, source_target_pairs={{0,10},{1,7},{2,8},{3,5},{4,14},{5,3},{6,12},{7,1},{8,2},{9,15},{1... | collective-permute-start | bytes 516104 | tf_op jit(solution)/shard_map/ppermute | solution.py:306
  47.9 13.9 %collective-permute-start.17 = (bf16[2,2,24,896]{3,2,1,0:T(8,128)(2,1)S(1)}, bf16[2,2,24,896]{3,2,1,0:T(8,128)(2,1)S(1)}, u32[]{:S(2)}, u32[]{:S(2)}) collective-permute-start(bf16[2,2,24,896]{3,2,1,0:T(8,128)(2,1)S(1)} %pad_maximum_fusion.12), channel_id=1, source_target_pairs={{0,8},{1,5},{2,10},{3,7},{4,12},{5,1},{6,14},{7,3},{8,0},{9,13},{1... | collective-permute-start | bytes 516104 | tf_op jit(solution)/shard_map/ppermute | solution.py:306
  50.4 11.4 %collective-permute-start.9 = (bf16[2,2,24,896]{3,2,1,0:T(8,128)(2,1)S(1)}, bf16[2,2,24,896]{3,2,1,0:T(8,128)(2,1)S(1)}, u32[]{:S(2)}, u32[]{:S(2)}) collective-permute-start(bf16[2,2,24,896]{3,2,1,0:T(8,128)(2,1)S(1)} %pad_maximum_fusion.10), channel_id=1, source_target_pairs={{0,12},{1,1},{2,14},{3,3},{4,8},{5,5},{6,10},{7,7},{8,4},{9,9},{10... | collective-permute-start | bytes 516104 | tf_op jit(solution)/shard_map/ppermute | solution.py:306
  62.0 1.7 %collective-permute-start.19 = (bf16[4,2,24,896]{3,2,1,0:T(8,128)(2,1)S(1)}, bf16[4,2,24,896]{3,2,1,0:T(8,128)(2,1)S(1)}, u32[]{:S(2)}, u32[]{:S(2)}) collective-permute-start(bf16[4,2,24,896]{3,2,1,0:T(8,128)(2,1)S(1)} %pad_maximum_fusion.9), channel_id=1, source_target_pairs={{0,1},{1,0},{2,3},{3,2},{4,5},{5,4},{6,7},{7,6},{8,9},{9,8},{10,11... | collective-permute-start | bytes 1032200 | tf_op jit(solution)/shard_map/ppermute | solution.py:195
  65.2 0.9 %copy-start.2 = (f32[64,3584]{1,0:T(8,128)}, f32[64,3584]{1,0:T(8,128)S(1)}, u32[]{:S(2)}) copy-start(f32[64,3584]{1,0:T(8,128)S(1)} %fusion.21) | copy-start | bytes 2752516

commit v8 on v7

--- a/solution.py
+++ b/solution.py
@@ -7,7 +7,7 @@
 import functools
 
 EXP_POD = 8
-CFG = {'C': [[0, 3], [1, 2]], 'H': [[0], [1]], 'order': [('z', 0), ('z', 3), ('z', 1), ('x', (0,)), ('z', 2), ('x', (3,)), ('c', 0), ('h', 0), ('x', (1,)), ('x', (2,)), ('c', 1), ('h', 1), ('q', (3, 0)), ('q', (2, 1)), ('v', ((3, 0), (2, 1)))], 'gates': {'qd3': ['xd11']}, 'apart': False}
+CFG = {'C': [[0, 3], [1, 2]], 'H': [[0], [1]], 'order': [('z', 3), ('z', 1), ('x', (3,)), ('z', 2), ('x', (2,)), ('z', 0), ('x', (0,)), ('c', 0), ('h', 0), ('r', 3), ('x', (1,)), ('c', 1), ('h', 1), ('r', 2), ('t', (0, 1)), ('w', (0, 1, 2, 3))], 'gates': {'cs1': ['zd3', 'xd01'], 'td01': ['xd01'], 'rd30': ['hd11'], 'hs1': ['xd11'], 'rs31': ['cd0']}, 'apart': False}
 
 
 def pick_kernel(n_out, capacity, pods, tokens_hbm, routes_hbm, fixed_hbm, *refs):

time: 67.2 us -> 67.4 us (level)
  waiting for transfers between devices: 27.9 us -> 30.3 us
  starting transfers between devices: 24.2 us -> 22.3 us
    ppermute x3 -> x6, waiting for transfers between devices: 7.55 us -> 17 us  [outer_xor(): lax.ppermute(p, 'outer', [(i, i ^ t) for i in range(n_out)])]
    ppermute x4 -> x2, waiting for transfers between devices: 8.04 us -> 0.01 us  [move(): return lax.ppermute(p, ('outer', 'local'), pairs)]
    ppermute x4 -> x2, starting transfers between devices: 9.75 us -> 5.62 us  [move(): return lax.ppermute(p, ('outer', 'local'), pairs)]
    ppermute x3 -> x6, starting transfers between devices: 5.69 us -> 7.77 us  [outer_xor(): lax.ppermute(p, 'outer', [(i, i ^ t) for i in range(n_out)])]
    ppermute x13 -> x12, waiting for transfers between devices: 12.3 us -> 13.3 us  [local_xor(): return lax.ppermute(v, 'local', [(i, i ^ m) for i in range(n_loc)])]
    ppermute x13 -> x12, starting transfers between devices: 8.72 us -> 8.94 us  [local_xor(): return lax.ppermute(v, 'local', [(i, i ^ m) for i in range(n_loc)])]
    unnamed x13 -> x19, local copies, waits for them, and re-layouts: 1.71 us -> 1.79 us
  transfers between devices with their start and end apart: 20 -> 20, of which waited for: 12 -> 10; matrix products, arithmetic and copies ran while one was open for 9% -> 10% of each run, Pallas kernels for 0% -> 0%
where the time goes in v8:
time: 67.4 us; the launch traced here: 67.2 us
  waiting for transfers between devices  30.3 us (45%)
  starting transfers between devices  22.3 us (33%)
  matrix products  8.71 us (13%)
  local copies, waits for them, and re-layouts  4.01 us (6%)
  other arithmetic  1.45 us (2%)
    ppermute x6, waiting for transfers between devices, outer_xor(): lax.ppermute(p, 'outer', [(i, i ^ t) for i in range(n_out)])  17 us
    ppermute x12, waiting for transfers between devices, local_xor(): return lax.ppermute(v, 'local', [(i, i ^ m) for i in range(n_loc)])  13.3 us
    ppermute x12, starting transfers between devices, local_xor(): return lax.ppermute(v, 'local', [(i, i ^ m) for i in range(n_loc)])  8.94 us
    ppermute x6, starting transfers between devices, outer_xor(): lax.ppermute(p, 'outer', [(i, i ^ t) for i in range(n_out)])  7.77 us
    ppermute x2, starting transfers between devices, move(): return lax.ppermute(p, ('outer', 'local'), pairs)  5.62 us
    unnamed x19, local copies, waits for them, and re-layouts  1.79 us
    dot_general x4, matrix products, first_half(): up_proj = jnp.dot(rows, up_local, preferred_element_type=jnp.float32)  1.73 us
    dot_general x4, matrix products, first_half(): gate_proj = jnp.dot(rows, gate_local, preferred_element_type=jnp.float32)  1.72 us
  transfers between devices with their start and end apart: 20, of which 10 were waited for; matrix products, arithmetic and copies ran while one was open for 10% of the time, Pallas kernels for 0%

profile of v8, /device:TPU:0, one launch (start us, length us, event | category | flops | bytes accessed | tf_op | source)
XLA Modules:
  0.0 67.2 jit_solution(8960575611536753441)
XLA Ops:
  0.0 0.9 %compare_reduce_fusion = pred[64,4]{0,1:T(4,128)(4,1)S(1)} fusion(s32[64,8]{0,1:T(8,128)} %param.7, s32[4]{0:T(128)S(1)} %xor_multiply_fusion), kind=kLoop, calls=%fused_computation.115 | loop fusion | flops 3840 | bytes 2320 | tf_op jit(solution)/shard_map/reduce_or | solution.py:171
  1.2 1.3 %convolution_convert_fusion = bf16[4,24,3584]{2,1,0:T(8,128)(2,1)S(1)} fusion(bf16[64,3584]{1,0:T(8,128)(2,1)} %param.6, s32[64,4]{0,1:T(4,128)S(1)} %add_select_fusion), kind=kOutput, calls=%fused_computation | convolution fusion | flops 44390400 | bytes 1147904 | tf_op jit(solution)/shard_map/tqc,td->qcd/dot_general | solution.py:174
  2.6 3.1 %collective-permute-start.6 = (bf16[24,3584]{1,0:T(8,128)(2,1)S(1)}, bf16[24,3584]{1,0:T(8,128)(2,1)S(1)}, u32[]{:S(2)}, u32[]{:S(2)}) collective-permute-start(bf16[24,3584]{1,0:T(8,128)(2,1)S(1)} %get-tuple-element.20), channel_id=1, source_target_pairs={{0,4},{4,0},{8,12},{12,8},{1,5},{5,1},{9,13},{13,9},{2,6},{6,2},{1... | collective-permute-start | bytes 516104 | tf_op jit(solution)/shard_map/ppermute | solution.py:192
  5.7 2.6 %collective-permute-start.7 = (bf16[24,3584]{1,0:T(8,128)(2,1)S(1)}, bf16[24,3584]{1,0:T(8,128)(2,1)S(1)}, u32[]{:S(2)}, u32[]{:S(2)}) collective-permute-start(bf16[24,3584]{1,0:T(8,128)(2,1)S(1)} %get-tuple-element.19), channel_id=1, source_target_pairs={{0,8},{4,12},{8,0},{12,4},{1,9},{5,13},{9,1},{13,5},{2,10},{6,14},... | collective-permute-start | bytes 516104 | tf_op jit(solution)/shard_map/ppermute | solution.py:192
  8.3 1.5 %collective-permute-start.1 = (bf16[24,3584]{1,0:T(8,128)(2,1)S(1)}, bf16[24,3584]{1,0:T(8,128)(2,1)S(1)}, u32[]{:S(2)}, u32[]{:S(2)}) collective-permute-start(bf16[24,3584]{1,0:T(8,128)(2,1)S(1)} %get-tuple-element.22), channel_id=1, source_target_pairs={{0,2},{1,3},{2,0},{3,1},{4,6},{5,7},{6,4},{7,5},{8,10},{9,11},{10,... | collective-permute-start | bytes 516104 | tf_op jit(solution)/shard_map/ppermute | solution.py:195
  10.3 1.6 %dynamic-slice_bitcast_fusion.3 = (bf16[256,896]{1,0:T(8,128)(2,1)S(1)}, bf16[256,896]{1,0:T(8,128)(2,1)S(1)}, bf16[256,896]{1,0:T(8,128)(2,1)S(1)}, bf16[256,896]{1,0:T(8,128)(2,1)S(1)}) fusion(bf16[1,1024,896]{2,1,0:T(8,128)(2,1)} %param.11, s32[]{:T(128)S(6)} %select_n.44, s32[]{:T(128)S(6)} %select_n.45, s32[]{:T(128)S(6)} %select_n.47, s32[]{:T(128)S(6)} %select_n.46), kind=kLoop, calls=%fused_computation.48 | loop fusion | bytes 3670032 | tf_op jit(solution)/shard_map/dynamic_slice | solution.py:155
  11.9 1.0 %collective-permute-done.6 = bf16[24,3584]{1,0:T(8,128)(2,1)S(1)} collective-permute-done((bf16[24,3584]{1,0:T(8,128)(2,1)S(1)}, bf16[24,3584]{1,0:T(8,128)(2,1)S(1)}, u32[]{:S(2)}, u32[]{:S(2)}) %collective-permute-start.6) | collective-permute-done | bytes 172064 | tf_op jit(solution)/shard_map/ppermute | solution.py:192
  12.9 1.7 %collective-permute-start.8 = (bf16[24,3584]{1,0:T(8,128)(2,1)S(1)}, bf16[24,3584]{1,0:T(8,128)(2,1)S(1)}, u32[]{:S(2)}, u32[]{:S(2)}) collective-permute-start(bf16[24,3584]{1,0:T(8,128)(2,1)S(1)} %collective-permute-done.6), channel_id=1, source_target_pairs={{0,2},{1,3},{2,0},{3,1},{4,6},{5,7},{6,4},{7,5},{8,10},{9,11},{10,... | collective-permute-start | bytes 516104 | tf_op jit(solution)/shard_map/ppermute | solution.py:195
  14.6 6.6 %collective-permute-done.7 = bf16[24,3584]{1,0:T(8,128)(2,1)S(1)} collective-permute-done((bf16[24,3584]{1,0:T(8,128)(2,1)S(1)}, bf16[24,3584]{1,0:T(8,128)(2,1)S(1)}, u32[]{:S(2)}, u32[]{:S(2)}) %collective-permute-start.7) | collective-permute-done | bytes 172064 | tf_op jit(solution)/shard_map/ppermute | solution.py:192
  21.1 1.6 %collective-permute-start.9 = (bf16[24,3584]{1,0:T(8,128)(2,1)S(1)}, bf16[24,3584]{1,0:T(8,128)(2,1)S(1)}, u32[]{:S(2)}, u32[]{:S(2)}) collective-permute-start(bf16[24,3584]{1,0:T(8,128)(2,1)S(1)} %collective-permute-done.7), channel_id=1, source_target_pairs={{0,2},{1,3},{2,0},{3,1},{4,6},{5,7},{6,4},{7,5},{8,10},{9,11},{10,... | collective-permute-start | bytes 516104 | tf_op jit(solution)/shard_map/ppermute | solution.py:195
  22.8 0.5 collective-permute-start.2
  23.3 3.3 %collective-permute-done.9 = bf16[24,3584]{1,0:T(8,128)(2,1)S(1)} collective-permute-done((bf16[24,3584]{1,0:T(8,128)(2,1)S(1)}, bf16[24,3584]{1,0:T(8,128)(2,1)S(1)}, u32[]{:S(2)}, u32[]{:S(2)}) %collective-permute-start.9) | collective-permute-done | bytes 172064 | tf_op jit(solution)/shard_map/ppermute | solution.py:195
  26.7 1.7 %collective-permute-done.2 = bf16[24,3584]{1,0:T(8,128)(2,1)S(1)} collective-permute-done((bf16[24,3584]{1,0:T(8,128)(2,1)S(1)}, bf16[24,3584]{1,0:T(8,128)(2,1)S(1)}, u32[]{:S(2)}, u32[]{:S(2)}) %collective-permute-start.2) | collective-permute-done | bytes 172064 | tf_op jit(solution)/shard_map/ppermute | solution.py:195
  29.0 1.0 %copy-done.1 = bf16[1,3584,256]{2,1,0:T(8,128)(2,1)S(1)} copy-done((bf16[1,3584,256]{2,1,0:T(8,128)(2,1)S(1)}, bf16[1,3584,256]{2,1,0:T(8,128)(2,1)}, u32[]{:S(2)}) %copy-start.1) | copy-done | bytes 1835032
  30.8 0.4 multiply_convert_fusion.1
  31.7 0.4 multiply_convert_fusion
  32.2 1.7 %collective-permute-start.11 = (bf16[2,2,48,256]{3,2,1,0:T(8,128)(2,1)S(1)}, bf16[2,2,48,256]{3,2,1,0:T(8,128)(2,1)S(1)}, u32[]{:S(2)}, u32[]{:S(2)}) collective-permute-start(bf16[2,2,48,256]{3,2,1,0:T(8,128)(2,1)S(1)} %pad_maximum_fusion.16), channel_id=1, source_target_pairs={{0,2},{1,3},{2,0},{3,1},{4,6},{5,7},{6,4},{7,5},{8,10},{9,11},{10,... | collective-permute-start | bytes 294920 | tf_op jit(solution)/shard_map/ppermute | solution.py:195
  34.3 0.4 multiply_convert_fusion.2
  34.7 0.5 collective-permute-start.4
  35.2 1.8 %collective-permute-done.11 = bf16[2,2,48,256]{3,2,1,0:T(8,128)(2,1)S(1)} collective-permute-done((bf16[2,2,48,256]{3,2,1,0:T(8,128)(2,1)S(1)}, bf16[2,2,48,256]{3,2,1,0:T(8,128)(2,1)S(1)}, u32[]{:S(2)}, u32[]{:S(2)}) %collective-permute-start.11) | collective-permute-done | bytes 98336 | tf_op jit(solution)/shard_map/ppermute | solution.py:195
  37.2 2.3 %collective-permute-done.4 = bf16[2,2,48,256]{3,2,1,0:T(8,128)(2,1)S(1)} collective-permute-done((bf16[2,2,48,256]{3,2,1,0:T(8,128)(2,1)S(1)}, bf16[2,2,48,256]{3,2,1,0:T(8,128)(2,1)S(1)}, u32[]{:S(2)}, u32[]{:S(2)}) %collective-permute-start.4) | collective-permute-done | bytes 98336 | tf_op jit(solution)/shard_map/ppermute | solution.py:195
  40.0 1.0 %collective-permute-done.5 = bf16[192,512]{1,0:T(8,128)(2,1)S(1)} collective-permute-done((bf16[192,512]{1,0:T(8,128)(2,1)S(1)}, bf16[192,512]{1,0:T(8,128)(2,1)S(1)}, u32[]{:S(2)}, u32[]{:S(2)}) %collective-permute-start.5) | collective-permute-done | bytes 196640 | tf_op jit(solution)/shard_map/ppermute | solution.py:195
  42.4 2.8 %collective-permute-start.18 = (bf16[2,24,896]{2,1,0:T(8,128)(2,1)S(1)}, bf16[2,24,896]{2,1,0:T(8,128)(2,1)S(1)}, u32[]{:S(2)}, u32[]{:S(2)}) collective-permute-start(bf16[2,24,896]{2,1,0:T(8,128)(2,1)S(1)} %get-tuple-element.12), channel_id=1, source_target_pairs={{0,14},{1,15},{2,12},{3,13},{4,10},{5,11},{6,8},{7,9},{8,6},{9,7},... | collective-permute-start | bytes 258056 | tf_op jit(solution)/shard_map/ppermute | solution.py:203
  45.2 1.2 %collective-permute-start.13 = (bf16[2,2,24,896]{3,2,0,1:T(8,128)(2,1)S(1)}, bf16[2,2,24,896]{3,2,0,1:T(8,128)(2,1)S(1)}, u32[]{:S(2)}, u32[]{:S(2)}) collective-permute-start(bf16[2,2,24,896]{3,2,0,1:T(8,128)(2,1)S(1)} %pad_maximum_fusion.9), channel_id=1, source_target_pairs={{0,2},{1,3},{2,0},{3,1},{4,6},{5,7},{6,4},{7,5},{8,10},{9,11},{10,... | collective-permute-start | bytes 516104 | tf_op jit(solution)/shard_map/ppermute | solution.py:195
  46.4 0.5 collective-permute-start.15
  46.9 2.8 %collective-permute-start.17 = (bf16[2,24,896]{2,1,0:T(8,128)(2,1)S(1)}, bf16[2,24,896]{2,1,0:T(8,128)(2,1)S(1)}, u32[]{:S(2)}, u32[]{:S(2)}) collective-permute-start(bf16[2,24,896]{2,1,0:T(8,128)(2,1)S(1)} %get-tuple-element.59), channel_id=1, source_target_pairs={{0,10},{1,11},{2,8},{3,9},{4,14},{5,15},{6,12},{7,13},{8,2},{9,3},... | collective-permute-start | bytes 258056 | tf_op jit(solution)/shard_map/ppermute | solution.py:203
  49.7 1.3 %collective-permute-start.16 = (bf16[2,24,896]{2,1,0:T(8,128)(2,1)S(1)}, bf16[2,24,896]{2,1,0:T(8,128)(2,1)S(1)}, u32[]{:S(2)}, u32[]{:S(2)}) collective-permute-start(bf16[2,24,896]{2,1,0:T(8,128)(2,1)S(1)} %get-tuple-element.35), channel_id=1, source_target_pairs={{0,12},{4,8},{8,4},{12,0},{1,13},{5,9},{9,5},{13,1},{2,14},{6,10},... | collective-permute-start | bytes 258056 | tf_op jit(solution)/shard_map/ppermute | solution.py:192
  51.0 2.3 %collective-permute-done.13 = bf16[2,2,24,896]{3,2,0,1:T(8,128)(2,1)S(1)} collective-permute-done((bf16[2,2,24,896]{3,2,0,1:T(8,128)(2,1)S(1)}, bf16[2,2,24,896]{3,2,0,1:T(8,128)(2,1)S(1)}, u32[]{:S(2)}, u32[]{:S(2)}) %collective-permute-start.13) | collective-permute-done | bytes 172064 | tf_op jit(solution)/shard_map/ppermute | solution.py:195
  53.4 9.5 %collective-permute-done.14 = bf16[2,2,24,896]{3,2,1,0:T(8,128)(2,1)S(1)} collective-permute-done((bf16[2,2,24,896]{3,2,1,0:T(8,128)(2,1)S(1)}, bf16[2,2,24,896]{3,2,1,0:T(8,128)(2,1)S(1)}, u32[]{:S(2)}, u32[]{:S(2)}) %collective-permute-start.14) | collective-permute-done | bytes 172064 | tf_op jit(solution)/shard_map/ppermute | solution.py:192
  63.8 0.9 %collective-permute-done.19 = bf16[8,24,896]{2,1,0:T(8,128)(2,1)S(1)} collective-permute-done((bf16[8,24,896]{2,1,0:T(8,128)(2,1)S(1)}, bf16[8,24,896]{2,1,0:T(8,128)(2,1)S(1)}, u32[]{:S(2)}, u32[]{:S(2)}) %collective-permute-start.19) | collective-permute-done | bytes 344096 | tf_op jit(solution)/shard_map/ppermute | solution.py:195
  65.6 0.7 %copy-done.2 = f32[64,3584]{1,0:T(8,128)} copy-done((f32[64,3584]{1,0:T(8,128)}, f32[64,3584]{1,0:T(8,128)S(1)}, u32[]{:S(2)}) %copy-start.2) | copy-done | bytes 917528
  66.3 0.9 %fusion.19 = f32[64,3584]{1,0:T(8,128)} fusion(f32[64,3584]{1,0:T(8,128)} %copy-done.2, s32[]{:T(128)S(6)} %select_n.51, f32[64,896]{1,0:T(8,128)S(1)} %convolution_multiply_fusion.1, bf16[64,96]{0,1:T(8,128)(2,1)S(1)} %get-tuple-element.54, bf16[24,896]{1,0:T(8,128)(2,1)S(1)} %get-tuple-element.26, bf16[24,896]{1,0:T(8,128)(2,1)S(1)} %get-tuple-element.27, ...), kind=kOutput, calls=%fused_computation.23 | convolution fusion | flops 11812864 | bytes 643076 | tf_op jit(solution)/shard_map/dot_general | solution.py:345
  (84 shorter events, 7.1 us)
Async XLA Ops:
  0.0 28.5 %copy-start = (bf16[1,3584,256]{2,1,0:T(8,128)(2,1)S(1)}, bf16[1,3584,256]{2,1,0:T(8,128)(2,1)}, u32[]{:S(2)}) copy-start(bf16[1,3584,256]{2,1,0:T(8,128)(2,1)} %param.9) | copy-start | bytes 5505028
  0.0 10.0 %copy-start.3 = (s32[64,8]{0,1:T(8,128)S(1)}, s32[64,8]{0,1:T(8,128)}, u32[]{:S(2)}) copy-start(s32[64,8]{0,1:T(8,128)} %param.7) | copy-start | bytes 6148
  0.0 10.0 %copy-start.4 = (s32[64,8]{0,1:T(8,128)S(1)}, s32[64,8]{0,1:T(8,128)}, u32[]{:S(2)}) copy-start(s32[64,8]{0,1:T(8,128)} %param.8) | copy-start | bytes 6148
  2.6 10.3 %collective-permute-start.6 = (bf16[24,3584]{1,0:T(8,128)(2,1)S(1)}, bf16[24,3584]{1,0:T(8,128)(2,1)S(1)}, u32[]{:S(2)}, u32[]{:S(2)}) collective-permute-start(bf16[24,3584]{1,0:T(8,128)(2,1)S(1)} %get-tuple-element.20), channel_id=1, source_target_pairs={{0,4},{4,0},{8,12},{12,8},{1,5},{5,1},{9,13},{13,9},{2,6},{6,2},{1... | collective-permute-start | bytes 516104 | tf_op jit(solution)/shard_map/ppermute | solution.py:192
  5.7 15.4 %collective-permute-start.7 = (bf16[24,3584]{1,0:T(8,128)(2,1)S(1)}, bf16[24,3584]{1,0:T(8,128)(2,1)S(1)}, u32[]{:S(2)}, u32[]{:S(2)}) collective-permute-start(bf16[24,3584]{1,0:T(8,128)(2,1)S(1)} %get-tuple-element.19), channel_id=1, source_target_pairs={{0,8},{4,12},{8,0},{12,4},{1,9},{5,13},{9,1},{13,5},{2,10},{6,14},... | collective-permute-start | bytes 516104 | tf_op jit(solution)/shard_map/ppermute | solution.py:192
  8.3 18.3 %collective-permute-start.1 = (bf16[24,3584]{1,0:T(8,128)(2,1)S(1)}, bf16[24,3584]{1,0:T(8,128)(2,1)S(1)}, u32[]{:S(2)}, u32[]{:S(2)}) collective-permute-start(bf16[24,3584]{1,0:T(8,128)(2,1)S(1)} %get-tuple-element.22), channel_id=1, source_target_pairs={{0,2},{1,3},{2,0},{3,1},{4,6},{5,7},{6,4},{7,5},{8,10},{9,11},{10,... | collective-permute-start | bytes 516104 | tf_op jit(solution)/shard_map/ppermute | solution.py:195
  9.8 13.0 %collective-permute-start = (bf16[24,3584]{1,0:T(8,128)(2,1)S(1)}, bf16[24,3584]{1,0:T(8,128)(2,1)S(1)}, u32[]{:S(2)}, u32[]{:S(2)}) collective-permute-start(bf16[24,3584]{1,0:T(8,128)(2,1)S(1)} %get-tuple-element.21), channel_id=1, source_target_pairs={{0,12},{4,8},{8,4},{12,0},{1,13},{5,9},{9,5},{13,1},{2,14},{6,10},... | collective-permute-start | bytes 516104 | tf_op jit(solution)/shard_map/ppermute | solution.py:192
  12.9 10.4 %collective-permute-start.8 = (bf16[24,3584]{1,0:T(8,128)(2,1)S(1)}, bf16[24,3584]{1,0:T(8,128)(2,1)S(1)}, u32[]{:S(2)}, u32[]{:S(2)}) collective-permute-start(bf16[24,3584]{1,0:T(8,128)(2,1)S(1)} %collective-permute-done.6), channel_id=1, source_target_pairs={{0,2},{1,3},{2,0},{3,1},{4,6},{5,7},{6,4},{7,5},{8,10},{9,11},{10,... | collective-permute-start | bytes 516104 | tf_op jit(solution)/shard_map/ppermute | solution.py:195
  21.1 5.4 %collective-permute-start.9 = (bf16[24,3584]{1,0:T(8,128)(2,1)S(1)}, bf16[24,3584]{1,0:T(8,128)(2,1)S(1)}, u32[]{:S(2)}, u32[]{:S(2)}) collective-permute-start(bf16[24,3584]{1,0:T(8,128)(2,1)S(1)} %collective-permute-done.7), channel_id=1, source_target_pairs={{0,2},{1,3},{2,0},{3,1},{4,6},{5,7},{6,4},{7,5},{8,10},{9,11},{10,... | collective-permute-start | bytes 516104 | tf_op jit(solution)/shard_map/ppermute | solution.py:195
  22.8 5.6 %collective-permute-start.2 = (bf16[24,3584]{1,0:T(8,128)(2,1)S(1)}, bf16[24,3584]{1,0:T(8,128)(2,1)S(1)}, u32[]{:S(2)}, u32[]{:S(2)}) collective-permute-start(bf16[24,3584]{1,0:T(8,128)(2,1)S(1)} %collective-permute-done), channel_id=1, source_target_pairs={{0,2},{1,3},{2,0},{3,1},{4,6},{5,7},{6,4},{7,5},{8,10},{9,11},{10,... | collective-permute-start | bytes 516104 | tf_op jit(solution)/shard_map/ppermute | solution.py:195
  26.6 4.7 %collective-permute-start.10 = (bf16[96,3584]{1,0:T(8,128)(2,1)S(1)}, bf16[96,3584]{1,0:T(8,128)(2,1)S(1)}, u32[]{:S(2)}, u32[]{:S(2)}) collective-permute-start(bf16[96,3584]{1,0:T(8,128)(2,1)S(1)} %constant_dynamic-update-slice_fusion), channel_id=1, source_target_pairs={{0,1},{1,0},{2,3},{3,2},{4,5},{5,4},{6,7},{7,6},{8,9},{9,8},{10,11... | collective-permute-start | bytes 2064392 | tf_op jit(solution)/shard_map/ppermute | solution.py:195
  28.5 1.5 %copy-start.1 = (bf16[1,3584,256]{2,1,0:T(8,128)(2,1)S(1)}, bf16[1,3584,256]{2,1,0:T(8,128)(2,1)}, u32[]{:S(2)}) copy-start(bf16[1,3584,256]{2,1,0:T(8,128)(2,1)} %param.10) | copy-start | bytes 5505028
  28.5 5.4 %collective-permute-start.3 = (bf16[96,3584]{1,0:T(8,128)(2,1)S(1)}, bf16[96,3584]{1,0:T(8,128)(2,1)S(1)}, u32[]{:S(2)}, u32[]{:S(2)}) collective-permute-start(bf16[96,3584]{1,0:T(8,128)(2,1)S(1)} %pad_maximum_fusion.2), channel_id=1, source_target_pairs={{0,1},{1,0},{2,3},{3,2},{4,5},{5,4},{6,7},{7,6},{8,9},{9,8},{10,11... | collective-permute-start | bytes 2064392 | tf_op jit(solution)/shard_map/ppermute | solution.py:195
  32.2 4.9 %collective-permute-start.11 = (bf16[2,2,48,256]{3,2,1,0:T(8,128)(2,1)S(1)}, bf16[2,2,48,256]{3,2,1,0:T(8,128)(2,1)S(1)}, u32[]{:S(2)}, u32[]{:S(2)}) collective-permute-start(bf16[2,2,48,256]{3,2,1,0:T(8,128)(2,1)S(1)} %pad_maximum_fusion.16), channel_id=1, source_target_pairs={{0,2},{1,3},{2,0},{3,1},{4,6},{5,7},{6,4},{7,5},{8,10},{9,11},{10,... | collective-permute-start | bytes 294920 | tf_op jit(solution)/shard_map/ppermute | solution.py:195
  34.7 4.7 %collective-permute-start.4 = (bf16[2,2,48,256]{3,2,1,0:T(8,128)(2,1)S(1)}, bf16[2,2,48,256]{3,2,1,0:T(8,128)(2,1)S(1)}, u32[]{:S(2)}, u32[]{:S(2)}) collective-permute-start(bf16[2,2,48,256]{3,2,1,0:T(8,128)(2,1)S(1)} %pad_maximum_fusion.15), channel_id=1, source_target_pairs={{0,2},{1,3},{2,0},{3,1},{4,6},{5,7},{6,4},{7,5},{8,10},{9,11},{10,... | collective-permute-start | bytes 294920 | tf_op jit(solution)/shard_map/ppermute | solution.py:195
  37.1 2.5 %collective-permute-start.12 = (bf16[192,512]{1,0:T(8,128)(2,1)S(1)}, bf16[192,512]{1,0:T(8,128)(2,1)S(1)}, u32[]{:S(2)}, u32[]{:S(2)}) collective-permute-start(bf16[192,512]{1,0:T(8,128)(2,1)S(1)} %bitcast.183), channel_id=1, source_target_pairs={{0,1},{1,0},{2,3},{3,2},{4,5},{5,4},{6,7},{7,6},{8,9},{9,8},{10,11... | collective-permute-start | bytes 589832 | tf_op jit(solution)/shard_map/ppermute | solution.py:195
  39.5 1.5 %collective-permute-start.5 = (bf16[192,512]{1,0:T(8,128)(2,1)S(1)}, bf16[192,512]{1,0:T(8,128)(2,1)S(1)}, u32[]{:S(2)}, u32[]{:S(2)}) collective-permute-start(bf16[192,512]{1,0:T(8,128)(2,1)S(1)} %bitcast.185), channel_id=1, source_target_pairs={{0,1},{1,0},{2,3},{3,2},{4,5},{5,4},{6,7},{7,6},{8,9},{9,8},{10,11... | collective-permute-start | bytes 589832 | tf_op jit(solution)/shard_map/ppermute | solution.py:195
  42.4 20.6 %collective-permute-start.18 = (bf16[2,24,896]{2,1,0:T(8,128)(2,1)S(1)}, bf16[2,24,896]{2,1,0:T(8,128)(2,1)S(1)}, u32[]{:S(2)}, u32[]{:S(2)}) collective-permute-start(bf16[2,24,896]{2,1,0:T(8,128)(2,1)S(1)} %get-tuple-element.12), channel_id=1, source_target_pairs={{0,14},{1,15},{2,12},{3,13},{4,10},{5,11},{6,8},{7,9},{8,6},{9,7},... | collective-permute-start | bytes 258056 | tf_op jit(solution)/shard_map/ppermute | solution.py:203
  45.2 8.0 %collective-permute-start.13 = (bf16[2,2,24,896]{3,2,0,1:T(8,128)(2,1)S(1)}, bf16[2,2,24,896]{3,2,0,1:T(8,128)(2,1)S(1)}, u32[]{:S(2)}, u32[]{:S(2)}) collective-permute-start(bf16[2,2,24,896]{3,2,0,1:T(8,128)(2,1)S(1)} %pad_maximum_fusion.9), channel_id=1, source_target_pairs={{0,2},{1,3},{2,0},{3,1},{4,6},{5,7},{6,4},{7,5},{8,10},{9,11},{10,... | collective-permute-start | bytes 516104 | tf_op jit(solution)/shard_map/ppermute | solution.py:195
  46.4 16.5 %collective-permute-start.15 = (bf16[2,24,896]{2,1,0:T(8,128)(2,1)S(1)}, bf16[2,24,896]{2,1,0:T(8,128)(2,1)S(1)}, u32[]{:S(2)}, u32[]{:S(2)}) collective-permute-start(bf16[2,24,896]{2,1,0:T(8,128)(2,1)S(1)} %get-tuple-element.58), channel_id=1, source_target_pairs={{0,8},{4,12},{8,0},{12,4},{1,9},{5,13},{9,1},{13,5},{2,10},{6,14},... | collective-permute-start | bytes 258056 | tf_op jit(solution)/shard_map/ppermute | solution.py:192
  46.9 16.1 %collective-permute-start.17 = (bf16[2,24,896]{2,1,0:T(8,128)(2,1)S(1)}, bf16[2,24,896]{2,1,0:T(8,128)(2,1)S(1)}, u32[]{:S(2)}, u32[]{:S(2)}) collective-permute-start(bf16[2,24,896]{2,1,0:T(8,128)(2,1)S(1)} %get-tuple-element.59), channel_id=1, source_target_pairs={{0,10},{1,11},{2,8},{3,9},{4,14},{5,15},{6,12},{7,13},{8,2},{9,3},... | collective-permute-start | bytes 258056 | tf_op jit(solution)/shard_map/ppermute | solution.py:203
  49.7 13.3 %collective-permute-start.16 = (bf16[2,24,896]{2,1,0:T(8,128)(2,1)S(1)}, bf16[2,24,896]{2,1,0:T(8,128)(2,1)S(1)}, u32[]{:S(2)}, u32[]{:S(2)}) collective-permute-start(bf16[2,24,896]{2,1,0:T(8,128)(2,1)S(1)} %get-tuple-element.35), channel_id=1, source_target_pairs={{0,12},{4,8},{8,4},{12,0},{1,13},{5,9},{9,5},{13,1},{2,14},{6,10},... | collective-permute-start | bytes 258056 | tf_op jit(solution)/shard_map/ppermute | solution.py:192
  53.3 9.6 %collective-permute-start.14 = (bf16[2,2,24,896]{3,2,1,0:T(8,128)(2,1)S(1)}, bf16[2,2,24,896]{3,2,1,0:T(8,128)(2,1)S(1)}, u32[]{:S(2)}, u32[]{:S(2)}) collective-permute-start(bf16[2,2,24,896]{3,2,1,0:T(8,128)(2,1)S(1)} %pad_maximum_fusion.10), channel_id=1, source_target_pairs={{0,4},{4,0},{8,12},{12,8},{1,5},{5,1},{9,13},{13,9},{2,6},{6,2},{1... | collective-permute-start | bytes 516104 | tf_op jit(solution)/shard_map/ppermute | solution.py:192
  63.0 1.7 %collective-permute-start.19 = (bf16[8,24,896]{2,1,0:T(8,128)(2,1)S(1)}, bf16[8,24,896]{2,1,0:T(8,128)(2,1)S(1)}, u32[]{:S(2)}, u32[]{:S(2)}) collective-permute-start(bf16[8,24,896]{2,1,0:T(8,128)(2,1)S(1)} %get-tuple-element.49), channel_id=1, source_target_pairs={{0,1},{1,0},{2,3},{3,2},{4,5},{5,4},{6,7},{7,6},{8,9},{9,8},{10,11... | collective-permute-start | bytes 1032200 | tf_op jit(solution)/shard_map/ppermute | solution.py:195
  65.4 0.9 %copy-start.2 = (f32[64,3584]{1,0:T(8,128)}, f32[64,3584]{1,0:T(8,128)S(1)}, u32[]{:S(2)}) copy-start(f32[64,3584]{1,0:T(8,128)S(1)} %fusion.21) | copy-start | bytes 2752516

commit v9 on v8

--- a/solution.py
+++ b/solution.py
@@ -7,7 +7,7 @@
 import functools
 
 EXP_POD = 8
-CFG = {'C': [[0, 3], [1, 2]], 'H': [[0], [1]], 'order': [('z', 3), ('z', 1), ('x', (3,)), ('z', 2), ('x', (2,)), ('z', 0), ('x', (0,)), ('c', 0), ('h', 0), ('r', 3), ('x', (1,)), ('c', 1), ('h', 1), ('r', 2), ('t', (0, 1)), ('w', (0, 1, 2, 3))], 'gates': {'cs1': ['zd3', 'xd01'], 'td01': ['xd01'], 'rd30': ['hd11'], 'hs1': ['xd11'], 'rs31': ['cd0']}, 'apart': False}
+CFG = {'C': [[0, 3], [1, 2]], 'H': [[0], [1]], 'order': [('z', 0), ('z', 1), ('z', 2), ('z', 3), ('x', (0,)), ('x', (1,)), ('x', (2,)), ('x', (3,)), ('c', 0), ('c', 1), ('h', 0), ('h', 1), ('a', 0)], 'gates': {}, 'apart': False}
 
 
 def pick_kernel(n_out, capacity, pods, tokens_hbm, routes_hbm, fixed_hbm, *refs):
@@ -160,17 +160,27 @@
 
     down_same, down_other = down_rows(0), down_rows(1)
     pods = (z ^ jnp.arange(n_out, dtype=jnp.int32)) * EXP_POD
+
+    def places(targets):
+        hit_mask = routes[:, :, None] == targets[None, None, :]
+        fixed = jnp.sum(jnp.where(hit_mask, combine_fixed[:, :, None], 0), axis=1)
+        is_live = jnp.any(hit_mask, axis=1).astype(jnp.int32)
+        slot_index = jnp.where(is_live == 1, jnp.cumsum(is_live, axis=0) - 1, -1)
+        placing = slot_index[:, :, None] == jnp.arange(capacity, dtype=jnp.int32)[None, None, :]
+        return placing, fixed
+
+    def pod_weights(targets):
+        placing, fixed = places(targets)
+        spread = jnp.where(placing, fixed[:, :, None], 0).reshape(tok_rows, -1)
+        return (spread >> 8).astype(jnp.bfloat16), (spread & 255).astype(jnp.bfloat16)
+
     in_kernels = False and capacity % 8 == 0 and part_out % 128 == 0
     if in_kernels:
         *panels, high, low = pick_call(tokens, routes, combine_fixed, pods, n_out, capacity)
         high = high.reshape(-1, tok_rows).T.astype(jnp.bfloat16)
         low = low.reshape(-1, tok_rows).T.astype(jnp.bfloat16)
     else:
-        hit_mask = routes[:, :, None] == pods[None, None, :]
-        fixed = jnp.sum(jnp.where(hit_mask, combine_fixed[:, :, None], 0), axis=1)
-        is_live = jnp.any(hit_mask, axis=1).astype(jnp.int32)
-        slot_index = jnp.where(is_live == 1, jnp.cumsum(is_live, axis=0) - 1, -1)
-        placing = slot_index[:, :, None] == jnp.arange(capacity, dtype=jnp.int32)[None, None, :]
+        placing, fixed = places(pods)
         panels = jnp.einsum(
             "tqc,td->qcd", placing.astype(jnp.bfloat16), tokens, preferred_element_type=jnp.float32
         ).astype(jnp.bfloat16)
@@ -288,6 +298,22 @@
                     moved = gated(f"rd{s}0", moved)
                     for x in range(n_chip):
                         landed[s, x] = moved[x]
+        elif kind == "a":
+            parts = []
+            for s in range(4):
+                block = outs[s].reshape(n_loc, span, capacity, part_out)
+                parts.append(block.transpose(1, 0, 2, 3) if span > 1 else block.reshape(1, *block.shape[:1], *block.shape[2:]))
+            blocks = jnp.concatenate(parts, axis=0).reshape(n_out * n_loc, capacity, part_out)
+            place = z * n_loc + l
+            blocks = jnp.concatenate(
+                [lax.dynamic_slice_in_dim(blocks, place ^ i, 1, 0) for i in range(n_out * n_loc)], axis=0
+            )
+            blocks = lax.all_to_all(blocks, ("outer", "local"), split_axis=0, concat_axis=0, tiled=True)
+            blocks = blocks.reshape(n_out, n_loc, capacity, part_out)
+            weights = jnp.concatenate(pod_weights(jnp.arange(n_out, dtype=jnp.int32) * EXP_POD), axis=0)
+            returned = blocks.transpose(0, 2, 1, 3).reshape(n_out * capacity, width)
+            both = jnp.dot(weights, returned, preferred_element_type=jnp.float32)
+            return both[:tok_rows] * (1.0 / 256.0) + both[tok_rows:] * (1.0 / 65536.0)
         elif kind == "q":
             a, b = arg
             core = l & 1

time: 67.4 us -> 75.7 us (1.12)
  local copies, waits for them, and re-layouts: 4.01 us -> 13.5 us
  starting transfers between devices: 22.3 us -> 17.7 us
  waiting for transfers between devices: 30.3 us -> 34.4 us
  matrix products: 8.71 us -> 6.82 us
  other arithmetic: 1.45 us -> 2.64 us
    all_to_all x0 -> x1, waiting for transfers between devices: none -> 16.8 us  [per_device(): lax.all_to_all(blocks, ('outer', 'local'), split_axis=0, concat_axis=0, t...]
    ppermute x6 -> x3, waiting for transfers between devices: 17 us -> 7.97 us  [outer_xor(): lax.ppermute(p, 'outer', [(i, i ^ t) for i in range(n_out)])]
    unnamed x19 -> x27, local copies, waits for them, and re-layouts: 1.79 us -> 10.4 us
    ppermute x2 -> x0, starting transfers between devices: 5.62 us -> none  [move(): return lax.ppermute(p, ('outer', 'local'), pairs)]
    all_to_all x0 -> x1, starting transfers between devices: none -> 4.13 us  [per_device(): lax.all_to_all(blocks, ('outer', 'local'), split_axis=0, concat_axis=0, t...]
    ppermute x12 -> x10, waiting for transfers between devices: 13.3 us -> 9.55 us  [local_xor(): return lax.ppermute(v, 'local', [(i, i ^ m) for i in range(n_loc)])]
    ppermute x6 -> x3, starting transfers between devices: 7.77 us -> 5.68 us  [outer_xor(): lax.ppermute(p, 'outer', [(i, i ^ t) for i in range(n_out)])]
    dot_general x8 -> x1, matrix products: 2.4 us -> 0.49 us  [per_device(): both = jnp.dot(weights, returned, preferred_element_type=jnp.float32)]
  transfers between devices with their start and end apart: 20 -> 14, of which waited for: 10 -> 8; matrix products, arithmetic and copies ran while one was open for 10% -> 8% of each run, Pallas kernels for 0% -> 0%
where the time goes in v9:
time: 75.7 us; the launch traced here: 75.4 us
  waiting for transfers between devices  34.4 us (45%)
  starting transfers between devices  17.7 us (23%)
  local copies, waits for them, and re-layouts  13.5 us (18%)
  matrix products  6.82 us (9%)
  other arithmetic  2.64 us (3%)
    all_to_all x1, waiting for transfers between devices, per_device(): lax.all_to_all(blocks, ('outer', 'local'), split_axis=0, concat_axis=0, t...  16.8 us
    unnamed x27, local copies, waits for them, and re-layouts  10.4 us
    ppermute x10, waiting for transfers between devices, local_xor(): return lax.ppermute(v, 'local', [(i, i ^ m) for i in range(n_loc)])  9.55 us
    ppermute x3, waiting for transfers between devices, outer_xor(): lax.ppermute(p, 'outer', [(i, i ^ t) for i in range(n_out)])  7.97 us
    ppermute x10, starting transfers between devices, local_xor(): return lax.ppermute(v, 'local', [(i, i ^ m) for i in range(n_loc)])  7.88 us
    ppermute x3, starting transfers between devices, outer_xor(): lax.ppermute(p, 'outer', [(i, i ^ t) for i in range(n_out)])  5.68 us
    all_to_all x1, starting transfers between devices, per_device(): lax.all_to_all(blocks, ('outer', 'local'), split_axis=0, concat_axis=0, t...  4.13 us
    dot_general x4, matrix products, first_half(): up_proj = jnp.dot(rows, up_local, preferred_element_type=jnp.float32)  1.73 us
  transfers between devices with their start and end apart: 14, of which 8 were waited for; matrix products, arithmetic and copies ran while one was open for 8% of the time, Pallas kernels for 0%

profile of v9, /device:TPU:0, one launch (start us, length us, event | category | flops | bytes accessed | tf_op | source)
XLA Modules:
  0.0 75.4 jit_solution(7286167950467698332)
XLA Ops:
  0.0 0.9 %compare_reduce_fusion = (pred[64,4]{0,1:T(4,128)(4,1)S(1)}, pred[64,4]{0,1:T(4,128)(4,1)S(1)}) fusion(s32[64,8]{0,1:T(8,128)} %param.7, s32[4]{0:T(128)S(1)} %iota_multiply_fusion, s32[4]{0:T(128)S(1)} %xor_multiply_fusion), kind=kLoop, calls=%fused_computation.82 | loop fusion | flops 7680 | bytes 2592 | tf_op jit(solution)/shard_map/reduce_or | solution.py:167
  1.5 1.3 %convolution_convert_fusion = bf16[4,24,3584]{2,1,0:T(8,128)(2,1)S(1)} fusion(bf16[64,3584]{1,0:T(8,128)(2,1)} %param.6, s32[64,4]{0,1:T(4,128)S(1)} %get-tuple-element.29), kind=kOutput, calls=%fused_computation | convolution fusion | flops 44390400 | bytes 1147904 | tf_op jit(solution)/shard_map/tqc,td->qcd/dot_general | solution.py:184
  2.9 3.1 %collective-permute-start.6 = (bf16[24,3584]{1,0:T(8,128)(2,1)S(1)}, bf16[24,3584]{1,0:T(8,128)(2,1)S(1)}, u32[]{:S(2)}, u32[]{:S(2)}) collective-permute-start(bf16[24,3584]{1,0:T(8,128)(2,1)S(1)} %get-tuple-element.14), channel_id=1, source_target_pairs={{0,4},{4,0},{8,12},{12,8},{1,5},{5,1},{9,13},{13,9},{2,6},{6,2},{1... | collective-permute-start | bytes 516104 | tf_op jit(solution)/shard_map/ppermute | solution.py:202
  6.0 2.6 %collective-permute-start.7 = (bf16[24,3584]{1,0:T(8,128)(2,1)S(1)}, bf16[24,3584]{1,0:T(8,128)(2,1)S(1)}, u32[]{:S(2)}, u32[]{:S(2)}) collective-permute-start(bf16[24,3584]{1,0:T(8,128)(2,1)S(1)} %get-tuple-element.13), channel_id=1, source_target_pairs={{0,8},{4,12},{8,0},{12,4},{1,9},{5,13},{9,1},{13,5},{2,10},{6,14},... | collective-permute-start | bytes 516104 | tf_op jit(solution)/shard_map/ppermute | solution.py:202
  8.6 1.7 %collective-permute-start.1 = (bf16[24,3584]{1,0:T(8,128)(2,1)S(1)}, bf16[24,3584]{1,0:T(8,128)(2,1)S(1)}, u32[]{:S(2)}, u32[]{:S(2)}) collective-permute-start(bf16[24,3584]{1,0:T(8,128)(2,1)S(1)} %get-tuple-element.16), channel_id=1, source_target_pairs={{0,2},{1,3},{2,0},{3,1},{4,6},{5,7},{6,4},{7,5},{8,10},{9,11},{10,... | collective-permute-start | bytes 516104 | tf_op jit(solution)/shard_map/ppermute | solution.py:205
  10.3 1.6 %dynamic-slice_bitcast_fusion.3 = (bf16[256,896]{1,0:T(8,128)(2,1)S(1)}, bf16[256,896]{1,0:T(8,128)(2,1)S(1)}, bf16[256,896]{1,0:T(8,128)(2,1)S(1)}, bf16[256,896]{1,0:T(8,128)(2,1)S(1)}) fusion(bf16[1,1024,896]{2,1,0:T(8,128)(2,1)} %param.11, s32[]{:T(128)S(6)} %select_n.88, s32[]{:T(128)S(6)} %select_n.89, s32[]{:T(128)S(6)} %select_n.91, s32[]{:T(128)S(6)} %select_n.90), kind=kLoop, calls=%fused_computation.36 | loop fusion | bytes 3670032 | tf_op jit(solution)/shard_map/dynamic_slice | solution.py:155
  11.9 1.2 %collective-permute-done.6 = bf16[24,3584]{1,0:T(8,128)(2,1)S(1)} collective-permute-done((bf16[24,3584]{1,0:T(8,128)(2,1)S(1)}, bf16[24,3584]{1,0:T(8,128)(2,1)S(1)}, u32[]{:S(2)}, u32[]{:S(2)}) %collective-permute-start.6) | collective-permute-done | bytes 172064 | tf_op jit(solution)/shard_map/ppermute | solution.py:202
  13.1 1.7 %collective-permute-start.8 = (bf16[24,3584]{1,0:T(8,128)(2,1)S(1)}, bf16[24,3584]{1,0:T(8,128)(2,1)S(1)}, u32[]{:S(2)}, u32[]{:S(2)}) collective-permute-start(bf16[24,3584]{1,0:T(8,128)(2,1)S(1)} %collective-permute-done.6), channel_id=1, source_target_pairs={{0,2},{1,3},{2,0},{3,1},{4,6},{5,7},{6,4},{7,5},{8,10},{9,11},{10,... | collective-permute-start | bytes 516104 | tf_op jit(solution)/shard_map/ppermute | solution.py:205
  14.8 6.8 %collective-permute-done.7 = bf16[24,3584]{1,0:T(8,128)(2,1)S(1)} collective-permute-done((bf16[24,3584]{1,0:T(8,128)(2,1)S(1)}, bf16[24,3584]{1,0:T(8,128)(2,1)S(1)}, u32[]{:S(2)}, u32[]{:S(2)}) %collective-permute-start.7) | collective-permute-done | bytes 172064 | tf_op jit(solution)/shard_map/ppermute | solution.py:202
  21.6 1.5 %collective-permute-start.9 = (bf16[24,3584]{1,0:T(8,128)(2,1)S(1)}, bf16[24,3584]{1,0:T(8,128)(2,1)S(1)}, u32[]{:S(2)}, u32[]{:S(2)}) collective-permute-start(bf16[24,3584]{1,0:T(8,128)(2,1)S(1)} %collective-permute-done.7), channel_id=1, source_target_pairs={{0,2},{1,3},{2,0},{3,1},{4,6},{5,7},{6,4},{7,5},{8,10},{9,11},{10,... | collective-permute-start | bytes 516104 | tf_op jit(solution)/shard_map/ppermute | solution.py:205
  23.6 3.3 %collective-permute-done.9 = bf16[24,3584]{1,0:T(8,128)(2,1)S(1)} collective-permute-done((bf16[24,3584]{1,0:T(8,128)(2,1)S(1)}, bf16[24,3584]{1,0:T(8,128)(2,1)S(1)}, u32[]{:S(2)}, u32[]{:S(2)}) %collective-permute-start.9) | collective-permute-done | bytes 172064 | tf_op jit(solution)/shard_map/ppermute | solution.py:205
  27.1 1.7 %collective-permute-done.2 = bf16[24,3584]{1,0:T(8,128)(2,1)S(1)} collective-permute-done((bf16[24,3584]{1,0:T(8,128)(2,1)S(1)}, bf16[24,3584]{1,0:T(8,128)(2,1)S(1)}, u32[]{:S(2)}, u32[]{:S(2)}) %collective-permute-start.2) | collective-permute-done | bytes 172064 | tf_op jit(solution)/shard_map/ppermute | solution.py:205
  29.4 1.0 %copy-done.1 = bf16[1,3584,256]{2,1,0:T(8,128)(2,1)S(1)} copy-done((bf16[1,3584,256]{2,1,0:T(8,128)(2,1)S(1)}, bf16[1,3584,256]{2,1,0:T(8,128)(2,1)}, u32[]{:S(2)}) %copy-start.1) | copy-done | bytes 1835032
  32.6 1.6 %collective-permute-start.11 = (bf16[2,2,48,256]{3,2,1,0:T(8,128)(2,1)S(1)}, bf16[2,2,48,256]{3,2,1,0:T(8,128)(2,1)S(1)}, u32[]{:S(2)}, u32[]{:S(2)}) collective-permute-start(bf16[2,2,48,256]{3,2,1,0:T(8,128)(2,1)S(1)} %pad_maximum_fusion.11), channel_id=1, source_target_pairs={{0,2},{1,3},{2,0},{3,1},{4,6},{5,7},{6,4},{7,5},{8,10},{9,11},{10,... | collective-permute-start | bytes 294920 | tf_op jit(solution)/shard_map/ppermute | solution.py:205
  35.6 2.0 %collective-permute-done.11 = bf16[2,2,48,256]{3,2,1,0:T(8,128)(2,1)S(1)} collective-permute-done((bf16[2,2,48,256]{3,2,1,0:T(8,128)(2,1)S(1)}, bf16[2,2,48,256]{3,2,1,0:T(8,128)(2,1)S(1)}, u32[]{:S(2)}, u32[]{:S(2)}) %collective-permute-start.11) | collective-permute-done | bytes 98336 | tf_op jit(solution)/shard_map/ppermute | solution.py:205
  37.7 2.0 %collective-permute-done.4 = bf16[2,2,48,256]{3,2,1,0:T(8,128)(2,1)S(1)} collective-permute-done((bf16[2,2,48,256]{3,2,1,0:T(8,128)(2,1)S(1)}, bf16[2,2,48,256]{3,2,1,0:T(8,128)(2,1)S(1)}, u32[]{:S(2)}, u32[]{:S(2)}) %collective-permute-start.4) | collective-permute-done | bytes 98336 | tf_op jit(solution)/shard_map/ppermute | solution.py:205
  42.3 0.6 constant_dynamic-update-slice_fusion.19
  42.9 0.6 constant_dynamic-update-slice_fusion.18
  43.5 0.6 constant_dynamic-update-slice_fusion.17
  44.2 0.6 constant_dynamic-update-slice_fusion.16
  44.8 0.6 constant_dynamic-update-slice_fusion.15
  45.4 0.6 constant_dynamic-update-slice_fusion.14
  46.0 0.6 constant_dynamic-update-slice_fusion.13
  46.7 0.6 constant_dynamic-update-slice_fusion.12
  47.3 0.6 constant_dynamic-update-slice_fusion.11
  47.9 0.6 constant_dynamic-update-slice_fusion.10
  48.5 0.6 constant_dynamic-update-slice_fusion.9
  49.1 0.6 constant_dynamic-update-slice_fusion.8
  51.6 0.6 constant_dynamic-update-slice_fusion.4
  52.3 4.1 %all-to-all-start = ((bf16[16,24,896]{2,1,0:T(8,128)(2,1)}), bf16[16,24,896]{2,1,0:T(8,128)(2,1)S(1)}, u32[]{:S(2)}, u32[]{:S(2)}) async-start(bf16[16,24,896]{2,1,0:T(8,128)(2,1)} %constant_dynamic-update-slice_fusion.4), calls=%async_computation | async-start | bytes 1376256 | tf_op jit(solution)/shard_map/all_to_all | solution.py:311
  56.7 16.8 %all-to-all-done = bf16[16,24,896]{2,1,0:T(8,128)(2,1)S(1)} async-done(((bf16[16,24,896]{2,1,0:T(8,128)(2,1)}), bf16[16,24,896]{2,1,0:T(8,128)(2,1)S(1)}, u32[]{:S(2)}, u32[]{:S(2)}) %all-to-all-start) | async-done | bytes 688160 | tf_op jit(solution)/shard_map/all_to_all | solution.py:311
  74.4 1.0 %fusion.18 = f32[64,3584]{1,0:T(8,128)} fusion(f32[128,3584]{1,0:T(8,128)S(1)} %fusion.26), kind=kLoop, calls=%fused_computation.22 | loop fusion | flops 688128 | bytes 2752512 | tf_op jit(solution)/shard_map/add | solution.py:316
  (73 shorter events, 11.0 us)
Async XLA Ops:
  0.0 29.0 %copy-start = (bf16[1,3584,256]{2,1,0:T(8,128)(2,1)S(1)}, bf16[1,3584,256]{2,1,0:T(8,128)(2,1)}, u32[]{:S(2)}) copy-start(bf16[1,3584,256]{2,1,0:T(8,128)(2,1)} %param.9) | copy-start | bytes 5505028
  2.9 10.2 %collective-permute-start.6 = (bf16[24,3584]{1,0:T(8,128)(2,1)S(1)}, bf16[24,3584]{1,0:T(8,128)(2,1)S(1)}, u32[]{:S(2)}, u32[]{:S(2)}) collective-permute-start(bf16[24,3584]{1,0:T(8,128)(2,1)S(1)} %get-tuple-element.14), channel_id=1, source_target_pairs={{0,4},{4,0},{8,12},{12,8},{1,5},{5,1},{9,13},{13,9},{2,6},{6,2},{1... | collective-permute-start | bytes 516104 | tf_op jit(solution)/shard_map/ppermute | solution.py:202
  6.0 15.6 %collective-permute-start.7 = (bf16[24,3584]{1,0:T(8,128)(2,1)S(1)}, bf16[24,3584]{1,0:T(8,128)(2,1)S(1)}, u32[]{:S(2)}, u32[]{:S(2)}) collective-permute-start(bf16[24,3584]{1,0:T(8,128)(2,1)S(1)} %get-tuple-element.13), channel_id=1, source_target_pairs={{0,8},{4,12},{8,0},{12,4},{1,9},{5,13},{9,1},{13,5},{2,10},{6,14},... | collective-permute-start | bytes 516104 | tf_op jit(solution)/shard_map/ppermute | solution.py:202
  8.6 14.5 %collective-permute-start = (bf16[24,3584]{1,0:T(8,128)(2,1)S(1)}, bf16[24,3584]{1,0:T(8,128)(2,1)S(1)}, u32[]{:S(2)}, u32[]{:S(2)}) collective-permute-start(bf16[24,3584]{1,0:T(8,128)(2,1)S(1)} %get-tuple-element.15), channel_id=1, source_target_pairs={{0,12},{4,8},{8,4},{12,0},{1,13},{5,9},{9,5},{13,1},{2,14},{6,10},... | collective-permute-start | bytes 516104 | tf_op jit(solution)/shard_map/ppermute | solution.py:202
  8.6 18.5 %collective-permute-start.1 = (bf16[24,3584]{1,0:T(8,128)(2,1)S(1)}, bf16[24,3584]{1,0:T(8,128)(2,1)S(1)}, u32[]{:S(2)}, u32[]{:S(2)}) collective-permute-start(bf16[24,3584]{1,0:T(8,128)(2,1)S(1)} %get-tuple-element.16), channel_id=1, source_target_pairs={{0,2},{1,3},{2,0},{3,1},{4,6},{5,7},{6,4},{7,5},{8,10},{9,11},{10,... | collective-permute-start | bytes 516104 | tf_op jit(solution)/shard_map/ppermute | solution.py:205
  13.1 10.5 %collective-permute-start.8 = (bf16[24,3584]{1,0:T(8,128)(2,1)S(1)}, bf16[24,3584]{1,0:T(8,128)(2,1)S(1)}, u32[]{:S(2)}, u32[]{:S(2)}) collective-permute-start(bf16[24,3584]{1,0:T(8,128)(2,1)S(1)} %collective-permute-done.6), channel_id=1, source_target_pairs={{0,2},{1,3},{2,0},{3,1},{4,6},{5,7},{6,4},{7,5},{8,10},{9,11},{10,... | collective-permute-start | bytes 516104 | tf_op jit(solution)/shard_map/ppermute | solution.py:205
  21.6 5.4 %collective-permute-start.9 = (bf16[24,3584]{1,0:T(8,128)(2,1)S(1)}, bf16[24,3584]{1,0:T(8,128)(2,1)S(1)}, u32[]{:S(2)}, u32[]{:S(2)}) collective-permute-start(bf16[24,3584]{1,0:T(8,128)(2,1)S(1)} %collective-permute-done.7), channel_id=1, source_target_pairs={{0,2},{1,3},{2,0},{3,1},{4,6},{5,7},{6,4},{7,5},{8,10},{9,11},{10,... | collective-permute-start | bytes 516104 | tf_op jit(solution)/shard_map/ppermute | solution.py:205
  23.1 5.8 %collective-permute-start.2 = (bf16[24,3584]{1,0:T(8,128)(2,1)S(1)}, bf16[24,3584]{1,0:T(8,128)(2,1)S(1)}, u32[]{:S(2)}, u32[]{:S(2)}) collective-permute-start(bf16[24,3584]{1,0:T(8,128)(2,1)S(1)} %collective-permute-done), channel_id=1, source_target_pairs={{0,2},{1,3},{2,0},{3,1},{4,6},{5,7},{6,4},{7,5},{8,10},{9,11},{10,... | collective-permute-start | bytes 516104 | tf_op jit(solution)/shard_map/ppermute | solution.py:205
  27.0 4.7 %collective-permute-start.10 = (bf16[96,3584]{1,0:T(8,128)(2,1)S(1)}, bf16[96,3584]{1,0:T(8,128)(2,1)S(1)}, u32[]{:S(2)}, u32[]{:S(2)}) collective-permute-start(bf16[96,3584]{1,0:T(8,128)(2,1)S(1)} %constant_dynamic-update-slice_fusion), channel_id=1, source_target_pairs={{0,1},{1,0},{2,3},{3,2},{4,5},{5,4},{6,7},{7,6},{8,9},{9,8},{10,11... | collective-permute-start | bytes 2064392 | tf_op jit(solution)/shard_map/ppermute | solution.py:205
  28.9 1.5 %copy-start.1 = (bf16[1,3584,256]{2,1,0:T(8,128)(2,1)S(1)}, bf16[1,3584,256]{2,1,0:T(8,128)(2,1)}, u32[]{:S(2)}) copy-start(bf16[1,3584,256]{2,1,0:T(8,128)(2,1)} %param.10) | copy-start | bytes 5505028
  28.9 5.2 %collective-permute-start.3 = (bf16[96,3584]{1,0:T(8,128)(2,1)S(1)}, bf16[96,3584]{1,0:T(8,128)(2,1)S(1)}, u32[]{:S(2)}, u32[]{:S(2)}) collective-permute-start(bf16[96,3584]{1,0:T(8,128)(2,1)S(1)} %pad_maximum_fusion.2), channel_id=1, source_target_pairs={{0,1},{1,0},{2,3},{3,2},{4,5},{5,4},{6,7},{7,6},{8,9},{9,8},{10,11... | collective-permute-start | bytes 2064392 | tf_op jit(solution)/shard_map/ppermute | solution.py:205
  32.6 5.0 %collective-permute-start.11 = (bf16[2,2,48,256]{3,2,1,0:T(8,128)(2,1)S(1)}, bf16[2,2,48,256]{3,2,1,0:T(8,128)(2,1)S(1)}, u32[]{:S(2)}, u32[]{:S(2)}) collective-permute-start(bf16[2,2,48,256]{3,2,1,0:T(8,128)(2,1)S(1)} %pad_maximum_fusion.11), channel_id=1, source_target_pairs={{0,2},{1,3},{2,0},{3,1},{4,6},{5,7},{6,4},{7,5},{8,10},{9,11},{10,... | collective-permute-start | bytes 294920 | tf_op jit(solution)/shard_map/ppermute | solution.py:205
  35.0 4.7 %collective-permute-start.4 = (bf16[2,2,48,256]{3,2,1,0:T(8,128)(2,1)S(1)}, bf16[2,2,48,256]{3,2,1,0:T(8,128)(2,1)S(1)}, u32[]{:S(2)}, u32[]{:S(2)}) collective-permute-start(bf16[2,2,48,256]{3,2,1,0:T(8,128)(2,1)S(1)} %pad_maximum_fusion.10), channel_id=1, source_target_pairs={{0,2},{1,3},{2,0},{3,1},{4,6},{5,7},{6,4},{7,5},{8,10},{9,11},{10,... | collective-permute-start | bytes 294920 | tf_op jit(solution)/shard_map/ppermute | solution.py:205
  37.6 2.2 %collective-permute-start.12 = (bf16[192,512]{1,0:T(8,128)(2,1)S(1)}, bf16[192,512]{1,0:T(8,128)(2,1)S(1)}, u32[]{:S(2)}, u32[]{:S(2)}) collective-permute-start(bf16[192,512]{1,0:T(8,128)(2,1)S(1)} %bitcast.140), channel_id=1, source_target_pairs={{0,1},{1,0},{2,3},{3,2},{4,5},{5,4},{6,7},{7,6},{8,9},{9,8},{10,11... | collective-permute-start | bytes 589832 | tf_op jit(solution)/shard_map/ppermute | solution.py:205
  39.7 1.5 %collective-permute-start.5 = (bf16[192,512]{1,0:T(8,128)(2,1)S(1)}, bf16[192,512]{1,0:T(8,128)(2,1)S(1)}, u32[]{:S(2)}, u32[]{:S(2)}) collective-permute-start(bf16[192,512]{1,0:T(8,128)(2,1)S(1)} %bitcast.138), channel_id=1, source_target_pairs={{0,1},{1,0},{2,3},{3,2},{4,5},{5,4},{6,7},{7,6},{8,9},{9,8},{10,11... | collective-permute-start | bytes 589832 | tf_op jit(solution)/shard_map/ppermute | solution.py:205
  42.2 14.3 %copy-start.2 = (s32[64,8]{0,1:T(8,128)S(1)}, s32[64,8]{0,1:T(8,128)}, u32[]{:S(2)}) copy-start(s32[64,8]{0,1:T(8,128)} %param.7) | copy-start | bytes 6148
  42.2 14.3 %copy-start.3 = (s32[64,8]{0,1:T(8,128)S(1)}, s32[64,8]{0,1:T(8,128)}, u32[]{:S(2)}) copy-start(s32[64,8]{0,1:T(8,128)} %param.8) | copy-start | bytes 6148
  52.3 21.3 %all-to-all-start = ((bf16[16,24,896]{2,1,0:T(8,128)(2,1)}), bf16[16,24,896]{2,1,0:T(8,128)(2,1)S(1)}, u32[]{:S(2)}, u32[]{:S(2)}) async-start(bf16[16,24,896]{2,1,0:T(8,128)(2,1)} %constant_dynamic-update-slice_fusion.4), calls=%async_computation | async-start | bytes 1376256 | tf_op jit(solution)/shard_map/all_to_all | solution.py:311

commit v10 on v8

--- a/solution.py
+++ b/solution.py
@@ -7,7 +7,7 @@
 import functools
 
 EXP_POD = 8
-CFG = {'C': [[0, 3], [1, 2]], 'H': [[0], [1]], 'order': [('z', 3), ('z', 1), ('x', (3,)), ('z', 2), ('x', (2,)), ('z', 0), ('x', (0,)), ('c', 0), ('h', 0), ('r', 3), ('x', (1,)), ('c', 1), ('h', 1), ('r', 2), ('t', (0, 1)), ('w', (0, 1, 2, 3))], 'gates': {'cs1': ['zd3', 'xd01'], 'td01': ['xd01'], 'rd30': ['hd11'], 'hs1': ['xd11'], 'rs31': ['cd0']}, 'apart': False}
+CFG = {'C': [[0, 1], [2, 3]], 'H': [[0], [1]], 'order': [('z', 0), ('z', 1), ('z', 2), ('z', 3), ('x', (0,)), ('x', (1,)), ('c', 0), ('x', (2,)), ('x', (3,)), ('h', 0), ('c', 1), ('h', 1), ('r', 2), ('r', 3), ('t', (0, 1)), ('w', (0, 1, 2, 3))], 'gates': {'rd10': ['rd20', 'rd21', 'rd30', 'rd31'], 'rs10': ['hd11'], 'xs21': ['cd0'], 'xs31': ['cd0'], 'ks0': ['xd21', 'xd31'], 'ts01': ['cd1']}, 'apart': False}
 
 
 def pick_kernel(n_out, capacity, pods, tokens_hbm, routes_hbm, fixed_hbm, *refs):

time: 67.4 us -> 73.5 us (1.091); the launches traced: 67.2 us -> 72 us
  waiting for transfers between devices: 30.3 us -> 34.3 us
    ppermute x12, waiting for transfers between devices: 13.3 us -> 18.1 us  [local_xor(): return lax.ppermute(v, 'local', [(i, i ^ m) for i in range(n_loc)])]
    ppermute x6, starting transfers between devices: 7.77 us -> 11.4 us  [outer_xor(): lax.ppermute(p, 'outer', [(i, i ^ t) for i in range(n_out)])]
    ppermute x2, starting transfers between devices: 5.62 us -> 2.49 us  [move(): return lax.ppermute(p, ('outer', 'local'), pairs)]
    ppermute x6, waiting for transfers between devices: 17 us -> 14.3 us  [outer_xor(): lax.ppermute(p, 'outer', [(i, i ^ t) for i in range(n_out)])]
    ppermute x2, waiting for transfers between devices: 0.01 us -> 1.87 us  [move(): return lax.ppermute(p, ('outer', 'local'), pairs)]
  transfers between devices with their start and end apart: 20 -> 20, of which waited for: 10 -> 11; matrix products, arithmetic and copies ran while one was open for 10% -> 10% of each run, Pallas kernels for 0% -> 0%
where the time goes in v10:
time: 73.5 us; the launch traced here: 72 us
  waiting for transfers between devices  34.3 us (47%)
  starting transfers between devices  23 us (31%)
  matrix products  8.71 us (12%)
  local copies, waits for them, and re-layouts  4.1 us (6%)
  other arithmetic  1.44 us (2%)
    ppermute x12, waiting for transfers between devices, local_xor(): return lax.ppermute(v, 'local', [(i, i ^ m) for i in range(n_loc)])  18.1 us
    ppermute x6, waiting for transfers between devices, outer_xor(): lax.ppermute(p, 'outer', [(i, i ^ t) for i in range(n_out)])  14.3 us
    ppermute x6, starting transfers between devices, outer_xor(): lax.ppermute(p, 'outer', [(i, i ^ t) for i in range(n_out)])  11.4 us
    ppermute x12, starting transfers between devices, local_xor(): return lax.ppermute(v, 'local', [(i, i ^ m) for i in range(n_loc)])  9.08 us
    ppermute x2, starting transfers between devices, move(): return lax.ppermute(p, ('outer', 'local'), pairs)  2.49 us
    unnamed x19, local copies, waits for them, and re-layouts  1.88 us
    ppermute x2, waiting for transfers between devices, move(): return lax.ppermute(p, ('outer', 'local'), pairs)  1.87 us
    dot_general x4, matrix products, first_half(): up_proj = jnp.dot(rows, up_local, preferred_element_type=jnp.float32)  1.73 us
  transfers between devices with their start and end apart: 20, of which 11 were waited for; matrix products, arithmetic and copies ran while one was open for 10% of the time, Pallas kernels for 0%

profile of v10, /device:TPU:0, one launch (start us, length us, event | category | flops | bytes accessed | tf_op | source)
XLA Modules:
  0.0 72.0 jit_solution(15938135471575114686)
XLA Ops:
  0.0 0.9 %compare_reduce_fusion = pred[64,4]{0,1:T(4,128)(4,1)S(1)} fusion(s32[64,8]{0,1:T(8,128)} %param.7, s32[4]{0:T(128)S(1)} %xor_multiply_fusion), kind=kLoop, calls=%fused_computation.114 | loop fusion | flops 3840 | bytes 2320 | tf_op jit(solution)/shard_map/reduce_or | solution.py:171
  1.2 1.3 %convolution_convert_fusion = bf16[4,24,3584]{2,1,0:T(8,128)(2,1)S(1)} fusion(bf16[64,3584]{1,0:T(8,128)(2,1)} %param.6, s32[64,4]{0,1:T(4,128)S(1)} %add_select_fusion), kind=kOutput, calls=%fused_computation | convolution fusion | flops 44390400 | bytes 1147904 | tf_op jit(solution)/shard_map/tqc,td->qcd/dot_general | solution.py:174
  2.6 3.1 %collective-permute-start = (bf16[24,3584]{1,0:T(8,128)(2,1)S(1)}, bf16[24,3584]{1,0:T(8,128)(2,1)S(1)}, u32[]{:S(2)}, u32[]{:S(2)}) collective-permute-start(bf16[24,3584]{1,0:T(8,128)(2,1)S(1)} %get-tuple-element.28), channel_id=1, source_target_pairs={{0,4},{4,0},{8,12},{12,8},{1,5},{5,1},{9,13},{13,9},{2,6},{6,2},{1... | collective-permute-start | bytes 516104 | tf_op jit(solution)/shard_map/ppermute | solution.py:192
  5.7 1.5 %collective-permute-start.1 = (bf16[24,3584]{1,0:T(8,128)(2,1)S(1)}, bf16[24,3584]{1,0:T(8,128)(2,1)S(1)}, u32[]{:S(2)}, u32[]{:S(2)}) collective-permute-start(bf16[24,3584]{1,0:T(8,128)(2,1)S(1)} %get-tuple-element.25), channel_id=1, source_target_pairs={{0,2},{1,3},{2,0},{3,1},{4,6},{5,7},{6,4},{7,5},{8,10},{9,11},{10,... | collective-permute-start | bytes 516104 | tf_op jit(solution)/shard_map/ppermute | solution.py:195
  7.2 2.5 %collective-permute-start.7 = (bf16[24,3584]{1,0:T(8,128)(2,1)S(1)}, bf16[24,3584]{1,0:T(8,128)(2,1)S(1)}, u32[]{:S(2)}, u32[]{:S(2)}) collective-permute-start(bf16[24,3584]{1,0:T(8,128)(2,1)S(1)} %get-tuple-element.26), channel_id=1, source_target_pairs={{0,12},{4,8},{8,4},{12,0},{1,13},{5,9},{9,5},{13,1},{2,14},{6,10},... | collective-permute-start | bytes 516104 | tf_op jit(solution)/shard_map/ppermute | solution.py:192
  10.1 1.9 %collective-permute-start.2 = (bf16[24,3584]{1,0:T(8,128)(2,1)S(1)}, bf16[24,3584]{1,0:T(8,128)(2,1)S(1)}, u32[]{:S(2)}, u32[]{:S(2)}) collective-permute-start(bf16[24,3584]{1,0:T(8,128)(2,1)S(1)} %collective-permute-done), channel_id=1, source_target_pairs={{0,2},{1,3},{2,0},{3,1},{4,6},{5,7},{6,4},{7,5},{8,10},{9,11},{10,... | collective-permute-start | bytes 516104 | tf_op jit(solution)/shard_map/ppermute | solution.py:195
  12.3 1.6 %dynamic-slice_bitcast_fusion.3 = (bf16[256,896]{1,0:T(8,128)(2,1)S(1)}, bf16[256,896]{1,0:T(8,128)(2,1)S(1)}, bf16[256,896]{1,0:T(8,128)(2,1)S(1)}, bf16[256,896]{1,0:T(8,128)(2,1)S(1)}) fusion(bf16[1,1024,896]{2,1,0:T(8,128)(2,1)} %param.11, s32[]{:T(128)S(6)} %select_n.44, s32[]{:T(128)S(6)} %select_n.45, s32[]{:T(128)S(6)} %select_n.47, s32[]{:T(128)S(6)} %select_n.46), kind=kLoop, calls=%fused_computation.48 | loop fusion | bytes 3670032 | tf_op jit(solution)/shard_map/dynamic_slice | solution.py:155
  13.9 1.8 %collective-permute-done.2 = bf16[24,3584]{1,0:T(8,128)(2,1)S(1)} collective-permute-done((bf16[24,3584]{1,0:T(8,128)(2,1)S(1)}, bf16[24,3584]{1,0:T(8,128)(2,1)S(1)}, u32[]{:S(2)}, u32[]{:S(2)}) %collective-permute-start.2) | collective-permute-done | bytes 172064 | tf_op jit(solution)/shard_map/ppermute | solution.py:195
  15.8 8.9 %collective-permute-done.5 = bf16[24,3584]{1,0:T(8,128)(2,1)S(1)} collective-permute-done((bf16[24,3584]{1,0:T(8,128)(2,1)S(1)}, bf16[24,3584]{1,0:T(8,128)(2,1)S(1)}, u32[]{:S(2)}, u32[]{:S(2)}) %collective-permute-start.5) | collective-permute-done | bytes 172064 | tf_op jit(solution)/shard_map/ppermute | solution.py:192
  24.7 0.4 fusion.14
  25.1 1.1 %copy-done.1 = bf16[1,3584,256]{2,1,0:T(8,128)(2,1)S(1)} copy-done((bf16[1,3584,256]{2,1,0:T(8,128)(2,1)S(1)}, bf16[1,3584,256]{2,1,0:T(8,128)(2,1)}, u32[]{:S(2)}) %copy-start.1) | copy-done | bytes 1835032
  27.1 0.4 multiply_convert_fusion.2
  27.5 0.6 collective-permute-start.4
  28.1 1.6 %collective-permute-start.8 = (bf16[24,3584]{1,0:T(8,128)(2,1)S(1)}, bf16[24,3584]{1,0:T(8,128)(2,1)S(1)}, u32[]{:S(2)}, u32[]{:S(2)}) collective-permute-start(bf16[24,3584]{1,0:T(8,128)(2,1)S(1)} %collective-permute-done.7), channel_id=1, source_target_pairs={{0,2},{1,3},{2,0},{3,1},{4,6},{5,7},{6,4},{7,5},{8,10},{9,11},{10,... | collective-permute-start | bytes 516104 | tf_op jit(solution)/shard_map/ppermute | solution.py:195
  29.7 0.5 collective-permute-start.6
  30.2 3.1 %collective-permute-done.4 = bf16[2,2,48,256]{3,2,1,0:T(8,128)(2,1)S(1)} collective-permute-done((bf16[2,2,48,256]{3,2,1,0:T(8,128)(2,1)S(1)}, bf16[2,2,48,256]{3,2,1,0:T(8,128)(2,1)S(1)}, u32[]{:S(2)}, u32[]{:S(2)}) %collective-permute-start.4) | collective-permute-done | bytes 98336 | tf_op jit(solution)/shard_map/ppermute | solution.py:195
  33.4 5.1 %collective-permute-done.6 = bf16[24,3584]{1,0:T(8,128)(2,1)S(1)} collective-permute-done((bf16[24,3584]{1,0:T(8,128)(2,1)S(1)}, bf16[24,3584]{1,0:T(8,128)(2,1)S(1)}, u32[]{:S(2)}, u32[]{:S(2)}) %collective-permute-start.6) | collective-permute-done | bytes 172064 | tf_op jit(solution)/shard_map/ppermute | solution.py:195
  39.0 0.6 collective-permute-start.9
  40.0 1.0 %collective-permute-done.9 = bf16[192,512]{1,0:T(8,128)(2,1)S(1)} collective-permute-done((bf16[192,512]{1,0:T(8,128)(2,1)S(1)}, bf16[192,512]{1,0:T(8,128)(2,1)S(1)}, u32[]{:S(2)}, u32[]{:S(2)}) %collective-permute-start.9) | collective-permute-done | bytes 196640 | tf_op jit(solution)/shard_map/ppermute | solution.py:195
  42.3 0.4 multiply_convert_fusion
  42.8 0.9 %collective-permute-start.12 = (bf16[2,2,48,256]{3,2,1,0:T(8,128)(2,1)S(1)}, bf16[2,2,48,256]{3,2,1,0:T(8,128)(2,1)S(1)}, u32[]{:S(2)}, u32[]{:S(2)}) collective-permute-start(bf16[2,2,48,256]{3,2,1,0:T(8,128)(2,1)S(1)} %pad_maximum_fusion.16), channel_id=1, source_target_pairs={{0,2},{1,3},{2,0},{3,1},{4,6},{5,7},{6,4},{7,5},{8,10},{9,11},{10,... | collective-permute-start | bytes 294920 | tf_op jit(solution)/shard_map/ppermute | solution.py:195
  43.6 1.3 %collective-permute-start.11 = (bf16[2,2,24,896]{3,2,0,1:T(8,128)(2,1)S(1)}, bf16[2,2,24,896]{3,2,0,1:T(8,128)(2,1)S(1)}, u32[]{:S(2)}, u32[]{:S(2)}) collective-permute-start(bf16[2,2,24,896]{3,2,0,1:T(8,128)(2,1)S(1)} %pad_maximum_fusion.9), channel_id=1, source_target_pairs={{0,2},{1,3},{2,0},{3,1},{4,6},{5,7},{6,4},{7,5},{8,10},{9,11},{10,... | collective-permute-start | bytes 516104 | tf_op jit(solution)/shard_map/ppermute | solution.py:195
  45.0 3.5 %collective-permute-done.12 = bf16[2,2,48,256]{3,2,1,0:T(8,128)(2,1)S(1)} collective-permute-done((bf16[2,2,48,256]{3,2,1,0:T(8,128)(2,1)S(1)}, bf16[2,2,48,256]{3,2,1,0:T(8,128)(2,1)S(1)}, u32[]{:S(2)}, u32[]{:S(2)}) %collective-permute-start.12) | collective-permute-done | bytes 98336 | tf_op jit(solution)/shard_map/ppermute | solution.py:195
  48.6 2.8 %collective-permute-done.11 = bf16[2,2,24,896]{3,2,0,1:T(8,128)(2,1)S(1)} collective-permute-done((bf16[2,2,24,896]{3,2,0,1:T(8,128)(2,1)S(1)}, bf16[2,2,24,896]{3,2,0,1:T(8,128)(2,1)S(1)}, u32[]{:S(2)}, u32[]{:S(2)}) %collective-permute-start.11) | collective-permute-done | bytes 172064 | tf_op jit(solution)/shard_map/ppermute | solution.py:195
  52.4 3.4 %collective-permute-start.15 = (bf16[2,24,896]{2,1,0:T(8,128)(2,1)S(1)}, bf16[2,24,896]{2,1,0:T(8,128)(2,1)S(1)}, u32[]{:S(2)}, u32[]{:S(2)}) collective-permute-start(bf16[2,24,896]{2,1,0:T(8,128)(2,1)S(1)} %get-tuple-element.40), channel_id=1, source_target_pairs={{0,8},{4,12},{8,0},{12,4},{1,9},{5,13},{9,1},{13,5},{2,10},{6,14},... | collective-permute-start | bytes 258056 | tf_op jit(solution)/shard_map/ppermute | solution.py:192
  56.1 2.3 %collective-permute-start.17 = (bf16[2,24,896]{2,1,0:T(8,128)(2,1)S(1)}, bf16[2,24,896]{2,1,0:T(8,128)(2,1)S(1)}, u32[]{:S(2)}, u32[]{:S(2)}) collective-permute-start(bf16[2,24,896]{2,1,0:T(8,128)(2,1)S(1)} %get-tuple-element.38), channel_id=1, source_target_pairs={{0,12},{4,8},{8,4},{12,0},{1,13},{5,9},{9,5},{13,1},{2,14},{6,10},... | collective-permute-start | bytes 258056 | tf_op jit(solution)/shard_map/ppermute | solution.py:192
  58.4 2.2 %collective-permute-start.18 = (bf16[2,24,896]{2,1,0:T(8,128)(2,1)S(1)}, bf16[2,24,896]{2,1,0:T(8,128)(2,1)S(1)}, u32[]{:S(2)}, u32[]{:S(2)}) collective-permute-start(bf16[2,24,896]{2,1,0:T(8,128)(2,1)S(1)} %get-tuple-element.37), channel_id=1, source_target_pairs={{0,14},{1,15},{2,12},{3,13},{4,10},{5,11},{6,8},{7,9},{8,6},{9,7},... | collective-permute-start | bytes 258056 | tf_op jit(solution)/shard_map/ppermute | solution.py:203
  60.6 5.1 %collective-permute-done.15 = bf16[2,24,896]{2,1,0:T(8,128)(2,1)S(1)} collective-permute-done((bf16[2,24,896]{2,1,0:T(8,128)(2,1)S(1)}, bf16[2,24,896]{2,1,0:T(8,128)(2,1)S(1)}, u32[]{:S(2)}, u32[]{:S(2)}) %collective-permute-start.15) | collective-permute-done | bytes 86048 | tf_op jit(solution)/shard_map/ppermute | solution.py:192
  65.8 1.9 %collective-permute-done.16 = bf16[2,24,896]{2,1,0:T(8,128)(2,1)S(1)} collective-permute-done((bf16[2,24,896]{2,1,0:T(8,128)(2,1)S(1)}, bf16[2,24,896]{2,1,0:T(8,128)(2,1)S(1)}, u32[]{:S(2)}, u32[]{:S(2)}) %collective-permute-start.16) | collective-permute-done | bytes 86048 | tf_op jit(solution)/shard_map/ppermute | solution.py:203
  68.6 0.9 %collective-permute-done.19 = bf16[8,24,896]{2,1,0:T(8,128)(2,1)S(1)} collective-permute-done((bf16[8,24,896]{2,1,0:T(8,128)(2,1)S(1)}, bf16[8,24,896]{2,1,0:T(8,128)(2,1)S(1)}, u32[]{:S(2)}, u32[]{:S(2)}) %collective-permute-start.19) | collective-permute-done | bytes 344096 | tf_op jit(solution)/shard_map/ppermute | solution.py:195
  70.4 0.7 copy-done.2
  71.1 0.9 %fusion.19 = f32[64,3584]{1,0:T(8,128)} fusion(f32[64,3584]{1,0:T(8,128)} %copy-done.2, s32[]{:T(128)S(6)} %select_n.51, f32[64,896]{1,0:T(8,128)S(1)} %convolution_multiply_fusion.1, bf16[64,96]{0,1:T(8,128)(2,1)S(1)} %get-tuple-element.58, bf16[24,896]{1,0:T(8,128)(2,1)S(1)} %get-tuple-element.30, bf16[24,896]{1,0:T(8,128)(2,1)S(1)} %get-tuple-element.31, ...), kind=kOutput, calls=%fused_computation.23 | convolution fusion | flops 11812864 | bytes 643076 | tf_op jit(solution)/shard_map/dot_general | solution.py:345
  (85 shorter events, 7.5 us)
Async XLA Ops:
  0.0 24.7 %copy-start = (bf16[1,3584,256]{2,1,0:T(8,128)(2,1)S(1)}, bf16[1,3584,256]{2,1,0:T(8,128)(2,1)}, u32[]{:S(2)}) copy-start(bf16[1,3584,256]{2,1,0:T(8,128)(2,1)} %param.9) | copy-start | bytes 5505028
  0.0 12.0 %copy-start.3 = (s32[64,8]{0,1:T(8,128)S(1)}, s32[64,8]{0,1:T(8,128)}, u32[]{:S(2)}) copy-start(s32[64,8]{0,1:T(8,128)} %param.7) | copy-start | bytes 6148
  0.0 12.0 %copy-start.4 = (s32[64,8]{0,1:T(8,128)S(1)}, s32[64,8]{0,1:T(8,128)}, u32[]{:S(2)}) copy-start(s32[64,8]{0,1:T(8,128)} %param.8) | copy-start | bytes 6148
  2.6 7.5 %collective-permute-start = (bf16[24,3584]{1,0:T(8,128)(2,1)S(1)}, bf16[24,3584]{1,0:T(8,128)(2,1)S(1)}, u32[]{:S(2)}, u32[]{:S(2)}) collective-permute-start(bf16[24,3584]{1,0:T(8,128)(2,1)S(1)} %get-tuple-element.28), channel_id=1, source_target_pairs={{0,4},{4,0},{8,12},{12,8},{1,5},{5,1},{9,13},{13,9},{2,6},{6,2},{1... | collective-permute-start | bytes 516104 | tf_op jit(solution)/shard_map/ppermute | solution.py:192
  5.7 8.2 %collective-permute-start.1 = (bf16[24,3584]{1,0:T(8,128)(2,1)S(1)}, bf16[24,3584]{1,0:T(8,128)(2,1)S(1)}, u32[]{:S(2)}, u32[]{:S(2)}) collective-permute-start(bf16[24,3584]{1,0:T(8,128)(2,1)S(1)} %get-tuple-element.25), channel_id=1, source_target_pairs={{0,2},{1,3},{2,0},{3,1},{4,6},{5,7},{6,4},{7,5},{8,10},{9,11},{10,... | collective-permute-start | bytes 516104 | tf_op jit(solution)/shard_map/ppermute | solution.py:195
  7.2 20.9 %collective-permute-start.7 = (bf16[24,3584]{1,0:T(8,128)(2,1)S(1)}, bf16[24,3584]{1,0:T(8,128)(2,1)S(1)}, u32[]{:S(2)}, u32[]{:S(2)}) collective-permute-start(bf16[24,3584]{1,0:T(8,128)(2,1)S(1)} %get-tuple-element.26), channel_id=1, source_target_pairs={{0,12},{4,8},{8,4},{12,0},{1,13},{5,9},{9,5},{13,1},{2,14},{6,10},... | collective-permute-start | bytes 516104 | tf_op jit(solution)/shard_map/ppermute | solution.py:192
  9.7 15.0 %collective-permute-start.5 = (bf16[24,3584]{1,0:T(8,128)(2,1)S(1)}, bf16[24,3584]{1,0:T(8,128)(2,1)S(1)}, u32[]{:S(2)}, u32[]{:S(2)}) collective-permute-start(bf16[24,3584]{1,0:T(8,128)(2,1)S(1)} %get-tuple-element.27), channel_id=1, source_target_pairs={{0,8},{4,12},{8,0},{12,4},{1,9},{5,13},{9,1},{13,5},{2,10},{6,14},... | collective-permute-start | bytes 516104 | tf_op jit(solution)/shard_map/ppermute | solution.py:192
  10.1 5.6 %collective-permute-start.2 = (bf16[24,3584]{1,0:T(8,128)(2,1)S(1)}, bf16[24,3584]{1,0:T(8,128)(2,1)S(1)}, u32[]{:S(2)}, u32[]{:S(2)}) collective-permute-start(bf16[24,3584]{1,0:T(8,128)(2,1)S(1)} %collective-permute-done), channel_id=1, source_target_pairs={{0,2},{1,3},{2,0},{3,1},{4,6},{5,7},{6,4},{7,5},{8,10},{9,11},{10,... | collective-permute-start | bytes 516104 | tf_op jit(solution)/shard_map/ppermute | solution.py:195
  15.7 10.9 %collective-permute-start.3 = (bf16[96,3584]{1,0:T(8,128)(2,1)S(1)}, bf16[96,3584]{1,0:T(8,128)(2,1)S(1)}, u32[]{:S(2)}, u32[]{:S(2)}) collective-permute-start(bf16[96,3584]{1,0:T(8,128)(2,1)S(1)} %pad_maximum_fusion.2), channel_id=1, source_target_pairs={{0,1},{1,0},{2,3},{3,2},{4,5},{5,4},{6,7},{7,6},{8,9},{9,8},{10,11... | collective-permute-start | bytes 2064392 | tf_op jit(solution)/shard_map/ppermute | solution.py:195
  24.7 1.5 %copy-start.1 = (bf16[1,3584,256]{2,1,0:T(8,128)(2,1)S(1)}, bf16[1,3584,256]{2,1,0:T(8,128)(2,1)}, u32[]{:S(2)}) copy-start(bf16[1,3584,256]{2,1,0:T(8,128)(2,1)} %param.10) | copy-start | bytes 5505028
  27.5 5.8 %collective-permute-start.4 = (bf16[2,2,48,256]{3,2,1,0:T(8,128)(2,1)S(1)}, bf16[2,2,48,256]{3,2,1,0:T(8,128)(2,1)S(1)}, u32[]{:S(2)}, u32[]{:S(2)}) collective-permute-start(bf16[2,2,48,256]{3,2,1,0:T(8,128)(2,1)S(1)} %pad_maximum_fusion.15), channel_id=1, source_target_pairs={{0,2},{1,3},{2,0},{3,1},{4,6},{5,7},{6,4},{7,5},{8,10},{9,11},{10,... | collective-permute-start | bytes 294920 | tf_op jit(solution)/shard_map/ppermute | solution.py:195
  28.1 10.3 %collective-permute-start.8 = (bf16[24,3584]{1,0:T(8,128)(2,1)S(1)}, bf16[24,3584]{1,0:T(8,128)(2,1)S(1)}, u32[]{:S(2)}, u32[]{:S(2)}) collective-permute-start(bf16[24,3584]{1,0:T(8,128)(2,1)S(1)} %collective-permute-done.7), channel_id=1, source_target_pairs={{0,2},{1,3},{2,0},{3,1},{4,6},{5,7},{6,4},{7,5},{8,10},{9,11},{10,... | collective-permute-start | bytes 516104 | tf_op jit(solution)/shard_map/ppermute | solution.py:195
  29.7 8.7 %collective-permute-start.6 = (bf16[24,3584]{1,0:T(8,128)(2,1)S(1)}, bf16[24,3584]{1,0:T(8,128)(2,1)S(1)}, u32[]{:S(2)}, u32[]{:S(2)}) collective-permute-start(bf16[24,3584]{1,0:T(8,128)(2,1)S(1)} %collective-permute-done.5), channel_id=1, source_target_pairs={{0,2},{1,3},{2,0},{3,1},{4,6},{5,7},{6,4},{7,5},{8,10},{9,11},{10,... | collective-permute-start | bytes 516104 | tf_op jit(solution)/shard_map/ppermute | solution.py:195
  38.4 3.4 %collective-permute-start.10 = (bf16[96,3584]{1,0:T(8,128)(2,1)S(1)}, bf16[96,3584]{1,0:T(8,128)(2,1)S(1)}, u32[]{:S(2)}, u32[]{:S(2)}) collective-permute-start(bf16[96,3584]{1,0:T(8,128)(2,1)S(1)} %constant_dynamic-update-slice_fusion), channel_id=1, source_target_pairs={{0,1},{1,0},{2,3},{3,2},{4,5},{5,4},{6,7},{7,6},{8,9},{9,8},{10,11... | collective-permute-start | bytes 2064392 | tf_op jit(solution)/shard_map/ppermute | solution.py:195
  39.0 2.0 %collective-permute-start.9 = (bf16[192,512]{1,0:T(8,128)(2,1)S(1)}, bf16[192,512]{1,0:T(8,128)(2,1)S(1)}, u32[]{:S(2)}, u32[]{:S(2)}) collective-permute-start(bf16[192,512]{1,0:T(8,128)(2,1)S(1)} %bitcast.187), channel_id=1, source_target_pairs={{0,1},{1,0},{2,3},{3,2},{4,5},{5,4},{6,7},{7,6},{8,9},{9,8},{10,11... | collective-permute-start | bytes 589832 | tf_op jit(solution)/shard_map/ppermute | solution.py:195
  42.8 5.7 %collective-permute-start.12 = (bf16[2,2,48,256]{3,2,1,0:T(8,128)(2,1)S(1)}, bf16[2,2,48,256]{3,2,1,0:T(8,128)(2,1)S(1)}, u32[]{:S(2)}, u32[]{:S(2)}) collective-permute-start(bf16[2,2,48,256]{3,2,1,0:T(8,128)(2,1)S(1)} %pad_maximum_fusion.16), channel_id=1, source_target_pairs={{0,2},{1,3},{2,0},{3,1},{4,6},{5,7},{6,4},{7,5},{8,10},{9,11},{10,... | collective-permute-start | bytes 294920 | tf_op jit(solution)/shard_map/ppermute | solution.py:195
  43.6 7.7 %collective-permute-start.11 = (bf16[2,2,24,896]{3,2,0,1:T(8,128)(2,1)S(1)}, bf16[2,2,24,896]{3,2,0,1:T(8,128)(2,1)S(1)}, u32[]{:S(2)}, u32[]{:S(2)}) collective-permute-start(bf16[2,2,24,896]{3,2,0,1:T(8,128)(2,1)S(1)} %pad_maximum_fusion.9), channel_id=1, source_target_pairs={{0,2},{1,3},{2,0},{3,1},{4,6},{5,7},{6,4},{7,5},{8,10},{9,11},{10,... | collective-permute-start | bytes 516104 | tf_op jit(solution)/shard_map/ppermute | solution.py:195
  48.5 3.0 %collective-permute-start.14 = (bf16[192,512]{1,0:T(8,128)(2,1)S(1)}, bf16[192,512]{1,0:T(8,128)(2,1)S(1)}, u32[]{:S(2)}, u32[]{:S(2)}) collective-permute-start(bf16[192,512]{1,0:T(8,128)(2,1)S(1)} %bitcast.189), channel_id=1, source_target_pairs={{0,1},{1,0},{2,3},{3,2},{4,5},{5,4},{6,7},{7,6},{8,9},{9,8},{10,11... | collective-permute-start | bytes 589832 | tf_op jit(solution)/shard_map/ppermute | solution.py:195
  51.4 9.2 %collective-permute-start.13 = (bf16[2,2,24,896]{3,2,1,0:T(8,128)(2,1)S(1)}, bf16[2,2,24,896]{3,2,1,0:T(8,128)(2,1)S(1)}, u32[]{:S(2)}, u32[]{:S(2)}) collective-permute-start(bf16[2,2,24,896]{3,2,1,0:T(8,128)(2,1)S(1)} %pad_maximum_fusion.10), channel_id=1, source_target_pairs={{0,4},{4,0},{8,12},{12,8},{1,5},{5,1},{9,13},{13,9},{2,6},{6,2},{1... | collective-permute-start | bytes 516104 | tf_op jit(solution)/shard_map/ppermute | solution.py:192
  52.4 13.3 %collective-permute-start.15 = (bf16[2,24,896]{2,1,0:T(8,128)(2,1)S(1)}, bf16[2,24,896]{2,1,0:T(8,128)(2,1)S(1)}, u32[]{:S(2)}, u32[]{:S(2)}) collective-permute-start(bf16[2,24,896]{2,1,0:T(8,128)(2,1)S(1)} %get-tuple-element.40), channel_id=1, source_target_pairs={{0,8},{4,12},{8,0},{12,4},{1,9},{5,13},{9,1},{13,5},{2,10},{6,14},... | collective-permute-start | bytes 258056 | tf_op jit(solution)/shard_map/ppermute | solution.py:192
  55.8 11.8 %collective-permute-start.16 = (bf16[2,24,896]{2,1,0:T(8,128)(2,1)S(1)}, bf16[2,24,896]{2,1,0:T(8,128)(2,1)S(1)}, u32[]{:S(2)}, u32[]{:S(2)}) collective-permute-start(bf16[2,24,896]{2,1,0:T(8,128)(2,1)S(1)} %get-tuple-element.39), channel_id=1, source_target_pairs={{0,10},{1,11},{2,8},{3,9},{4,14},{5,15},{6,12},{7,13},{8,2},{9,3},... | collective-permute-start | bytes 258056 | tf_op jit(solution)/shard_map/ppermute | solution.py:203
  56.1 11.5 %collective-permute-start.17 = (bf16[2,24,896]{2,1,0:T(8,128)(2,1)S(1)}, bf16[2,24,896]{2,1,0:T(8,128)(2,1)S(1)}, u32[]{:S(2)}, u32[]{:S(2)}) collective-permute-start(bf16[2,24,896]{2,1,0:T(8,128)(2,1)S(1)} %get-tuple-element.38), channel_id=1, source_target_pairs={{0,12},{4,8},{8,4},{12,0},{1,13},{5,9},{9,5},{13,1},{2,14},{6,10},... | collective-permute-start | bytes 258056 | tf_op jit(solution)/shard_map/ppermute | solution.py:192
  58.4 9.2 %collective-permute-start.18 = (bf16[2,24,896]{2,1,0:T(8,128)(2,1)S(1)}, bf16[2,24,896]{2,1,0:T(8,128)(2,1)S(1)}, u32[]{:S(2)}, u32[]{:S(2)}) collective-permute-start(bf16[2,24,896]{2,1,0:T(8,128)(2,1)S(1)} %get-tuple-element.37), channel_id=1, source_target_pairs={{0,14},{1,15},{2,12},{3,13},{4,10},{5,11},{6,8},{7,9},{8,6},{9,7},... | collective-permute-start | bytes 258056 | tf_op jit(solution)/shard_map/ppermute | solution.py:203
  67.8 1.7 %collective-permute-start.19 = (bf16[8,24,896]{2,1,0:T(8,128)(2,1)S(1)}, bf16[8,24,896]{2,1,0:T(8,128)(2,1)S(1)}, u32[]{:S(2)}, u32[]{:S(2)}) collective-permute-start(bf16[8,24,896]{2,1,0:T(8,128)(2,1)S(1)} %get-tuple-element.53), channel_id=1, source_target_pairs={{0,1},{1,0},{2,3},{3,2},{4,5},{5,4},{6,7},{7,6},{8,9},{9,8},{10,11... | collective-permute-start | bytes 1032200 | tf_op jit(solution)/shard_map/ppermute | solution.py:195
  70.2 0.9 %copy-start.2 = (f32[64,3584]{1,0:T(8,128)}, f32[64,3584]{1,0:T(8,128)S(1)}, u32[]{:S(2)}) copy-start(f32[64,3584]{1,0:T(8,128)S(1)} %fusion.21) | copy-start | bytes 2752516
